TPU v7x, 32 devices: a whole 2x2x4 slice. The times are simulated.
32 devices in a mesh: groups: 2 (over y), ex: 8 (over z, x), dim: 2 (over core).
Axes of the slice: x: 2, y: 2, z: 4, core: 2. Of those that a mesh axis runs over, the one named last changes fastest.
Arguments:
- queries: bfloat16 [8, 64, 16384], P('ex', None, 'dim'), may hold values from -0.078125 to 0.078125
- codes: bfloat16 [4096, 16384], P(('groups', 'ex'), 'dim'), parts along dimension 0, may hold values from -3.75 to 3.75, as said below
- exponents: int32 [4096, 128], P(('groups', 'ex'), 'dim'), parts along dimension 0, may hold values from -3 to 0
- example_ids: int32 [16, 256], P(('groups', 'ex')), parts along dimension 0, may hold values from 0 to 255, each once within a row
Outputs:
- scores: float32 [8, 64, 4096], P(None, 'dim', ('groups', 'ex')), parts along dimension 2
There are 2 independent parts, one for each index of `groups`. A program takes and returns all parts, laid end to end along the dimension named above; an argument that names none is the same for every part. Nothing has to cross between parts.
Inputs may be any that keep to these rules, and one draw needn't show every extreme that they name: `example_ids`: each row is a permutation of 0 to 255. `codes`: every value is an 8-bit e4m3 float of the form sign * (1 + m / 8) * 2 ** e with whole m from 0 to 7 and whole e from -3 to 1.
All inputs are finite; a program needn't handle non-finite values.
Results may differ from a plain program's by a relative error of at most 0.0003.
Values may be sent and summed in bfloat16 or wider, within the bound.
No kernel may reach another device: no remote copies, remote signals or barrier semaphores. Data moves between devices by JAX's collectives and lax.ppermute only.
A program may use at most 64 MiB of HBM per device.

v0:
```python
import jax
import jax.numpy as jnp
from jax import lax
from jax.sharding import PartitionSpec as P

BLOCK = 128


def dequantize(codes, exponents):
    rows, width = codes.shape
    blocks = width // BLOCK
    scaled = (
        codes.reshape(rows, blocks, BLOCK).astype(jnp.float32)
        * jnp.exp2(exponents.astype(jnp.float32))[:, :, None]
    )
    return scaled.astype(jnp.bfloat16).reshape(rows, width)


def shards(queries, codes, exponents, example_ids):
    grads = dequantize(codes, exponents)
    partial_scores = jnp.einsum(
        "nho,so->nhs",
        lax.all_gather(queries, "ex", axis=0, tiled=True),
        grads,
        preferred_element_type=jnp.float32,
    )
    raw = lax.psum_scatter(partial_scores, "dim", scatter_dimension=1, tiled=True)
    count = example_ids.shape[1]
    placement_table = (
        example_ids[0][:, None] == jnp.arange(count, dtype=jnp.int32)[None, :]
    ).astype(jnp.float32)
    return jnp.einsum("bqe,em->bqm", raw, placement_table, precision=lax.Precision.HIGHEST)


def solution(mesh):
    placed = (
        P("ex", None, "dim"),
        P(("groups", "ex"), "dim"),
        P(("groups", "ex"), "dim"),
        P(("groups", "ex"), None),
    )
    return jax.shard_map(
        shards,
        mesh=mesh,
        in_specs=placed,
        out_specs=P(None, "dim", ("groups", "ex")),
        check_vma=False,
    )
```

profile of v0, /device:TPU:0, one launch (start us, length us, event | category | flops | bytes accessed | tf_op | source)
XLA Modules:
  0.0 164.3 jit_solution(8810323169155778939)
XLA Ops:
  6.5 0.0 all-gather.2.cloned.1.call-start
  6.5 0.7 all-gather.2.cloned.1.call-update
  7.3 0.0 reduce-scatter.2.cloned.1.call-start
  7.3 0.9 multiply_exponential_fusion
  8.2 0.1 copy.6
  8.3 128.9 %all-gather.2.cloned.1.call-done = bf16[8,64,8192]{2,1,0:T(8,128)(2,1)} async-done(((bf16[1,64,8192]{2,1,0:T(8,128)(2,1)}), bf16[8,64,8192]{2,1,0:T(8,128)(2,1)}) %all-gather.2.cloned.1.call-update) | async-done | bytes 8388624 | tf_op jit(solution)/shard_map/all_gather | solution.py:23
  137.1 0.0 copy-start.1
  137.1 2.3 %mul.11 = f32[256,64,128]{2,1,0:T(8,128)S(1)} broadcast(f32[256,64]{1,0:T(8,128)S(1)} %copy.6), dimensions={0,1} | broadcast | bytes 8454144 | tf_op jit(solution)/shard_map/mul | solution.py:13
  139.4 1.1 copy-done.1
  140.5 0.0 copy-start
  140.5 8.6 %fusion.4 = f32[8,64,256]{2,1,0:T(8,128)} fusion(bf16[8,64,8192]{2,1,0:T(8,128)(2,1)S(1)} %copy-done.1, f32[32,8,64,128]{3,2,1,0:T(8,128)S(1)} %bitcast.23, bf16[256,8192]{1,0:T(8,128)(2,1)} %param.5), kind=kOutput, calls=%fused_computation.4 | convolution fusion | flops 2153775104 | bytes 21495808 | tf_op jit(solution)/shard_map/nho,so->nhs/dot_general | solution.py:21
  149.2 0.0 reduce-scatter.2.cloned.1.call-update
  149.2 6.3 %reduce-scatter.2.cloned.1.call-done = f32[8,32,256]{2,1,0:T(8,128)} async-done(((f32[8,64,256]{2,1,0:T(8,128)}), f32[8,32,256]{2,1,0:T(8,128)}) %reduce-scatter.2.cloned.1.call-update) | async-done | bytes 262160 | tf_op jit(solution)/shard_map/reduce_scatter | solution.py:27
  155.5 0.0 copy-done
  155.5 2.0 %fusion.8 = f32[8,32,256]{2,1,0:T(8,128)} fusion(f32[8,32,256]{2,1,0:T(8,128)} %reduce-scatter.2.cloned.1.call-done, s32[256]{0:T(256)S(1)} %bitcast.24), kind=kOutput, calls=%fused_computation.7 | convolution fusion | flops 201392128 | bytes 525312 | tf_op jit(solution)/shard_map/bqe,em->bqm/dot_general | solution.py:32
Async XLA Ops:
  6.5 130.6 %all-gather.2.cloned.1.call-start = ((), (), s32[]{:S(2)}) async-start(), calls=%async_computation.1 | async-start | bytes 9437184 | tf_op jit(solution)/shard_map/all_gather | solution.py:23
  7.3 148.2 %reduce-scatter.2.cloned.1.call-start = ((), (), s32[]{:S(2)}) async-start(), calls=%async_computation.2 | async-start | bytes 786432 | tf_op jit(solution)/shard_map/reduce_scatter | solution.py:27
  137.1 3.4 %copy-start.1 = (bf16[8,64,8192]{2,1,0:T(8,128)(2,1)S(1)}, bf16[8,64,8192]{2,1,0:T(8,128)(2,1)}, u32[]{:S(2)}) copy-start(bf16[8,64,8192]{2,1,0:T(8,128)(2,1)} %all-gather.2.cloned.1.call-done) | copy-start | bytes 25165828
  140.5 15.0 %copy-start = (s32[1,256]{1,0:T(1,128)S(1)}, s32[1,256]{1,0:T(1,128)}, u32[]{:S(2)}) copy-start(s32[1,256]{1,0:T(1,128)} %param.7) | copy-start | bytes 3076
Sparse Core Ops, SparseCore 0:
  9.5 127.6 all-gather.1
  149.3 6.1 reduce-scatter.1
where the time goes:
time: 165 us; the launch traced here: 164 us
  waiting for transfers between devices  136 us (82%)
  between operations  13.4 us (8%)
  matrix products  10.7 us (6%)
  local copies, waits for them, and re-layouts  3.47 us (2%)
    all_gather x1, waiting for transfers between devices, shards(): lax.all_gather(queries, 'ex', axis=0, tiled=True)  129 us
    dot_general x1, matrix products, shards(): jnp.einsum('nho,so->nhs', lax.all_gather(queries, 'ex', axis=0, tiled=Tru...  8.65 us
    reduce_scatter x1, waiting for transfers between devices, shards(): lax.psum_scatter(partial_scores, 'dim', scatter_dimension=1, tiled=True)  6.28 us
  transfers between devices with their start and end apart: 2, of which 2 were waited for; matrix products, arithmetic and copies ran while one was open for 1% of the time, Pallas kernels for 0%

commit v1 on v0

v1 whole, which is shorter than its diff:
```python
import functools

import jax
import jax.numpy as jnp
from jax import lax
from jax.experimental import pallas as pl
from jax.experimental.pallas import tpu as pltpu
from jax.sharding import PartitionSpec as P

BLOCK = 128
SENT_CHUNKS = 2
QUERY_CHUNKS = 2


def fast_length(mesh):
    line = list(mesh.devices[0, :, 0])
    size = len(line)
    if size < 2 or not all(hasattr(device, "coords") for device in line):
        return 2 if size % 2 == 0 else size

    def moved(a, b):
        return tuple(i for i, (p, q) in enumerate(zip(a.coords, b.coords)) if p != q)

    along = moved(line[0], line[1])
    length = 2
    while length < size and moved(line[0], line[length]) == along:
        length += 1
    return length if size % length == 0 else size


def scale_kernel(half_ref, codes_ref, scales_ref, out_ref):
    for block in range(codes_ref.shape[1] // BLOCK):
        columns = pl.ds(block * BLOCK, BLOCK)
        out_ref[:, columns] = codes_ref[:, columns] * scales_ref[:, block : block + 1].astype(jnp.bfloat16)


def dequantize(codes, scales, half, first, rows, parts):
    width = codes.shape[1] // parts
    tile = min(rows, 64)
    return pl.pallas_call(
        scale_kernel,
        out_shape=jax.ShapeDtypeStruct((rows, width), jnp.bfloat16),
        grid_spec=pltpu.PrefetchScalarGridSpec(
            num_scalar_prefetch=1,
            grid=(rows // tile,),
            in_specs=[
                pl.BlockSpec((tile, width), lambda i, half: (first // tile + i, half[0])),
                pl.BlockSpec((tile, width // BLOCK), lambda i, half: (first // tile + i, 0)),
            ],
            out_specs=pl.BlockSpec((tile, width), lambda i, half: (i, 0)),
        ),
        compiler_params=pltpu.CompilerParams(vmem_limit_bytes=16 << 20),
        cost_estimate=pl.CostEstimate(flops=rows * width, bytes_accessed=4 * rows * width, transcendentals=0),
        name="scale_codes",
    )(half, codes, scales)


def place_kernel(rows, order_ref, ids_ref, own_ref, received_ref, out_ref):
    raw = own_ref[...] + received_ref[...]
    count = raw.shape[1]
    slots = lax.broadcasted_iota(jnp.int32, (count, count), 0)
    table = (slots == jnp.broadcast_to(ids_ref[...], (count, count))).astype(jnp.float32)
    placed = lax.dot_general(
        raw, table, (((1,), (1,)), ((), ())),
        precision=lax.Precision.HIGHEST, preferred_element_type=jnp.float32,
    )
    for j in range(raw.shape[0] // rows):
        out_ref[order_ref[j]] = placed[j * rows : (j + 1) * rows]


def place(order, ids, own, received, rows):
    vmem = pl.BlockSpec(memory_space=pltpu.VMEM)
    return pl.pallas_call(
        functools.partial(place_kernel, rows),
        out_shape=jax.ShapeDtypeStruct((own.shape[0] // rows, rows, own.shape[1]), jnp.float32),
        in_specs=[pl.BlockSpec(memory_space=pltpu.SMEM), vmem, vmem, vmem],
        out_specs=vmem,
        compiler_params=pltpu.CompilerParams(vmem_limit_bytes=16 << 20),
        name="place_scores",
    )(order, ids, own, received)


def line_arrivals(length):
    table = []
    for p in range(length):
        arrivals = []
        for s in range(1, length):
            if p - s >= 0:
                arrivals.append(("up", s, p - s))
            if p + s < length:
                arrivals.append(("down", s, p + s))
        table.append(arrivals)
    return table


def chosen(position, where, value, other):
    return jnp.where(functools.reduce(jnp.logical_or, [position == p for p in where]), value, other)


def gather_line(block, position, length, stride, total):
    if length == 1:
        return [block]

    def shift(value, by):
        pairs = [
            (i, i + by * stride)
            for i in range(total)
            if 0 <= (i // stride) % length + by < length
        ]
        return lax.ppermute(value, "ex", pairs)

    if length == 2:
        pairs = [(i, i + stride if (i // stride) % 2 == 0 else i - stride) for i in range(total)]
        return [block, lax.ppermute(block, "ex", pairs)]
    came = {("up", 0): block, ("down", 0): block}
    for s in range(1, length):
        came["up", s] = shift(came["up", s - 1], 1)
        came["down", s] = shift(came["down", s - 1], -1)
    table = line_arrivals(length)
    blocks = [block]
    for j in range(length - 1):
        ways = {}
        for p in range(length):
            ways.setdefault(table[p][j][:2], []).append(p)
        (way, _), *rest = sorted(ways.items())
        value = came[way]
        for way, where in rest:
            value = chosen(position, where, came[way], value)
        blocks.append(value)
    return blocks


def line_sources(position, length):
    if length == 2:
        return [position, 1 - position]
    table = line_arrivals(length)
    sources = [position]
    for j in range(length - 1):
        value = jnp.int32(table[0][j][2])
        for p in range(1, length):
            value = jnp.where(position == p, table[p][j][2], value)
        sources.append(value)
    return sources


def shards(fast, parts, total, queries, codes, exponents, example_ids):
    part = lax.axis_index("groups")
    here = lax.axis_index("ex")
    half = lax.axis_index("dim")
    slow = total // fast
    rows, width = queries.shape[1], queries.shape[2] // parts
    count = codes.shape[0]
    blocks = exponents.shape[1] // parts

    mine = lax.dynamic_slice(queries[0], (0, part * width), (rows, width))
    chunks = QUERY_CHUNKS if rows % (16 * QUERY_CHUNKS) == 0 else 1
    step = rows // chunks
    arrived = []
    for c in range(chunks):
        column = gather_line(mine[c * step : (c + 1) * step], here // fast, slow, fast, total)
        arrived.append([b for block in column for b in gather_line(block, here % fast, fast, 1, total)])

    scales = (jnp.int32(1) << (exponents + 3)).astype(jnp.float32) * 0.125
    other = 1 - part
    sent_scales = lax.dynamic_slice(scales, (0, other * blocks), (count, blocks))
    kept_scales = lax.dynamic_slice(scales, (0, part * blocks), (count, blocks))
    swap = [(i, parts - 1 - i) for i in range(parts)]
    piece = count // SENT_CHUNKS
    theirs = [
        lax.ppermute(dequantize(codes, sent_scales, other[None], c * piece, piece, parts), "groups", swap)
        for c in range(SENT_CHUNKS)
    ]
    ours = dequantize(codes, kept_scales, part[None], 0, count, parts)

    def score(block, grads):
        return lax.dot_general(block, grads, (((1,), (1,)), ((), ())), preferred_element_type=jnp.float32)

    sums = []
    for j in range(total):
        for c in range(chunks):
            sums.append(jnp.concatenate([score(arrived[c][j], g) for g in [ours] + theirs], axis=1))
    sums = jnp.stack(sums).reshape(total, 2, rows // 2, 2 * count)

    keep = lax.dynamic_index_in_dim(sums, half, 1, keepdims=False)
    send = lax.dynamic_index_in_dim(sums, 1 - half, 1, keepdims=False)
    sums = keep + lax.ppermute(send, "dim", [(0, 1), (1, 0)])
    own, given = sums[..., :count], sums[..., count:]
    received = lax.ppermute(given, "groups", swap)

    order = jnp.stack([
        jnp.asarray(s * fast + f, jnp.int32)
        for s in line_sources(here // fast, slow)
        for f in line_sources(here % fast, fast)
    ])
    flat = (total * (rows // 2), count)
    return place(order, example_ids, own.reshape(flat), received.reshape(flat), rows // 2)


def solution(mesh):
    placed = (
        P("ex", None, "dim"),
        P(("groups", "ex"), "dim"),
        P(("groups", "ex"), "dim"),
        P(("groups", "ex"), None),
    )
    return jax.shard_map(
        functools.partial(shards, fast_length(mesh), mesh.shape["groups"], mesh.shape["ex"]),
        mesh=mesh,
        in_specs=placed,
        out_specs=P(None, "dim", ("groups", "ex")),
        check_vma=False,
    )
```

time: 165 us -> 122 us (0.74)
  waiting for transfers between devices: 136 us -> 24.3 us
  starting transfers between devices: 0.04 us -> 48.9 us
  matrix products: 10.7 us -> 32.3 us
  between operations: 13.4 us -> 0.5 us
  local copies, waits for them, and re-layouts: 3.47 us -> 8.36 us
  Pallas kernels: 0 us -> 4.15 us
  other arithmetic: 0.86 us -> 2.58 us
    all_gather x1 -> x0, waiting for transfers between devices: 129 us -> none  [shards(): lax.all_gather(queries, 'ex', axis=0, tiled=True)]
    ppermute x0 -> x24, starting transfers between devices: none -> 48.9 us  [the longest x12 36.7 us: shift(): return lax.ppermute(value, 'ex', pairs)]
    ppermute x0 -> x24, waiting for transfers between devices: none -> 24.3 us  [the longest x2 12.5 us: shards(): lax.ppermute(dequantize(codes, sent_scales, other[None], c * piece, piece...]
    dot_general x2 -> x48, matrix products: 10.7 us -> 32.3 us  [score(): lax.dot_general(block, grads, (((1,), (1,)), ((), ())), preferred_element...]
    reduce_scatter x1 -> x0, waiting for transfers between devices: 6.28 us -> none  [shards(): lax.psum_scatter(partial_scores, 'dim', scatter_dimension=1, tiled=True)]
    unnamed x4 -> x11, local copies, waits for them, and re-layouts: 1.08 us -> 6.31 us
    pallas_call x0 -> x4, Pallas kernels: none -> 4.15 us  [the longest x3 2.49 us: dequantize(): pl.pallas_call(scale_kernel, out_shape=jax.ShapeDtypeStruct((rows, width)...]
    mul x1 -> x0, local copies, waits for them, and re-layouts: 2.3 us -> none  [dequantize(): codes.reshape(rows, blocks, BLOCK).astype(jnp.float32)]
  transfers between devices with their start and end apart: 2 -> 24, of which waited for: 2 -> 5; matrix products, arithmetic and copies ran while one was open for 1% -> 28% of each run, Pallas kernels for 0% -> 2%
where the time goes in v1:
time: 122 us; the launch traced here: 121 us
  starting transfers between devices  48.9 us (40%)
  matrix products  32.3 us (26%)
  waiting for transfers between devices  24.3 us (20%)
  local copies, waits for them, and re-layouts  8.36 us (7%)
  Pallas kernels  4.15 us (3%)
  other arithmetic  2.58 us (2%)
    ppermute x12, starting transfers between devices, shift(): return lax.ppermute(value, 'ex', pairs)  36.7 us
    dot_general x48, matrix products, score(): lax.dot_general(block, grads, (((1,), (1,)), ((), ())), preferred_element...  32.3 us
    ppermute x2, waiting for transfers between devices, shards(): lax.ppermute(dequantize(codes, sent_scales, other[None], c * piece, piece...  12.5 us
    ppermute x8, starting transfers between devices, gather_line(): return [block, lax.ppermute(block, 'ex', pairs)]  8.43 us
    ppermute x1, waiting for transfers between devices, shards(): received = lax.ppermute(given, 'groups', swap)  6.74 us
    unnamed x11, local copies, waits for them, and re-layouts  6.31 us
    pallas_call x3, Pallas kernels, dequantize(): pl.pallas_call(scale_kernel, out_shape=jax.ShapeDtypeStruct((rows, width)...  2.49 us
  transfers between devices with their start and end apart: 24, of which 5 were waited for; matrix products, arithmetic and copies ran while one was open for 28% of the time, Pallas kernels for 2%

profile of v1, /device:TPU:0, one launch (start us, length us, event | category | flops | bytes accessed | tf_op | source)
XLA Modules:
  0.0 121.2 jit_solution(9627351203730938749)
XLA Ops:
  0.0 1.8 %dynamic-slice_bitcast_fusion.1 = (bf16[32,4096]{1,0:T(8,128)(2,1)S(1)}, bf16[32,4096]{1,0:T(8,128)(2,1)}) fusion(bf16[1,64,8192]{2,1,0:T(8,128)(2,1)} %param.4, s32[]{:T(128)S(6)} %add.75, s32[]{:T(128)S(6)} %select_n.126), kind=kLoop, calls=%fused_computation.2 | loop fusion | bytes 1048584 | tf_op jit(solution)/shard_map/slice | solution.py:160
  1.8 1.3 %collective-permute-start.7 = (bf16[32,4096]{1,0:T(8,128)(2,1)S(1)}, bf16[32,4096]{1,0:T(8,128)(2,1)}, u32[]{:S(2)}, u32[]{:S(2)}) collective-permute-start(bf16[32,4096]{1,0:T(8,128)(2,1)S(1)} %get-tuple-element.5), channel_id=1, source_target_pairs={{4,0},{6,2},{8,4},{10,6},{12,8},{14,10},{5,1},{7,3},{9,5},{11,7},{... | collective-permute-start | bytes 786440 | tf_op jit(solution)/shard_map/ppermute | solution.py:110
  3.1 6.3 %collective-permute-start.6 = (bf16[32,4096]{1,0:T(8,128)(2,1)S(1)}, bf16[32,4096]{1,0:T(8,128)(2,1)}, u32[]{:S(2)}, u32[]{:S(2)}) collective-permute-start(bf16[32,4096]{1,0:T(8,128)(2,1)S(1)} %get-tuple-element.5), channel_id=1, source_target_pairs={{0,4},{2,6},{4,8},{6,10},{8,12},{10,14},{1,5},{3,7},{5,9},{7,11},{... | collective-permute-start | bytes 786440 | tf_op jit(solution)/shard_map/ppermute | solution.py:110
  9.3 1.9 %collective-permute-start.3 = (bf16[32,4096]{1,0:T(8,128)(2,1)S(1)}, bf16[32,4096]{1,0:T(8,128)(2,1)}, u32[]{:S(2)}, u32[]{:S(2)}) collective-permute-start(bf16[32,4096]{1,0:T(8,128)(2,1)S(1)} %get-tuple-element.5), channel_id=1, source_target_pairs={{0,2},{2,0},{4,6},{6,4},{8,10},{10,8},{12,14},{14,12},{1,3},{3,1},... | collective-permute-start | bytes 786440 | tf_op jit(solution)/shard_map/ppermute | solution.py:114
  11.3 1.3 %collective-permute-start.5 = (bf16[32,4096]{1,0:T(8,128)(2,1)}, bf16[32,4096]{1,0:T(8,128)(2,1)}, u32[]{:S(2)}, u32[]{:S(2)}) collective-permute-start(bf16[32,4096]{1,0:T(8,128)(2,1)} %get-tuple-element.6), channel_id=1, source_target_pairs={{4,0},{6,2},{8,4},{10,6},{12,8},{14,10},{5,1},{7,3},{9,5},{11,7},{... | collective-permute-start | bytes 786440 | tf_op jit(solution)/shard_map/ppermute | solution.py:110
  12.5 5.3 %collective-permute-start.4 = (bf16[32,4096]{1,0:T(8,128)(2,1)}, bf16[32,4096]{1,0:T(8,128)(2,1)}, u32[]{:S(2)}, u32[]{:S(2)}) collective-permute-start(bf16[32,4096]{1,0:T(8,128)(2,1)} %get-tuple-element.6), channel_id=1, source_target_pairs={{0,4},{2,6},{4,8},{6,10},{8,12},{10,14},{1,5},{3,7},{5,9},{7,11},{... | collective-permute-start | bytes 786440 | tf_op jit(solution)/shard_map/ppermute | solution.py:110
  17.8 0.9 copy.6
  18.9 2.2 %copy-done = bf16[256,8192]{1,0:T(8,128)(2,1)S(1)} copy-done((bf16[256,8192]{1,0:T(8,128)(2,1)S(1)}, bf16[256,8192]{1,0:T(8,128)(2,1)}, u32[]{:S(2)}) %copy-start) | copy-done | bytes 4194328
  21.1 0.6 scale_codes.5
  21.7 0.6 scale_codes.4
  22.4 1.0 copy-done.2
  23.4 2.2 %copy-done.1 = bf16[256,8192]{1,0:T(8,128)(2,1)S(1)} copy-done((bf16[256,8192]{1,0:T(8,128)(2,1)S(1)}, bf16[256,8192]{1,0:T(8,128)(2,1)}, u32[]{:S(2)}) %copy-start.1) | copy-done | bytes 4194328
  25.6 1.2 %scale_codes.3 = bf16[256,4096]{1,0:T(8,128)(2,1)S(1)} custom-call(s32[1]{0:T(128)} %bitcast.9.half_ref, bf16[256,8192]{1,0:T(8,128)(2,1)S(1)} %copy-done.1, f32[256,32]{1,0:T(8,128)S(1)} %get-tuple-element.15.scales_ref), custom_call_target="tpu_custom_call" | custom-call | flops 1048576 | bytes 4194304 | tf_op jit(solution)/shard_map/scale_codes/pallas_call | solution.py:40
  26.8 0.7 fusion.20
  27.5 1.8 %fusion.17 = f32[32,256]{1,0:T(8,128)S(1)} fusion(bf16[32,4096]{1,0:T(8,128)(2,1)} %get-tuple-element.6, bf16[256,4096]{1,0:T(8,128)(2,1)S(1)} %scale_codes.3), kind=kOutput, calls=%fused_computation.46 | convolution fusion | flops 67108864 | bytes 2392064 | tf_op jit(solution)/shard_map/dot_general | solution.py:176
  29.5 1.3 %collective-permute-start.13 = (bf16[32,4096]{1,0:T(8,128)(2,1)}, bf16[32,4096]{1,0:T(8,128)(2,1)S(1)}, u32[]{:S(2)}, u32[]{:S(2)}) collective-permute-start(bf16[32,4096]{1,0:T(8,128)(2,1)} %collective-permute-done.7), channel_id=1, source_target_pairs={{4,0},{6,2},{8,4},{10,6},{12,8},{14,10},{5,1},{7,3},{9,5},{11,7},{... | collective-permute-start | bytes 786440 | tf_op jit(solution)/shard_map/ppermute | solution.py:110
  30.8 4.6 %collective-permute-start.12 = (bf16[32,4096]{1,0:T(8,128)(2,1)}, bf16[32,4096]{1,0:T(8,128)(2,1)S(1)}, u32[]{:S(2)}, u32[]{:S(2)}) collective-permute-start(bf16[32,4096]{1,0:T(8,128)(2,1)} %collective-permute-done.6), channel_id=1, source_target_pairs={{0,4},{2,6},{4,8},{6,10},{8,12},{10,14},{1,5},{3,7},{5,9},{7,11},{... | collective-permute-start | bytes 786440 | tf_op jit(solution)/shard_map/ppermute | solution.py:110
  35.3 1.7 %fusion.26 = f32[32,256]{1,0:T(8,128)S(1)} fusion(bf16[32,4096]{1,0:T(8,128)(2,1)} %collective-permute-done.3, bf16[256,4096]{1,0:T(8,128)(2,1)S(1)} %scale_codes.3), kind=kOutput, calls=%fused_computation.55 | convolution fusion | flops 67108864 | bytes 2392064 | tf_op jit(solution)/shard_map/dot_general | solution.py:176
  37.1 2.0 %collective-permute-start = (bf16[128,4096]{1,0:T(8,128)(2,1)S(1)}, bf16[128,4096]{1,0:T(8,128)(2,1)S(1)}, u32[]{:S(2)}, u32[]{:S(2)}) collective-permute-start(bf16[128,4096]{1,0:T(8,128)(2,1)S(1)} %copy-done.3), channel_id=1, source_target_pairs={{0,16},{16,0},{1,17},{17,1},{2,18},{18,2},{3,19},{19,3},{4,20},{20... | collective-permute-start | bytes 3145736 | tf_op jit(solution)/shard_map/ppermute | solution.py:170
  39.1 1.3 %collective-permute-start.11 = (bf16[32,4096]{1,0:T(8,128)(2,1)}, bf16[32,4096]{1,0:T(8,128)(2,1)S(1)}, u32[]{:S(2)}, u32[]{:S(2)}) collective-permute-start(bf16[32,4096]{1,0:T(8,128)(2,1)} %collective-permute-done.5), channel_id=1, source_target_pairs={{4,0},{6,2},{8,4},{10,6},{12,8},{14,10},{5,1},{7,3},{9,5},{11,7},{... | collective-permute-start | bytes 786440 | tf_op jit(solution)/shard_map/ppermute | solution.py:110
  40.4 4.6 %collective-permute-start.10 = (bf16[32,4096]{1,0:T(8,128)(2,1)}, bf16[32,4096]{1,0:T(8,128)(2,1)S(1)}, u32[]{:S(2)}, u32[]{:S(2)}) collective-permute-start(bf16[32,4096]{1,0:T(8,128)(2,1)} %collective-permute-done.4), channel_id=1, source_target_pairs={{0,4},{2,6},{4,8},{6,10},{8,12},{10,14},{1,5},{3,7},{5,9},{7,11},{... | collective-permute-start | bytes 786440 | tf_op jit(solution)/shard_map/ppermute | solution.py:110
  45.0 1.3 %collective-permute-start.19 = (bf16[32,4096]{1,0:T(8,128)(2,1)S(1)}, bf16[32,4096]{1,0:T(8,128)(2,1)S(1)}, u32[]{:S(2)}, u32[]{:S(2)}) collective-permute-start(bf16[32,4096]{1,0:T(8,128)(2,1)S(1)} %collective-permute-done.13), channel_id=1, source_target_pairs={{4,0},{6,2},{8,4},{10,6},{12,8},{14,10},{5,1},{7,3},{9,5},{11,7},{... | collective-permute-start | bytes 786440 | tf_op jit(solution)/shard_map/ppermute | solution.py:110
  46.3 4.6 %collective-permute-start.18 = (bf16[32,4096]{1,0:T(8,128)(2,1)S(1)}, bf16[32,4096]{1,0:T(8,128)(2,1)S(1)}, u32[]{:S(2)}, u32[]{:S(2)}) collective-permute-start(bf16[32,4096]{1,0:T(8,128)(2,1)S(1)} %collective-permute-done.12), channel_id=1, source_target_pairs={{0,4},{2,6},{4,8},{6,10},{8,12},{10,14},{1,5},{3,7},{5,9},{7,11},{... | collective-permute-start | bytes 786440 | tf_op jit(solution)/shard_map/ppermute | solution.py:110
  50.8 0.7 fusion.23
  51.7 1.3 %collective-permute-start.17 = (bf16[32,4096]{1,0:T(8,128)(2,1)S(1)}, bf16[32,4096]{1,0:T(8,128)(2,1)S(1)}, u32[]{:S(2)}, u32[]{:S(2)}) collective-permute-start(bf16[32,4096]{1,0:T(8,128)(2,1)S(1)} %collective-permute-done.11), channel_id=1, source_target_pairs={{4,0},{6,2},{8,4},{10,6},{12,8},{14,10},{5,1},{7,3},{9,5},{11,7},{... | collective-permute-start | bytes 786440 | tf_op jit(solution)/shard_map/ppermute | solution.py:110
  53.0 1.0 collective-permute-done.19
  54.0 3.8 %collective-permute-start.16 = (bf16[32,4096]{1,0:T(8,128)(2,1)S(1)}, bf16[32,4096]{1,0:T(8,128)(2,1)S(1)}, u32[]{:S(2)}, u32[]{:S(2)}) collective-permute-start(bf16[32,4096]{1,0:T(8,128)(2,1)S(1)} %collective-permute-done.10), channel_id=1, source_target_pairs={{0,4},{2,6},{4,8},{6,10},{8,12},{10,14},{1,5},{3,7},{5,9},{7,11},{... | collective-permute-start | bytes 786440 | tf_op jit(solution)/shard_map/ppermute | solution.py:110
  57.8 1.1 select_select_fusion
  58.9 2.0 %collective-permute-start.21 = (bf16[32,4096]{1,0:T(8,128)(2,1)S(1)}, bf16[32,4096]{1,0:T(8,128)(2,1)S(1)}, u32[]{:S(2)}, u32[]{:S(2)}) collective-permute-start(bf16[32,4096]{1,0:T(8,128)(2,1)S(1)} %get-tuple-element.9), channel_id=1, source_target_pairs={{0,2},{2,0},{4,6},{6,4},{8,10},{10,8},{12,14},{14,12},{1,3},{3,1},... | collective-permute-start | bytes 786440 | tf_op jit(solution)/shard_map/ppermute | solution.py:114
  60.9 0.7 fusion.56
  61.6 0.7 fusion.44
  62.5 1.9 %collective-permute-start.9 = (bf16[32,4096]{1,0:T(8,128)(2,1)S(1)}, bf16[32,4096]{1,0:T(8,128)(2,1)S(1)}, u32[]{:S(2)}, u32[]{:S(2)}) collective-permute-start(bf16[32,4096]{1,0:T(8,128)(2,1)S(1)} %get-tuple-element.14), channel_id=1, source_target_pairs={{0,2},{2,0},{4,6},{6,4},{8,10},{10,8},{12,14},{14,12},{1,3},{3,1},... | collective-permute-start | bytes 786440 | tf_op jit(solution)/shard_map/ppermute | solution.py:114
  64.5 1.1 select_select_fusion.1
  65.6 0.7 fusion.32
  66.3 0.7 fusion.53
  67.0 0.7 fusion.41
  67.8 0.7 fusion.29
  68.7 1.4 %fusion.18 = f32[32,128]{1,0:T(8,128)S(1)} fusion(bf16[32,4096]{1,0:T(8,128)(2,1)} %get-tuple-element.6, bf16[128,4096]{1,0:T(8,128)(2,1)S(1)} %collective-permute-done), kind=kOutput, calls=%fused_computation.47 | convolution fusion | flops 33554432 | bytes 1327104 | tf_op jit(solution)/shard_map/dot_general | solution.py:176
  70.1 12.4 %collective-permute-done.1 = bf16[128,4096]{1,0:T(8,128)(2,1)S(1)} collective-permute-done((bf16[128,4096]{1,0:T(8,128)(2,1)S(1)}, bf16[128,4096]{1,0:T(8,128)(2,1)S(1)}, u32[]{:S(2)}, u32[]{:S(2)}) %collective-permute-start.1) | collective-permute-done | bytes 1048608 | tf_op jit(solution)/shard_map/ppermute | solution.py:170
  82.5 1.6 %collective-permute-start.8 = (bf16[32,4096]{1,0:T(8,128)(2,1)S(1)}, bf16[32,4096]{1,0:T(8,128)(2,1)S(1)}, u32[]{:S(2)}, u32[]{:S(2)}) collective-permute-start(bf16[32,4096]{1,0:T(8,128)(2,1)S(1)} %get-tuple-element.13), channel_id=1, source_target_pairs={{0,2},{2,0},{4,6},{6,4},{8,10},{10,8},{12,14},{14,12},{1,3},{3,1},... | collective-permute-start | bytes 786440 | tf_op jit(solution)/shard_map/ppermute | solution.py:114
  84.2 1.4 %fusion.19 = f32[32,128]{1,0:T(8,128)S(1)} fusion(bf16[32,4096]{1,0:T(8,128)(2,1)} %get-tuple-element.6, bf16[128,4096]{1,0:T(8,128)(2,1)S(1)} %collective-permute-done.1), kind=kOutput, calls=%fused_computation.48 | convolution fusion | flops 33554432 | bytes 1327104 | tf_op jit(solution)/shard_map/dot_general | solution.py:176
  86.1 0.5 fusion.22
  87.0 0.5 fusion.25
  87.5 1.4 %fusion.27 = f32[32,128]{1,0:T(8,128)S(1)} fusion(bf16[32,4096]{1,0:T(8,128)(2,1)} %collective-permute-done.3, bf16[128,4096]{1,0:T(8,128)(2,1)S(1)} %collective-permute-done), kind=kOutput, calls=%fused_computation.56 | convolution fusion | flops 33554432 | bytes 1327104 | tf_op jit(solution)/shard_map/dot_general | solution.py:176
  88.9 1.4 %fusion.28 = f32[32,128]{1,0:T(8,128)S(1)} fusion(bf16[32,4096]{1,0:T(8,128)(2,1)} %collective-permute-done.3, bf16[128,4096]{1,0:T(8,128)(2,1)S(1)} %collective-permute-done.1), kind=kOutput, calls=%fused_computation.57 | convolution fusion | flops 33554432 | bytes 1327104 | tf_op jit(solution)/shard_map/dot_general | solution.py:176
  90.8 0.5 fusion.31
  91.8 0.5 fusion.42
  92.7 0.5 fusion.34
  95.0 0.7 fusion.35
  96.7 0.5 fusion.40
  97.2 0.7 fusion.38
  98.0 2.1 %collective-permute-done.14 = bf16[32,4096]{1,0:T(8,128)(2,1)S(1)} collective-permute-done((bf16[32,4096]{1,0:T(8,128)(2,1)S(1)}, bf16[32,4096]{1,0:T(8,128)(2,1)S(1)}, u32[]{:S(2)}, u32[]{:S(2)}) %collective-permute-start.14) | collective-permute-done | bytes 262176 | tf_op jit(solution)/shard_map/ppermute | solution.py:114
  101.0 0.7 fusion.47
  102.7 0.5 fusion.52
  103.2 0.9 fusion.50
  105.0 0.5 fusion.61
  105.5 0.5 fusion.58
  106.4 0.7 fusion.59
  107.7 0.5 fusion.64
  108.2 0.7 fusion.62
  109.1 1.9 %collective-permute-done.22 = f32[8,32,512]{2,1,0:T(8,128)S(1)} collective-permute-done((f32[8,32,512]{2,1,0:T(8,128)S(1)}, f32[8,32,512]{2,1,0:T(8,128)S(1)}, u32[]{:S(2)}, u32[]{:S(2)}) %collective-permute-start.22) | collective-permute-done | bytes 524320 | tf_op jit(solution)/shard_map/ppermute | solution.py:186
  111.1 1.6 %collective-permute-start.23 = (f32[8,32,256]{2,1,0:T(8,128)S(1)}, f32[8,32,256]{2,1,0:T(8,128)S(1)}, u32[]{:S(2)}, u32[]{:S(2)}) collective-permute-start(f32[8,32,256]{2,1,0:T(8,128)S(1)} %get-tuple-element.7), channel_id=1, source_target_pairs={{0,16},{16,0},{1,17},{17,1},{2,18},{18,2},{3,19},{19,3},{4,20},{20... | collective-permute-start | bytes 786440 | tf_op jit(solution)/shard_map/ppermute | solution.py:188
  112.8 6.7 %collective-permute-done.23 = f32[8,32,256]{2,1,0:T(8,128)S(1)} collective-permute-done((f32[8,32,256]{2,1,0:T(8,128)S(1)}, f32[8,32,256]{2,1,0:T(8,128)S(1)}, u32[]{:S(2)}, u32[]{:S(2)}) %collective-permute-start.23) | collective-permute-done | bytes 262176 | tf_op jit(solution)/shard_map/ppermute | solution.py:188
  119.5 1.7 %place_scores.1 = f32[8,32,256]{2,1,0:T(8,128)} custom-call(s32[8]{0:T(128)S(1)} %stack.86.order_ref, s32[1,256]{1,0:T(1,128)S(1)} %copy-done.4, f32[256,256]{1,0:T(8,128)S(1)} %bitcast.181, f32[256,256]{1,0:T(8,128)S(1)} %bitcast.182), custom_call_target="tpu_custom_call" | custom-call | tf_op jit(solution)/shard_map/place_scores/pallas_call | solution.py:73
  (72 shorter events, 10.1 us)
Async XLA Ops:
  1.8 27.5 %collective-permute-start.7 = (bf16[32,4096]{1,0:T(8,128)(2,1)S(1)}, bf16[32,4096]{1,0:T(8,128)(2,1)}, u32[]{:S(2)}, u32[]{:S(2)}) collective-permute-start(bf16[32,4096]{1,0:T(8,128)(2,1)S(1)} %get-tuple-element.5), channel_id=1, source_target_pairs={{4,0},{6,2},{8,4},{10,6},{12,8},{14,10},{5,1},{7,3},{9,5},{11,7},{... | collective-permute-start | bytes 786440 | tf_op jit(solution)/shard_map/ppermute | solution.py:110
  3.1 26.4 %collective-permute-start.6 = (bf16[32,4096]{1,0:T(8,128)(2,1)S(1)}, bf16[32,4096]{1,0:T(8,128)(2,1)}, u32[]{:S(2)}, u32[]{:S(2)}) collective-permute-start(bf16[32,4096]{1,0:T(8,128)(2,1)S(1)} %get-tuple-element.5), channel_id=1, source_target_pairs={{0,4},{2,6},{4,8},{6,10},{8,12},{10,14},{1,5},{3,7},{5,9},{7,11},{... | collective-permute-start | bytes 786440 | tf_op jit(solution)/shard_map/ppermute | solution.py:110
  9.3 21.4 %collective-permute-start.3 = (bf16[32,4096]{1,0:T(8,128)(2,1)S(1)}, bf16[32,4096]{1,0:T(8,128)(2,1)}, u32[]{:S(2)}, u32[]{:S(2)}) collective-permute-start(bf16[32,4096]{1,0:T(8,128)(2,1)S(1)} %get-tuple-element.5), channel_id=1, source_target_pairs={{0,2},{2,0},{4,6},{6,4},{8,10},{10,8},{12,14},{14,12},{1,3},{3,1},... | collective-permute-start | bytes 786440 | tf_op jit(solution)/shard_map/ppermute | solution.py:114
  11.3 25.8 %collective-permute-start.5 = (bf16[32,4096]{1,0:T(8,128)(2,1)}, bf16[32,4096]{1,0:T(8,128)(2,1)}, u32[]{:S(2)}, u32[]{:S(2)}) collective-permute-start(bf16[32,4096]{1,0:T(8,128)(2,1)} %get-tuple-element.6), channel_id=1, source_target_pairs={{4,0},{6,2},{8,4},{10,6},{12,8},{14,10},{5,1},{7,3},{9,5},{11,7},{... | collective-permute-start | bytes 786440 | tf_op jit(solution)/shard_map/ppermute | solution.py:110
  12.5 26.5 %collective-permute-start.4 = (bf16[32,4096]{1,0:T(8,128)(2,1)}, bf16[32,4096]{1,0:T(8,128)(2,1)}, u32[]{:S(2)}, u32[]{:S(2)}) collective-permute-start(bf16[32,4096]{1,0:T(8,128)(2,1)} %get-tuple-element.6), channel_id=1, source_target_pairs={{0,4},{2,6},{4,8},{6,10},{8,12},{10,14},{1,5},{3,7},{5,9},{7,11},{... | collective-permute-start | bytes 786440 | tf_op jit(solution)/shard_map/ppermute | solution.py:110
  18.9 2.2 %copy-start = (bf16[256,8192]{1,0:T(8,128)(2,1)S(1)}, bf16[256,8192]{1,0:T(8,128)(2,1)}, u32[]{:S(2)}) copy-start(bf16[256,8192]{1,0:T(8,128)(2,1)} %codes_ref.5) | copy-start | bytes 12582916
  22.4 1.0 copy-start.2
  23.4 2.2 %copy-start.1 = (bf16[256,8192]{1,0:T(8,128)(2,1)S(1)}, bf16[256,8192]{1,0:T(8,128)(2,1)}, u32[]{:S(2)}) copy-start(bf16[256,8192]{1,0:T(8,128)(2,1)} %codes_ref.5) | copy-start | bytes 12582916
  27.5 9.5 %copy-start.3 = (bf16[128,4096]{1,0:T(8,128)(2,1)S(1)}, bf16[128,4096]{1,0:T(8,128)(2,1)}, u32[]{:S(2)}) copy-start(bf16[128,4096]{1,0:T(8,128)(2,1)} %copy-done.2) | copy-start | bytes 3145732
  29.3 11.1 %collective-permute-start.2 = (bf16[32,4096]{1,0:T(8,128)(2,1)}, bf16[32,4096]{1,0:T(8,128)(2,1)S(1)}, u32[]{:S(2)}, u32[]{:S(2)}) collective-permute-start(bf16[32,4096]{1,0:T(8,128)(2,1)} %get-tuple-element.6), channel_id=1, source_target_pairs={{0,2},{2,0},{4,6},{6,4},{8,10},{10,8},{12,14},{14,12},{1,3},{3,1},... | collective-permute-start | bytes 786440 | tf_op jit(solution)/shard_map/ppermute | solution.py:114
  29.5 15.5 %collective-permute-start.13 = (bf16[32,4096]{1,0:T(8,128)(2,1)}, bf16[32,4096]{1,0:T(8,128)(2,1)S(1)}, u32[]{:S(2)}, u32[]{:S(2)}) collective-permute-start(bf16[32,4096]{1,0:T(8,128)(2,1)} %collective-permute-done.7), channel_id=1, source_target_pairs={{4,0},{6,2},{8,4},{10,6},{12,8},{14,10},{5,1},{7,3},{9,5},{11,7},{... | collective-permute-start | bytes 786440 | tf_op jit(solution)/shard_map/ppermute | solution.py:110
  30.8 15.5 %collective-permute-start.12 = (bf16[32,4096]{1,0:T(8,128)(2,1)}, bf16[32,4096]{1,0:T(8,128)(2,1)S(1)}, u32[]{:S(2)}, u32[]{:S(2)}) collective-permute-start(bf16[32,4096]{1,0:T(8,128)(2,1)} %collective-permute-done.6), channel_id=1, source_target_pairs={{0,4},{2,6},{4,8},{6,10},{8,12},{10,14},{1,5},{3,7},{5,9},{7,11},{... | collective-permute-start | bytes 786440 | tf_op jit(solution)/shard_map/ppermute | solution.py:110
  37.1 31.5 %collective-permute-start = (bf16[128,4096]{1,0:T(8,128)(2,1)S(1)}, bf16[128,4096]{1,0:T(8,128)(2,1)S(1)}, u32[]{:S(2)}, u32[]{:S(2)}) collective-permute-start(bf16[128,4096]{1,0:T(8,128)(2,1)S(1)} %copy-done.3), channel_id=1, source_target_pairs={{0,16},{16,0},{1,17},{17,1},{2,18},{18,2},{3,19},{19,3},{4,20},{20... | collective-permute-start | bytes 3145736 | tf_op jit(solution)/shard_map/ppermute | solution.py:170
  39.1 12.5 %collective-permute-start.11 = (bf16[32,4096]{1,0:T(8,128)(2,1)}, bf16[32,4096]{1,0:T(8,128)(2,1)S(1)}, u32[]{:S(2)}, u32[]{:S(2)}) collective-permute-start(bf16[32,4096]{1,0:T(8,128)(2,1)} %collective-permute-done.5), channel_id=1, source_target_pairs={{4,0},{6,2},{8,4},{10,6},{12,8},{14,10},{5,1},{7,3},{9,5},{11,7},{... | collective-permute-start | bytes 786440 | tf_op jit(solution)/shard_map/ppermute | solution.py:110
  40.4 11.3 %collective-permute-start.10 = (bf16[32,4096]{1,0:T(8,128)(2,1)}, bf16[32,4096]{1,0:T(8,128)(2,1)S(1)}, u32[]{:S(2)}, u32[]{:S(2)}) collective-permute-start(bf16[32,4096]{1,0:T(8,128)(2,1)} %collective-permute-done.4), channel_id=1, source_target_pairs={{0,4},{2,6},{4,8},{6,10},{8,12},{10,14},{1,5},{3,7},{5,9},{7,11},{... | collective-permute-start | bytes 786440 | tf_op jit(solution)/shard_map/ppermute | solution.py:110
  45.0 9.0 %collective-permute-start.19 = (bf16[32,4096]{1,0:T(8,128)(2,1)S(1)}, bf16[32,4096]{1,0:T(8,128)(2,1)S(1)}, u32[]{:S(2)}, u32[]{:S(2)}) collective-permute-start(bf16[32,4096]{1,0:T(8,128)(2,1)S(1)} %collective-permute-done.13), channel_id=1, source_target_pairs={{4,0},{6,2},{8,4},{10,6},{12,8},{14,10},{5,1},{7,3},{9,5},{11,7},{... | collective-permute-start | bytes 786440 | tf_op jit(solution)/shard_map/ppermute | solution.py:110
  46.3 11.5 %collective-permute-start.18 = (bf16[32,4096]{1,0:T(8,128)(2,1)S(1)}, bf16[32,4096]{1,0:T(8,128)(2,1)S(1)}, u32[]{:S(2)}, u32[]{:S(2)}) collective-permute-start(bf16[32,4096]{1,0:T(8,128)(2,1)S(1)} %collective-permute-done.12), channel_id=1, source_target_pairs={{0,4},{2,6},{4,8},{6,10},{8,12},{10,14},{1,5},{3,7},{5,9},{7,11},{... | collective-permute-start | bytes 786440 | tf_op jit(solution)/shard_map/ppermute | solution.py:110
  51.6 30.9 %collective-permute-start.1 = (bf16[128,4096]{1,0:T(8,128)(2,1)S(1)}, bf16[128,4096]{1,0:T(8,128)(2,1)S(1)}, u32[]{:S(2)}, u32[]{:S(2)}) collective-permute-start(bf16[128,4096]{1,0:T(8,128)(2,1)S(1)} %scale_codes.5), channel_id=1, source_target_pairs={{0,16},{16,0},{1,17},{17,1},{2,18},{18,2},{3,19},{19,3},{4,20},{20... | collective-permute-start | bytes 3145736 | tf_op jit(solution)/shard_map/ppermute | solution.py:170
  51.7 10.6 %collective-permute-start.17 = (bf16[32,4096]{1,0:T(8,128)(2,1)S(1)}, bf16[32,4096]{1,0:T(8,128)(2,1)S(1)}, u32[]{:S(2)}, u32[]{:S(2)}) collective-permute-start(bf16[32,4096]{1,0:T(8,128)(2,1)S(1)} %collective-permute-done.11), channel_id=1, source_target_pairs={{4,0},{6,2},{8,4},{10,6},{12,8},{14,10},{5,1},{7,3},{9,5},{11,7},{... | collective-permute-start | bytes 786440 | tf_op jit(solution)/shard_map/ppermute | solution.py:110
  54.0 8.5 %collective-permute-start.16 = (bf16[32,4096]{1,0:T(8,128)(2,1)S(1)}, bf16[32,4096]{1,0:T(8,128)(2,1)S(1)}, u32[]{:S(2)}, u32[]{:S(2)}) collective-permute-start(bf16[32,4096]{1,0:T(8,128)(2,1)S(1)} %collective-permute-done.10), channel_id=1, source_target_pairs={{0,4},{2,6},{4,8},{6,10},{8,12},{10,14},{1,5},{3,7},{5,9},{7,11},{... | collective-permute-start | bytes 786440 | tf_op jit(solution)/shard_map/ppermute | solution.py:110
  58.9 48.4 %collective-permute-start.21 = (bf16[32,4096]{1,0:T(8,128)(2,1)S(1)}, bf16[32,4096]{1,0:T(8,128)(2,1)S(1)}, u32[]{:S(2)}, u32[]{:S(2)}) collective-permute-start(bf16[32,4096]{1,0:T(8,128)(2,1)S(1)} %get-tuple-element.9), channel_id=1, source_target_pairs={{0,2},{2,0},{4,6},{6,4},{8,10},{10,8},{12,14},{14,12},{1,3},{3,1},... | collective-permute-start | bytes 786440 | tf_op jit(solution)/shard_map/ppermute | solution.py:114
  62.4 39.9 %collective-permute-start.15 = (bf16[32,4096]{1,0:T(8,128)(2,1)S(1)}, bf16[32,4096]{1,0:T(8,128)(2,1)S(1)}, u32[]{:S(2)}, u32[]{:S(2)}) collective-permute-start(bf16[32,4096]{1,0:T(8,128)(2,1)S(1)} %get-tuple-element.10), channel_id=1, source_target_pairs={{0,2},{2,0},{4,6},{6,4},{8,10},{10,8},{12,14},{14,12},{1,3},{3,1},... | collective-permute-start | bytes 786440 | tf_op jit(solution)/shard_map/ppermute | solution.py:114
  62.5 33.7 %collective-permute-start.9 = (bf16[32,4096]{1,0:T(8,128)(2,1)S(1)}, bf16[32,4096]{1,0:T(8,128)(2,1)S(1)}, u32[]{:S(2)}, u32[]{:S(2)}) collective-permute-start(bf16[32,4096]{1,0:T(8,128)(2,1)S(1)} %get-tuple-element.14), channel_id=1, source_target_pairs={{0,2},{2,0},{4,6},{6,4},{8,10},{10,8},{12,14},{14,12},{1,3},{3,1},... | collective-permute-start | bytes 786440 | tf_op jit(solution)/shard_map/ppermute | solution.py:114
  68.5 36.1 %collective-permute-start.20 = (bf16[32,4096]{1,0:T(8,128)(2,1)S(1)}, bf16[32,4096]{1,0:T(8,128)(2,1)S(1)}, u32[]{:S(2)}, u32[]{:S(2)}) collective-permute-start(bf16[32,4096]{1,0:T(8,128)(2,1)S(1)} %get-tuple-element.11), channel_id=1, source_target_pairs={{0,2},{2,0},{4,6},{6,4},{8,10},{10,8},{12,14},{14,12},{1,3},{3,1},... | collective-permute-start | bytes 786440 | tf_op jit(solution)/shard_map/ppermute | solution.py:114
  82.5 11.1 %collective-permute-start.8 = (bf16[32,4096]{1,0:T(8,128)(2,1)S(1)}, bf16[32,4096]{1,0:T(8,128)(2,1)S(1)}, u32[]{:S(2)}, u32[]{:S(2)}) collective-permute-start(bf16[32,4096]{1,0:T(8,128)(2,1)S(1)} %get-tuple-element.13), channel_id=1, source_target_pairs={{0,2},{2,0},{4,6},{6,4},{8,10},{10,8},{12,14},{14,12},{1,3},{3,1},... | collective-permute-start | bytes 786440 | tf_op jit(solution)/shard_map/ppermute | solution.py:114
  93.7 6.4 %collective-permute-start.14 = (bf16[32,4096]{1,0:T(8,128)(2,1)S(1)}, bf16[32,4096]{1,0:T(8,128)(2,1)S(1)}, u32[]{:S(2)}, u32[]{:S(2)}) collective-permute-start(bf16[32,4096]{1,0:T(8,128)(2,1)S(1)} %get-tuple-element.12), channel_id=1, source_target_pairs={{0,2},{2,0},{4,6},{6,4},{8,10},{10,8},{12,14},{14,12},{1,3},{3,1},... | collective-permute-start | bytes 786440 | tf_op jit(solution)/shard_map/ppermute | solution.py:114
  108.9 10.6 %copy-start.4 = (s32[1,256]{1,0:T(1,128)S(1)}, s32[1,256]{1,0:T(1,128)}, u32[]{:S(2)}) copy-start(s32[1,256]{1,0:T(1,128)} %ids_ref.1) | copy-start | bytes 3076
  109.0 2.0 %collective-permute-start.22 = (f32[8,32,512]{2,1,0:T(8,128)S(1)}, f32[8,32,512]{2,1,0:T(8,128)S(1)}, u32[]{:S(2)}, u32[]{:S(2)}) collective-permute-start(f32[8,32,512]{2,1,0:T(8,128)S(1)} %dynamic-slice_bitcast_fusion), channel_id=1, source_target_pairs={{0,1},{1,0},{2,3},{3,2},{4,5},{5,4},{6,7},{7,6},{8,9},{9,8},{10,11... | collective-permute-start | bytes 1572872 | tf_op jit(solution)/shard_map/ppermute | solution.py:186
  111.1 8.4 %collective-permute-start.23 = (f32[8,32,256]{2,1,0:T(8,128)S(1)}, f32[8,32,256]{2,1,0:T(8,128)S(1)}, u32[]{:S(2)}, u32[]{:S(2)}) collective-permute-start(f32[8,32,256]{2,1,0:T(8,128)S(1)} %get-tuple-element.7), channel_id=1, source_target_pairs={{0,16},{16,0},{1,17},{17,1},{2,18},{18,2},{3,19},{19,3},{4,20},{20... | collective-permute-start | bytes 786440 | tf_op jit(solution)/shard_map/ppermute | solution.py:188

commit v2 on v0

v2 whole, which is shorter than its diff:
```python
import functools

import jax
import jax.numpy as jnp
from jax import lax
from jax.experimental import pallas as pl
from jax.experimental.pallas import tpu as pltpu
from jax.sharding import PartitionSpec as P

BLOCK = 128
VMEM = pl.BlockSpec(memory_space=pltpu.VMEM)
SMEM = pl.BlockSpec(memory_space=pltpu.SMEM)
NT = (((1,), (1,)), ((), ()))


def fast_length(mesh):
    line = list(mesh.devices[0, :, 0])
    size = len(line)
    if size < 2 or not all(hasattr(device, "coords") for device in line):
        return 2 if size % 2 == 0 else size

    def moved(a, b):
        return tuple(i for i, (p, q) in enumerate(zip(a.coords, b.coords)) if p != q)

    along = moved(line[0], line[1])
    length = 2
    while length < size and moved(line[0], line[length]) == along:
        length += 1
    return length if size % length == 0 else size


def scale_kernel(alone, tile, starts_ref, codes_ref, given_ref, kept_ref, sent_ref, grads_ref, buffer, sems):
    count = codes_ref.shape[0]

    def fetch(i):
        return pltpu.make_async_copy(codes_ref.at[pl.ds(i * tile, tile)], buffer.at[i], sems.at[i])

    tiles = count // tile
    for i in range(tiles):
        fetch(i).start()
    for i in range(tiles):
        fetch(i).wait()
        rows = pl.ds(i * tile, tile)

        def scaled(first, block, scales_ref, at):
            columns = pl.ds(pl.multiple_of((first + block) * BLOCK, BLOCK), BLOCK)
            return buffer[i, :, columns] * scales_ref[rows, at : at + 1].astype(jnp.bfloat16)

        for block in range(alone):
            sent_ref[rows, block * BLOCK : (block + 1) * BLOCK] = scaled(starts_ref[1], block, given_ref, block)
        for block in range(grads_ref.shape[1] // BLOCK):
            first = starts_ref[0] if block < alone else 0
            grads_ref[rows, block * BLOCK : (block + 1) * BLOCK] = scaled(first, block, kept_ref, block)


def scale_codes(codes, starts, given, kept, alone):
    count = codes.shape[0]
    tile = min(count, 64)
    blocks = kept.shape[1]
    return pl.pallas_call(
        functools.partial(scale_kernel, alone, tile),
        out_shape=[
            jax.ShapeDtypeStruct((count, alone * BLOCK), jnp.bfloat16),
            jax.ShapeDtypeStruct((count, blocks * BLOCK), jnp.bfloat16),
        ],
        in_specs=[SMEM, pl.BlockSpec(memory_space=pltpu.HBM), VMEM, VMEM],
        out_specs=[VMEM, VMEM],
        scratch_shapes=[
            pltpu.VMEM((count // tile, tile, codes.shape[1]), codes.dtype),
            pltpu.SemaphoreType.DMA((count // tile,)),
        ],
        compiler_params=pltpu.CompilerParams(vmem_limit_bytes=16 << 20),
        cost_estimate=pl.CostEstimate(flops=codes.size, bytes_accessed=4 * codes.size, transcendentals=0),
        name="scale_codes",
    )(starts, codes, given, kept)


def score_kernel(parts, *refs):
    *refs, out_ref = refs
    query_refs, grad_refs = refs[: sum(parts)], refs[sum(parts) :]
    at = 0
    row = 0
    for part in parts:
        pieces = query_refs[at : at + part]
        at += part
        rows = pieces[0].shape[0]
        column = 0
        for grads in grad_refs:
            total = None
            first = 0
            for piece in pieces:
                width = min(piece.shape[1], grads.shape[1] - first)
                if width <= 0:
                    break
                term = lax.dot_general(
                    piece[:, :width], grads[:, first : first + width], NT, preferred_element_type=jnp.float32
                )
                total = term if total is None else total + term
                first += width
            out_ref[row : row + rows, column : column + grads.shape[0]] = total
            column += grads.shape[0]
        row += rows


def score(queries, grads):
    rows = sum(pieces[0].shape[0] for pieces in queries)
    columns = sum(g.shape[0] for g in grads)
    operands = [piece for pieces in queries for piece in pieces] + list(grads)
    flops = 2 * rows * sum(g.size for g in grads)
    return pl.pallas_call(
        functools.partial(score_kernel, [len(pieces) for pieces in queries]),
        out_shape=jax.ShapeDtypeStruct((rows, columns), jnp.float32),
        in_specs=[VMEM] * len(operands),
        out_specs=VMEM,
        compiler_params=pltpu.CompilerParams(vmem_limit_bytes=16 << 20),
        cost_estimate=pl.CostEstimate(
            flops=flops, bytes_accessed=2 * sum(o.size for o in operands), transcendentals=0
        ),
        name="score",
    )(*operands)


def place_kernel(rows, order_ref, ids_ref, own_ref, received_ref, out_ref):
    raw = own_ref[...] + received_ref[...]
    count = raw.shape[1]
    slots = lax.broadcasted_iota(jnp.int32, (count, count), 0)
    table = (slots == jnp.broadcast_to(ids_ref[...], (count, count))).astype(jnp.float32)
    placed = lax.dot_general(raw, table, NT, precision=lax.Precision.HIGHEST, preferred_element_type=jnp.float32)
    for j in range(raw.shape[0] // rows):
        out_ref[order_ref[j]] = placed[j * rows : (j + 1) * rows]


def place(order, ids, own, received, rows):
    return pl.pallas_call(
        functools.partial(place_kernel, rows),
        out_shape=jax.ShapeDtypeStruct((own.shape[0] // rows, rows, own.shape[1]), jnp.float32),
        in_specs=[SMEM, VMEM, VMEM, VMEM],
        out_specs=VMEM,
        compiler_params=pltpu.CompilerParams(vmem_limit_bytes=16 << 20),
        name="place_scores",
    )(order, ids, own, received)


def shards(fast, parts, total, queries, codes, exponents, example_ids):
    part = lax.axis_index("groups")
    here = lax.axis_index("ex")
    half = lax.axis_index("dim")
    slow = total // fast
    rows = queries.shape[1]
    count = codes.shape[0]
    blocks = exponents.shape[1]
    alone = blocks * 25 // 64
    shared = blocks - parts * alone
    held = alone + shared
    direct = held * 33 // 39

    def step(value, length, stride):
        pairs = [
            (i, i + stride if (i // stride) % length < length - 1 else i - (length - 1) * stride)
            for i in range(total)
        ]
        return lax.ppermute(value, "ex", pairs)

    def along_fast(value):
        values = [value]
        for _ in range(fast - 1):
            values.append(step(values[-1], fast, 1))
        return values

    first = part * (blocks - alone)
    rest = (1 - part) * (blocks - alone)

    def columns(array, start, width, unit=1):
        return lax.dynamic_slice(array, (0, start * unit), (array.shape[0], width * unit))

    mine = jnp.concatenate(
        [columns(queries[0], first, alone, BLOCK), columns(queries[0], alone, shared, BLOCK)], axis=1
    )
    cut = direct * BLOCK
    direct_columns = [mine[:, :cut]]
    for _ in range(slow - 1):
        direct_columns.append(step(direct_columns[-1], slow, fast))
    whole = along_fast(mine)
    pairs = [jnp.concatenate([block[:, cut:] for block in whole], axis=0)]
    for _ in range(slow - 1):
        pairs.append(step(pairs[-1], slow, fast))

    scales = (jnp.int32(1) << (exponents + 3)).astype(jnp.float32) * 0.125
    kept_scales = jnp.concatenate([columns(scales, first, alone), columns(scales, alone, shared)], axis=1)
    sent, ours = scale_codes(codes, jnp.stack([first, rest]), columns(scales, rest, alone), kept_scales, alone)
    swap = [(i, parts - 1 - i) for i in range(parts)]
    theirs = lax.ppermute(sent, "groups", swap)

    arrived = [[[block] for block in whole]]
    for s in range(1, slow):
        near = along_fast(direct_columns[s])
        arrived.append([[block, pairs[s][t * rows : (t + 1) * rows]] for t, block in enumerate(near)])

    def summed(steps):
        given = [pieces for s in steps for pieces in arrived[s]]
        if rows % 16:
            given = [[jnp.concatenate([block[0][:, :cut] for block in arrived[s]]), pairs[s]] for s in steps]
        sums = jnp.concatenate([score(given, [ours]), score(given, [theirs])], axis=1)
        sums = sums.reshape(-1, 2, rows // 2, 2 * count)
        keep = lax.dynamic_index_in_dim(sums, half, 1, keepdims=False)
        send = lax.dynamic_index_in_dim(sums, 1 - half, 1, keepdims=False)
        sums = keep + lax.ppermute(send, "dim", [(0, 1), (1, 0)])
        received = lax.ppermute(sums[..., count:], "groups", swap)
        return sums[..., :count].reshape(-1, count), received.reshape(-1, count)

    early, late = summed(range(slow - 1)), summed([slow - 1])
    own, received = (jnp.concatenate([e, l]) for e, l in zip(early, late))
    order = jnp.stack([
        lax.rem(here // fast + slow - s, slow) * fast + lax.rem(here % fast + fast - t, fast)
        for s in range(slow)
        for t in range(fast)
    ]).astype(jnp.int32)
    return place(order, example_ids, own, received, rows // 2)


def solution(mesh):
    placed = (
        P("ex", None, "dim"),
        P(("groups", "ex"), "dim"),
        P(("groups", "ex"), "dim"),
        P(("groups", "ex"), None),
    )
    return jax.shard_map(
        functools.partial(shards, fast_length(mesh), mesh.shape["groups"], mesh.shape["ex"]),
        mesh=mesh,
        in_specs=placed,
        out_specs=P(None, "dim", ("groups", "ex")),
        check_vma=False,
    )
```

time: 165 us -> 103 us (0.62)
  waiting for transfers between devices: 136 us -> 52.2 us
  Pallas kernels: 0 us -> 22.2 us
  starting transfers between devices: 0.04 us -> 13.4 us
  between operations: 13.4 us -> 0.27 us
  matrix products: 10.7 us -> 0 us
  local copies, waits for them, and re-layouts: 3.47 us -> 11.2 us
  other arithmetic: 0.86 us -> 3.02 us
    all_gather x1 -> x0, waiting for transfers between devices: 129 us -> none  [shards(): lax.all_gather(queries, 'ex', axis=0, tiled=True)]
    ppermute x0 -> x15, waiting for transfers between devices: none -> 52.2 us  [the longest x10 45 us: step(): return lax.ppermute(value, 'ex', pairs)]
    pallas_call x0 -> x6, Pallas kernels: none -> 22.2 us  [the longest x4 16.9 us: score(): pl.pallas_call(functools.partial(score_kernel, [len(pieces) for pieces in...]
    ppermute x0 -> x15, starting transfers between devices: none -> 13.4 us  [the longest x10 10.3 us: step(): return lax.ppermute(value, 'ex', pairs)]
    dot_general x2 -> x0, matrix products: 10.7 us -> none  [the longest x1 8.65 us: shards(): jnp.einsum('nho,so->nhs', lax.all_gather(queries, 'ex', axis=0, tiled=Tru...]
    reduce_scatter x1 -> x0, waiting for transfers between devices: 6.28 us -> none  [shards(): lax.psum_scatter(partial_scores, 'dim', scatter_dimension=1, tiled=True)]
    unnamed x4 -> x19, local copies, waits for them, and re-layouts: 1.08 us -> 5.07 us
    slice x0 -> x7, local copies, waits for them, and re-layouts: none -> 2.87 us  [the longest x3 1.92 us: shards(): pairs[s][t * rows:(t + 1) * rows]]
  transfers between devices with their start and end apart: 2 -> 15, of which waited for: 2 -> 10; matrix products, arithmetic and copies ran while one was open for 1% -> 6% of each run, Pallas kernels for 0% -> 15%
where the time goes in v2:
time: 103 us; the launch traced here: 102 us
  waiting for transfers between devices  52.2 us (51%)
  Pallas kernels  22.2 us (22%)
  starting transfers between devices  13.4 us (13%)
  local copies, waits for them, and re-layouts  11.2 us (11%)
  other arithmetic  3.02 us (3%)
    ppermute x10, waiting for transfers between devices, step(): return lax.ppermute(value, 'ex', pairs)  45 us
    pallas_call x4, Pallas kernels, score(): pl.pallas_call(functools.partial(score_kernel, [len(pieces) for pieces in...  16.9 us
    ppermute x10, starting transfers between devices, step(): return lax.ppermute(value, 'ex', pairs)  10.3 us
    ppermute x2, waiting for transfers between devices, summed(): received = lax.ppermute(sums[..., count:], 'groups', swap)  6.54 us
    unnamed x19, local copies, waits for them, and re-layouts  5.07 us
    pallas_call x1, Pallas kernels, scale_codes(): pl.pallas_call(functools.partial(scale_kernel, alone, tile), out_shape=[j...  3.67 us
    dynamic_slice x4, local copies, waits for them, and re-layouts, columns(): lax.dynamic_slice(array, (0, start * unit), (array.shape[0], width * unit))  2.24 us
  transfers between devices with their start and end apart: 15, of which 10 were waited for; matrix products, arithmetic and copies ran while one was open for 6% of the time, Pallas kernels for 15%

profile of v2, /device:TPU:0, one launch (start us, length us, event | category | flops | bytes accessed | tf_op | source)
XLA Modules:
  0.0 102.3 jit_solution(7373526302249510999)
XLA Ops:
  0.0 1.0 dynamic_slice.41
  1.0 1.0 %dynamic-slice_bitcast_fusion = bf16[64,3200]{1,0:T(8,128)(2,1)S(1)} fusion(bf16[1,64,8192]{2,1,0:T(8,128)(2,1)} %param.4, s32[]{:T(128)S(6)} %select_n.53), kind=kLoop, calls=%fused_computation.5 | loop fusion | bytes 819204 | tf_op jit(solution)/shard_map/dynamic_slice | solution.py:174
  2.0 0.0 copy-start.5
  2.0 0.7 copy-done.5
  2.8 0.8 fusion
  3.6 3.0 %collective-permute-start.1 = (bf16[64,4224]{1,0:T(8,128)(2,1)}, bf16[64,4224]{1,0:T(8,128)(2,1)}, u32[]{:S(2)}, u32[]{:S(2)}) collective-permute-start(bf16[64,4224]{1,0:T(8,128)(2,1)} %fusion), channel_id=1, source_target_pairs={{0,4},{2,6},{4,8},{6,10},{8,12},{10,14},{12,0},{14,2},{1,5},{3,7},... | collective-permute-start | bytes 1622024 | tf_op jit(solution)/shard_map/ppermute | solution.py:162
  6.6 0.0 copy-done.8
  6.6 0.1 copy.10
  6.8 0.1 dynamic_slice.42
  6.9 0.1 pad_add_fusion.starts_ref
  6.9 0.1 constant_dynamic-slice_fusion
  7.1 0.1 pad_maximum_fusion.6.kept_ref
  7.2 0.0 copy-start
  7.2 2.2 %copy-done = bf16[256,8192]{1,0:T(8,128)(2,1)S(1)} copy-done((bf16[256,8192]{1,0:T(8,128)(2,1)S(1)}, bf16[256,8192]{1,0:T(8,128)(2,1)}, u32[]{:S(2)}) %copy-start) | copy-done | bytes 4194328
  9.4 3.7 %scale_codes.1 = (bf16[256,3200]{1,0:T(8,128)(2,1)}, bf16[256,4992]{1,0:T(8,128)(2,1)S(1)}) custom-call(s32[2]{0:T(128)S(1)} %pad_add_fusion.starts_ref, bf16[256,8192]{1,0:T(8,128)(2,1)S(1)} %copy-done, f32[256,25]{1,0:T(8,128)S(1)} %get-tuple-element.20.given_ref, f32[256,39]{1,0:T(8,128)S(1)} %pad_maximum_fusion.6.kept_ref), custom_call_target="tpu_custom_call" | custom-call | flops 2097152 | bytes 8388608 | tf_op jit(solution)/shard_map/scale_codes/pallas_call | solution.py:60
  13.1 1.6 %collective-permute-start.7 = (bf16[256,3200]{1,0:T(8,128)(2,1)}, bf16[256,3200]{1,0:T(8,128)(2,1)}, u32[]{:S(2)}, u32[]{:S(2)}) collective-permute-start(bf16[256,3200]{1,0:T(8,128)(2,1)} %get-tuple-element.8), channel_id=1, source_target_pairs={{0,16},{16,0},{1,17},{17,1},{2,18},{18,2},{3,19},{19,3},{4,20},{20... | collective-permute-start | bytes 4915208 | tf_op jit(solution)/shard_map/ppermute | solution.py:192
  14.6 0.0 copy-done.6
  14.7 1.6 %collective-permute-start = (bf16[64,4992]{1,0:T(8,128)(2,1)S(1)}, bf16[64,4992]{1,0:T(8,128)(2,1)S(1)}, u32[]{:S(2)}, u32[]{:S(2)}) collective-permute-start(bf16[64,4992]{1,0:T(8,128)(2,1)S(1)} %pad_maximum_fusion.1.refs_0_), channel_id=1, source_target_pairs={{0,2},{2,0},{4,6},{6,4},{8,10},{10,8},{12,14},{14,12},{1,3},{3,1},... | collective-permute-start | bytes 1916936 | tf_op jit(solution)/shard_map/ppermute | solution.py:162
  16.3 5.0 %collective-permute-done.1.refs_2_ = bf16[64,4224]{1,0:T(8,128)(2,1)} collective-permute-done((bf16[64,4224]{1,0:T(8,128)(2,1)}, bf16[64,4224]{1,0:T(8,128)(2,1)}, u32[]{:S(2)}, u32[]{:S(2)}) %collective-permute-start.1) | collective-permute-done | bytes 540704 | tf_op jit(solution)/shard_map/ppermute | solution.py:162
  21.3 0.0 collective-permute-start.4
  21.3 0.9 slice.55
  22.2 8.2 %collective-permute-done.refs_1_ = bf16[64,4992]{1,0:T(8,128)(2,1)S(1)} collective-permute-done((bf16[64,4992]{1,0:T(8,128)(2,1)S(1)}, bf16[64,4992]{1,0:T(8,128)(2,1)S(1)}, u32[]{:S(2)}, u32[]{:S(2)}) %collective-permute-start) | collective-permute-done | bytes 639008 | tf_op jit(solution)/shard_map/ppermute | solution.py:162
  30.3 0.8 copy-done.1
  31.2 0.7 pad_maximum_fusion.5
  31.9 1.6 %collective-permute-start.2 = (bf16[128,768]{1,0:T(8,128)(2,1)}, bf16[128,768]{1,0:T(8,128)(2,1)S(1)}, u32[]{:S(2)}, u32[]{:S(2)}) collective-permute-start(bf16[128,768]{1,0:T(8,128)(2,1)} %pad_maximum_fusion.5), channel_id=1, source_target_pairs={{0,4},{2,6},{4,8},{6,10},{8,12},{10,14},{12,0},{14,2},{1,5},{3,7},... | collective-permute-start | bytes 589832 | tf_op jit(solution)/shard_map/ppermute | solution.py:162
  33.4 1.5 %collective-permute-start.3 = (bf16[64,4224]{1,0:T(8,128)(2,1)}, bf16[64,4224]{1,0:T(8,128)(2,1)}, u32[]{:S(2)}, u32[]{:S(2)}) collective-permute-start(bf16[64,4224]{1,0:T(8,128)(2,1)} %collective-permute-done.1.refs_2_), channel_id=1, source_target_pairs={{0,2},{2,0},{4,6},{6,4},{8,10},{10,8},{12,14},{14,12},{1,3},{3,1},... | collective-permute-start | bytes 1622024 | tf_op jit(solution)/shard_map/ppermute | solution.py:162
  34.9 3.6 %collective-permute-done.4.refs_6_ = bf16[64,4224]{1,0:T(8,128)(2,1)} collective-permute-done((bf16[64,4224]{1,0:T(8,128)(2,1)}, bf16[64,4224]{1,0:T(8,128)(2,1)}, u32[]{:S(2)}, u32[]{:S(2)}) %collective-permute-start.4) | collective-permute-done | bytes 540704 | tf_op jit(solution)/shard_map/ppermute | solution.py:162
  38.6 1.0 collective-permute-start.6
  39.6 1.4 %collective-permute-done.2 = bf16[128,768]{1,0:T(8,128)(2,1)S(1)} collective-permute-done((bf16[128,768]{1,0:T(8,128)(2,1)}, bf16[128,768]{1,0:T(8,128)(2,1)S(1)}, u32[]{:S(2)}, u32[]{:S(2)}) %collective-permute-start.2) | collective-permute-done | bytes 196640 | tf_op jit(solution)/shard_map/ppermute | solution.py:162
  40.9 0.0 collective-permute-start.5
  41.0 0.1 collective-permute-start.9
  41.0 9.7 %collective-permute-done.5 = bf16[128,768]{1,0:T(8,128)(2,1)} collective-permute-done((bf16[128,768]{1,0:T(8,128)(2,1)S(1)}, bf16[128,768]{1,0:T(8,128)(2,1)}, u32[]{:S(2)}, u32[]{:S(2)}) %collective-permute-start.5) | collective-permute-done | bytes 196640 | tf_op jit(solution)/shard_map/ppermute | solution.py:162
  50.7 1.0 fusion.2
  51.6 0.1 collective-permute-start.10
  51.7 0.0 collective-permute-done.3.refs_4_
  51.7 6.0 %collective-permute-done.6.refs_8_ = bf16[64,4224]{1,0:T(8,128)(2,1)} collective-permute-done((bf16[64,4224]{1,0:T(8,128)(2,1)}, bf16[64,4224]{1,0:T(8,128)(2,1)}, u32[]{:S(2)}, u32[]{:S(2)}) %collective-permute-start.6) | collective-permute-done | bytes 540704 | tf_op jit(solution)/shard_map/ppermute | solution.py:162
  57.7 1.1 %copy-done.2 = bf16[64,4992]{1,0:T(8,128)(2,1)S(1)} copy-done((bf16[64,4992]{1,0:T(8,128)(2,1)S(1)}, bf16[64,4992]{1,0:T(8,128)(2,1)}, u32[]{:S(2)}) %copy-start.2) | copy-done | bytes 639000
  58.8 6.3 %score.4 = f32[384,256]{1,0:T(8,128)S(1)} custom-call(bf16[64,4992]{1,0:T(8,128)(2,1)S(1)} %pad_maximum_fusion.1.refs_0_, bf16[64,4992]{1,0:T(8,128)(2,1)S(1)} %copy-done.2, bf16[64,4224]{1,0:T(8,128)(2,1)} %collective-permute-done.1.refs_2_, bf16[64,768]{1,0:T(8,128)(2,1)S(1)} %get-tuple-element.14.refs_3_, ...), custom_call_target="tpu_custom_call" | custom-call | flops 981467136 | bytes 6389760 | tf_op jit(solution)/shard_map/score/pallas_call | solution.py:110
  65.1 0.0 collective-permute-done.7.refs_10_.refs_4_
  65.1 0.0 copy-done.3
  65.1 5.2 %score.5 = f32[384,256]{1,0:T(8,128)S(1)} custom-call(bf16[64,4992]{1,0:T(8,128)(2,1)S(1)} %pad_maximum_fusion.1.refs_0_, bf16[64,4992]{1,0:T(8,128)(2,1)S(1)} %copy-done.3, bf16[64,4224]{1,0:T(8,128)(2,1)} %collective-permute-done.1.refs_2_, bf16[64,768]{1,0:T(8,128)(2,1)S(1)} %get-tuple-element.14.refs_3_, ...), custom_call_target="tpu_custom_call" | custom-call | flops 629145600 | bytes 5472256 | tf_op jit(solution)/shard_map/score/pallas_call | solution.py:110
  70.3 0.1 pad_maximum_fusion
  70.4 0.9 dynamic-slice_bitcast_fusion.1
  71.3 0.0 collective-permute-start.8
  71.3 0.1 copy-done.7
  71.4 0.0 collective-permute-done.9.refs_0_
  71.4 1.5 %collective-permute-start.11 = (bf16[64,4224]{1,0:T(8,128)(2,1)}, bf16[64,4224]{1,0:T(8,128)(2,1)S(1)}, u32[]{:S(2)}, u32[]{:S(2)}) collective-permute-start(bf16[64,4224]{1,0:T(8,128)(2,1)} %collective-permute-done.9.refs_0_), channel_id=1, source_target_pairs={{0,2},{2,0},{4,6},{6,4},{8,10},{10,8},{12,14},{14,12},{1,3},{3,1},... | collective-permute-start | bytes 1622024 | tf_op jit(solution)/shard_map/ppermute | solution.py:162
  72.9 0.1 stack.44.order_ref
  73.0 0.0 collective-permute-done.10
  73.0 1.0 fusion.4
  74.0 0.0 collective-permute-done.8
  74.0 1.1 %bitcast_add_fusion = f32[6,32,512]{2,1,0:T(8,128)S(1)} fusion(f32[6,32,512]{2,1,0:T(8,128)S(1)} %collective-permute-done.8, f32[6,2,32,512]{3,2,1,0:T(8,128)} %bitcast.28, s32[]{:T(128)S(6)} %select_n.56), kind=kLoop, calls=%fused_computation.6 | loop fusion | flops 98304 | bytes 1179652 | tf_op jit(solution)/shard_map/add | solution.py:207
  75.1 11.1 %collective-permute-done.11.refs_2_ = bf16[64,4224]{1,0:T(8,128)(2,1)S(1)} collective-permute-done((bf16[64,4224]{1,0:T(8,128)(2,1)}, bf16[64,4224]{1,0:T(8,128)(2,1)S(1)}, u32[]{:S(2)}, u32[]{:S(2)}) %collective-permute-start.11) | collective-permute-done | bytes 540704 | tf_op jit(solution)/shard_map/ppermute | solution.py:162
  86.2 2.7 %score.6 = f32[128,256]{1,0:T(8,128)S(1)} custom-call(bf16[64,4224]{1,0:T(8,128)(2,1)} %collective-permute-done.9.refs_0_, bf16[64,768]{1,0:T(8,128)(2,1)S(1)} %get-tuple-element.16.refs_1_, bf16[64,4224]{1,0:T(8,128)(2,1)S(1)} %collective-permute-done.11.refs_2_, bf16[64,768]{1,0:T(8,128)(2,1)S(1)} %get-tuple-element.15.refs_3_, ...), custom_call_target="tpu_custom_call" | custom-call | flops 327155712 | bytes 3833856 | tf_op jit(solution)/shard_map/score/pallas_call | solution.py:110
  88.9 2.7 %score.7 = f32[128,256]{1,0:T(8,128)S(1)} custom-call(bf16[64,4224]{1,0:T(8,128)(2,1)} %collective-permute-done.9.refs_0_, bf16[64,768]{1,0:T(8,128)(2,1)S(1)} %get-tuple-element.16.refs_1_, bf16[64,4224]{1,0:T(8,128)(2,1)S(1)} %collective-permute-done.11.refs_2_, bf16[64,768]{1,0:T(8,128)(2,1)S(1)} %get-tuple-element.15.refs_3_, ...), custom_call_target="tpu_custom_call" | custom-call | flops 209715200 | bytes 2916352 | tf_op jit(solution)/shard_map/score/pallas_call | solution.py:110
  91.7 0.0 copy-start.4
  91.7 0.1 collective-permute-start.12
  91.8 0.6 collective-permute-start.13
  92.4 0.7 collective-permute-done.12
  93.1 0.9 collective-permute-start.14
  94.0 5.5 %collective-permute-done.13 = f32[6,32,256]{2,1,0:T(8,128)S(1)} collective-permute-done((f32[6,32,256]{2,1,0:T(8,128)S(1)}, f32[6,32,256]{2,1,0:T(8,128)S(1)}, u32[]{:S(2)}, u32[]{:S(2)}) %collective-permute-start.13) | collective-permute-done | bytes 196640 | tf_op jit(solution)/shard_map/ppermute | solution.py:208
  99.6 1.0 collective-permute-done.14
  100.6 0.0 copy-done.4
  100.6 1.7 %place_scores.1 = f32[8,32,256]{2,1,0:T(8,128)} custom-call(s32[8]{0:T(128)S(1)} %stack.44.order_ref, s32[1,256]{1,0:T(1,128)S(1)} %copy-done.4, f32[256,256]{1,0:T(8,128)S(1)} %pad_maximum_fusion.3.own_ref, f32[256,256]{1,0:T(8,128)S(1)} %pad_maximum_fusion.4.received_ref), custom_call_target="tpu_custom_call" | custom-call | tf_op jit(solution)/shard_map/place_scores/pallas_call | solution.py:134
  (17 shorter events, 0.2 us)
Async XLA Ops:
  0.0 6.6 %copy-start.8 = (s32[256,64]{0,1:T(8,128)S(1)}, s32[256,64]{0,1:T(8,128)}, u32[]{:S(2)}) copy-start(s32[256,64]{0,1:T(8,128)} %param.6) | copy-start | bytes 196612
  2.0 0.7 copy-start.5
  3.6 17.6 %collective-permute-start.1 = (bf16[64,4224]{1,0:T(8,128)(2,1)}, bf16[64,4224]{1,0:T(8,128)(2,1)}, u32[]{:S(2)}, u32[]{:S(2)}) collective-permute-start(bf16[64,4224]{1,0:T(8,128)(2,1)} %fusion), channel_id=1, source_target_pairs={{0,4},{2,6},{4,8},{6,10},{8,12},{10,14},{12,0},{14,2},{1,5},{3,7},... | collective-permute-start | bytes 1622024 | tf_op jit(solution)/shard_map/ppermute | solution.py:162
  7.2 2.2 %copy-start = (bf16[256,8192]{1,0:T(8,128)(2,1)S(1)}, bf16[256,8192]{1,0:T(8,128)(2,1)}, u32[]{:S(2)}) copy-start(bf16[256,8192]{1,0:T(8,128)(2,1)} %codes_ref.1) | copy-start | bytes 12582916
  9.4 5.3 %copy-start.6 = (bf16[64,3200]{1,0:T(8,128)(2,1)S(1)}, bf16[64,3200]{1,0:T(8,128)(2,1)}, u32[]{:S(2)}) copy-start(bf16[64,3200]{1,0:T(8,128)(2,1)} %copy-done.5) | copy-start | bytes 1228804
  13.1 52.0 %collective-permute-start.7 = (bf16[256,3200]{1,0:T(8,128)(2,1)}, bf16[256,3200]{1,0:T(8,128)(2,1)}, u32[]{:S(2)}, u32[]{:S(2)}) collective-permute-start(bf16[256,3200]{1,0:T(8,128)(2,1)} %get-tuple-element.8), channel_id=1, source_target_pairs={{0,16},{16,0},{1,17},{17,1},{2,18},{18,2},{3,19},{19,3},{4,20},{20... | collective-permute-start | bytes 4915208 | tf_op jit(solution)/shard_map/ppermute | solution.py:192
  14.7 15.6 %collective-permute-start = (bf16[64,4992]{1,0:T(8,128)(2,1)S(1)}, bf16[64,4992]{1,0:T(8,128)(2,1)S(1)}, u32[]{:S(2)}, u32[]{:S(2)}) collective-permute-start(bf16[64,4992]{1,0:T(8,128)(2,1)S(1)} %pad_maximum_fusion.1.refs_0_), channel_id=1, source_target_pairs={{0,2},{2,0},{4,6},{6,4},{8,10},{10,8},{12,14},{14,12},{1,3},{3,1},... | collective-permute-start | bytes 1916936 | tf_op jit(solution)/shard_map/ppermute | solution.py:162
  21.3 17.3 %collective-permute-start.4 = (bf16[64,4224]{1,0:T(8,128)(2,1)}, bf16[64,4224]{1,0:T(8,128)(2,1)}, u32[]{:S(2)}, u32[]{:S(2)}) collective-permute-start(bf16[64,4224]{1,0:T(8,128)(2,1)} %collective-permute-done.1.refs_2_), channel_id=1, source_target_pairs={{0,4},{2,6},{4,8},{6,10},{8,12},{10,14},{12,0},{14,2},{1,5},{3,7},... | collective-permute-start | bytes 1622024 | tf_op jit(solution)/shard_map/ppermute | solution.py:162
  30.3 0.8 copy-start.1
  31.9 9.1 %collective-permute-start.2 = (bf16[128,768]{1,0:T(8,128)(2,1)}, bf16[128,768]{1,0:T(8,128)(2,1)S(1)}, u32[]{:S(2)}, u32[]{:S(2)}) collective-permute-start(bf16[128,768]{1,0:T(8,128)(2,1)} %pad_maximum_fusion.5), channel_id=1, source_target_pairs={{0,4},{2,6},{4,8},{6,10},{8,12},{10,14},{12,0},{14,2},{1,5},{3,7},... | collective-permute-start | bytes 589832 | tf_op jit(solution)/shard_map/ppermute | solution.py:162
  33.4 18.3 %collective-permute-start.3 = (bf16[64,4224]{1,0:T(8,128)(2,1)}, bf16[64,4224]{1,0:T(8,128)(2,1)}, u32[]{:S(2)}, u32[]{:S(2)}) collective-permute-start(bf16[64,4224]{1,0:T(8,128)(2,1)} %collective-permute-done.1.refs_2_), channel_id=1, source_target_pairs={{0,2},{2,0},{4,6},{6,4},{8,10},{10,8},{12,14},{14,12},{1,3},{3,1},... | collective-permute-start | bytes 1622024 | tf_op jit(solution)/shard_map/ppermute | solution.py:162
  38.6 19.1 %collective-permute-start.6 = (bf16[64,4224]{1,0:T(8,128)(2,1)}, bf16[64,4224]{1,0:T(8,128)(2,1)}, u32[]{:S(2)}, u32[]{:S(2)}) collective-permute-start(bf16[64,4224]{1,0:T(8,128)(2,1)} %collective-permute-done.4.refs_6_), channel_id=1, source_target_pairs={{0,2},{2,0},{4,6},{6,4},{8,10},{10,8},{12,14},{14,12},{1,3},{3,1},... | collective-permute-start | bytes 1622024 | tf_op jit(solution)/shard_map/ppermute | solution.py:162
  40.9 9.7 %collective-permute-start.5 = (bf16[128,768]{1,0:T(8,128)(2,1)S(1)}, bf16[128,768]{1,0:T(8,128)(2,1)}, u32[]{:S(2)}, u32[]{:S(2)}) collective-permute-start(bf16[128,768]{1,0:T(8,128)(2,1)S(1)} %collective-permute-done.2), channel_id=1, source_target_pairs={{0,4},{2,6},{4,8},{6,10},{8,12},{10,14},{12,0},{14,2},{1,5},{3,7},... | collective-permute-start | bytes 589832 | tf_op jit(solution)/shard_map/ppermute | solution.py:162
  41.0 30.5 %collective-permute-start.9 = (bf16[64,4224]{1,0:T(8,128)(2,1)}, bf16[64,4224]{1,0:T(8,128)(2,1)}, u32[]{:S(2)}, u32[]{:S(2)}) collective-permute-start(bf16[64,4224]{1,0:T(8,128)(2,1)} %collective-permute-done.4.refs_6_), channel_id=1, source_target_pairs={{0,4},{2,6},{4,8},{6,10},{8,12},{10,14},{12,0},{14,2},{1,5},{3,7},... | collective-permute-start | bytes 1622024 | tf_op jit(solution)/shard_map/ppermute | solution.py:162
  51.6 21.4 %collective-permute-start.10 = (bf16[128,768]{1,0:T(8,128)(2,1)}, bf16[128,768]{1,0:T(8,128)(2,1)}, u32[]{:S(2)}, u32[]{:S(2)}) collective-permute-start(bf16[128,768]{1,0:T(8,128)(2,1)} %collective-permute-done.5), channel_id=1, source_target_pairs={{0,4},{2,6},{4,8},{6,10},{8,12},{10,14},{12,0},{14,2},{1,5},{3,7},... | collective-permute-start | bytes 589832 | tf_op jit(solution)/shard_map/ppermute | solution.py:162
  57.7 1.1 %copy-start.2 = (bf16[64,4992]{1,0:T(8,128)(2,1)S(1)}, bf16[64,4992]{1,0:T(8,128)(2,1)}, u32[]{:S(2)}) copy-start(bf16[64,4992]{1,0:T(8,128)(2,1)} %copy-done.1) | copy-start | bytes 1916932
  58.8 6.3 %copy-start.3 = (bf16[64,4992]{1,0:T(8,128)(2,1)S(1)}, bf16[64,4992]{1,0:T(8,128)(2,1)}, u32[]{:S(2)}) copy-start(bf16[64,4992]{1,0:T(8,128)(2,1)} %copy-done.1) | copy-start | bytes 1916932
  70.4 1.0 copy-start.7
  71.3 2.7 %collective-permute-start.8 = (f32[6,32,512]{2,1,0:T(8,128)}, f32[6,32,512]{2,1,0:T(8,128)S(1)}, u32[]{:S(2)}, u32[]{:S(2)}) collective-permute-start(f32[6,32,512]{2,1,0:T(8,128)} %dynamic-slice_bitcast_fusion.1), channel_id=1, source_target_pairs={{0,1},{1,0},{2,3},{3,2},{4,5},{5,4},{6,7},{7,6},{8,9},{9,8},{10,11... | collective-permute-start | bytes 1179656 | tf_op jit(solution)/shard_map/ppermute | solution.py:207
  71.4 14.8 %collective-permute-start.11 = (bf16[64,4224]{1,0:T(8,128)(2,1)}, bf16[64,4224]{1,0:T(8,128)(2,1)S(1)}, u32[]{:S(2)}, u32[]{:S(2)}) collective-permute-start(bf16[64,4224]{1,0:T(8,128)(2,1)} %collective-permute-done.9.refs_0_), channel_id=1, source_target_pairs={{0,2},{2,0},{4,6},{6,4},{8,10},{10,8},{12,14},{14,12},{1,3},{3,1},... | collective-permute-start | bytes 1622024 | tf_op jit(solution)/shard_map/ppermute | solution.py:162
  91.7 8.9 %copy-start.4 = (s32[1,256]{1,0:T(1,128)S(1)}, s32[1,256]{1,0:T(1,128)}, u32[]{:S(2)}) copy-start(s32[1,256]{1,0:T(1,128)} %ids_ref.1) | copy-start | bytes 3076
  91.7 1.4 %collective-permute-start.12 = (f32[2,32,512]{2,1,0:T(8,128)S(1)}, f32[2,32,512]{2,1,0:T(8,128)S(1)}, u32[]{:S(2)}, u32[]{:S(2)}) collective-permute-start(f32[2,32,512]{2,1,0:T(8,128)S(1)} %dynamic-slice_bitcast_fusion.2), channel_id=1, source_target_pairs={{0,1},{1,0},{2,3},{3,2},{4,5},{5,4},{6,7},{7,6},{8,9},{9,8},{10,11... | collective-permute-start | bytes 393224 | tf_op jit(solution)/shard_map/ppermute | solution.py:207
  91.8 7.8 %collective-permute-start.13 = (f32[6,32,256]{2,1,0:T(8,128)S(1)}, f32[6,32,256]{2,1,0:T(8,128)S(1)}, u32[]{:S(2)}, u32[]{:S(2)}) collective-permute-start(f32[6,32,256]{2,1,0:T(8,128)S(1)} %get-tuple-element.9), channel_id=1, source_target_pairs={{0,16},{16,0},{1,17},{17,1},{2,18},{18,2},{3,19},{19,3},{4,20},{20... | collective-permute-start | bytes 589832 | tf_op jit(solution)/shard_map/ppermute | solution.py:208
  93.1 7.4 %collective-permute-start.14 = (f32[2,32,256]{2,1,0:T(8,128)S(1)}, f32[2,32,256]{2,1,0:T(8,128)S(1)}, u32[]{:S(2)}, u32[]{:S(2)}) collective-permute-start(f32[2,32,256]{2,1,0:T(8,128)S(1)} %get-tuple-element.17), channel_id=1, source_target_pairs={{0,16},{16,0},{1,17},{17,1},{2,18},{18,2},{3,19},{19,3},{4,20},{20... | collective-permute-start | bytes 196616 | tf_op jit(solution)/shard_map/ppermute | solution.py:208

commit v3 on v0

v3 whole, which is shorter than its diff:
```python
import functools

import jax
import jax.numpy as jnp
from jax import lax
from jax.experimental import pallas as pl
from jax.experimental.pallas import tpu as pltpu
from jax.sharding import PartitionSpec as P

BLOCK = 128
ALONE = 28
CHUNKS = 2
FIRST_VMEM = 60 << 20
VMEM = pl.BlockSpec(memory_space=pltpu.VMEM)
SMEM = pl.BlockSpec(memory_space=pltpu.SMEM)
NT = (((1,), (1,)), ((), ()))


def fast_length(mesh):
    line = list(mesh.devices[0, :, 0])
    size = len(line)
    if size < 2 or not all(hasattr(device, "coords") for device in line):
        return 2 if size % 2 == 0 else size

    def moved(a, b):
        return tuple(i for i, (p, q) in enumerate(zip(a.coords, b.coords)) if p != q)

    along = moved(line[0], line[1])
    length = 2
    while length < size and moved(line[0], line[length]) == along:
        length += 1
    return length if size % length == 0 else size


def scaled(codes, scales, at):
    return codes * scales[:, at : at + 1].astype(jnp.bfloat16)


def scales_of(exponents):
    powers = (jnp.int32(1) << (exponents + 3)).astype(jnp.float32) * 0.125
    return powers.T


def cut_kernel(alone, cuts, tile, part_ref, queries_ref, codes_ref, exponents_ref, *refs):
    *chunk_refs, sent_ref, codes_buffer, sent_buffer, query_sems, fetch_sems, store_sems = refs
    part = part_ref[0]
    blocks = exponents_ref.shape[0]
    far = (blocks - alone) * BLOCK
    first = pl.multiple_of(part * far, BLOCK)
    rest = pl.multiple_of((1 - part) * far, BLOCK)
    wide = alone * BLOCK

    copies = []

    def copy_columns(out_ref, start, stop):
        if start < wide:
            width = min(stop, wide) - start
            copies.append((
                queries_ref.at[0, :, pl.ds(pl.multiple_of(first + start, BLOCK), width)],
                out_ref.at[:, pl.ds(0, width)],
            ))
        if stop > wide:
            begin = max(start, wide)
            copies.append((
                queries_ref.at[0, :, pl.ds(begin, stop - begin)],
                out_ref.at[:, pl.ds(begin - start, stop - begin)],
            ))

    for out_ref, start, stop in zip(chunk_refs, cuts[:-1], cuts[1:]):
        copy_columns(out_ref, start, stop)
    moves = [pltpu.make_async_copy(a, b, query_sems.at[i]) for i, (a, b) in enumerate(copies)]
    tiles = codes_buffer.shape[0]

    def fetch(i):
        return pltpu.make_async_copy(
            codes_ref.at[pl.ds(i * tile, tile), pl.ds(rest, wide)], codes_buffer.at[i], fetch_sems.at[i]
        )

    def store(i):
        return pltpu.make_async_copy(sent_buffer.at[i], sent_ref.at[pl.ds(i * tile, tile)], store_sems.at[i])

    for i in range(tiles):
        fetch(i).start()
    for move in moves:
        move.start()
    near = exponents_ref[0:alone, :]
    away = exponents_ref[blocks - alone : blocks, :]
    pad = jnp.zeros((-alone % 8, near.shape[1]), jnp.int32)
    scales = scales_of(jnp.concatenate([jnp.where(part == 0, away, near), pad], axis=0))
    for i in range(tiles):
        fetch(i).wait()
        for block in range(alone):
            columns = slice(block * BLOCK, (block + 1) * BLOCK)
            sent_buffer[i, :, columns] = scaled(
                codes_buffer[i, :, columns], scales[i * tile : (i + 1) * tile], block
            )
        store(i).start()
    for move in moves:
        move.wait()
    for i in range(tiles):
        store(i).wait()


def cut(part, queries, codes, exponents, alone, cuts):
    rows = queries.shape[1]
    count = codes.shape[0]
    blocks = exponents.shape[0]
    tile = min(count, 64)
    tiles = count // tile
    anywhere = pl.BlockSpec(memory_space=pl.ANY)
    wide = alone * BLOCK
    chunks = len(cuts) - 1
    return pl.pallas_call(
        functools.partial(cut_kernel, alone, cuts, tile),
        out_shape=[jax.ShapeDtypeStruct((rows, b - a), jnp.bfloat16) for a, b in zip(cuts[:-1], cuts[1:])]
        + [jax.ShapeDtypeStruct((count, wide), jnp.bfloat16)],
        in_specs=[SMEM, anywhere, anywhere, VMEM],
        out_specs=[anywhere] * (chunks + 1),
        scratch_shapes=[
            pltpu.VMEM((tiles, tile, wide), jnp.bfloat16),
            pltpu.VMEM((tiles, tile, wide), jnp.bfloat16),
            pltpu.SemaphoreType.DMA((2 * chunks,)),
            pltpu.SemaphoreType.DMA((tiles,)),
            pltpu.SemaphoreType.DMA((tiles,)),
        ],
        compiler_params=pltpu.CompilerParams(vmem_limit_bytes=FIRST_VMEM),
        cost_estimate=pl.CostEstimate(flops=codes.size, bytes_accessed=2 * codes.size, transcendentals=0),
        name="cut_queries",
    )(part, queries, codes, exponents)


def scale_kernel(alone, part_ref, codes_ref, exponents_ref, out_ref):
    part = part_ref[0]
    blocks = exponents_ref.shape[0]
    far = blocks - alone
    own = jnp.where(part == 0, exponents_ref[0:alone, :], exponents_ref[far:blocks, :])
    kept = jnp.concatenate([own, exponents_ref[alone:far, :]], axis=0)
    pad = jnp.zeros((-kept.shape[0] % 8, kept.shape[1]), jnp.int32)
    scales = scales_of(jnp.concatenate([kept, pad], axis=0))
    for block in range(far):
        start = pl.multiple_of((part * far + block) * BLOCK, BLOCK) if block < alone else block * BLOCK
        out_ref[:, block * BLOCK : (block + 1) * BLOCK] = scaled(codes_ref[:, pl.ds(start, BLOCK)], scales, block)


def scale(part, codes, exponents, alone):
    shape = (codes.shape[0], (exponents.shape[0] - alone) * BLOCK)
    return pl.pallas_call(
        functools.partial(scale_kernel, alone),
        out_shape=jax.ShapeDtypeStruct(shape, jnp.bfloat16),
        in_specs=[SMEM, VMEM, VMEM],
        out_specs=VMEM,
        compiler_params=pltpu.CompilerParams(vmem_limit_bytes=16 << 20),
        cost_estimate=pl.CostEstimate(flops=codes.size, bytes_accessed=4 * codes.size, transcendentals=0),
        name="scale_codes",
    )(part, codes, exponents)


def product(pieces, grads_ref):
    total = None
    first = 0
    for refs in pieces:
        width = min(refs[0].shape[1], grads_ref.shape[1] - first)
        if width <= 0:
            break
        rows = [ref[:, :width] for ref in refs]
        rows = jnp.concatenate(rows, axis=0) if len(rows) > 1 else rows[0]
        term = lax.dot_general(rows, grads_ref[:, first : first + width], NT, preferred_element_type=jnp.float32)
        total = term if total is None else total + term
        first += width
    return total


def unflatten(layout, refs):
    refs = list(refs)
    return [[refs.pop(0) for _ in range(arrays)] for arrays in layout]


def score_kernel(layout, rows, half_ref, *refs):
    *query_refs, grads_ref, keep_ref, send_ref = refs
    total = product(unflatten(layout, query_refs), grads_ref)
    for j in range(total.shape[0] // rows):
        low = total[j * rows : j * rows + rows // 2]
        high = total[j * rows + rows // 2 : (j + 1) * rows]
        keep_ref[j] = jnp.where(half_ref[0] == 0, low, high)
        send_ref[j] = jnp.where(half_ref[0] == 0, high, low)


def score(half, rows, pieces, grads):
    operands = [array for arrays in pieces for array in arrays]
    stacked = sum(array.shape[0] for array in pieces[0])
    shape = jax.ShapeDtypeStruct((stacked // rows, rows // 2, grads.shape[0]), jnp.float32)
    return pl.pallas_call(
        functools.partial(score_kernel, [len(arrays) for arrays in pieces], rows),
        out_shape=[shape, shape],
        in_specs=[SMEM] + [VMEM] * (len(operands) + 1),
        out_specs=[VMEM, VMEM],
        compiler_params=pltpu.CompilerParams(vmem_limit_bytes=16 << 20),
        cost_estimate=pl.CostEstimate(
            flops=2 * stacked * grads.size, bytes_accessed=2 * grads.size, transcendentals=0
        ),
        name="score",
    )(half, *operands, grads)


def place_kernel(rows, order_ref, ids_ref, *refs):
    *share_refs, out_ref = refs
    count = ids_ref.shape[1]
    slots = lax.broadcasted_iota(jnp.int32, (count, count), 0)
    table = (slots == jnp.broadcast_to(ids_ref[...], (count, count))).astype(jnp.float32)
    j = 0
    for first in range(0, len(share_refs), 4):
        a, b, c, d = (ref[...] for ref in share_refs[first : first + 4])
        raw = (d + c) + (b + a)
        placed = lax.dot_general(
            raw, table, NT, precision=lax.Precision.HIGHEST, preferred_element_type=jnp.float32
        )
        for i in range(raw.shape[0] // rows):
            out_ref[order_ref[j]] = placed[i * rows : (i + 1) * rows]
            j += 1


def place(order, ids, shares, rows):
    return pl.pallas_call(
        functools.partial(place_kernel, rows),
        out_shape=jax.ShapeDtypeStruct((order.shape[0], rows, ids.shape[1]), jnp.float32),
        in_specs=[SMEM] + [VMEM] * (len(shares) + 1),
        out_specs=VMEM,
        compiler_params=pltpu.CompilerParams(vmem_limit_bytes=16 << 20),
        name="place_scores",
    )(order, ids, *shares)


def shards(fast, parts, total, queries, codes, exponents, example_ids):
    part = lax.axis_index("groups")
    here = lax.axis_index("ex")
    half = lax.axis_index("dim")[None]
    slow = total // fast
    rows = queries.shape[1]
    count = codes.shape[0]
    blocks = exponents.shape[1]
    alone = blocks * ALONE // 64
    held = blocks - alone
    cuts = [i * held // CHUNKS * BLOCK for i in range(CHUNKS + 1)]

    def step(value, length, stride):
        pairs = [
            (i, i + stride if (i // stride) % length < length - 1 else i - (length - 1) * stride)
            for i in range(total)
        ]
        return lax.ppermute(value, "ex", pairs)

    def along_fast(value):
        values = [value]
        for _ in range(fast - 1):
            values.append(step(values[-1], fast, 1))
        return values

    swap = [(i, parts - 1 - i) for i in range(parts)]
    by_block = exponents.T
    *chunks, sent = cut(part[None], queries, codes, by_block, alone, cuts)
    theirs = lax.ppermute(sent, "groups", swap)
    ours = scale(part[None], codes, by_block, alone)
    near = [[] for _ in range(slow)]
    for c, chunk in enumerate(chunks):
        for s in range(slow):
            values = along_fast(chunk)
            if s < slow - 1:
                chunk, *values = lax.optimization_barrier([step(chunk, slow, fast)] + values)
                if c == CHUNKS - 1 and s == 0:
                    chunk, ours = lax.optimization_barrier((chunk, ours))
            near[s].append(values)

    def stack(arrays):
        return arrays if rows % 16 == 0 else [jnp.concatenate(arrays, axis=0)]

    def pieces_of(steps):
        return [[a for s in steps for a in stack(near[s][c])] for c in range(CHUNKS)]

    across = [(i, 3 - i) for i in range(4)]
    shares = []
    for steps in (range(slow - 1), [slow - 1]):
        pieces = pieces_of(steps)
        keep, send = score(half, rows, pieces, theirs)
        theirs, keep, send = lax.optimization_barrier((theirs, keep, send))
        shares += [lax.ppermute(send, ("groups", "dim"), across), lax.ppermute(keep, "groups", swap)]
        keep, send = score(half, rows, pieces, ours)
        shares += [lax.ppermute(send, "dim", [(0, 1), (1, 0)]), keep]
    shares = [share.reshape(-1, count) for share in shares]
    order = jnp.stack([
        lax.rem(here // fast + slow - s, slow) * fast + lax.rem(here % fast + fast - t, fast)
        for s in range(slow)
        for t in range(fast)
    ]).astype(jnp.int32)
    return place(order, example_ids, shares, rows // 2)


def solution(mesh):
    placed = (
        P("ex", None, "dim"),
        P(("groups", "ex"), "dim"),
        P(("groups", "ex"), "dim"),
        P(("groups", "ex"), None),
    )
    return jax.shard_map(
        functools.partial(shards, fast_length(mesh), mesh.shape["groups"], mesh.shape["ex"]),
        mesh=mesh,
        in_specs=placed,
        out_specs=P(None, "dim", ("groups", "ex")),
        check_vma=False,
    )
```

time: 165 us -> 98 us (0.59)
  waiting for transfers between devices: 136 us -> 22 us
  Pallas kernels: 0 us -> 31.7 us
  starting transfers between devices: 0.04 us -> 26.1 us
  local copies, waits for them, and re-layouts: 3.47 us -> 17.4 us
  between operations: 13.4 us -> 0.15 us
  matrix products: 10.7 us -> 0 us
    all_gather x1 -> x0, waiting for transfers between devices: 129 us -> none  [shards(): lax.all_gather(queries, 'ex', axis=0, tiled=True)]
    pallas_call x0 -> x7, Pallas kernels: none -> 31.7 us  [the longest x1 20 us: cut(): pl.pallas_call(functools.partial(cut_kernel, alone, cuts, tile), out_shap...]
    ppermute x0 -> x21, starting transfers between devices: none -> 26.1 us  [the longest x14 18.7 us: step(): return lax.ppermute(value, 'ex', pairs)]
    ppermute x0 -> x21, waiting for transfers between devices: none -> 22 us  [the longest x14 17.5 us: step(): return lax.ppermute(value, 'ex', pairs)]
    unnamed x4 -> x50, local copies, waits for them, and re-layouts: 1.08 us -> 17.3 us
    dot_general x2 -> x0, matrix products: 10.7 us -> none  [the longest x1 8.65 us: shards(): jnp.einsum('nho,so->nhs', lax.all_gather(queries, 'ex', axis=0, tiled=Tru...]
    reduce_scatter x1 -> x0, waiting for transfers between devices: 6.28 us -> none  [shards(): lax.psum_scatter(partial_scores, 'dim', scatter_dimension=1, tiled=True)]
    mul x1 -> x0, local copies, waits for them, and re-layouts: 2.3 us -> none  [dequantize(): codes.reshape(rows, blocks, BLOCK).astype(jnp.float32)]
  transfers between devices with their start and end apart: 2 -> 21, of which waited for: 2 -> 8; matrix products, arithmetic and copies ran while one was open for 1% -> 0% of each run, Pallas kernels for 0% -> 10%
where the time goes in v3:
time: 98 us; the launch traced here: 97.4 us
  Pallas kernels  31.7 us (32%)
  starting transfers between devices  26.1 us (27%)
  waiting for transfers between devices  22 us (22%)
  local copies, waits for them, and re-layouts  17.4 us (18%)
    pallas_call x1, Pallas kernels, cut(): pl.pallas_call(functools.partial(cut_kernel, alone, cuts, tile), out_shap...  20 us
    ppermute x14, starting transfers between devices, step(): return lax.ppermute(value, 'ex', pairs)  18.7 us
    ppermute x14, waiting for transfers between devices, step(): return lax.ppermute(value, 'ex', pairs)  17.5 us
    unnamed x50, local copies, waits for them, and re-layouts  17.3 us
    pallas_call x4, Pallas kernels, score(): pl.pallas_call(functools.partial(score_kernel, [len(arrays) for arrays in...  8.96 us
    ppermute x2, starting transfers between devices, shards(): lax.ppermute(keep, 'groups', swap)  3.05 us
    ppermute x1, starting transfers between devices, shards(): theirs = lax.ppermute(sent, 'groups', swap)  3.03 us
    ppermute x2, waiting for transfers between devices, shards(): lax.ppermute(send, ('groups', 'dim'), across)  2.51 us
  transfers between devices with their start and end apart: 21, of which 8 were waited for; matrix products, arithmetic and copies ran while one was open for 0% of the time, Pallas kernels for 10%

profile of v3, /device:TPU:0, one launch (start us, length us, event | category | flops | bytes accessed | tf_op | source)
XLA Modules:
  0.0 97.4 jit_solution(8135477712036048292)
XLA Ops:
  0.0 20.0 %cut_queries.1 = (bf16[64,2304]{1,0:T(8,128)(2,1)}, bf16[64,2304]{1,0:T(8,128)(2,1)}, bf16[256,3584]{1,0:T(8,128)(2,1)}) custom-call(s32[1]{0:T(128)} %bitcast.8.part_ref, bf16[1,64,8192]{2,1,0:T(8,128)(2,1)} %queries_ref.1, bf16[256,8192]{1,0:T(8,128)(2,1)} %codes_ref.3, s32[64,256]{1,0:T(8,128)} %bitcast.19), custom_call_target="tpu_custom_call" | custom-call | flops 2097152 | bytes 4194304 | tf_op jit(solution)/shard_map/cut_queries/pallas_call | solution.py:113
  20.0 3.0 %collective-permute-start = (bf16[256,3584]{1,0:T(8,128)(2,1)}, bf16[256,3584]{1,0:T(8,128)(2,1)}, u32[]{:S(2)}, u32[]{:S(2)}) collective-permute-start(bf16[256,3584]{1,0:T(8,128)(2,1)} %get-tuple-element.41), channel_id=1, source_target_pairs={{0,16},{16,0},{1,17},{17,1},{2,18},{18,2},{3,19},{19,3},{4,20},{20... | collective-permute-start | bytes 5505032 | tf_op jit(solution)/shard_map/ppermute | solution.py:261
  23.0 1.6 %collective-permute-start.1 = (bf16[64,2304]{1,0:T(8,128)(2,1)}, bf16[64,2304]{1,0:T(8,128)(2,1)S(1)}, u32[]{:S(2)}, u32[]{:S(2)}) collective-permute-start(bf16[64,2304]{1,0:T(8,128)(2,1)} %get-tuple-element.43.refs_0_), channel_id=1, source_target_pairs={{0,4},{2,6},{4,8},{6,10},{8,12},{10,14},{12,0},{14,2},{1,5},{3,7},... | collective-permute-start | bytes 884744 | tf_op jit(solution)/shard_map/ppermute | solution.py:250
  24.6 1.5 %collective-permute-start.2 = (bf16[64,2304]{1,0:T(8,128)(2,1)}, bf16[64,2304]{1,0:T(8,128)(2,1)S(1)}, u32[]{:S(2)}, u32[]{:S(2)}) collective-permute-start(bf16[64,2304]{1,0:T(8,128)(2,1)} %get-tuple-element.43.refs_0_), channel_id=1, source_target_pairs={{0,2},{2,0},{4,6},{6,4},{8,10},{10,8},{12,14},{14,12},{1,3},{3,1},... | collective-permute-start | bytes 884744 | tf_op jit(solution)/shard_map/ppermute | solution.py:250
  26.1 1.6 %collective-permute-start.7 = (bf16[64,2304]{1,0:T(8,128)(2,1)}, bf16[64,2304]{1,0:T(8,128)(2,1)S(1)}, u32[]{:S(2)}, u32[]{:S(2)}) collective-permute-start(bf16[64,2304]{1,0:T(8,128)(2,1)} %get-tuple-element.52.refs_6_), channel_id=1, source_target_pairs={{0,4},{2,6},{4,8},{6,10},{8,12},{10,14},{12,0},{14,2},{1,5},{3,7},... | collective-permute-start | bytes 884744 | tf_op jit(solution)/shard_map/ppermute | solution.py:250
  27.7 0.5 collective-permute-start.8
  28.2 2.2 %copy-done = bf16[256,8192]{1,0:T(8,128)(2,1)S(1)} copy-done((bf16[256,8192]{1,0:T(8,128)(2,1)S(1)}, bf16[256,8192]{1,0:T(8,128)(2,1)}, u32[]{:S(2)}) %copy-start) | copy-done | bytes 4194328
  30.4 0.8 scale_codes.1.refs_12_.refs_4_
  31.3 3.7 %collective-permute-done.1.refs_2_ = bf16[64,2304]{1,0:T(8,128)(2,1)S(1)} collective-permute-done((bf16[64,2304]{1,0:T(8,128)(2,1)}, bf16[64,2304]{1,0:T(8,128)(2,1)S(1)}, u32[]{:S(2)}, u32[]{:S(2)}) %collective-permute-start.1) | collective-permute-done | bytes 294944 | tf_op jit(solution)/shard_map/ppermute | solution.py:250
  35.0 0.0 collective-permute-done.2.refs_1_
  35.0 1.4 %collective-permute-start.3 = (bf16[64,2304]{1,0:T(8,128)(2,1)S(1)}, bf16[64,2304]{1,0:T(8,128)(2,1)S(1)}, u32[]{:S(2)}, u32[]{:S(2)}) collective-permute-start(bf16[64,2304]{1,0:T(8,128)(2,1)S(1)} %collective-permute-done.1.refs_2_), channel_id=1, source_target_pairs={{0,4},{2,6},{4,8},{6,10},{8,12},{10,14},{12,0},{14,2},{1,5},{3,7},... | collective-permute-start | bytes 884744 | tf_op jit(solution)/shard_map/ppermute | solution.py:250
  36.3 1.5 %collective-permute-start.4 = (bf16[64,2304]{1,0:T(8,128)(2,1)S(1)}, bf16[64,2304]{1,0:T(8,128)(2,1)S(1)}, u32[]{:S(2)}, u32[]{:S(2)}) collective-permute-start(bf16[64,2304]{1,0:T(8,128)(2,1)S(1)} %collective-permute-done.1.refs_2_), channel_id=1, source_target_pairs={{0,2},{2,0},{4,6},{6,4},{8,10},{10,8},{12,14},{14,12},{1,3},{3,1},... | collective-permute-start | bytes 884744 | tf_op jit(solution)/shard_map/ppermute | solution.py:250
  37.8 3.5 %collective-permute-done.7.refs_8_ = bf16[64,2304]{1,0:T(8,128)(2,1)S(1)} collective-permute-done((bf16[64,2304]{1,0:T(8,128)(2,1)}, bf16[64,2304]{1,0:T(8,128)(2,1)S(1)}, u32[]{:S(2)}, u32[]{:S(2)}) %collective-permute-start.7) | collective-permute-done | bytes 294944 | tf_op jit(solution)/shard_map/ppermute | solution.py:250
  41.3 0.0 collective-permute-done.8.refs_7_
  41.3 0.7 copy-done.5
  42.0 1.4 %collective-permute-start.9 = (bf16[64,2304]{1,0:T(8,128)(2,1)S(1)}, bf16[64,2304]{1,0:T(8,128)(2,1)S(1)}, u32[]{:S(2)}, u32[]{:S(2)}) collective-permute-start(bf16[64,2304]{1,0:T(8,128)(2,1)S(1)} %collective-permute-done.7.refs_8_), channel_id=1, source_target_pairs={{0,4},{2,6},{4,8},{6,10},{8,12},{10,14},{12,0},{14,2},{1,5},{3,7},... | collective-permute-start | bytes 884744 | tf_op jit(solution)/shard_map/ppermute | solution.py:250
  43.4 1.5 %collective-permute-start.10 = (bf16[64,2304]{1,0:T(8,128)(2,1)S(1)}, bf16[64,2304]{1,0:T(8,128)(2,1)S(1)}, u32[]{:S(2)}, u32[]{:S(2)}) collective-permute-start(bf16[64,2304]{1,0:T(8,128)(2,1)S(1)} %collective-permute-done.7.refs_8_), channel_id=1, source_target_pairs={{0,2},{2,0},{4,6},{6,4},{8,10},{10,8},{12,14},{14,12},{1,3},{3,1},... | collective-permute-start | bytes 884744 | tf_op jit(solution)/shard_map/ppermute | solution.py:250
  44.9 0.7 copy-done.3
  45.6 2.0 %collective-permute-done.3.refs_4_ = bf16[64,2304]{1,0:T(8,128)(2,1)S(1)} collective-permute-done((bf16[64,2304]{1,0:T(8,128)(2,1)S(1)}, bf16[64,2304]{1,0:T(8,128)(2,1)S(1)}, u32[]{:S(2)}, u32[]{:S(2)}) %collective-permute-start.3) | collective-permute-done | bytes 294944 | tf_op jit(solution)/shard_map/ppermute | solution.py:250
  47.6 0.0 collective-permute-done.4.refs_3_
  47.6 0.7 copy-done.9
  48.3 1.4 %collective-permute-start.5 = (bf16[64,2304]{1,0:T(8,128)(2,1)S(1)}, bf16[64,2304]{1,0:T(8,128)(2,1)}, u32[]{:S(2)}, u32[]{:S(2)}) collective-permute-start(bf16[64,2304]{1,0:T(8,128)(2,1)S(1)} %collective-permute-done.3.refs_4_), channel_id=1, source_target_pairs={{0,4},{2,6},{4,8},{6,10},{8,12},{10,14},{12,0},{14,2},{1,5},{3,7},... | collective-permute-start | bytes 884744 | tf_op jit(solution)/shard_map/ppermute | solution.py:250
  49.7 1.5 %collective-permute-start.6 = (bf16[64,2304]{1,0:T(8,128)(2,1)S(1)}, bf16[64,2304]{1,0:T(8,128)(2,1)S(1)}, u32[]{:S(2)}, u32[]{:S(2)}) collective-permute-start(bf16[64,2304]{1,0:T(8,128)(2,1)S(1)} %collective-permute-done.3.refs_4_), channel_id=1, source_target_pairs={{0,2},{2,0},{4,6},{6,4},{8,10},{10,8},{12,14},{14,12},{1,3},{3,1},... | collective-permute-start | bytes 884744 | tf_op jit(solution)/shard_map/ppermute | solution.py:250
  51.2 0.7 copy-done.7
  51.9 2.0 %collective-permute-done.9.refs_10_ = bf16[64,2304]{1,0:T(8,128)(2,1)S(1)} collective-permute-done((bf16[64,2304]{1,0:T(8,128)(2,1)S(1)}, bf16[64,2304]{1,0:T(8,128)(2,1)S(1)}, u32[]{:S(2)}, u32[]{:S(2)}) %collective-permute-start.9) | collective-permute-done | bytes 294944 | tf_op jit(solution)/shard_map/ppermute | solution.py:250
  53.9 0.0 collective-permute-done.10.refs_9_
  53.9 0.7 copy-done.13
  54.7 1.4 %collective-permute-start.11 = (bf16[64,2304]{1,0:T(8,128)(2,1)S(1)}, bf16[64,2304]{1,0:T(8,128)(2,1)}, u32[]{:S(2)}, u32[]{:S(2)}) collective-permute-start(bf16[64,2304]{1,0:T(8,128)(2,1)S(1)} %collective-permute-done.9.refs_10_), channel_id=1, source_target_pairs={{0,4},{2,6},{4,8},{6,10},{8,12},{10,14},{12,0},{14,2},{1,5},{3,7},... | collective-permute-start | bytes 884744 | tf_op jit(solution)/shard_map/ppermute | solution.py:250
  56.0 1.5 %collective-permute-start.12 = (bf16[64,2304]{1,0:T(8,128)(2,1)S(1)}, bf16[64,2304]{1,0:T(8,128)(2,1)S(1)}, u32[]{:S(2)}, u32[]{:S(2)}) collective-permute-start(bf16[64,2304]{1,0:T(8,128)(2,1)S(1)} %collective-permute-done.9.refs_10_), channel_id=1, source_target_pairs={{0,2},{2,0},{4,6},{6,4},{8,10},{10,8},{12,14},{14,12},{1,3},{3,1},... | collective-permute-start | bytes 884744 | tf_op jit(solution)/shard_map/ppermute | solution.py:250
  57.5 0.7 copy-done.11
  58.3 2.1 %collective-permute-done.5.refs_0_ = bf16[64,2304]{1,0:T(8,128)(2,1)} collective-permute-done((bf16[64,2304]{1,0:T(8,128)(2,1)S(1)}, bf16[64,2304]{1,0:T(8,128)(2,1)}, u32[]{:S(2)}, u32[]{:S(2)}) %collective-permute-start.5) | collective-permute-done | bytes 294944 | tf_op jit(solution)/shard_map/ppermute | solution.py:250
  60.4 0.7 copy-done.15
  61.1 4.2 %collective-permute-done.11.refs_2_ = bf16[64,2304]{1,0:T(8,128)(2,1)} collective-permute-done((bf16[64,2304]{1,0:T(8,128)(2,1)S(1)}, bf16[64,2304]{1,0:T(8,128)(2,1)}, u32[]{:S(2)}, u32[]{:S(2)}) %collective-permute-start.11) | collective-permute-done | bytes 294944 | tf_op jit(solution)/shard_map/ppermute | solution.py:250
  65.3 0.0 collective-permute-done.12.refs_11_
  65.3 0.7 copy-done.17
  66.0 1.5 %collective-permute-start.16 = (bf16[64,2304]{1,0:T(8,128)(2,1)}, bf16[64,2304]{1,0:T(8,128)(2,1)}, u32[]{:S(2)}, u32[]{:S(2)}) collective-permute-start(bf16[64,2304]{1,0:T(8,128)(2,1)} %collective-permute-done.5.refs_0_), channel_id=1, source_target_pairs={{0,2},{2,0},{4,6},{6,4},{8,10},{10,8},{12,14},{14,12},{1,3},{3,1},... | collective-permute-start | bytes 884744 | tf_op jit(solution)/shard_map/ppermute | solution.py:250
  67.5 0.5 collective-permute-start.17
  68.0 1.0 copy-done.4
  69.0 1.0 copy-done.6
  70.0 1.0 copy-done.8
  70.9 1.0 copy-done.10
  71.9 1.0 copy-done.12
  72.9 1.0 copy-done.14
  73.8 1.0 copy-done.16
  74.8 1.0 copy-done.18
  75.7 1.1 %score.5 = (f32[6,32,256]{2,1,0:T(8,128)S(1)}, f32[6,32,256]{2,1,0:T(8,128)S(1)}) custom-call(s32[1]{0:T(128)} %bitcast.10.half_ref, bf16[64,2304]{1,0:T(8,128)(2,1)S(1)} %copy-done.1, bf16[64,2304]{1,0:T(8,128)(2,1)S(1)} %collective-permute-done.2.refs_1_, bf16[64,2304]{1,0:T(8,128)(2,1)S(1)} %collective-permute-done.1.refs_2_, ...), custom_call_target="tpu_custom_call" | custom-call | flops 905969664 | bytes 2359296 | tf_op jit(solution)/shard_map/score/pallas_call | solution.py:192
  76.9 0.1 collective-permute-start.15
  77.0 3.2 %score.4 = (f32[6,32,256]{2,1,0:T(8,128)}, f32[6,32,256]{2,1,0:T(8,128)}) custom-call(s32[1]{0:T(128)} %bitcast.10.half_ref, bf16[64,2304]{1,0:T(8,128)(2,1)S(1)} %copy-done.1, bf16[64,2304]{1,0:T(8,128)(2,1)S(1)} %collective-permute-done.2.refs_1_, bf16[64,2304]{1,0:T(8,128)(2,1)S(1)} %collective-permute-done.1.refs_2_, bf16[64,2304]{1,0:T(8,128)(2,1)S(1)} %copy-done.10, ...), custom_call_target="tpu_custom_call" | custom-call | flops 704643072 | bytes 1835008 | tf_op jit(solution)/shard_map/score/pallas_call | solution.py:192
  80.1 0.6 collective-permute-start.13
  80.7 1.5 %collective-permute-start.14 = (f32[6,32,256]{2,1,0:T(8,128)}, f32[6,32,256]{2,1,0:T(8,128)S(1)}, u32[]{:S(2)}, u32[]{:S(2)}) collective-permute-start(f32[6,32,256]{2,1,0:T(8,128)} %get-tuple-element.64), channel_id=1, source_target_pairs={{0,16},{16,0},{1,17},{17,1},{2,18},{18,2},{3,19},{19,3},{4,20},{20... | collective-permute-start | bytes 589832 | tf_op jit(solution)/shard_map/ppermute | solution.py:285
  82.2 0.0 collective-permute-done.16.refs_1_
  82.2 2.1 %score.7 = (f32[2,32,256]{2,1,0:T(8,128)S(1)}, f32[2,32,256]{2,1,0:T(8,128)S(1)}) custom-call(s32[1]{0:T(128)} %bitcast.10.half_ref, bf16[64,2304]{1,0:T(8,128)(2,1)} %collective-permute-done.5.refs_0_, bf16[64,2304]{1,0:T(8,128)(2,1)} %collective-permute-done.16.refs_1_, bf16[64,2304]{1,0:T(8,128)(2,1)} %collective-permute-done.11.refs_2_, ...), custom_call_target="tpu_custom_call" | custom-call | flops 301989888 | bytes 2359296 | tf_op jit(solution)/shard_map/score/pallas_call | solution.py:192
  84.4 0.0 copy-start.24
  84.4 0.1 collective-permute-start.20
  84.5 2.6 %score.6 = (f32[2,32,256]{2,1,0:T(8,128)S(1)}, f32[2,32,256]{2,1,0:T(8,128)S(1)}) custom-call(s32[1]{0:T(128)} %bitcast.10.half_ref, bf16[64,2304]{1,0:T(8,128)(2,1)} %collective-permute-done.5.refs_0_, bf16[64,2304]{1,0:T(8,128)(2,1)} %collective-permute-done.16.refs_1_, bf16[64,2304]{1,0:T(8,128)(2,1)} %collective-permute-done.11.refs_2_, ...), custom_call_target="tpu_custom_call" | custom-call | flops 234881024 | bytes 1835008 | tf_op jit(solution)/shard_map/score/pallas_call | solution.py:192
  87.1 0.7 collective-permute-start.18
  87.7 0.0 collective-permute-done.15
  87.7 0.7 copy-done.22
  88.4 1.5 %collective-permute-start.19 = (f32[2,32,256]{2,1,0:T(8,128)S(1)}, f32[2,32,256]{2,1,0:T(8,128)S(1)}, u32[]{:S(2)}, u32[]{:S(2)}) collective-permute-start(f32[2,32,256]{2,1,0:T(8,128)S(1)} %get-tuple-element.74), channel_id=1, source_target_pairs={{0,16},{16,0},{1,17},{17,1},{2,18},{18,2},{3,19},{19,3},{4,20},{20... | collective-permute-start | bytes 196616 | tf_op jit(solution)/shard_map/ppermute | solution.py:285
  89.9 0.1 stack.35.order_ref
  90.0 2.5 %collective-permute-done.18 = f32[2,32,256]{2,1,0:T(8,128)S(1)} collective-permute-done((f32[2,32,256]{2,1,0:T(8,128)S(1)}, f32[2,32,256]{2,1,0:T(8,128)S(1)}, u32[]{:S(2)}, u32[]{:S(2)}) %collective-permute-start.18) | collective-permute-done | bytes 65568 | tf_op jit(solution)/shard_map/ppermute | solution.py:285
  92.5 2.0 %collective-permute-done.19 = f32[2,32,256]{2,1,0:T(8,128)S(1)} collective-permute-done((f32[2,32,256]{2,1,0:T(8,128)S(1)}, f32[2,32,256]{2,1,0:T(8,128)S(1)}, u32[]{:S(2)}, u32[]{:S(2)}) %collective-permute-start.19) | collective-permute-done | bytes 65568 | tf_op jit(solution)/shard_map/ppermute | solution.py:285
  94.6 0.9 copy-done.23
  95.5 1.9 %place_scores.1 = f32[8,32,256]{2,1,0:T(8,128)} custom-call(s32[8]{0:T(128)S(1)} %stack.35.order_ref, s32[1,256]{1,0:T(1,128)S(1)} %copy-done.24, f32[192,256]{1,0:T(8,128)S(1)} %bitcast.23, f32[192,256]{1,0:T(8,128)S(1)} %bitcast.24, f32[192,256]{1,0:T(8,128)S(1)} %bitcast.22, f32[192,256]{1,0:T(8,128)S(1)} %bitcast.21, f32[64,256]{1,0:T(8,128)S(1)} %bitcast.27, ...), custom_call_target="tpu_custom_call" | custom-call | tf_op jit(solution)/shard_map/place_scores/pallas_call | solution.py:223
  (36 shorter events, 0.1 us)
Async XLA Ops:
  0.0 28.2 %copy-start.19 = (s32[256,64]{0,1:T(8,128)S(1)}, s32[256,64]{0,1:T(8,128)}, u32[]{:S(2)}) copy-start(s32[256,64]{0,1:T(8,128)} %param.6) | copy-start | bytes 196612
  20.0 56.9 %collective-permute-start = (bf16[256,3584]{1,0:T(8,128)(2,1)}, bf16[256,3584]{1,0:T(8,128)(2,1)}, u32[]{:S(2)}, u32[]{:S(2)}) collective-permute-start(bf16[256,3584]{1,0:T(8,128)(2,1)} %get-tuple-element.41), channel_id=1, source_target_pairs={{0,16},{16,0},{1,17},{17,1},{2,18},{18,2},{3,19},{19,3},{4,20},{20... | collective-permute-start | bytes 5505032 | tf_op jit(solution)/shard_map/ppermute | solution.py:261
  23.0 11.9 %collective-permute-start.1 = (bf16[64,2304]{1,0:T(8,128)(2,1)}, bf16[64,2304]{1,0:T(8,128)(2,1)S(1)}, u32[]{:S(2)}, u32[]{:S(2)}) collective-permute-start(bf16[64,2304]{1,0:T(8,128)(2,1)} %get-tuple-element.43.refs_0_), channel_id=1, source_target_pairs={{0,4},{2,6},{4,8},{6,10},{8,12},{10,14},{12,0},{14,2},{1,5},{3,7},... | collective-permute-start | bytes 884744 | tf_op jit(solution)/shard_map/ppermute | solution.py:250
  24.6 10.4 %collective-permute-start.2 = (bf16[64,2304]{1,0:T(8,128)(2,1)}, bf16[64,2304]{1,0:T(8,128)(2,1)S(1)}, u32[]{:S(2)}, u32[]{:S(2)}) collective-permute-start(bf16[64,2304]{1,0:T(8,128)(2,1)} %get-tuple-element.43.refs_0_), channel_id=1, source_target_pairs={{0,2},{2,0},{4,6},{6,4},{8,10},{10,8},{12,14},{14,12},{1,3},{3,1},... | collective-permute-start | bytes 884744 | tf_op jit(solution)/shard_map/ppermute | solution.py:250
  26.1 15.2 %collective-permute-start.7 = (bf16[64,2304]{1,0:T(8,128)(2,1)}, bf16[64,2304]{1,0:T(8,128)(2,1)S(1)}, u32[]{:S(2)}, u32[]{:S(2)}) collective-permute-start(bf16[64,2304]{1,0:T(8,128)(2,1)} %get-tuple-element.52.refs_6_), channel_id=1, source_target_pairs={{0,4},{2,6},{4,8},{6,10},{8,12},{10,14},{12,0},{14,2},{1,5},{3,7},... | collective-permute-start | bytes 884744 | tf_op jit(solution)/shard_map/ppermute | solution.py:250
  27.7 13.6 %collective-permute-start.8 = (bf16[64,2304]{1,0:T(8,128)(2,1)}, bf16[64,2304]{1,0:T(8,128)(2,1)S(1)}, u32[]{:S(2)}, u32[]{:S(2)}) collective-permute-start(bf16[64,2304]{1,0:T(8,128)(2,1)} %get-tuple-element.52.refs_6_), channel_id=1, source_target_pairs={{0,2},{2,0},{4,6},{6,4},{8,10},{10,8},{12,14},{14,12},{1,3},{3,1},... | collective-permute-start | bytes 884744 | tf_op jit(solution)/shard_map/ppermute | solution.py:250
  28.2 2.2 %copy-start = (bf16[256,8192]{1,0:T(8,128)(2,1)S(1)}, bf16[256,8192]{1,0:T(8,128)(2,1)}, u32[]{:S(2)}) copy-start(bf16[256,8192]{1,0:T(8,128)(2,1)} %codes_ref.3) | copy-start | bytes 12582916
  30.4 37.6 %copy-start.1 = (bf16[64,2304]{1,0:T(8,128)(2,1)S(1)}, bf16[64,2304]{1,0:T(8,128)(2,1)}, u32[]{:S(2)}) copy-start(bf16[64,2304]{1,0:T(8,128)(2,1)} %get-tuple-element.43.refs_0_) | copy-start | bytes 884740
  30.4 37.6 %copy-start.2 = (bf16[64,2304]{1,0:T(8,128)(2,1)S(1)}, bf16[64,2304]{1,0:T(8,128)(2,1)}, u32[]{:S(2)}) copy-start(bf16[64,2304]{1,0:T(8,128)(2,1)} %get-tuple-element.52.refs_6_) | copy-start | bytes 884740
  35.0 12.6 %collective-permute-start.3 = (bf16[64,2304]{1,0:T(8,128)(2,1)S(1)}, bf16[64,2304]{1,0:T(8,128)(2,1)S(1)}, u32[]{:S(2)}, u32[]{:S(2)}) collective-permute-start(bf16[64,2304]{1,0:T(8,128)(2,1)S(1)} %collective-permute-done.1.refs_2_), channel_id=1, source_target_pairs={{0,4},{2,6},{4,8},{6,10},{8,12},{10,14},{12,0},{14,2},{1,5},{3,7},... | collective-permute-start | bytes 884744 | tf_op jit(solution)/shard_map/ppermute | solution.py:250
  36.3 11.3 %collective-permute-start.4 = (bf16[64,2304]{1,0:T(8,128)(2,1)S(1)}, bf16[64,2304]{1,0:T(8,128)(2,1)S(1)}, u32[]{:S(2)}, u32[]{:S(2)}) collective-permute-start(bf16[64,2304]{1,0:T(8,128)(2,1)S(1)} %collective-permute-done.1.refs_2_), channel_id=1, source_target_pairs={{0,2},{2,0},{4,6},{6,4},{8,10},{10,8},{12,14},{14,12},{1,3},{3,1},... | collective-permute-start | bytes 884744 | tf_op jit(solution)/shard_map/ppermute | solution.py:250
  41.3 0.7 copy-start.5
  42.0 11.9 %collective-permute-start.9 = (bf16[64,2304]{1,0:T(8,128)(2,1)S(1)}, bf16[64,2304]{1,0:T(8,128)(2,1)S(1)}, u32[]{:S(2)}, u32[]{:S(2)}) collective-permute-start(bf16[64,2304]{1,0:T(8,128)(2,1)S(1)} %collective-permute-done.7.refs_8_), channel_id=1, source_target_pairs={{0,4},{2,6},{4,8},{6,10},{8,12},{10,14},{12,0},{14,2},{1,5},{3,7},... | collective-permute-start | bytes 884744 | tf_op jit(solution)/shard_map/ppermute | solution.py:250
  43.4 10.5 %collective-permute-start.10 = (bf16[64,2304]{1,0:T(8,128)(2,1)S(1)}, bf16[64,2304]{1,0:T(8,128)(2,1)S(1)}, u32[]{:S(2)}, u32[]{:S(2)}) collective-permute-start(bf16[64,2304]{1,0:T(8,128)(2,1)S(1)} %collective-permute-done.7.refs_8_), channel_id=1, source_target_pairs={{0,2},{2,0},{4,6},{6,4},{8,10},{10,8},{12,14},{14,12},{1,3},{3,1},... | collective-permute-start | bytes 884744 | tf_op jit(solution)/shard_map/ppermute | solution.py:250
  44.9 0.7 copy-start.3
  47.6 0.7 copy-start.9
  48.3 12.0 %collective-permute-start.5 = (bf16[64,2304]{1,0:T(8,128)(2,1)S(1)}, bf16[64,2304]{1,0:T(8,128)(2,1)}, u32[]{:S(2)}, u32[]{:S(2)}) collective-permute-start(bf16[64,2304]{1,0:T(8,128)(2,1)S(1)} %collective-permute-done.3.refs_4_), channel_id=1, source_target_pairs={{0,4},{2,6},{4,8},{6,10},{8,12},{10,14},{12,0},{14,2},{1,5},{3,7},... | collective-permute-start | bytes 884744 | tf_op jit(solution)/shard_map/ppermute | solution.py:250
  49.7 10.6 %collective-permute-start.6 = (bf16[64,2304]{1,0:T(8,128)(2,1)S(1)}, bf16[64,2304]{1,0:T(8,128)(2,1)S(1)}, u32[]{:S(2)}, u32[]{:S(2)}) collective-permute-start(bf16[64,2304]{1,0:T(8,128)(2,1)S(1)} %collective-permute-done.3.refs_4_), channel_id=1, source_target_pairs={{0,2},{2,0},{4,6},{6,4},{8,10},{10,8},{12,14},{14,12},{1,3},{3,1},... | collective-permute-start | bytes 884744 | tf_op jit(solution)/shard_map/ppermute | solution.py:250
  51.2 0.7 copy-start.7
  53.9 0.7 copy-start.13
  54.7 10.6 %collective-permute-start.11 = (bf16[64,2304]{1,0:T(8,128)(2,1)S(1)}, bf16[64,2304]{1,0:T(8,128)(2,1)}, u32[]{:S(2)}, u32[]{:S(2)}) collective-permute-start(bf16[64,2304]{1,0:T(8,128)(2,1)S(1)} %collective-permute-done.9.refs_10_), channel_id=1, source_target_pairs={{0,4},{2,6},{4,8},{6,10},{8,12},{10,14},{12,0},{14,2},{1,5},{3,7},... | collective-permute-start | bytes 884744 | tf_op jit(solution)/shard_map/ppermute | solution.py:250
  56.0 9.2 %collective-permute-start.12 = (bf16[64,2304]{1,0:T(8,128)(2,1)S(1)}, bf16[64,2304]{1,0:T(8,128)(2,1)S(1)}, u32[]{:S(2)}, u32[]{:S(2)}) collective-permute-start(bf16[64,2304]{1,0:T(8,128)(2,1)S(1)} %collective-permute-done.9.refs_10_), channel_id=1, source_target_pairs={{0,2},{2,0},{4,6},{6,4},{8,10},{10,8},{12,14},{14,12},{1,3},{3,1},... | collective-permute-start | bytes 884744 | tf_op jit(solution)/shard_map/ppermute | solution.py:250
  57.5 0.7 copy-start.11
  60.4 0.7 copy-start.15
  65.3 0.7 copy-start.17
  66.0 16.2 %collective-permute-start.16 = (bf16[64,2304]{1,0:T(8,128)(2,1)}, bf16[64,2304]{1,0:T(8,128)(2,1)}, u32[]{:S(2)}, u32[]{:S(2)}) collective-permute-start(bf16[64,2304]{1,0:T(8,128)(2,1)} %collective-permute-done.5.refs_0_), channel_id=1, source_target_pairs={{0,2},{2,0},{4,6},{6,4},{8,10},{10,8},{12,14},{14,12},{1,3},{3,1},... | collective-permute-start | bytes 884744 | tf_op jit(solution)/shard_map/ppermute | solution.py:250
  67.5 14.7 %collective-permute-start.17 = (bf16[64,2304]{1,0:T(8,128)(2,1)}, bf16[64,2304]{1,0:T(8,128)(2,1)}, u32[]{:S(2)}, u32[]{:S(2)}) collective-permute-start(bf16[64,2304]{1,0:T(8,128)(2,1)} %collective-permute-done.11.refs_2_), channel_id=1, source_target_pairs={{0,2},{2,0},{4,6},{6,4},{8,10},{10,8},{12,14},{14,12},{1,3},{3,1},... | collective-permute-start | bytes 884744 | tf_op jit(solution)/shard_map/ppermute | solution.py:250
  68.0 1.0 copy-start.4
  69.0 1.0 copy-start.6
  70.0 1.0 copy-start.8
  70.9 1.0 copy-start.10
  71.9 1.0 copy-start.12
  72.9 1.0 copy-start.14
  73.8 1.0 copy-start.16
  74.8 1.0 copy-start.18
  76.9 3.3 %copy-start.20 = (f32[6,32,256]{2,1,0:T(8,128)}, f32[6,32,256]{2,1,0:T(8,128)S(1)}, u32[]{:S(2)}) copy-start(f32[6,32,256]{2,1,0:T(8,128)S(1)} %get-tuple-element.67) | copy-start | bytes 589828
  76.9 10.8 %collective-permute-start.15 = (f32[6,32,256]{2,1,0:T(8,128)S(1)}, f32[6,32,256]{2,1,0:T(8,128)S(1)}, u32[]{:S(2)}, u32[]{:S(2)}) collective-permute-start(f32[6,32,256]{2,1,0:T(8,128)S(1)} %get-tuple-element.66), channel_id=1, source_target_pairs={{0,1},{1,0},{2,3},{3,2},{4,5},{5,4},{6,7},{7,6},{8,9},{9,8},{10,11... | collective-permute-start | bytes 589832 | tf_op jit(solution)/shard_map/ppermute | solution.py:287
  80.1 14.4 %collective-permute-start.13 = (f32[6,32,256]{2,1,0:T(8,128)}, f32[6,32,256]{2,1,0:T(8,128)S(1)}, u32[]{:S(2)}, u32[]{:S(2)}) collective-permute-start(f32[6,32,256]{2,1,0:T(8,128)} %get-tuple-element.63), channel_id=1, source_target_pairs={{0,17},{1,16},{16,1},{17,0},{2,19},{3,18},{18,3},{19,2},{4,21},{5,... | collective-permute-start | bytes 589832 | tf_op jit(solution)/shard_map/ppermute | solution.py:285
  80.7 13.8 %collective-permute-start.14 = (f32[6,32,256]{2,1,0:T(8,128)}, f32[6,32,256]{2,1,0:T(8,128)S(1)}, u32[]{:S(2)}, u32[]{:S(2)}) collective-permute-start(f32[6,32,256]{2,1,0:T(8,128)} %get-tuple-element.64), channel_id=1, source_target_pairs={{0,16},{16,0},{1,17},{17,1},{2,18},{18,2},{3,19},{19,3},{4,20},{20... | collective-permute-start | bytes 589832 | tf_op jit(solution)/shard_map/ppermute | solution.py:285
  84.3 10.2 %copy-start.21 = (f32[6,32,256]{2,1,0:T(8,128)S(1)}, f32[6,32,256]{2,1,0:T(8,128)}, u32[]{:S(2)}) copy-start(f32[6,32,256]{2,1,0:T(8,128)} %copy-done.20) | copy-start | bytes 589828
  84.4 10.2 %copy-start.24 = (s32[1,256]{1,0:T(1,128)S(1)}, s32[1,256]{1,0:T(1,128)}, u32[]{:S(2)}) copy-start(s32[1,256]{1,0:T(1,128)} %ids_ref.1) | copy-start | bytes 3076
  84.4 5.7 %collective-permute-start.20 = (f32[2,32,256]{2,1,0:T(8,128)S(1)}, f32[2,32,256]{2,1,0:T(8,128)S(1)}, u32[]{:S(2)}, u32[]{:S(2)}) collective-permute-start(f32[2,32,256]{2,1,0:T(8,128)S(1)} %get-tuple-element.75), channel_id=1, source_target_pairs={{0,1},{1,0},{2,3},{3,2},{4,5},{5,4},{6,7},{7,6},{8,9},{9,8},{10,11... | collective-permute-start | bytes 196616 | tf_op jit(solution)/shard_map/ppermute | solution.py:287
  87.1 5.5 %collective-permute-start.18 = (f32[2,32,256]{2,1,0:T(8,128)S(1)}, f32[2,32,256]{2,1,0:T(8,128)S(1)}, u32[]{:S(2)}, u32[]{:S(2)}) collective-permute-start(f32[2,32,256]{2,1,0:T(8,128)S(1)} %get-tuple-element.73), channel_id=1, source_target_pairs={{0,17},{1,16},{16,1},{17,0},{2,19},{3,18},{18,3},{19,2},{4,21},{5,... | collective-permute-start | bytes 196616 | tf_op jit(solution)/shard_map/ppermute | solution.py:285
  87.7 0.7 copy-start.22
  88.4 6.1 %collective-permute-start.19 = (f32[2,32,256]{2,1,0:T(8,128)S(1)}, f32[2,32,256]{2,1,0:T(8,128)S(1)}, u32[]{:S(2)}, u32[]{:S(2)}) collective-permute-start(f32[2,32,256]{2,1,0:T(8,128)S(1)} %get-tuple-element.74), channel_id=1, source_target_pairs={{0,16},{16,0},{1,17},{17,1},{2,18},{18,2},{3,19},{19,3},{4,20},{20... | collective-permute-start | bytes 196616 | tf_op jit(solution)/shard_map/ppermute | solution.py:285
  94.6 0.9 copy-start.23

commit v4 on v3

--- a/solution.py
+++ b/solution.py
@@ -10,10 +10,17 @@
 BLOCK = 128
 ALONE = 28
 CHUNKS = 2
-FIRST_VMEM = 60 << 20
 VMEM = pl.BlockSpec(memory_space=pltpu.VMEM)
 SMEM = pl.BlockSpec(memory_space=pltpu.SMEM)
 NT = (((1,), (1,)), ((), ()))
+
+
+def in_vmem(arrays):
+    return [pltpu.with_memory_space_constraint(array, pltpu.VMEM) for array in arrays]
+
+
+def in_hbm(array):
+    return pltpu.with_memory_space_constraint(array, pltpu.HBM)
 
 
 def fast_length(mesh):
@@ -42,7 +49,7 @@
 
 
 def cut_kernel(alone, cuts, tile, part_ref, queries_ref, codes_ref, exponents_ref, *refs):
-    *chunk_refs, sent_ref, codes_buffer, sent_buffer, query_sems, fetch_sems, store_sems = refs
+    *chunk_refs, sent_ref, codes_buffer, powers, query_sems, fetch_sems, powers_sem = refs
     part = part_ref[0]
     blocks = exponents_ref.shape[0]
     far = (blocks - alone) * BLOCK
@@ -76,35 +83,31 @@
             codes_ref.at[pl.ds(i * tile, tile), pl.ds(rest, wide)], codes_buffer.at[i], fetch_sems.at[i]
         )
 
-    def store(i):
-        return pltpu.make_async_copy(sent_buffer.at[i], sent_ref.at[pl.ds(i * tile, tile)], store_sems.at[i])
-
+    powers_copy = pltpu.make_async_copy(exponents_ref, powers, powers_sem)
+    powers_copy.start()
     for i in range(tiles):
         fetch(i).start()
     for move in moves:
         move.start()
-    near = exponents_ref[0:alone, :]
-    away = exponents_ref[blocks - alone : blocks, :]
+    powers_copy.wait()
+    near = powers[0:alone, :]
+    away = powers[blocks - alone : blocks, :]
     pad = jnp.zeros((-alone % 8, near.shape[1]), jnp.int32)
     scales = scales_of(jnp.concatenate([jnp.where(part == 0, away, near), pad], axis=0))
     for i in range(tiles):
         fetch(i).wait()
         for block in range(alone):
             columns = slice(block * BLOCK, (block + 1) * BLOCK)
-            sent_buffer[i, :, columns] = scaled(
+            sent_ref[i * tile : (i + 1) * tile, columns] = scaled(
                 codes_buffer[i, :, columns], scales[i * tile : (i + 1) * tile], block
             )
-        store(i).start()
     for move in moves:
         move.wait()
-    for i in range(tiles):
-        store(i).wait()
 
 
 def cut(part, queries, codes, exponents, alone, cuts):
     rows = queries.shape[1]
     count = codes.shape[0]
-    blocks = exponents.shape[0]
     tile = min(count, 64)
     tiles = count // tile
     anywhere = pl.BlockSpec(memory_space=pl.ANY)
@@ -112,47 +115,73 @@
     chunks = len(cuts) - 1
     return pl.pallas_call(
         functools.partial(cut_kernel, alone, cuts, tile),
-        out_shape=[jax.ShapeDtypeStruct((rows, b - a), jnp.bfloat16) for a, b in zip(cuts[:-1], cuts[1:])]
-        + [jax.ShapeDtypeStruct((count, wide), jnp.bfloat16)],
-        in_specs=[SMEM, anywhere, anywhere, VMEM],
-        out_specs=[anywhere] * (chunks + 1),
+        out_shape=[pltpu.VMEM((rows, b - a), jnp.bfloat16) for a, b in zip(cuts[:-1], cuts[1:])]
+        + [pltpu.VMEM((count, wide), jnp.bfloat16)],
+        in_specs=[SMEM, anywhere, anywhere, anywhere],
+        out_specs=[VMEM] * (chunks + 1),
         scratch_shapes=[
             pltpu.VMEM((tiles, tile, wide), jnp.bfloat16),
-            pltpu.VMEM((tiles, tile, wide), jnp.bfloat16),
+            pltpu.VMEM(exponents.shape, exponents.dtype),
             pltpu.SemaphoreType.DMA((2 * chunks,)),
             pltpu.SemaphoreType.DMA((tiles,)),
-            pltpu.SemaphoreType.DMA((tiles,)),
+            pltpu.SemaphoreType.DMA,
         ],
-        compiler_params=pltpu.CompilerParams(vmem_limit_bytes=FIRST_VMEM),
+        compiler_params=pltpu.CompilerParams(vmem_limit_bytes=16 << 20),
         cost_estimate=pl.CostEstimate(flops=codes.size, bytes_accessed=2 * codes.size, transcendentals=0),
         name="cut_queries",
-    )(part, queries, codes, exponents)
-
-
-def scale_kernel(alone, part_ref, codes_ref, exponents_ref, out_ref):
+    )(part, in_hbm(queries), in_hbm(codes), in_hbm(exponents))
+
+
+def scale_kernel(alone, tile, part_ref, codes_ref, exponents_ref, out_ref, buffer, powers, sems, powers_sem):
     part = part_ref[0]
     blocks = exponents_ref.shape[0]
     far = blocks - alone
-    own = jnp.where(part == 0, exponents_ref[0:alone, :], exponents_ref[far:blocks, :])
-    kept = jnp.concatenate([own, exponents_ref[alone:far, :]], axis=0)
+    tiles = buffer.shape[0]
+
+    def fetch(i):
+        start = pl.multiple_of(part * alone * BLOCK, BLOCK)
+        return pltpu.make_async_copy(
+            codes_ref.at[pl.ds(i * tile, tile), pl.ds(start, far * BLOCK)], buffer.at[i], sems.at[i]
+        )
+
+    powers_copy = pltpu.make_async_copy(exponents_ref, powers, powers_sem)
+    powers_copy.start()
+    for i in range(tiles):
+        fetch(i).start()
+    powers_copy.wait()
+    own = jnp.where(part == 0, powers[0:alone, :], powers[far:blocks, :])
+    kept = jnp.concatenate([own, powers[alone:far, :]], axis=0)
     pad = jnp.zeros((-kept.shape[0] % 8, kept.shape[1]), jnp.int32)
     scales = scales_of(jnp.concatenate([kept, pad], axis=0))
-    for block in range(far):
-        start = pl.multiple_of((part * far + block) * BLOCK, BLOCK) if block < alone else block * BLOCK
-        out_ref[:, block * BLOCK : (block + 1) * BLOCK] = scaled(codes_ref[:, pl.ds(start, BLOCK)], scales, block)
+    shared = far - alone
+    for i in range(tiles):
+        fetch(i).wait()
+        rows = slice(i * tile, (i + 1) * tile)
+        for block in range(far):
+            at = block + part * shared if block < alone else block - part * alone
+            columns = pl.ds(pl.multiple_of(at * BLOCK, BLOCK), BLOCK)
+            out_ref[rows, block * BLOCK : (block + 1) * BLOCK] = scaled(buffer[i, :, columns], scales[rows], block)
 
 
 def scale(part, codes, exponents, alone):
-    shape = (codes.shape[0], (exponents.shape[0] - alone) * BLOCK)
+    count = codes.shape[0]
+    width = (exponents.shape[0] - alone) * BLOCK
+    tile = min(count, 64)
     return pl.pallas_call(
-        functools.partial(scale_kernel, alone),
-        out_shape=jax.ShapeDtypeStruct(shape, jnp.bfloat16),
-        in_specs=[SMEM, VMEM, VMEM],
+        functools.partial(scale_kernel, alone, tile),
+        out_shape=pltpu.VMEM((count, width), jnp.bfloat16),
+        in_specs=[SMEM] + [pl.BlockSpec(memory_space=pl.ANY)] * 2,
         out_specs=VMEM,
+        scratch_shapes=[
+            pltpu.VMEM((count // tile, tile, width), jnp.bfloat16),
+            pltpu.VMEM(exponents.shape, exponents.dtype),
+            pltpu.SemaphoreType.DMA((count // tile,)),
+            pltpu.SemaphoreType.DMA,
+        ],
         compiler_params=pltpu.CompilerParams(vmem_limit_bytes=16 << 20),
         cost_estimate=pl.CostEstimate(flops=codes.size, bytes_accessed=4 * codes.size, transcendentals=0),
         name="scale_codes",
-    )(part, codes, exponents)
+    )(part, in_hbm(codes), in_hbm(exponents))
 
 
 def product(pieces, grads_ref):
@@ -188,7 +217,7 @@
 def score(half, rows, pieces, grads):
     operands = [array for arrays in pieces for array in arrays]
     stacked = sum(array.shape[0] for array in pieces[0])
-    shape = jax.ShapeDtypeStruct((stacked // rows, rows // 2, grads.shape[0]), jnp.float32)
+    shape = pltpu.VMEM((stacked // rows, rows // 2, grads.shape[0]), jnp.float32)
     return pl.pallas_call(
         functools.partial(score_kernel, [len(arrays) for arrays in pieces], rows),
         out_shape=[shape, shape],
@@ -199,7 +228,7 @@
             flops=2 * stacked * grads.size, bytes_accessed=2 * grads.size, transcendentals=0
         ),
         name="score",
-    )(half, *operands, grads)
+    )(half, *in_vmem([*operands, grads]))
 
 
 def place_kernel(rows, order_ref, ids_ref, *refs):
@@ -227,7 +256,7 @@
         out_specs=VMEM,
         compiler_params=pltpu.CompilerParams(vmem_limit_bytes=16 << 20),
         name="place_scores",
-    )(order, ids, *shares)
+    )(order, ids, *in_vmem(shares))
 
 
 def shards(fast, parts, total, queries, codes, exponents, example_ids):

time: 98 us -> 81.4 us (0.83)
  Pallas kernels: 31.7 us -> 17.2 us
  local copies, waits for them, and re-layouts: 17.4 us -> 15.1 us
    pallas_call x1, Pallas kernels: 20 us -> 3.74 us  [cut(): pl.pallas_call(functools.partial(cut_kernel, alone, cuts, tile), out_shap...]
    unnamed x50 -> x42, local copies, waits for them, and re-layouts: 17.3 us -> 15.1 us
    pallas_call x1, Pallas kernels: 0.85 us -> 2.63 us  [scale(): pl.pallas_call(functools.partial(scale_kernel, alone, tile), out_shape=pl...]
  transfers between devices with their start and end apart: 21 -> 21, of which waited for: 8 -> 8; matrix products, arithmetic and copies ran while one was open for 0% -> 0% of each run, Pallas kernels for 10% -> 14%
where the time goes in v4:
time: 81.4 us; the launch traced here: 80.9 us
  starting transfers between devices  26.1 us (32%)
  waiting for transfers between devices  22.3 us (27%)
  Pallas kernels  17.2 us (21%)
  local copies, waits for them, and re-layouts  15.1 us (19%)
    ppermute x14, starting transfers between devices, step(): return lax.ppermute(value, 'ex', pairs)  18.7 us
    ppermute x14, waiting for transfers between devices, step(): return lax.ppermute(value, 'ex', pairs)  17.7 us
    unnamed x42, local copies, waits for them, and re-layouts  15.1 us
    pallas_call x4, Pallas kernels, score(): pl.pallas_call(functools.partial(score_kernel, [len(arrays) for arrays in...  8.94 us
    pallas_call x1, Pallas kernels, cut(): pl.pallas_call(functools.partial(cut_kernel, alone, cuts, tile), out_shap...  3.74 us
    ppermute x2, starting transfers between devices, shards(): lax.ppermute(keep, 'groups', swap)  3.03 us
    ppermute x1, starting transfers between devices, shards(): theirs = lax.ppermute(sent, 'groups', swap)  3.03 us
    pallas_call x1, Pallas kernels, scale(): pl.pallas_call(functools.partial(scale_kernel, alone, tile), out_shape=pl...  2.63 us
  transfers between devices with their start and end apart: 21, of which 8 were waited for; matrix products, arithmetic and copies ran while one was open for 0% of the time, Pallas kernels for 14%

profile of v4, /device:TPU:0, one launch (start us, length us, event | category | flops | bytes accessed | tf_op | source)
XLA Modules:
  0.0 80.9 jit_solution(10988275258758261335)
XLA Ops:
  0.0 3.7 %cut_queries.1 = (bf16[64,2304]{1,0:T(8,128)(2,1)S(1)}, bf16[64,2304]{1,0:T(8,128)(2,1)S(1)}, bf16[256,3584]{1,0:T(8,128)(2,1)}) custom-call(s32[1]{0:T(128)} %bitcast.8.part_ref, bf16[1,64,8192]{2,1,0:T(8,128)(2,1)} %queries_ref.1, bf16[256,8192]{1,0:T(8,128)(2,1)} %codes_ref.3, s32[64,256]{1,0:T(8,128)} %bitcast.27), custom_call_target="tpu_custom_call" | custom-call | flops 2097152 | bytes 4194304 | tf_op jit(solution)/shard_map/cut_queries/pallas_call | solution.py:116
  3.8 3.0 %collective-permute-start = (bf16[256,3584]{1,0:T(8,128)(2,1)}, bf16[256,3584]{1,0:T(8,128)(2,1)}, u32[]{:S(2)}, u32[]{:S(2)}) collective-permute-start(bf16[256,3584]{1,0:T(8,128)(2,1)} %get-tuple-element.41), channel_id=1, source_target_pairs={{0,16},{16,0},{1,17},{17,1},{2,18},{18,2},{3,19},{19,3},{4,20},{20... | collective-permute-start | bytes 5505032 | tf_op jit(solution)/shard_map/ppermute | solution.py:290
  6.8 1.6 %collective-permute-start.1 = (bf16[64,2304]{1,0:T(8,128)(2,1)S(1)}, bf16[64,2304]{1,0:T(8,128)(2,1)S(1)}, u32[]{:S(2)}, u32[]{:S(2)}) collective-permute-start(bf16[64,2304]{1,0:T(8,128)(2,1)S(1)} %get-tuple-element.43.refs_0_), channel_id=1, source_target_pairs={{0,4},{2,6},{4,8},{6,10},{8,12},{10,14},{12,0},{14,2},{1,5},{3,7},... | collective-permute-start | bytes 884744 | tf_op jit(solution)/shard_map/ppermute | solution.py:279
  8.4 1.5 %collective-permute-start.2 = (bf16[64,2304]{1,0:T(8,128)(2,1)S(1)}, bf16[64,2304]{1,0:T(8,128)(2,1)S(1)}, u32[]{:S(2)}, u32[]{:S(2)}) collective-permute-start(bf16[64,2304]{1,0:T(8,128)(2,1)S(1)} %get-tuple-element.43.refs_0_), channel_id=1, source_target_pairs={{0,2},{2,0},{4,6},{6,4},{8,10},{10,8},{12,14},{14,12},{1,3},{3,1},... | collective-permute-start | bytes 884744 | tf_op jit(solution)/shard_map/ppermute | solution.py:279
  9.9 1.6 %collective-permute-start.7 = (bf16[64,2304]{1,0:T(8,128)(2,1)S(1)}, bf16[64,2304]{1,0:T(8,128)(2,1)S(1)}, u32[]{:S(2)}, u32[]{:S(2)}) collective-permute-start(bf16[64,2304]{1,0:T(8,128)(2,1)S(1)} %get-tuple-element.52.refs_6_), channel_id=1, source_target_pairs={{0,4},{2,6},{4,8},{6,10},{8,12},{10,14},{12,0},{14,2},{1,5},{3,7},... | collective-permute-start | bytes 884744 | tf_op jit(solution)/shard_map/ppermute | solution.py:279
  11.4 0.5 collective-permute-start.8
  12.0 2.6 %scale_codes.1.refs_12_.refs_4_ = bf16[256,4608]{1,0:T(8,128)(2,1)S(1)} custom-call(s32[1]{0:T(128)} %bitcast.8.part_ref, bf16[256,8192]{1,0:T(8,128)(2,1)} %codes_ref.3, s32[64,256]{1,0:T(8,128)} %bitcast.28), custom_call_target="tpu_custom_call" | custom-call | flops 2097152 | bytes 8388608 | tf_op jit(solution)/shard_map/scale_codes/pallas_call | solution.py:170
  14.6 3.9 %collective-permute-done.1.refs_2_ = bf16[64,2304]{1,0:T(8,128)(2,1)S(1)} collective-permute-done((bf16[64,2304]{1,0:T(8,128)(2,1)S(1)}, bf16[64,2304]{1,0:T(8,128)(2,1)S(1)}, u32[]{:S(2)}, u32[]{:S(2)}) %collective-permute-start.1) | collective-permute-done | bytes 294944 | tf_op jit(solution)/shard_map/ppermute | solution.py:279
  18.5 0.0 collective-permute-done.2.refs_1_
  18.5 1.4 %collective-permute-start.3 = (bf16[64,2304]{1,0:T(8,128)(2,1)S(1)}, bf16[64,2304]{1,0:T(8,128)(2,1)S(1)}, u32[]{:S(2)}, u32[]{:S(2)}) collective-permute-start(bf16[64,2304]{1,0:T(8,128)(2,1)S(1)} %collective-permute-done.1.refs_2_), channel_id=1, source_target_pairs={{0,4},{2,6},{4,8},{6,10},{8,12},{10,14},{12,0},{14,2},{1,5},{3,7},... | collective-permute-start | bytes 884744 | tf_op jit(solution)/shard_map/ppermute | solution.py:279
  19.9 1.5 %collective-permute-start.4 = (bf16[64,2304]{1,0:T(8,128)(2,1)S(1)}, bf16[64,2304]{1,0:T(8,128)(2,1)S(1)}, u32[]{:S(2)}, u32[]{:S(2)}) collective-permute-start(bf16[64,2304]{1,0:T(8,128)(2,1)S(1)} %collective-permute-done.1.refs_2_), channel_id=1, source_target_pairs={{0,2},{2,0},{4,6},{6,4},{8,10},{10,8},{12,14},{14,12},{1,3},{3,1},... | collective-permute-start | bytes 884744 | tf_op jit(solution)/shard_map/ppermute | solution.py:279
  21.4 3.5 %collective-permute-done.7.refs_8_ = bf16[64,2304]{1,0:T(8,128)(2,1)S(1)} collective-permute-done((bf16[64,2304]{1,0:T(8,128)(2,1)S(1)}, bf16[64,2304]{1,0:T(8,128)(2,1)S(1)}, u32[]{:S(2)}, u32[]{:S(2)}) %collective-permute-start.7) | collective-permute-done | bytes 294944 | tf_op jit(solution)/shard_map/ppermute | solution.py:279
  24.8 0.0 collective-permute-done.8.refs_7_
  24.8 0.7 copy-done.2
  25.6 1.4 %collective-permute-start.9 = (bf16[64,2304]{1,0:T(8,128)(2,1)S(1)}, bf16[64,2304]{1,0:T(8,128)(2,1)S(1)}, u32[]{:S(2)}, u32[]{:S(2)}) collective-permute-start(bf16[64,2304]{1,0:T(8,128)(2,1)S(1)} %collective-permute-done.7.refs_8_), channel_id=1, source_target_pairs={{0,4},{2,6},{4,8},{6,10},{8,12},{10,14},{12,0},{14,2},{1,5},{3,7},... | collective-permute-start | bytes 884744 | tf_op jit(solution)/shard_map/ppermute | solution.py:279
  26.9 1.5 %collective-permute-start.10 = (bf16[64,2304]{1,0:T(8,128)(2,1)S(1)}, bf16[64,2304]{1,0:T(8,128)(2,1)S(1)}, u32[]{:S(2)}, u32[]{:S(2)}) collective-permute-start(bf16[64,2304]{1,0:T(8,128)(2,1)S(1)} %collective-permute-done.7.refs_8_), channel_id=1, source_target_pairs={{0,2},{2,0},{4,6},{6,4},{8,10},{10,8},{12,14},{14,12},{1,3},{3,1},... | collective-permute-start | bytes 884744 | tf_op jit(solution)/shard_map/ppermute | solution.py:279
  28.4 0.7 copy-done
  29.1 2.0 %collective-permute-done.3.refs_4_ = bf16[64,2304]{1,0:T(8,128)(2,1)S(1)} collective-permute-done((bf16[64,2304]{1,0:T(8,128)(2,1)S(1)}, bf16[64,2304]{1,0:T(8,128)(2,1)S(1)}, u32[]{:S(2)}, u32[]{:S(2)}) %collective-permute-start.3) | collective-permute-done | bytes 294944 | tf_op jit(solution)/shard_map/ppermute | solution.py:279
  31.1 0.0 collective-permute-done.4.refs_3_
  31.2 0.7 copy-done.6
  31.9 1.4 %collective-permute-start.5 = (bf16[64,2304]{1,0:T(8,128)(2,1)S(1)}, bf16[64,2304]{1,0:T(8,128)(2,1)}, u32[]{:S(2)}, u32[]{:S(2)}) collective-permute-start(bf16[64,2304]{1,0:T(8,128)(2,1)S(1)} %collective-permute-done.3.refs_4_), channel_id=1, source_target_pairs={{0,4},{2,6},{4,8},{6,10},{8,12},{10,14},{12,0},{14,2},{1,5},{3,7},... | collective-permute-start | bytes 884744 | tf_op jit(solution)/shard_map/ppermute | solution.py:279
  33.2 1.5 %collective-permute-start.6 = (bf16[64,2304]{1,0:T(8,128)(2,1)S(1)}, bf16[64,2304]{1,0:T(8,128)(2,1)S(1)}, u32[]{:S(2)}, u32[]{:S(2)}) collective-permute-start(bf16[64,2304]{1,0:T(8,128)(2,1)S(1)} %collective-permute-done.3.refs_4_), channel_id=1, source_target_pairs={{0,2},{2,0},{4,6},{6,4},{8,10},{10,8},{12,14},{14,12},{1,3},{3,1},... | collective-permute-start | bytes 884744 | tf_op jit(solution)/shard_map/ppermute | solution.py:279
  34.7 0.7 copy-done.4
  35.5 2.0 %collective-permute-done.9.refs_10_ = bf16[64,2304]{1,0:T(8,128)(2,1)S(1)} collective-permute-done((bf16[64,2304]{1,0:T(8,128)(2,1)S(1)}, bf16[64,2304]{1,0:T(8,128)(2,1)S(1)}, u32[]{:S(2)}, u32[]{:S(2)}) %collective-permute-start.9) | collective-permute-done | bytes 294944 | tf_op jit(solution)/shard_map/ppermute | solution.py:279
  37.5 0.0 collective-permute-done.10.refs_9_
  37.5 0.7 copy-done.10
  38.2 1.4 %collective-permute-start.11 = (bf16[64,2304]{1,0:T(8,128)(2,1)S(1)}, bf16[64,2304]{1,0:T(8,128)(2,1)}, u32[]{:S(2)}, u32[]{:S(2)}) collective-permute-start(bf16[64,2304]{1,0:T(8,128)(2,1)S(1)} %collective-permute-done.9.refs_10_), channel_id=1, source_target_pairs={{0,4},{2,6},{4,8},{6,10},{8,12},{10,14},{12,0},{14,2},{1,5},{3,7},... | collective-permute-start | bytes 884744 | tf_op jit(solution)/shard_map/ppermute | solution.py:279
  39.6 1.5 %collective-permute-start.12 = (bf16[64,2304]{1,0:T(8,128)(2,1)S(1)}, bf16[64,2304]{1,0:T(8,128)(2,1)S(1)}, u32[]{:S(2)}, u32[]{:S(2)}) collective-permute-start(bf16[64,2304]{1,0:T(8,128)(2,1)S(1)} %collective-permute-done.9.refs_10_), channel_id=1, source_target_pairs={{0,2},{2,0},{4,6},{6,4},{8,10},{10,8},{12,14},{14,12},{1,3},{3,1},... | collective-permute-start | bytes 884744 | tf_op jit(solution)/shard_map/ppermute | solution.py:279
  41.0 0.7 copy-done.8
  41.8 2.1 %collective-permute-done.5.refs_0_ = bf16[64,2304]{1,0:T(8,128)(2,1)} collective-permute-done((bf16[64,2304]{1,0:T(8,128)(2,1)S(1)}, bf16[64,2304]{1,0:T(8,128)(2,1)}, u32[]{:S(2)}, u32[]{:S(2)}) %collective-permute-start.5) | collective-permute-done | bytes 294944 | tf_op jit(solution)/shard_map/ppermute | solution.py:279
  43.9 0.0 collective-permute-done.6.refs_5_
  43.9 0.7 copy-done.12
  44.6 4.2 %collective-permute-done.11.refs_2_ = bf16[64,2304]{1,0:T(8,128)(2,1)} collective-permute-done((bf16[64,2304]{1,0:T(8,128)(2,1)S(1)}, bf16[64,2304]{1,0:T(8,128)(2,1)}, u32[]{:S(2)}, u32[]{:S(2)}) %collective-permute-start.11) | collective-permute-done | bytes 294944 | tf_op jit(solution)/shard_map/ppermute | solution.py:279
  48.8 0.0 collective-permute-done.12.refs_11_
  48.8 0.7 copy-done.14
  49.5 1.5 %collective-permute-start.16 = (bf16[64,2304]{1,0:T(8,128)(2,1)}, bf16[64,2304]{1,0:T(8,128)(2,1)}, u32[]{:S(2)}, u32[]{:S(2)}) collective-permute-start(bf16[64,2304]{1,0:T(8,128)(2,1)} %collective-permute-done.5.refs_0_), channel_id=1, source_target_pairs={{0,2},{2,0},{4,6},{6,4},{8,10},{10,8},{12,14},{14,12},{1,3},{3,1},... | collective-permute-start | bytes 884744 | tf_op jit(solution)/shard_map/ppermute | solution.py:279
  51.0 0.5 collective-permute-start.17
  51.6 1.0 %copy-done.1 = bf16[64,2304]{1,0:T(8,128)(2,1)S(1)} copy-done((bf16[64,2304]{1,0:T(8,128)(2,1)S(1)}, bf16[64,2304]{1,0:T(8,128)(2,1)}, u32[]{:S(2)}) %copy-start.1) | copy-done | bytes 294936
  52.5 1.0 %copy-done.3 = bf16[64,2304]{1,0:T(8,128)(2,1)S(1)} copy-done((bf16[64,2304]{1,0:T(8,128)(2,1)S(1)}, bf16[64,2304]{1,0:T(8,128)(2,1)}, u32[]{:S(2)}) %copy-start.3) | copy-done | bytes 294936
  53.5 1.0 %copy-done.5 = bf16[64,2304]{1,0:T(8,128)(2,1)S(1)} copy-done((bf16[64,2304]{1,0:T(8,128)(2,1)S(1)}, bf16[64,2304]{1,0:T(8,128)(2,1)}, u32[]{:S(2)}) %copy-start.5) | copy-done | bytes 294936
  54.5 1.0 %copy-done.7 = bf16[64,2304]{1,0:T(8,128)(2,1)S(1)} copy-done((bf16[64,2304]{1,0:T(8,128)(2,1)S(1)}, bf16[64,2304]{1,0:T(8,128)(2,1)}, u32[]{:S(2)}) %copy-start.7) | copy-done | bytes 294936
  55.4 1.0 %copy-done.9 = bf16[64,2304]{1,0:T(8,128)(2,1)S(1)} copy-done((bf16[64,2304]{1,0:T(8,128)(2,1)S(1)}, bf16[64,2304]{1,0:T(8,128)(2,1)}, u32[]{:S(2)}) %copy-start.9) | copy-done | bytes 294936
  56.4 1.0 %copy-done.11 = bf16[64,2304]{1,0:T(8,128)(2,1)S(1)} copy-done((bf16[64,2304]{1,0:T(8,128)(2,1)S(1)}, bf16[64,2304]{1,0:T(8,128)(2,1)}, u32[]{:S(2)}) %copy-start.11) | copy-done | bytes 294936
  57.3 1.0 %copy-done.13 = bf16[64,2304]{1,0:T(8,128)(2,1)S(1)} copy-done((bf16[64,2304]{1,0:T(8,128)(2,1)S(1)}, bf16[64,2304]{1,0:T(8,128)(2,1)}, u32[]{:S(2)}) %copy-start.13) | copy-done | bytes 294936
  58.3 1.0 %copy-done.15 = bf16[64,2304]{1,0:T(8,128)(2,1)S(1)} copy-done((bf16[64,2304]{1,0:T(8,128)(2,1)S(1)}, bf16[64,2304]{1,0:T(8,128)(2,1)}, u32[]{:S(2)}) %copy-start.15) | copy-done | bytes 294936
  59.3 1.1 %score.5 = (f32[6,32,256]{2,1,0:T(8,128)S(1)}, f32[6,32,256]{2,1,0:T(8,128)S(1)}) custom-call(s32[1]{0:T(128)} %bitcast.10.half_ref, bf16[64,2304]{1,0:T(8,128)(2,1)S(1)} %get-tuple-element.43.refs_0_, bf16[64,2304]{1,0:T(8,128)(2,1)S(1)} %collective-permute-done.2.refs_1_, bf16[64,2304]{1,0:T(8,128)(2,1)S(1)} %collective-permute-done.1.refs_2_, ...), custom_call_target="tpu_custom_call" | custom-call | flops 905969664 | bytes 2359296 | tf_op jit(solution)/shard_map/score/pallas_call | solution.py:221
  60.4 0.1 collective-permute-start.15
  60.5 3.1 %score.4 = (f32[6,32,256]{2,1,0:T(8,128)}, f32[6,32,256]{2,1,0:T(8,128)}) custom-call(s32[1]{0:T(128)} %bitcast.10.half_ref, bf16[64,2304]{1,0:T(8,128)(2,1)S(1)} %get-tuple-element.43.refs_0_, bf16[64,2304]{1,0:T(8,128)(2,1)S(1)} %collective-permute-done.2.refs_1_, bf16[64,2304]{1,0:T(8,128)(2,1)S(1)} %collective-permute-done.1.refs_2_, ...), custom_call_target="tpu_custom_call" | custom-call | flops 704643072 | bytes 1835008 | tf_op jit(solution)/shard_map/score/pallas_call | solution.py:221
  63.6 0.6 collective-permute-start.13
  64.2 1.5 %collective-permute-start.14 = (f32[6,32,256]{2,1,0:T(8,128)}, f32[6,32,256]{2,1,0:T(8,128)S(1)}, u32[]{:S(2)}, u32[]{:S(2)}) collective-permute-start(f32[6,32,256]{2,1,0:T(8,128)} %get-tuple-element.64), channel_id=1, source_target_pairs={{0,16},{16,0},{1,17},{17,1},{2,18},{18,2},{3,19},{19,3},{4,20},{20... | collective-permute-start | bytes 589832 | tf_op jit(solution)/shard_map/ppermute | solution.py:314
  65.8 2.1 %score.7 = (f32[2,32,256]{2,1,0:T(8,128)S(1)}, f32[2,32,256]{2,1,0:T(8,128)S(1)}) custom-call(s32[1]{0:T(128)} %bitcast.10.half_ref, bf16[64,2304]{1,0:T(8,128)(2,1)} %collective-permute-done.5.refs_0_, bf16[64,2304]{1,0:T(8,128)(2,1)} %collective-permute-done.16.refs_1_, bf16[64,2304]{1,0:T(8,128)(2,1)} %collective-permute-done.11.refs_2_, ...), custom_call_target="tpu_custom_call" | custom-call | flops 301989888 | bytes 2359296 | tf_op jit(solution)/shard_map/score/pallas_call | solution.py:221
  67.9 0.0 copy-start.20
  67.9 0.1 collective-permute-start.20
  68.0 2.6 %score.6 = (f32[2,32,256]{2,1,0:T(8,128)S(1)}, f32[2,32,256]{2,1,0:T(8,128)S(1)}) custom-call(s32[1]{0:T(128)} %bitcast.10.half_ref, bf16[64,2304]{1,0:T(8,128)(2,1)} %collective-permute-done.5.refs_0_, bf16[64,2304]{1,0:T(8,128)(2,1)} %collective-permute-done.16.refs_1_, bf16[64,2304]{1,0:T(8,128)(2,1)} %collective-permute-done.11.refs_2_, ...), custom_call_target="tpu_custom_call" | custom-call | flops 234881024 | bytes 1835008 | tf_op jit(solution)/shard_map/score/pallas_call | solution.py:221
  70.6 0.7 collective-permute-start.18
  71.2 0.0 collective-permute-done.15
  71.2 0.7 copy-done.18
  71.9 1.5 %collective-permute-start.19 = (f32[2,32,256]{2,1,0:T(8,128)S(1)}, f32[2,32,256]{2,1,0:T(8,128)S(1)}, u32[]{:S(2)}, u32[]{:S(2)}) collective-permute-start(f32[2,32,256]{2,1,0:T(8,128)S(1)} %get-tuple-element.74), channel_id=1, source_target_pairs={{0,16},{16,0},{1,17},{17,1},{2,18},{18,2},{3,19},{19,3},{4,20},{20... | collective-permute-start | bytes 196616 | tf_op jit(solution)/shard_map/ppermute | solution.py:314
  73.4 0.1 stack.35.order_ref
  73.5 0.0 collective-permute-done.20
  73.5 2.5 %collective-permute-done.18 = f32[2,32,256]{2,1,0:T(8,128)S(1)} collective-permute-done((f32[2,32,256]{2,1,0:T(8,128)S(1)}, f32[2,32,256]{2,1,0:T(8,128)S(1)}, u32[]{:S(2)}, u32[]{:S(2)}) %collective-permute-start.18) | collective-permute-done | bytes 65568 | tf_op jit(solution)/shard_map/ppermute | solution.py:314
  76.0 2.0 %collective-permute-done.19 = f32[2,32,256]{2,1,0:T(8,128)S(1)} collective-permute-done((f32[2,32,256]{2,1,0:T(8,128)S(1)}, f32[2,32,256]{2,1,0:T(8,128)S(1)}, u32[]{:S(2)}, u32[]{:S(2)}) %collective-permute-start.19) | collective-permute-done | bytes 65568 | tf_op jit(solution)/shard_map/ppermute | solution.py:314
  78.1 0.9 %copy-done.19 = f32[6,32,256]{2,1,0:T(8,128)S(1)} copy-done((f32[6,32,256]{2,1,0:T(8,128)S(1)}, f32[6,32,256]{2,1,0:T(8,128)}, u32[]{:S(2)}) %copy-start.19) | copy-done | bytes 196632
  79.0 1.9 %place_scores.1 = f32[8,32,256]{2,1,0:T(8,128)} custom-call(s32[8]{0:T(128)S(1)} %stack.35.order_ref, s32[1,256]{1,0:T(1,128)S(1)} %copy-done.20, f32[192,256]{1,0:T(8,128)S(1)} %bitcast.21, f32[192,256]{1,0:T(8,128)S(1)} %bitcast.22, f32[192,256]{1,0:T(8,128)S(1)} %bitcast.20, f32[192,256]{1,0:T(8,128)S(1)} %bitcast.19, f32[64,256]{1,0:T(8,128)S(1)} %bitcast.25, ...), custom_call_target="tpu_custom_call" | custom-call | tf_op jit(solution)/shard_map/place_scores/pallas_call | solution.py:252
  (28 shorter events, 0.1 us)
Async XLA Ops:
  3.8 56.7 %collective-permute-start = (bf16[256,3584]{1,0:T(8,128)(2,1)}, bf16[256,3584]{1,0:T(8,128)(2,1)}, u32[]{:S(2)}, u32[]{:S(2)}) collective-permute-start(bf16[256,3584]{1,0:T(8,128)(2,1)} %get-tuple-element.41), channel_id=1, source_target_pairs={{0,16},{16,0},{1,17},{17,1},{2,18},{18,2},{3,19},{19,3},{4,20},{20... | collective-permute-start | bytes 5505032 | tf_op jit(solution)/shard_map/ppermute | solution.py:290
  6.8 11.7 %collective-permute-start.1 = (bf16[64,2304]{1,0:T(8,128)(2,1)S(1)}, bf16[64,2304]{1,0:T(8,128)(2,1)S(1)}, u32[]{:S(2)}, u32[]{:S(2)}) collective-permute-start(bf16[64,2304]{1,0:T(8,128)(2,1)S(1)} %get-tuple-element.43.refs_0_), channel_id=1, source_target_pairs={{0,4},{2,6},{4,8},{6,10},{8,12},{10,14},{12,0},{14,2},{1,5},{3,7},... | collective-permute-start | bytes 884744 | tf_op jit(solution)/shard_map/ppermute | solution.py:279
  8.4 10.2 %collective-permute-start.2 = (bf16[64,2304]{1,0:T(8,128)(2,1)S(1)}, bf16[64,2304]{1,0:T(8,128)(2,1)S(1)}, u32[]{:S(2)}, u32[]{:S(2)}) collective-permute-start(bf16[64,2304]{1,0:T(8,128)(2,1)S(1)} %get-tuple-element.43.refs_0_), channel_id=1, source_target_pairs={{0,2},{2,0},{4,6},{6,4},{8,10},{10,8},{12,14},{14,12},{1,3},{3,1},... | collective-permute-start | bytes 884744 | tf_op jit(solution)/shard_map/ppermute | solution.py:279
  9.9 15.0 %collective-permute-start.7 = (bf16[64,2304]{1,0:T(8,128)(2,1)S(1)}, bf16[64,2304]{1,0:T(8,128)(2,1)S(1)}, u32[]{:S(2)}, u32[]{:S(2)}) collective-permute-start(bf16[64,2304]{1,0:T(8,128)(2,1)S(1)} %get-tuple-element.52.refs_6_), channel_id=1, source_target_pairs={{0,4},{2,6},{4,8},{6,10},{8,12},{10,14},{12,0},{14,2},{1,5},{3,7},... | collective-permute-start | bytes 884744 | tf_op jit(solution)/shard_map/ppermute | solution.py:279
  11.4 13.4 %collective-permute-start.8 = (bf16[64,2304]{1,0:T(8,128)(2,1)S(1)}, bf16[64,2304]{1,0:T(8,128)(2,1)S(1)}, u32[]{:S(2)}, u32[]{:S(2)}) collective-permute-start(bf16[64,2304]{1,0:T(8,128)(2,1)S(1)} %get-tuple-element.52.refs_6_), channel_id=1, source_target_pairs={{0,2},{2,0},{4,6},{6,4},{8,10},{10,8},{12,14},{14,12},{1,3},{3,1},... | collective-permute-start | bytes 884744 | tf_op jit(solution)/shard_map/ppermute | solution.py:279
  18.5 12.6 %collective-permute-start.3 = (bf16[64,2304]{1,0:T(8,128)(2,1)S(1)}, bf16[64,2304]{1,0:T(8,128)(2,1)S(1)}, u32[]{:S(2)}, u32[]{:S(2)}) collective-permute-start(bf16[64,2304]{1,0:T(8,128)(2,1)S(1)} %collective-permute-done.1.refs_2_), channel_id=1, source_target_pairs={{0,4},{2,6},{4,8},{6,10},{8,12},{10,14},{12,0},{14,2},{1,5},{3,7},... | collective-permute-start | bytes 884744 | tf_op jit(solution)/shard_map/ppermute | solution.py:279
  19.9 11.3 %collective-permute-start.4 = (bf16[64,2304]{1,0:T(8,128)(2,1)S(1)}, bf16[64,2304]{1,0:T(8,128)(2,1)S(1)}, u32[]{:S(2)}, u32[]{:S(2)}) collective-permute-start(bf16[64,2304]{1,0:T(8,128)(2,1)S(1)} %collective-permute-done.1.refs_2_), channel_id=1, source_target_pairs={{0,2},{2,0},{4,6},{6,4},{8,10},{10,8},{12,14},{14,12},{1,3},{3,1},... | collective-permute-start | bytes 884744 | tf_op jit(solution)/shard_map/ppermute | solution.py:279
  24.8 0.7 copy-start.2
  25.6 11.9 %collective-permute-start.9 = (bf16[64,2304]{1,0:T(8,128)(2,1)S(1)}, bf16[64,2304]{1,0:T(8,128)(2,1)S(1)}, u32[]{:S(2)}, u32[]{:S(2)}) collective-permute-start(bf16[64,2304]{1,0:T(8,128)(2,1)S(1)} %collective-permute-done.7.refs_8_), channel_id=1, source_target_pairs={{0,4},{2,6},{4,8},{6,10},{8,12},{10,14},{12,0},{14,2},{1,5},{3,7},... | collective-permute-start | bytes 884744 | tf_op jit(solution)/shard_map/ppermute | solution.py:279
  26.9 10.5 %collective-permute-start.10 = (bf16[64,2304]{1,0:T(8,128)(2,1)S(1)}, bf16[64,2304]{1,0:T(8,128)(2,1)S(1)}, u32[]{:S(2)}, u32[]{:S(2)}) collective-permute-start(bf16[64,2304]{1,0:T(8,128)(2,1)S(1)} %collective-permute-done.7.refs_8_), channel_id=1, source_target_pairs={{0,2},{2,0},{4,6},{6,4},{8,10},{10,8},{12,14},{14,12},{1,3},{3,1},... | collective-permute-start | bytes 884744 | tf_op jit(solution)/shard_map/ppermute | solution.py:279
  28.4 0.7 copy-start
  31.2 0.7 copy-start.6
  31.9 12.0 %collective-permute-start.5 = (bf16[64,2304]{1,0:T(8,128)(2,1)S(1)}, bf16[64,2304]{1,0:T(8,128)(2,1)}, u32[]{:S(2)}, u32[]{:S(2)}) collective-permute-start(bf16[64,2304]{1,0:T(8,128)(2,1)S(1)} %collective-permute-done.3.refs_4_), channel_id=1, source_target_pairs={{0,4},{2,6},{4,8},{6,10},{8,12},{10,14},{12,0},{14,2},{1,5},{3,7},... | collective-permute-start | bytes 884744 | tf_op jit(solution)/shard_map/ppermute | solution.py:279
  33.2 10.7 %collective-permute-start.6 = (bf16[64,2304]{1,0:T(8,128)(2,1)S(1)}, bf16[64,2304]{1,0:T(8,128)(2,1)S(1)}, u32[]{:S(2)}, u32[]{:S(2)}) collective-permute-start(bf16[64,2304]{1,0:T(8,128)(2,1)S(1)} %collective-permute-done.3.refs_4_), channel_id=1, source_target_pairs={{0,2},{2,0},{4,6},{6,4},{8,10},{10,8},{12,14},{14,12},{1,3},{3,1},... | collective-permute-start | bytes 884744 | tf_op jit(solution)/shard_map/ppermute | solution.py:279
  34.7 0.7 copy-start.4
  37.5 0.7 copy-start.10
  38.2 10.6 %collective-permute-start.11 = (bf16[64,2304]{1,0:T(8,128)(2,1)S(1)}, bf16[64,2304]{1,0:T(8,128)(2,1)}, u32[]{:S(2)}, u32[]{:S(2)}) collective-permute-start(bf16[64,2304]{1,0:T(8,128)(2,1)S(1)} %collective-permute-done.9.refs_10_), channel_id=1, source_target_pairs={{0,4},{2,6},{4,8},{6,10},{8,12},{10,14},{12,0},{14,2},{1,5},{3,7},... | collective-permute-start | bytes 884744 | tf_op jit(solution)/shard_map/ppermute | solution.py:279
  39.6 9.3 %collective-permute-start.12 = (bf16[64,2304]{1,0:T(8,128)(2,1)S(1)}, bf16[64,2304]{1,0:T(8,128)(2,1)S(1)}, u32[]{:S(2)}, u32[]{:S(2)}) collective-permute-start(bf16[64,2304]{1,0:T(8,128)(2,1)S(1)} %collective-permute-done.9.refs_10_), channel_id=1, source_target_pairs={{0,2},{2,0},{4,6},{6,4},{8,10},{10,8},{12,14},{14,12},{1,3},{3,1},... | collective-permute-start | bytes 884744 | tf_op jit(solution)/shard_map/ppermute | solution.py:279
  41.0 0.7 copy-start.8
  43.9 0.7 copy-start.12
  48.8 0.7 copy-start.14
  49.5 16.2 %collective-permute-start.16 = (bf16[64,2304]{1,0:T(8,128)(2,1)}, bf16[64,2304]{1,0:T(8,128)(2,1)}, u32[]{:S(2)}, u32[]{:S(2)}) collective-permute-start(bf16[64,2304]{1,0:T(8,128)(2,1)} %collective-permute-done.5.refs_0_), channel_id=1, source_target_pairs={{0,2},{2,0},{4,6},{6,4},{8,10},{10,8},{12,14},{14,12},{1,3},{3,1},... | collective-permute-start | bytes 884744 | tf_op jit(solution)/shard_map/ppermute | solution.py:279
  51.0 14.7 %collective-permute-start.17 = (bf16[64,2304]{1,0:T(8,128)(2,1)}, bf16[64,2304]{1,0:T(8,128)(2,1)}, u32[]{:S(2)}, u32[]{:S(2)}) collective-permute-start(bf16[64,2304]{1,0:T(8,128)(2,1)} %collective-permute-done.11.refs_2_), channel_id=1, source_target_pairs={{0,2},{2,0},{4,6},{6,4},{8,10},{10,8},{12,14},{14,12},{1,3},{3,1},... | collective-permute-start | bytes 884744 | tf_op jit(solution)/shard_map/ppermute | solution.py:279
  51.6 1.0 %copy-start.1 = (bf16[64,2304]{1,0:T(8,128)(2,1)S(1)}, bf16[64,2304]{1,0:T(8,128)(2,1)}, u32[]{:S(2)}) copy-start(bf16[64,2304]{1,0:T(8,128)(2,1)} %copy-done) | copy-start | bytes 884740
  52.5 1.0 %copy-start.3 = (bf16[64,2304]{1,0:T(8,128)(2,1)S(1)}, bf16[64,2304]{1,0:T(8,128)(2,1)}, u32[]{:S(2)}) copy-start(bf16[64,2304]{1,0:T(8,128)(2,1)} %copy-done.2) | copy-start | bytes 884740
  53.5 1.0 %copy-start.5 = (bf16[64,2304]{1,0:T(8,128)(2,1)S(1)}, bf16[64,2304]{1,0:T(8,128)(2,1)}, u32[]{:S(2)}) copy-start(bf16[64,2304]{1,0:T(8,128)(2,1)} %copy-done.4) | copy-start | bytes 884740
  54.5 1.0 %copy-start.7 = (bf16[64,2304]{1,0:T(8,128)(2,1)S(1)}, bf16[64,2304]{1,0:T(8,128)(2,1)}, u32[]{:S(2)}) copy-start(bf16[64,2304]{1,0:T(8,128)(2,1)} %copy-done.6) | copy-start | bytes 884740
  55.4 1.0 %copy-start.9 = (bf16[64,2304]{1,0:T(8,128)(2,1)S(1)}, bf16[64,2304]{1,0:T(8,128)(2,1)}, u32[]{:S(2)}) copy-start(bf16[64,2304]{1,0:T(8,128)(2,1)} %copy-done.8) | copy-start | bytes 884740
  56.4 1.0 %copy-start.11 = (bf16[64,2304]{1,0:T(8,128)(2,1)S(1)}, bf16[64,2304]{1,0:T(8,128)(2,1)}, u32[]{:S(2)}) copy-start(bf16[64,2304]{1,0:T(8,128)(2,1)} %copy-done.10) | copy-start | bytes 884740
  57.3 1.0 %copy-start.13 = (bf16[64,2304]{1,0:T(8,128)(2,1)S(1)}, bf16[64,2304]{1,0:T(8,128)(2,1)}, u32[]{:S(2)}) copy-start(bf16[64,2304]{1,0:T(8,128)(2,1)} %copy-done.12) | copy-start | bytes 884740
  58.3 1.0 %copy-start.15 = (bf16[64,2304]{1,0:T(8,128)(2,1)S(1)}, bf16[64,2304]{1,0:T(8,128)(2,1)}, u32[]{:S(2)}) copy-start(bf16[64,2304]{1,0:T(8,128)(2,1)} %copy-done.14) | copy-start | bytes 884740
  60.4 3.3 %copy-start.16 = (f32[6,32,256]{2,1,0:T(8,128)}, f32[6,32,256]{2,1,0:T(8,128)S(1)}, u32[]{:S(2)}) copy-start(f32[6,32,256]{2,1,0:T(8,128)S(1)} %get-tuple-element.67) | copy-start | bytes 589828
  60.4 10.8 %collective-permute-start.15 = (f32[6,32,256]{2,1,0:T(8,128)S(1)}, f32[6,32,256]{2,1,0:T(8,128)S(1)}, u32[]{:S(2)}, u32[]{:S(2)}) collective-permute-start(f32[6,32,256]{2,1,0:T(8,128)S(1)} %get-tuple-element.66), channel_id=1, source_target_pairs={{0,1},{1,0},{2,3},{3,2},{4,5},{5,4},{6,7},{7,6},{8,9},{9,8},{10,11... | collective-permute-start | bytes 589832 | tf_op jit(solution)/shard_map/ppermute | solution.py:316
  63.6 14.4 %collective-permute-start.13 = (f32[6,32,256]{2,1,0:T(8,128)}, f32[6,32,256]{2,1,0:T(8,128)S(1)}, u32[]{:S(2)}, u32[]{:S(2)}) collective-permute-start(f32[6,32,256]{2,1,0:T(8,128)} %get-tuple-element.63), channel_id=1, source_target_pairs={{0,17},{1,16},{16,1},{17,0},{2,19},{3,18},{18,3},{19,2},{4,21},{5,... | collective-permute-start | bytes 589832 | tf_op jit(solution)/shard_map/ppermute | solution.py:314
  64.2 13.8 %collective-permute-start.14 = (f32[6,32,256]{2,1,0:T(8,128)}, f32[6,32,256]{2,1,0:T(8,128)S(1)}, u32[]{:S(2)}, u32[]{:S(2)}) collective-permute-start(f32[6,32,256]{2,1,0:T(8,128)} %get-tuple-element.64), channel_id=1, source_target_pairs={{0,16},{16,0},{1,17},{17,1},{2,18},{18,2},{3,19},{19,3},{4,20},{20... | collective-permute-start | bytes 589832 | tf_op jit(solution)/shard_map/ppermute | solution.py:314
  67.9 10.2 %copy-start.17 = (f32[6,32,256]{2,1,0:T(8,128)S(1)}, f32[6,32,256]{2,1,0:T(8,128)}, u32[]{:S(2)}) copy-start(f32[6,32,256]{2,1,0:T(8,128)} %copy-done.16) | copy-start | bytes 589828
  67.9 10.2 %copy-start.20 = (s32[1,256]{1,0:T(1,128)S(1)}, s32[1,256]{1,0:T(1,128)}, u32[]{:S(2)}) copy-start(s32[1,256]{1,0:T(1,128)} %ids_ref.1) | copy-start | bytes 3076
  67.9 5.6 %collective-permute-start.20 = (f32[2,32,256]{2,1,0:T(8,128)S(1)}, f32[2,32,256]{2,1,0:T(8,128)S(1)}, u32[]{:S(2)}, u32[]{:S(2)}) collective-permute-start(f32[2,32,256]{2,1,0:T(8,128)S(1)} %get-tuple-element.75), channel_id=1, source_target_pairs={{0,1},{1,0},{2,3},{3,2},{4,5},{5,4},{6,7},{7,6},{8,9},{9,8},{10,11... | collective-permute-start | bytes 196616 | tf_op jit(solution)/shard_map/ppermute | solution.py:316
  70.6 5.5 %collective-permute-start.18 = (f32[2,32,256]{2,1,0:T(8,128)S(1)}, f32[2,32,256]{2,1,0:T(8,128)S(1)}, u32[]{:S(2)}, u32[]{:S(2)}) collective-permute-start(f32[2,32,256]{2,1,0:T(8,128)S(1)} %get-tuple-element.73), channel_id=1, source_target_pairs={{0,17},{1,16},{16,1},{17,0},{2,19},{3,18},{18,3},{19,2},{4,21},{5,... | collective-permute-start | bytes 196616 | tf_op jit(solution)/shard_map/ppermute | solution.py:314
  71.2 0.7 copy-start.18
  71.9 6.2 %collective-permute-start.19 = (f32[2,32,256]{2,1,0:T(8,128)S(1)}, f32[2,32,256]{2,1,0:T(8,128)S(1)}, u32[]{:S(2)}, u32[]{:S(2)}) collective-permute-start(f32[2,32,256]{2,1,0:T(8,128)S(1)} %get-tuple-element.74), channel_id=1, source_target_pairs={{0,16},{16,0},{1,17},{17,1},{2,18},{18,2},{3,19},{19,3},{4,20},{20... | collective-permute-start | bytes 196616 | tf_op jit(solution)/shard_map/ppermute | solution.py:314
  78.1 0.9 %copy-start.19 = (f32[6,32,256]{2,1,0:T(8,128)S(1)}, f32[6,32,256]{2,1,0:T(8,128)}, u32[]{:S(2)}) copy-start(f32[6,32,256]{2,1,0:T(8,128)} %copy-done.18) | copy-start | bytes 589828

commit v5 on v4

--- a/solution.py
+++ b/solution.py
@@ -9,6 +9,7 @@
 
 BLOCK = 128
 ALONE = 28
+RUN = 6 * BLOCK
 CHUNKS = 2
 VMEM = pl.BlockSpec(memory_space=pltpu.VMEM)
 SMEM = pl.BlockSpec(memory_space=pltpu.SMEM)
@@ -44,22 +45,24 @@
 
 
 def scales_of(exponents):
-    powers = (jnp.int32(1) << (exponents + 3)).astype(jnp.float32) * 0.125
-    return powers.T
-
-
-def cut_kernel(alone, cuts, tile, part_ref, queries_ref, codes_ref, exponents_ref, *refs):
-    *chunk_refs, sent_ref, codes_buffer, powers, query_sems, fetch_sems, powers_sem = refs
+    return (jnp.int32(1) << (exponents + 3)).astype(jnp.float32) * 0.125
+
+
+def by_example(scales):
+    pad = jnp.zeros((-scales.shape[0] % 8, scales.shape[1]), scales.dtype)
+    return jnp.concatenate([scales, pad], axis=0).T
+
+
+def cut_kernel(alone, cuts, part_ref, queries_ref, codes_ref, exponents_ref, *refs):
+    *chunk_refs, sent_ref, sent_scales_ref, powers, sems = refs
     part = part_ref[0]
     blocks = exponents_ref.shape[0]
     far = (blocks - alone) * BLOCK
     first = pl.multiple_of(part * far, BLOCK)
     rest = pl.multiple_of((1 - part) * far, BLOCK)
     wide = alone * BLOCK
-
-    copies = []
-
-    def copy_columns(out_ref, start, stop):
+    copies = [(exponents_ref, powers)]
+    for out_ref, start, stop in zip(chunk_refs, cuts[:-1], cuts[1:]):
         if start < wide:
             width = min(stop, wide) - start
             copies.append((
@@ -72,62 +75,36 @@
                 queries_ref.at[0, :, pl.ds(begin, stop - begin)],
                 out_ref.at[:, pl.ds(begin - start, stop - begin)],
             ))
-
-    for out_ref, start, stop in zip(chunk_refs, cuts[:-1], cuts[1:]):
-        copy_columns(out_ref, start, stop)
-    moves = [pltpu.make_async_copy(a, b, query_sems.at[i]) for i, (a, b) in enumerate(copies)]
-    tiles = codes_buffer.shape[0]
-
-    def fetch(i):
-        return pltpu.make_async_copy(
-            codes_ref.at[pl.ds(i * tile, tile), pl.ds(rest, wide)], codes_buffer.at[i], fetch_sems.at[i]
-        )
-
-    powers_copy = pltpu.make_async_copy(exponents_ref, powers, powers_sem)
-    powers_copy.start()
-    for i in range(tiles):
-        fetch(i).start()
-    for move in moves:
-        move.start()
-    powers_copy.wait()
+    copies.append((codes_ref.at[:, pl.ds(rest, wide)], sent_ref))
+    copies = [pltpu.make_async_copy(a, b, sems.at[i]) for i, (a, b) in enumerate(copies)]
+    for copy in copies:
+        copy.start()
+    copies[0].wait()
     near = powers[0:alone, :]
     away = powers[blocks - alone : blocks, :]
-    pad = jnp.zeros((-alone % 8, near.shape[1]), jnp.int32)
-    scales = scales_of(jnp.concatenate([jnp.where(part == 0, away, near), pad], axis=0))
-    for i in range(tiles):
-        fetch(i).wait()
-        for block in range(alone):
-            columns = slice(block * BLOCK, (block + 1) * BLOCK)
-            sent_ref[i * tile : (i + 1) * tile, columns] = scaled(
-                codes_buffer[i, :, columns], scales[i * tile : (i + 1) * tile], block
-            )
-    for move in moves:
-        move.wait()
+    sent_scales_ref[...] = scales_of(jnp.where(part == 0, away, near))
+    for copy in copies[1:]:
+        copy.wait()
 
 
 def cut(part, queries, codes, exponents, alone, cuts):
     rows = queries.shape[1]
     count = codes.shape[0]
-    tile = min(count, 64)
-    tiles = count // tile
     anywhere = pl.BlockSpec(memory_space=pl.ANY)
     wide = alone * BLOCK
     chunks = len(cuts) - 1
     return pl.pallas_call(
-        functools.partial(cut_kernel, alone, cuts, tile),
+        functools.partial(cut_kernel, alone, cuts),
         out_shape=[pltpu.VMEM((rows, b - a), jnp.bfloat16) for a, b in zip(cuts[:-1], cuts[1:])]
-        + [pltpu.VMEM((count, wide), jnp.bfloat16)],
+        + [pltpu.VMEM((count, wide), jnp.bfloat16), pltpu.VMEM((alone, count), jnp.float32)],
         in_specs=[SMEM, anywhere, anywhere, anywhere],
-        out_specs=[VMEM] * (chunks + 1),
+        out_specs=[VMEM] * (chunks + 2),
         scratch_shapes=[
-            pltpu.VMEM((tiles, tile, wide), jnp.bfloat16),
             pltpu.VMEM(exponents.shape, exponents.dtype),
-            pltpu.SemaphoreType.DMA((2 * chunks,)),
-            pltpu.SemaphoreType.DMA((tiles,)),
-            pltpu.SemaphoreType.DMA,
+            pltpu.SemaphoreType.DMA((2 * chunks + 2,)),
         ],
         compiler_params=pltpu.CompilerParams(vmem_limit_bytes=16 << 20),
-        cost_estimate=pl.CostEstimate(flops=codes.size, bytes_accessed=2 * codes.size, transcendentals=0),
+        cost_estimate=pl.CostEstimate(flops=0, bytes_accessed=2 * codes.size, transcendentals=0),
         name="cut_queries",
     )(part, in_hbm(queries), in_hbm(codes), in_hbm(exponents))
 
@@ -151,8 +128,7 @@
     powers_copy.wait()
     own = jnp.where(part == 0, powers[0:alone, :], powers[far:blocks, :])
     kept = jnp.concatenate([own, powers[alone:far, :]], axis=0)
-    pad = jnp.zeros((-kept.shape[0] % 8, kept.shape[1]), jnp.int32)
-    scales = scales_of(jnp.concatenate([kept, pad], axis=0))
+    scales = by_example(scales_of(kept))
     shared = far - alone
     for i in range(tiles):
         fetch(i).wait()
@@ -184,6 +160,45 @@
     )(part, in_hbm(codes), in_hbm(exponents))
 
 
+def stash_kernel(row, *refs):
+    *array_refs, out_ref = refs
+    array_refs = array_refs[1:] if row else array_refs
+    for ref in array_refs:
+        out_ref[row : row + ref.shape[0]] = ref[...]
+        row += ref.shape[0]
+
+
+def stash(held, arrays, row, rows):
+    operands = ([held] if row else []) + arrays
+    return pl.pallas_call(
+        functools.partial(stash_kernel, row),
+        out_shape=pltpu.VMEM((rows, arrays[0].shape[1]), arrays[0].dtype),
+        in_specs=[VMEM] * len(operands),
+        out_specs=VMEM,
+        input_output_aliases={0: 0} if row else {},
+        compiler_params=pltpu.CompilerParams(vmem_limit_bytes=16 << 20),
+        cost_estimate=pl.CostEstimate(flops=0, bytes_accessed=4 * sum(a.size for a in arrays), transcendentals=0),
+        name="stash",
+    )(*in_vmem(operands))
+
+
+def dot(rows, grads):
+    return lax.dot_general(rows, grads, NT, preferred_element_type=jnp.float32)
+
+
+def stacked(refs, columns):
+    rows = [ref[:, columns] for ref in refs]
+    return jnp.concatenate(rows, axis=0) if len(rows) > 1 else rows[0]
+
+
+def halves(half, total, rows, keep_ref, send_ref):
+    for j in range(total.shape[0] // rows):
+        low = total[j * rows : j * rows + rows // 2]
+        high = total[j * rows + rows // 2 : (j + 1) * rows]
+        keep_ref[j] = jnp.where(half == 0, low, high)
+        send_ref[j] = jnp.where(half == 0, high, low)
+
+
 def product(pieces, grads_ref):
     total = None
     first = 0
@@ -191,44 +206,81 @@
         width = min(refs[0].shape[1], grads_ref.shape[1] - first)
         if width <= 0:
             break
-        rows = [ref[:, :width] for ref in refs]
-        rows = jnp.concatenate(rows, axis=0) if len(rows) > 1 else rows[0]
-        term = lax.dot_general(rows, grads_ref[:, first : first + width], NT, preferred_element_type=jnp.float32)
+        term = dot(stacked(refs, slice(0, width)), grads_ref[:, first : first + width])
         total = term if total is None else total + term
         first += width
     return total
 
 
-def unflatten(layout, refs):
+def score_kernel(counts, grads_given, rows, half_ref, *refs):
     refs = list(refs)
-    return [[refs.pop(0) for _ in range(arrays)] for arrays in layout]
-
-
-def score_kernel(layout, rows, half_ref, *refs):
-    *query_refs, grads_ref, keep_ref, send_ref = refs
-    total = product(unflatten(layout, query_refs), grads_ref)
-    for j in range(total.shape[0] // rows):
-        low = total[j * rows : j * rows + rows // 2]
-        high = total[j * rows + rows // 2 : (j + 1) * rows]
-        keep_ref[j] = jnp.where(half_ref[0] == 0, low, high)
-        send_ref[j] = jnp.where(half_ref[0] == 0, high, low)
+    pieces = [[refs.pop(0) for _ in range(arrays)] for arrays in counts]
+    grad_refs, outs = refs[:grads_given], refs[grads_given:]
+    for i, grads_ref in enumerate(grad_refs):
+        halves(half_ref[0], product(pieces, grads_ref), rows, *outs[2 * i : 2 * i + 2])
 
 
 def score(half, rows, pieces, grads):
     operands = [array for arrays in pieces for array in arrays]
-    stacked = sum(array.shape[0] for array in pieces[0])
-    shape = pltpu.VMEM((stacked // rows, rows // 2, grads.shape[0]), jnp.float32)
-    return pl.pallas_call(
-        functools.partial(score_kernel, [len(arrays) for arrays in pieces], rows),
-        out_shape=[shape, shape],
-        in_specs=[SMEM] + [VMEM] * (len(operands) + 1),
-        out_specs=[VMEM, VMEM],
+    height = sum(array.shape[0] for array in pieces[0])
+    shape = pltpu.VMEM((height // rows, rows // 2, grads[0].shape[0]), jnp.float32)
+    return pl.pallas_call(
+        functools.partial(score_kernel, [len(arrays) for arrays in pieces], len(grads), rows),
+        out_shape=[shape] * (2 * len(grads)),
+        in_specs=[SMEM] + [VMEM] * (len(operands) + len(grads)),
+        out_specs=[VMEM] * (2 * len(grads)),
         compiler_params=pltpu.CompilerParams(vmem_limit_bytes=16 << 20),
         cost_estimate=pl.CostEstimate(
-            flops=2 * stacked * grads.size, bytes_accessed=2 * grads.size, transcendentals=0
+            flops=2 * height * sum(g.size for g in grads), bytes_accessed=2 * grads[0].size, transcendentals=0
         ),
         name="score",
-    )(half, *in_vmem([*operands, grads]))
+    )(half, *in_vmem([*operands, *grads]))
+
+
+def received_kernel(pieces_given, runs, rows, half_ref, codes_ref, scales_ref, *refs):
+    *piece_refs, grads_ref, keep_ref, send_ref, buffer, sems = refs
+
+    def fetch(i):
+        _, start, width, _ = runs[i]
+        columns = pl.ds(start, width)
+        return pltpu.make_async_copy(codes_ref.at[:, columns], buffer.at[:, columns], sems.at[i])
+
+    for i in range(len(runs)):
+        fetch(i).start()
+    scales = by_example(scales_ref[...])
+    total = None
+    for i, (piece, start, width, at) in enumerate(runs):
+        fetch(i).wait()
+        for first in range(start, start + width, BLOCK):
+            columns = slice(first, first + BLOCK)
+            grads_ref[:, columns] = scaled(buffer[:, columns], scales, first // BLOCK)
+        term = dot(piece_refs[piece][:, at : at + width], grads_ref[:, start : start + width])
+        total = term if total is None else total + term
+    halves(half_ref[0], total, rows, keep_ref, send_ref)
+
+
+def score_received(half, rows, pieces, codes, scales):
+    runs = []
+    first = 0
+    for i, piece in enumerate(pieces):
+        width = min(piece.shape[1], codes.shape[1] - first)
+        for at in range(0, max(width, 0), RUN):
+            runs.append((i, first + at, min(RUN, width - at), at))
+        first += max(width, 0)
+    height = pieces[0].shape[0]
+    shape = pltpu.VMEM((height // rows, rows // 2, codes.shape[0]), jnp.float32)
+    return pl.pallas_call(
+        functools.partial(received_kernel, len(pieces), runs, rows),
+        out_shape=[pltpu.VMEM(codes.shape, codes.dtype), shape, shape],
+        in_specs=[SMEM, pl.BlockSpec(memory_space=pl.ANY)] + [VMEM] * (len(pieces) + 1),
+        out_specs=[VMEM] * 3,
+        scratch_shapes=[pltpu.VMEM(codes.shape, codes.dtype), pltpu.SemaphoreType.DMA((len(runs),))],
+        compiler_params=pltpu.CompilerParams(vmem_limit_bytes=16 << 20),
+        cost_estimate=pl.CostEstimate(
+            flops=2 * height * codes.size, bytes_accessed=2 * codes.size, transcendentals=0
+        ),
+        name="score_received",
+    )(half, in_hbm(codes), *in_vmem([scales, *pieces]))
 
 
 def place_kernel(rows, order_ref, ids_ref, *refs):
@@ -286,35 +338,46 @@
 
     swap = [(i, parts - 1 - i) for i in range(parts)]
     by_block = exponents.T
-    *chunks, sent = cut(part[None], queries, codes, by_block, alone, cuts)
+    *chunks, sent, sent_scales = cut(part[None], queries, codes, by_block, alone, cuts)
     theirs = lax.ppermute(sent, "groups", swap)
+    their_scales = lax.ppermute(sent_scales, "groups", swap)
     ours = scale(part[None], codes, by_block, alone)
-    near = [[] for _ in range(slow)]
+
+    def stack(arrays):
+        return arrays if rows % 16 == 0 else [jnp.concatenate(arrays, axis=0)]
+
+    early_rows = (slow - 1) * fast * rows
+    early, late = [], []
     for c, chunk in enumerate(chunks):
+        held = []
         for s in range(slow):
             values = along_fast(chunk)
-            if s < slow - 1:
-                chunk, *values = lax.optimization_barrier([step(chunk, slow, fast)] + values)
-                if c == CHUNKS - 1 and s == 0:
-                    chunk, ours = lax.optimization_barrier((chunk, ours))
-            near[s].append(values)
-
-    def stack(arrays):
-        return arrays if rows % 16 == 0 else [jnp.concatenate(arrays, axis=0)]
-
-    def pieces_of(steps):
-        return [[a for s in steps for a in stack(near[s][c])] for c in range(CHUNKS)]
-
-    across = [(i, 3 - i) for i in range(4)]
-    shares = []
-    for steps in (range(slow - 1), [slow - 1]):
-        pieces = pieces_of(steps)
-        keep, send = score(half, rows, pieces, theirs)
-        theirs, keep, send = lax.optimization_barrier((theirs, keep, send))
-        shares += [lax.ppermute(send, ("groups", "dim"), across), lax.ppermute(keep, "groups", swap)]
-        keep, send = score(half, rows, pieces, ours)
-        shares += [lax.ppermute(send, "dim", [(0, 1), (1, 0)]), keep]
-    shares = [share.reshape(-1, count) for share in shares]
+            if s == slow - 1:
+                late.append(stack(values))
+                break
+            tied = [step(chunk, slow, fast), *values] + held
+            if c == CHUNKS - 1 and s == 0:
+                *tied, ours, their_scales = lax.optimization_barrier(tied + [ours, their_scales])
+            else:
+                tied = lax.optimization_barrier(tied)
+            chunk, values, held = tied[0], tied[1 : fast + 1], tied[fast + 1 :]
+            held = [stash(held[0] if s else None, stack(values), s * fast * rows, early_rows)]
+        early += held
+
+    def shares_of(their_keep, their_send, keep, send):
+        across = [(i, 3 - i) for i in range(4)]
+        shares = [
+            lax.ppermute(their_send, ("groups", "dim"), across),
+            lax.ppermute(their_keep, "groups", swap),
+            lax.ppermute(send, "dim", [(0, 1), (1, 0)]),
+            keep,
+        ]
+        return [share.reshape(-1, count) for share in shares]
+
+    theirs, *their_early = score_received(half, rows, early, theirs, their_scales)
+    theirs, *their_early = lax.optimization_barrier((theirs, *their_early))
+    shares = shares_of(*their_early, *score(half, rows, [[held] for held in early], [ours]))
+    shares += shares_of(*score(half, rows, late, [theirs, ours]))
     order = jnp.stack([
         lax.rem(here // fast + slow - s, slow) * fast + lax.rem(here % fast + fast - t, fast)
         for s in range(slow)

time: 81.4 us -> 113 us (1.39)
  waiting for transfers between devices: 22.3 us -> 60.8 us
  local copies, waits for them, and re-layouts: 15.1 us -> 10.4 us
  Pallas kernels: 17.2 us -> 15.8 us
    ppermute x6 -> x7, waiting for transfers between devices: 4.57 us -> 42.6 us  [the longest x1 35.8 us: shards(): their_scales = lax.ppermute(sent_scales, 'groups', swap)]
    pallas_call x4 -> x2, Pallas kernels: 8.94 us -> 3.83 us  [score(): pl.pallas_call(functools.partial(score_kernel, [len(arrays) for arrays in...]
    unnamed x42 -> x34, local copies, waits for them, and re-layouts: 15.1 us -> 10.3 us
    pallas_call x1 -> x8, Pallas kernels: 3.74 us -> 7.47 us  [the longest x1 4.14 us: score_received(): pl.pallas_call(functools.partial(received_kernel, len(pieces), runs, rows...]
    ppermute x6 -> x7, starting transfers between devices: 4.45 us -> 4.21 us  [the longest x2 2.61 us: shares_of(): lax.ppermute(their_send, ('groups', 'dim'), across)]
  transfers between devices with their start and end apart: 21 -> 22, of which waited for: 8 -> 8; matrix products, arithmetic and copies ran while one was open for 0% -> 0% of each run, Pallas kernels for 14% -> 10%
where the time goes in v5:
time: 113 us
  waiting for transfers between devices  60.8 us (54%)
  starting transfers between devices  25.5 us (23%)
  Pallas kernels  15.8 us (14%)
  local copies, waits for them, and re-layouts  10.4 us (9%)
    ppermute x1, waiting for transfers between devices, shards(): their_scales = lax.ppermute(sent_scales, 'groups', swap)  35.8 us
    ppermute x14, starting transfers between devices, step(): return lax.ppermute(value, 'ex', pairs)  18.3 us
    ppermute x14, waiting for transfers between devices, step(): return lax.ppermute(value, 'ex', pairs)  18.2 us
    unnamed x34, local copies, waits for them, and re-layouts  10.3 us
    ppermute x2, waiting for transfers between devices, shares_of(): lax.ppermute(their_send, ('groups', 'dim'), across)  5.12 us
    pallas_call x1, Pallas kernels, score_received(): pl.pallas_call(functools.partial(received_kernel, len(pieces), runs, rows...  4.14 us
    pallas_call x2, Pallas kernels, score(): pl.pallas_call(functools.partial(score_kernel, [len(arrays) for arrays in...  3.83 us
    pallas_call x1, Pallas kernels, cut(): pl.pallas_call(functools.partial(cut_kernel, alone, cuts), out_shape=[plt...  3.09 us
  transfers between devices with their start and end apart: 22, of which 8 were waited for; matrix products, arithmetic and copies ran while one was open for 0% of the time, Pallas kernels for 10%

profile of v5, /device:TPU:0, one launch (start us, length us, event | category | flops | bytes accessed | tf_op | source)
XLA Modules:
  0.0 112.8 jit_solution(10425494573638674204)
XLA Ops:
  0.0 3.1 %cut_queries.1 = (bf16[64,2304]{1,0:T(8,128)(2,1)S(1)}, bf16[64,2304]{1,0:T(8,128)(2,1)S(1)}, bf16[256,3584]{1,0:T(8,128)(2,1)}, f32[28,256]{1,0:T(8,128)S(1)}) custom-call(s32[1]{0:T(128)} %bitcast.9.part_ref, bf16[1,64,8192]{2,1,0:T(8,128)(2,1)} %queries_ref.1, bf16[256,8192]{1,0:T(8,128)(2,1)} %codes_ref.3, s32[64,256]{1,0:T(8,128)} %bitcast.27), custom_call_target="tpu_custom_call" | custom-call | bytes 4194304 | tf_op jit(solution)/shard_map/cut_queries/pallas_call | solution.py:96
  3.1 3.0 %collective-permute-start = (bf16[256,3584]{1,0:T(8,128)(2,1)}, bf16[256,3584]{1,0:T(8,128)(2,1)}, u32[]{:S(2)}, u32[]{:S(2)}) collective-permute-start(bf16[256,3584]{1,0:T(8,128)(2,1)} %get-tuple-element.42), channel_id=1, source_target_pairs={{0,16},{16,0},{1,17},{17,1},{2,18},{18,2},{3,19},{19,3},{4,20},{20... | collective-permute-start | bytes 5505032 | tf_op jit(solution)/shard_map/ppermute | solution.py:342
  6.1 0.1 collective-permute-start.3
  6.2 2.0 %collective-permute-start.1 = (bf16[64,2304]{1,0:T(8,128)(2,1)S(1)}, bf16[64,2304]{1,0:T(8,128)(2,1)S(1)}, u32[]{:S(2)}, u32[]{:S(2)}) collective-permute-start(bf16[64,2304]{1,0:T(8,128)(2,1)S(1)} %get-tuple-element.58.refs_0_), channel_id=1, source_target_pairs={{0,4},{2,6},{4,8},{6,10},{8,12},{10,14},{12,0},{14,2},{1,5},{3,7},... | collective-permute-start | bytes 884744 | tf_op jit(solution)/shard_map/ppermute | solution.py:331
  8.2 1.5 %collective-permute-start.2 = (bf16[64,2304]{1,0:T(8,128)(2,1)S(1)}, bf16[64,2304]{1,0:T(8,128)(2,1)S(1)}, u32[]{:S(2)}, u32[]{:S(2)}) collective-permute-start(bf16[64,2304]{1,0:T(8,128)(2,1)S(1)} %get-tuple-element.58.refs_0_), channel_id=1, source_target_pairs={{0,2},{2,0},{4,6},{6,4},{8,10},{10,8},{12,14},{14,12},{1,3},{3,1},... | collective-permute-start | bytes 884744 | tf_op jit(solution)/shard_map/ppermute | solution.py:331
  9.7 1.6 %collective-permute-start.4 = (bf16[64,2304]{1,0:T(8,128)(2,1)S(1)}, bf16[64,2304]{1,0:T(8,128)(2,1)S(1)}, u32[]{:S(2)}, u32[]{:S(2)}) collective-permute-start(bf16[64,2304]{1,0:T(8,128)(2,1)S(1)} %get-tuple-element.48.refs_0_), channel_id=1, source_target_pairs={{0,4},{2,6},{4,8},{6,10},{8,12},{10,14},{12,0},{14,2},{1,5},{3,7},... | collective-permute-start | bytes 884744 | tf_op jit(solution)/shard_map/ppermute | solution.py:331
  11.3 35.8 %collective-permute-done.3.scales_ref = f32[28,256]{1,0:T(8,128)S(1)} collective-permute-done((f32[28,256]{1,0:T(8,128)S(1)}, f32[28,256]{1,0:T(8,128)S(1)}, u32[]{:S(2)}, u32[]{:S(2)}) %collective-permute-start.3) | collective-permute-done | bytes 28704 | tf_op jit(solution)/shard_map/ppermute | solution.py:343
  47.1 0.6 copy-done.14
  47.7 1.7 %collective-permute-start.5 = (bf16[64,2304]{1,0:T(8,128)(2,1)S(1)}, bf16[64,2304]{1,0:T(8,128)(2,1)S(1)}, u32[]{:S(2)}, u32[]{:S(2)}) collective-permute-start(bf16[64,2304]{1,0:T(8,128)(2,1)S(1)} %get-tuple-element.48.refs_0_), channel_id=1, source_target_pairs={{0,2},{2,0},{4,6},{6,4},{8,10},{10,8},{12,14},{14,12},{1,3},{3,1},... | collective-permute-start | bytes 884744 | tf_op jit(solution)/shard_map/ppermute | solution.py:331
  49.4 2.6 %scale_codes.1.refs_2_.refs_5_ = bf16[256,4608]{1,0:T(8,128)(2,1)S(1)} custom-call(s32[1]{0:T(128)} %bitcast.9.part_ref, bf16[256,8192]{1,0:T(8,128)(2,1)} %codes_ref.3, s32[64,256]{1,0:T(8,128)} %bitcast.28), custom_call_target="tpu_custom_call" | custom-call | flops 2097152 | bytes 8388608 | tf_op jit(solution)/shard_map/scale_codes/pallas_call | solution.py:146
  52.0 1.4 %copy-done = bf16[256,4608]{1,0:T(8,128)(2,1)} copy-done((bf16[256,4608]{1,0:T(8,128)(2,1)}, bf16[256,4608]{1,0:T(8,128)(2,1)S(1)}, u32[]{:S(2)}) %copy-start) | copy-done | bytes 2359320
  53.4 0.0 collective-permute-done.1.refs_1_
  53.4 0.0 collective-permute-done.2.refs_1_
  53.4 1.6 %collective-permute-start.10 = (bf16[64,2304]{1,0:T(8,128)(2,1)S(1)}, bf16[64,2304]{1,0:T(8,128)(2,1)S(1)}, u32[]{:S(2)}, u32[]{:S(2)}) collective-permute-start(bf16[64,2304]{1,0:T(8,128)(2,1)S(1)} %collective-permute-done.1.refs_1_), channel_id=1, source_target_pairs={{0,4},{2,6},{4,8},{6,10},{8,12},{10,14},{12,0},{14,2},{1,5},{3,7},... | collective-permute-start | bytes 884744 | tf_op jit(solution)/shard_map/ppermute | solution.py:331
  55.0 0.5 collective-permute-start.11
  55.6 0.0 collective-permute-done.4.refs_1_
  55.6 0.4 collective-permute-done.5.refs_1_
  56.0 1.5 %collective-permute-start.6 = (bf16[64,2304]{1,0:T(8,128)(2,1)S(1)}, bf16[64,2304]{1,0:T(8,128)(2,1)S(1)}, u32[]{:S(2)}, u32[]{:S(2)}) collective-permute-start(bf16[64,2304]{1,0:T(8,128)(2,1)S(1)} %collective-permute-done.4.refs_1_), channel_id=1, source_target_pairs={{0,4},{2,6},{4,8},{6,10},{8,12},{10,14},{12,0},{14,2},{1,5},{3,7},... | collective-permute-start | bytes 884744 | tf_op jit(solution)/shard_map/ppermute | solution.py:331
  57.4 2.1 %collective-permute-start.7 = (bf16[64,2304]{1,0:T(8,128)(2,1)S(1)}, bf16[64,2304]{1,0:T(8,128)(2,1)S(1)}, u32[]{:S(2)}, u32[]{:S(2)}) collective-permute-start(bf16[64,2304]{1,0:T(8,128)(2,1)S(1)} %collective-permute-done.4.refs_1_), channel_id=1, source_target_pairs={{0,2},{2,0},{4,6},{6,4},{8,10},{10,8},{12,14},{14,12},{1,3},{3,1},... | collective-permute-start | bytes 884744 | tf_op jit(solution)/shard_map/ppermute | solution.py:331
  59.7 5.5 %collective-permute-done.10.refs_1_ = bf16[64,2304]{1,0:T(8,128)(2,1)S(1)} collective-permute-done((bf16[64,2304]{1,0:T(8,128)(2,1)S(1)}, bf16[64,2304]{1,0:T(8,128)(2,1)S(1)}, u32[]{:S(2)}, u32[]{:S(2)}) %collective-permute-start.10) | collective-permute-done | bytes 294944 | tf_op jit(solution)/shard_map/ppermute | solution.py:331
  65.2 0.0 collective-permute-done.11.refs_2_
  65.2 1.3 %collective-permute-start.12 = (bf16[64,2304]{1,0:T(8,128)(2,1)S(1)}, bf16[64,2304]{1,0:T(8,128)(2,1)}, u32[]{:S(2)}, u32[]{:S(2)}) collective-permute-start(bf16[64,2304]{1,0:T(8,128)(2,1)S(1)} %collective-permute-done.10.refs_1_), channel_id=1, source_target_pairs={{0,4},{2,6},{4,8},{6,10},{8,12},{10,14},{12,0},{14,2},{1,5},{3,7},... | collective-permute-start | bytes 884744 | tf_op jit(solution)/shard_map/ppermute | solution.py:331
  66.5 0.5 collective-permute-start.13
  67.1 4.4 %collective-permute-done.6.refs_1_ = bf16[64,2304]{1,0:T(8,128)(2,1)S(1)} collective-permute-done((bf16[64,2304]{1,0:T(8,128)(2,1)S(1)}, bf16[64,2304]{1,0:T(8,128)(2,1)S(1)}, u32[]{:S(2)}, u32[]{:S(2)}) %collective-permute-start.6) | collective-permute-done | bytes 294944 | tf_op jit(solution)/shard_map/ppermute | solution.py:331
  71.5 0.0 collective-permute-done.7.refs_2_
  71.5 1.3 %collective-permute-start.8 = (bf16[64,2304]{1,0:T(8,128)(2,1)S(1)}, bf16[64,2304]{1,0:T(8,128)(2,1)}, u32[]{:S(2)}, u32[]{:S(2)}) collective-permute-start(bf16[64,2304]{1,0:T(8,128)(2,1)S(1)} %collective-permute-done.6.refs_1_), channel_id=1, source_target_pairs={{0,4},{2,6},{4,8},{6,10},{8,12},{10,14},{12,0},{14,2},{1,5},{3,7},... | collective-permute-start | bytes 884744 | tf_op jit(solution)/shard_map/ppermute | solution.py:331
  72.9 0.5 collective-permute-start.9
  73.5 4.4 %collective-permute-done.12.refs_2_ = bf16[64,2304]{1,0:T(8,128)(2,1)} collective-permute-done((bf16[64,2304]{1,0:T(8,128)(2,1)S(1)}, bf16[64,2304]{1,0:T(8,128)(2,1)}, u32[]{:S(2)}, u32[]{:S(2)}) %collective-permute-start.12) | collective-permute-done | bytes 294944 | tf_op jit(solution)/shard_map/ppermute | solution.py:331
  77.9 0.0 collective-permute-done.13.refs_2_
  77.9 0.7 copy-done.6
  78.7 3.4 %collective-permute-done.8.refs_0_ = bf16[64,2304]{1,0:T(8,128)(2,1)} collective-permute-done((bf16[64,2304]{1,0:T(8,128)(2,1)S(1)}, bf16[64,2304]{1,0:T(8,128)(2,1)}, u32[]{:S(2)}, u32[]{:S(2)}) %collective-permute-start.8) | collective-permute-done | bytes 294944 | tf_op jit(solution)/shard_map/ppermute | solution.py:331
  82.1 0.0 collective-permute-done.9.refs_2_
  82.1 0.7 copy-done.8
  82.8 0.6 collective-permute-start.18
  83.4 1.5 %collective-permute-start.17 = (bf16[64,2304]{1,0:T(8,128)(2,1)}, bf16[64,2304]{1,0:T(8,128)(2,1)}, u32[]{:S(2)}, u32[]{:S(2)}) collective-permute-start(bf16[64,2304]{1,0:T(8,128)(2,1)} %collective-permute-done.8.refs_0_), channel_id=1, source_target_pairs={{0,2},{2,0},{4,6},{6,4},{8,10},{10,8},{12,14},{14,12},{1,3},{3,1},... | collective-permute-start | bytes 884744 | tf_op jit(solution)/shard_map/ppermute | solution.py:331
  84.8 1.0 copy-done.3
  85.8 1.0 copy-done.7
  86.8 0.9 copy-done.5
  87.7 0.1 copy-done.9
  87.9 1.6 %copy-done.1 = bf16[256,4608]{1,0:T(8,128)(2,1)S(1)} copy-done((bf16[256,4608]{1,0:T(8,128)(2,1)S(1)}, bf16[256,4608]{1,0:T(8,128)(2,1)}, u32[]{:S(2)}) %copy-start.1) | copy-done | bytes 2359320
  89.5 1.1 score.2
  90.6 0.7 copy-done.10
  91.3 0.0 collective-permute-start.16
  91.3 0.0 collective-permute-done.codes_ref
  91.3 4.1 %score_received.1 = (bf16[256,3584]{1,0:T(8,128)(2,1)S(1)}, f32[6,32,256]{2,1,0:T(8,128)}, f32[6,32,256]{2,1,0:T(8,128)}) custom-call(s32[1]{0:T(128)} %bitcast.8.half_ref, bf16[256,3584]{1,0:T(8,128)(2,1)} %collective-permute-done.codes_ref, f32[28,256]{1,0:T(8,128)S(1)} %copy-done.15, bf16[384,2304]{1,0:T(8,128)(2,1)S(1)} %stash.8.refs_0_, ...), custom_call_target="tpu_custom_call" | custom-call | flops 704643072 | bytes 1835008 | tf_op jit(solution)/shard_map/score_received/pallas_call | solution.py:272
  95.4 1.7 %collective-permute-start.14 = (f32[6,32,256]{2,1,0:T(8,128)}, f32[6,32,256]{2,1,0:T(8,128)S(1)}, u32[]{:S(2)}, u32[]{:S(2)}) collective-permute-start(f32[6,32,256]{2,1,0:T(8,128)} %get-tuple-element.67), channel_id=1, source_target_pairs={{0,17},{1,16},{16,1},{17,0},{2,19},{3,18},{18,3},{19,2},{4,21},{5,... | collective-permute-start | bytes 589832 | tf_op jit(solution)/shard_map/ppermute | solution.py:370
  97.1 0.5 collective-permute-start.15
  97.6 0.0 collective-permute-done.18.refs_3_
  97.6 0.0 collective-permute-done.17.refs_1_
  97.7 0.0 copy-start.16
  97.7 2.7 %score.3 = (f32[2,32,256]{2,1,0:T(8,128)S(1)}, f32[2,32,256]{2,1,0:T(8,128)S(1)}, f32[2,32,256]{2,1,0:T(8,128)S(1)}, f32[2,32,256]{2,1,0:T(8,128)S(1)}) custom-call(s32[1]{0:T(128)} %bitcast.8.half_ref, bf16[64,2304]{1,0:T(8,128)(2,1)} %collective-permute-done.8.refs_0_, bf16[64,2304]{1,0:T(8,128)(2,1)} %collective-permute-done.17.refs_1_, ...), custom_call_target="tpu_custom_call" | custom-call | flops 536870912 | bytes 1835008 | tf_op jit(solution)/shard_map/score/pallas_call | solution.py:227
  100.4 0.9 collective-permute-start.19
  101.3 0.7 collective-permute-start.20
  102.1 0.0 collective-permute-done.16
  102.1 0.7 copy-done.12
  102.7 0.3 collective-permute-start.21
  103.0 0.1 stack.35.order_ref
  103.1 5.1 %collective-permute-done.19 = f32[2,32,256]{2,1,0:T(8,128)S(1)} collective-permute-done((f32[2,32,256]{2,1,0:T(8,128)S(1)}, f32[2,32,256]{2,1,0:T(8,128)S(1)}, u32[]{:S(2)}, u32[]{:S(2)}) %collective-permute-start.19) | collective-permute-done | bytes 65568 | tf_op jit(solution)/shard_map/ppermute | solution.py:370
  108.2 1.7 %collective-permute-done.20 = f32[2,32,256]{2,1,0:T(8,128)S(1)} collective-permute-done((f32[2,32,256]{2,1,0:T(8,128)S(1)}, f32[2,32,256]{2,1,0:T(8,128)S(1)}, u32[]{:S(2)}, u32[]{:S(2)}) %collective-permute-start.20) | collective-permute-done | bytes 65568 | tf_op jit(solution)/shard_map/ppermute | solution.py:371
  109.9 0.0 collective-permute-done.21
  109.9 0.0 collective-permute-done.14
  109.9 0.0 collective-permute-done.15
  110.0 0.9 copy-done.13
  110.9 1.9 %place_scores.1 = f32[8,32,256]{2,1,0:T(8,128)} custom-call(s32[8]{0:T(128)S(1)} %stack.35.order_ref, s32[1,256]{1,0:T(1,128)S(1)} %copy-done.16, f32[192,256]{1,0:T(8,128)S(1)} %bitcast.21, f32[192,256]{1,0:T(8,128)S(1)} %bitcast.22, f32[192,256]{1,0:T(8,128)S(1)} %bitcast.20, f32[192,256]{1,0:T(8,128)S(1)} %bitcast.19, f32[64,256]{1,0:T(8,128)S(1)} %bitcast.24, ...), custom_call_target="tpu_custom_call" | custom-call | tf_op jit(solution)/shard_map/place_scores/pallas_call | solution.py:304
  (27 shorter events, 0.3 us)
Async XLA Ops:
  3.1 88.2 %collective-permute-start = (bf16[256,3584]{1,0:T(8,128)(2,1)}, bf16[256,3584]{1,0:T(8,128)(2,1)}, u32[]{:S(2)}, u32[]{:S(2)}) collective-permute-start(bf16[256,3584]{1,0:T(8,128)(2,1)} %get-tuple-element.42), channel_id=1, source_target_pairs={{0,16},{16,0},{1,17},{17,1},{2,18},{18,2},{3,19},{19,3},{4,20},{20... | collective-permute-start | bytes 5505032 | tf_op jit(solution)/shard_map/ppermute | solution.py:342
  6.1 40.9 %collective-permute-start.3 = (f32[28,256]{1,0:T(8,128)S(1)}, f32[28,256]{1,0:T(8,128)S(1)}, u32[]{:S(2)}, u32[]{:S(2)}) collective-permute-start(f32[28,256]{1,0:T(8,128)S(1)} %get-tuple-element.44), channel_id=1, source_target_pairs={{0,16},{16,0},{1,17},{17,1},{2,18},{18,2},{3,19},{19,3},{4,20},{20... | collective-permute-start | bytes 86024 | tf_op jit(solution)/shard_map/ppermute | solution.py:343
  6.2 47.2 %collective-permute-start.1 = (bf16[64,2304]{1,0:T(8,128)(2,1)S(1)}, bf16[64,2304]{1,0:T(8,128)(2,1)S(1)}, u32[]{:S(2)}, u32[]{:S(2)}) collective-permute-start(bf16[64,2304]{1,0:T(8,128)(2,1)S(1)} %get-tuple-element.58.refs_0_), channel_id=1, source_target_pairs={{0,4},{2,6},{4,8},{6,10},{8,12},{10,14},{12,0},{14,2},{1,5},{3,7},... | collective-permute-start | bytes 884744 | tf_op jit(solution)/shard_map/ppermute | solution.py:331
  8.2 45.2 %collective-permute-start.2 = (bf16[64,2304]{1,0:T(8,128)(2,1)S(1)}, bf16[64,2304]{1,0:T(8,128)(2,1)S(1)}, u32[]{:S(2)}, u32[]{:S(2)}) collective-permute-start(bf16[64,2304]{1,0:T(8,128)(2,1)S(1)} %get-tuple-element.58.refs_0_), channel_id=1, source_target_pairs={{0,2},{2,0},{4,6},{6,4},{8,10},{10,8},{12,14},{14,12},{1,3},{3,1},... | collective-permute-start | bytes 884744 | tf_op jit(solution)/shard_map/ppermute | solution.py:331
  9.7 45.9 %collective-permute-start.4 = (bf16[64,2304]{1,0:T(8,128)(2,1)S(1)}, bf16[64,2304]{1,0:T(8,128)(2,1)S(1)}, u32[]{:S(2)}, u32[]{:S(2)}) collective-permute-start(bf16[64,2304]{1,0:T(8,128)(2,1)S(1)} %get-tuple-element.48.refs_0_), channel_id=1, source_target_pairs={{0,4},{2,6},{4,8},{6,10},{8,12},{10,14},{12,0},{14,2},{1,5},{3,7},... | collective-permute-start | bytes 884744 | tf_op jit(solution)/shard_map/ppermute | solution.py:331
  47.1 0.6 copy-start.14
  47.7 8.3 %collective-permute-start.5 = (bf16[64,2304]{1,0:T(8,128)(2,1)S(1)}, bf16[64,2304]{1,0:T(8,128)(2,1)S(1)}, u32[]{:S(2)}, u32[]{:S(2)}) collective-permute-start(bf16[64,2304]{1,0:T(8,128)(2,1)S(1)} %get-tuple-element.48.refs_0_), channel_id=1, source_target_pairs={{0,2},{2,0},{4,6},{6,4},{8,10},{10,8},{12,14},{14,12},{1,3},{3,1},... | collective-permute-start | bytes 884744 | tf_op jit(solution)/shard_map/ppermute | solution.py:331
  52.0 1.4 %copy-start = (bf16[256,4608]{1,0:T(8,128)(2,1)}, bf16[256,4608]{1,0:T(8,128)(2,1)S(1)}, u32[]{:S(2)}) copy-start(bf16[256,4608]{1,0:T(8,128)(2,1)S(1)} %scale_codes.1.refs_2_.refs_5_) | copy-start | bytes 7077892
  53.4 11.7 %collective-permute-start.10 = (bf16[64,2304]{1,0:T(8,128)(2,1)S(1)}, bf16[64,2304]{1,0:T(8,128)(2,1)S(1)}, u32[]{:S(2)}, u32[]{:S(2)}) collective-permute-start(bf16[64,2304]{1,0:T(8,128)(2,1)S(1)} %collective-permute-done.1.refs_1_), channel_id=1, source_target_pairs={{0,4},{2,6},{4,8},{6,10},{8,12},{10,14},{12,0},{14,2},{1,5},{3,7},... | collective-permute-start | bytes 884744 | tf_op jit(solution)/shard_map/ppermute | solution.py:331
  55.0 10.2 %collective-permute-start.11 = (bf16[64,2304]{1,0:T(8,128)(2,1)S(1)}, bf16[64,2304]{1,0:T(8,128)(2,1)S(1)}, u32[]{:S(2)}, u32[]{:S(2)}) collective-permute-start(bf16[64,2304]{1,0:T(8,128)(2,1)S(1)} %collective-permute-done.1.refs_1_), channel_id=1, source_target_pairs={{0,2},{2,0},{4,6},{6,4},{8,10},{10,8},{12,14},{14,12},{1,3},{3,1},... | collective-permute-start | bytes 884744 | tf_op jit(solution)/shard_map/ppermute | solution.py:331
  56.0 15.5 %collective-permute-start.6 = (bf16[64,2304]{1,0:T(8,128)(2,1)S(1)}, bf16[64,2304]{1,0:T(8,128)(2,1)S(1)}, u32[]{:S(2)}, u32[]{:S(2)}) collective-permute-start(bf16[64,2304]{1,0:T(8,128)(2,1)S(1)} %collective-permute-done.4.refs_1_), channel_id=1, source_target_pairs={{0,4},{2,6},{4,8},{6,10},{8,12},{10,14},{12,0},{14,2},{1,5},{3,7},... | collective-permute-start | bytes 884744 | tf_op jit(solution)/shard_map/ppermute | solution.py:331
  57.4 14.1 %collective-permute-start.7 = (bf16[64,2304]{1,0:T(8,128)(2,1)S(1)}, bf16[64,2304]{1,0:T(8,128)(2,1)S(1)}, u32[]{:S(2)}, u32[]{:S(2)}) collective-permute-start(bf16[64,2304]{1,0:T(8,128)(2,1)S(1)} %collective-permute-done.4.refs_1_), channel_id=1, source_target_pairs={{0,2},{2,0},{4,6},{6,4},{8,10},{10,8},{12,14},{14,12},{1,3},{3,1},... | collective-permute-start | bytes 884744 | tf_op jit(solution)/shard_map/ppermute | solution.py:331
  65.2 8.3 %copy-start.2 = (bf16[64,2304]{1,0:T(8,128)(2,1)}, bf16[64,2304]{1,0:T(8,128)(2,1)S(1)}, u32[]{:S(2)}) copy-start(bf16[64,2304]{1,0:T(8,128)(2,1)S(1)} %collective-permute-done.10.refs_1_) | copy-start | bytes 884740
  65.2 12.7 %collective-permute-start.12 = (bf16[64,2304]{1,0:T(8,128)(2,1)S(1)}, bf16[64,2304]{1,0:T(8,128)(2,1)}, u32[]{:S(2)}, u32[]{:S(2)}) collective-permute-start(bf16[64,2304]{1,0:T(8,128)(2,1)S(1)} %collective-permute-done.10.refs_1_), channel_id=1, source_target_pairs={{0,4},{2,6},{4,8},{6,10},{8,12},{10,14},{12,0},{14,2},{1,5},{3,7},... | collective-permute-start | bytes 884744 | tf_op jit(solution)/shard_map/ppermute | solution.py:331
  66.5 11.4 %collective-permute-start.13 = (bf16[64,2304]{1,0:T(8,128)(2,1)S(1)}, bf16[64,2304]{1,0:T(8,128)(2,1)S(1)}, u32[]{:S(2)}, u32[]{:S(2)}) collective-permute-start(bf16[64,2304]{1,0:T(8,128)(2,1)S(1)} %collective-permute-done.10.refs_1_), channel_id=1, source_target_pairs={{0,2},{2,0},{4,6},{6,4},{8,10},{10,8},{12,14},{14,12},{1,3},{3,1},... | collective-permute-start | bytes 884744 | tf_op jit(solution)/shard_map/ppermute | solution.py:331
  71.5 1.9 %copy-start.4 = (bf16[64,2304]{1,0:T(8,128)(2,1)}, bf16[64,2304]{1,0:T(8,128)(2,1)S(1)}, u32[]{:S(2)}) copy-start(bf16[64,2304]{1,0:T(8,128)(2,1)S(1)} %collective-permute-done.6.refs_1_) | copy-start | bytes 884740
  71.5 10.6 %collective-permute-start.8 = (bf16[64,2304]{1,0:T(8,128)(2,1)S(1)}, bf16[64,2304]{1,0:T(8,128)(2,1)}, u32[]{:S(2)}, u32[]{:S(2)}) collective-permute-start(bf16[64,2304]{1,0:T(8,128)(2,1)S(1)} %collective-permute-done.6.refs_1_), channel_id=1, source_target_pairs={{0,4},{2,6},{4,8},{6,10},{8,12},{10,14},{12,0},{14,2},{1,5},{3,7},... | collective-permute-start | bytes 884744 | tf_op jit(solution)/shard_map/ppermute | solution.py:331
  72.9 9.2 %collective-permute-start.9 = (bf16[64,2304]{1,0:T(8,128)(2,1)S(1)}, bf16[64,2304]{1,0:T(8,128)(2,1)S(1)}, u32[]{:S(2)}, u32[]{:S(2)}) collective-permute-start(bf16[64,2304]{1,0:T(8,128)(2,1)S(1)} %collective-permute-done.6.refs_1_), channel_id=1, source_target_pairs={{0,2},{2,0},{4,6},{6,4},{8,10},{10,8},{12,14},{14,12},{1,3},{3,1},... | collective-permute-start | bytes 884744 | tf_op jit(solution)/shard_map/ppermute | solution.py:331
  77.9 0.7 copy-start.6
  82.1 0.7 copy-start.8
  82.8 14.8 %collective-permute-start.18 = (bf16[64,2304]{1,0:T(8,128)(2,1)}, bf16[64,2304]{1,0:T(8,128)(2,1)}, u32[]{:S(2)}, u32[]{:S(2)}) collective-permute-start(bf16[64,2304]{1,0:T(8,128)(2,1)} %collective-permute-done.12.refs_2_), channel_id=1, source_target_pairs={{0,2},{2,0},{4,6},{6,4},{8,10},{10,8},{12,14},{14,12},{1,3},{3,1},... | collective-permute-start | bytes 884744 | tf_op jit(solution)/shard_map/ppermute | solution.py:331
  83.4 14.3 %collective-permute-start.17 = (bf16[64,2304]{1,0:T(8,128)(2,1)}, bf16[64,2304]{1,0:T(8,128)(2,1)}, u32[]{:S(2)}, u32[]{:S(2)}) collective-permute-start(bf16[64,2304]{1,0:T(8,128)(2,1)} %collective-permute-done.8.refs_0_), channel_id=1, source_target_pairs={{0,2},{2,0},{4,6},{6,4},{8,10},{10,8},{12,14},{14,12},{1,3},{3,1},... | collective-permute-start | bytes 884744 | tf_op jit(solution)/shard_map/ppermute | solution.py:331
  84.8 1.0 copy-start.3
  85.8 1.0 copy-start.7
  86.8 1.0 copy-start.5
  86.8 1.0 copy-start.9
  87.8 1.7 %copy-start.1 = (bf16[256,4608]{1,0:T(8,128)(2,1)S(1)}, bf16[256,4608]{1,0:T(8,128)(2,1)}, u32[]{:S(2)}) copy-start(bf16[256,4608]{1,0:T(8,128)(2,1)} %copy-done) | copy-start | bytes 7077892
  89.5 1.8 %copy-start.15 = (f32[28,256]{1,0:T(8,128)S(1)}, f32[28,256]{1,0:T(8,128)}, u32[]{:S(2)}) copy-start(f32[28,256]{1,0:T(8,128)} %copy-done.14) | copy-start | bytes 86020
  90.6 0.7 copy-start.10
  91.3 10.8 %collective-permute-start.16 = (f32[6,32,256]{2,1,0:T(8,128)S(1)}, f32[6,32,256]{2,1,0:T(8,128)S(1)}, u32[]{:S(2)}, u32[]{:S(2)}) collective-permute-start(f32[6,32,256]{2,1,0:T(8,128)S(1)} %get-tuple-element.70), channel_id=1, source_target_pairs={{0,1},{1,0},{2,3},{3,2},{4,5},{5,4},{6,7},{7,6},{8,9},{9,8},{10,11... | collective-permute-start | bytes 589832 | tf_op jit(solution)/shard_map/ppermute | solution.py:372
  95.4 14.5 %collective-permute-start.14 = (f32[6,32,256]{2,1,0:T(8,128)}, f32[6,32,256]{2,1,0:T(8,128)S(1)}, u32[]{:S(2)}, u32[]{:S(2)}) collective-permute-start(f32[6,32,256]{2,1,0:T(8,128)} %get-tuple-element.67), channel_id=1, source_target_pairs={{0,17},{1,16},{16,1},{17,0},{2,19},{3,18},{18,3},{19,2},{4,21},{5,... | collective-permute-start | bytes 589832 | tf_op jit(solution)/shard_map/ppermute | solution.py:370
  97.1 12.8 %collective-permute-start.15 = (f32[6,32,256]{2,1,0:T(8,128)}, f32[6,32,256]{2,1,0:T(8,128)S(1)}, u32[]{:S(2)}, u32[]{:S(2)}) collective-permute-start(f32[6,32,256]{2,1,0:T(8,128)} %get-tuple-element.68), channel_id=1, source_target_pairs={{0,16},{16,0},{1,17},{17,1},{2,18},{18,2},{3,19},{19,3},{4,20},{20... | collective-permute-start | bytes 589832 | tf_op jit(solution)/shard_map/ppermute | solution.py:371
  97.6 12.3 %copy-start.11 = (f32[6,32,256]{2,1,0:T(8,128)S(1)}, f32[6,32,256]{2,1,0:T(8,128)}, u32[]{:S(2)}) copy-start(f32[6,32,256]{2,1,0:T(8,128)} %copy-done.10) | copy-start | bytes 589828
  97.7 12.3 %copy-start.16 = (s32[1,256]{1,0:T(1,128)S(1)}, s32[1,256]{1,0:T(1,128)}, u32[]{:S(2)}) copy-start(s32[1,256]{1,0:T(1,128)} %ids_ref.1) | copy-start | bytes 3076
  100.4 7.8 %collective-permute-start.19 = (f32[2,32,256]{2,1,0:T(8,128)S(1)}, f32[2,32,256]{2,1,0:T(8,128)S(1)}, u32[]{:S(2)}, u32[]{:S(2)}) collective-permute-start(f32[2,32,256]{2,1,0:T(8,128)S(1)} %get-tuple-element.75), channel_id=1, source_target_pairs={{0,17},{1,16},{16,1},{17,0},{2,19},{3,18},{18,3},{19,2},{4,21},{5,... | collective-permute-start | bytes 196616 | tf_op jit(solution)/shard_map/ppermute | solution.py:370
  101.3 8.6 %collective-permute-start.20 = (f32[2,32,256]{2,1,0:T(8,128)S(1)}, f32[2,32,256]{2,1,0:T(8,128)S(1)}, u32[]{:S(2)}, u32[]{:S(2)}) collective-permute-start(f32[2,32,256]{2,1,0:T(8,128)S(1)} %get-tuple-element.76), channel_id=1, source_target_pairs={{0,16},{16,0},{1,17},{17,1},{2,18},{18,2},{3,19},{19,3},{4,20},{20... | collective-permute-start | bytes 196616 | tf_op jit(solution)/shard_map/ppermute | solution.py:371
  102.1 0.7 copy-start.12
  102.7 7.2 %collective-permute-start.21 = (f32[2,32,256]{2,1,0:T(8,128)S(1)}, f32[2,32,256]{2,1,0:T(8,128)S(1)}, u32[]{:S(2)}, u32[]{:S(2)}) collective-permute-start(f32[2,32,256]{2,1,0:T(8,128)S(1)} %get-tuple-element.77), channel_id=1, source_target_pairs={{0,1},{1,0},{2,3},{3,2},{4,5},{5,4},{6,7},{7,6},{8,9},{9,8},{10,11... | collective-permute-start | bytes 196616 | tf_op jit(solution)/shard_map/ppermute | solution.py:372
  110.0 0.9 copy-start.13

commit v6 on v5

--- a/solution.py
+++ b/solution.py
@@ -9,7 +9,6 @@
 
 BLOCK = 128
 ALONE = 28
-RUN = 6 * BLOCK
 CHUNKS = 2
 VMEM = pl.BlockSpec(memory_space=pltpu.VMEM)
 SMEM = pl.BlockSpec(memory_space=pltpu.SMEM)
@@ -53,15 +52,11 @@
     return jnp.concatenate([scales, pad], axis=0).T
 
 
-def cut_kernel(alone, cuts, part_ref, queries_ref, codes_ref, exponents_ref, *refs):
-    *chunk_refs, sent_ref, sent_scales_ref, powers, sems = refs
-    part = part_ref[0]
-    blocks = exponents_ref.shape[0]
-    far = (blocks - alone) * BLOCK
-    first = pl.multiple_of(part * far, BLOCK)
-    rest = pl.multiple_of((1 - part) * far, BLOCK)
+def cut_kernel(alone, blocks, cuts, part_ref, queries_ref, *refs):
+    *chunk_refs, sems = refs
+    first = pl.multiple_of(part_ref[0] * (blocks - alone) * BLOCK, BLOCK)
     wide = alone * BLOCK
-    copies = [(exponents_ref, powers)]
+    copies = []
     for out_ref, start, stop in zip(chunk_refs, cuts[:-1], cuts[1:]):
         if start < wide:
             width = min(stop, wide) - start
@@ -75,50 +70,40 @@
                 queries_ref.at[0, :, pl.ds(begin, stop - begin)],
                 out_ref.at[:, pl.ds(begin - start, stop - begin)],
             ))
-    copies.append((codes_ref.at[:, pl.ds(rest, wide)], sent_ref))
     copies = [pltpu.make_async_copy(a, b, sems.at[i]) for i, (a, b) in enumerate(copies)]
     for copy in copies:
         copy.start()
-    copies[0].wait()
-    near = powers[0:alone, :]
-    away = powers[blocks - alone : blocks, :]
-    sent_scales_ref[...] = scales_of(jnp.where(part == 0, away, near))
-    for copy in copies[1:]:
+    for copy in copies:
         copy.wait()
 
 
-def cut(part, queries, codes, exponents, alone, cuts):
+def cut(part, queries, alone, cuts):
     rows = queries.shape[1]
-    count = codes.shape[0]
-    anywhere = pl.BlockSpec(memory_space=pl.ANY)
-    wide = alone * BLOCK
     chunks = len(cuts) - 1
     return pl.pallas_call(
-        functools.partial(cut_kernel, alone, cuts),
-        out_shape=[pltpu.VMEM((rows, b - a), jnp.bfloat16) for a, b in zip(cuts[:-1], cuts[1:])]
-        + [pltpu.VMEM((count, wide), jnp.bfloat16), pltpu.VMEM((alone, count), jnp.float32)],
-        in_specs=[SMEM, anywhere, anywhere, anywhere],
-        out_specs=[VMEM] * (chunks + 2),
-        scratch_shapes=[
-            pltpu.VMEM(exponents.shape, exponents.dtype),
-            pltpu.SemaphoreType.DMA((2 * chunks + 2,)),
-        ],
-        compiler_params=pltpu.CompilerParams(vmem_limit_bytes=16 << 20),
-        cost_estimate=pl.CostEstimate(flops=0, bytes_accessed=2 * codes.size, transcendentals=0),
+        functools.partial(cut_kernel, alone, queries.shape[2] // BLOCK, cuts),
+        out_shape=[pltpu.VMEM((rows, b - a), jnp.bfloat16) for a, b in zip(cuts[:-1], cuts[1:])],
+        in_specs=[SMEM, pl.BlockSpec(memory_space=pl.ANY)],
+        out_specs=[VMEM] * chunks,
+        scratch_shapes=[pltpu.SemaphoreType.DMA((2 * chunks,))],
+        compiler_params=pltpu.CompilerParams(vmem_limit_bytes=16 << 20),
+        cost_estimate=pl.CostEstimate(flops=0, bytes_accessed=2 * queries.size, transcendentals=0),
         name="cut_queries",
-    )(part, in_hbm(queries), in_hbm(codes), in_hbm(exponents))
-
-
-def scale_kernel(alone, tile, part_ref, codes_ref, exponents_ref, out_ref, buffer, powers, sems, powers_sem):
+    )(part, in_hbm(queries))
+
+
+def scale_kernel(alone, tile, sent, part_ref, codes_ref, exponents_ref, out_ref, buffer, powers, sems, powers_sem):
     part = part_ref[0]
     blocks = exponents_ref.shape[0]
     far = blocks - alone
-    tiles = buffer.shape[0]
+    shared = far - alone
+    tiles, _, width = buffer.shape
+    begin = (1 - part) * far if sent else part * alone
 
     def fetch(i):
-        start = pl.multiple_of(part * alone * BLOCK, BLOCK)
+        start = pl.multiple_of(begin * BLOCK, BLOCK)
         return pltpu.make_async_copy(
-            codes_ref.at[pl.ds(i * tile, tile), pl.ds(start, far * BLOCK)], buffer.at[i], sems.at[i]
+            codes_ref.at[pl.ds(i * tile, tile), pl.ds(start, width)], buffer.at[i], sems.at[i]
         )
 
     powers_copy = pltpu.make_async_copy(exponents_ref, powers, powers_sem)
@@ -126,25 +111,29 @@
     for i in range(tiles):
         fetch(i).start()
     powers_copy.wait()
-    own = jnp.where(part == 0, powers[0:alone, :], powers[far:blocks, :])
-    kept = jnp.concatenate([own, powers[alone:far, :]], axis=0)
-    scales = by_example(scales_of(kept))
-    shared = far - alone
+    near, away = powers[0:alone, :], powers[far:blocks, :]
+    if sent:
+        scales = by_example(scales_of(jnp.where(part == 0, away, near)))
+    else:
+        own = jnp.where(part == 0, near, away)
+        scales = by_example(scales_of(jnp.concatenate([own, powers[alone:far, :]], axis=0)))
     for i in range(tiles):
         fetch(i).wait()
         rows = slice(i * tile, (i + 1) * tile)
-        for block in range(far):
-            at = block + part * shared if block < alone else block - part * alone
+        for block in range(width // BLOCK):
+            at = block
+            if not sent:
+                at = block + part * shared if block < alone else block - part * alone
             columns = pl.ds(pl.multiple_of(at * BLOCK, BLOCK), BLOCK)
             out_ref[rows, block * BLOCK : (block + 1) * BLOCK] = scaled(buffer[i, :, columns], scales[rows], block)
 
 
-def scale(part, codes, exponents, alone):
+def scale(part, codes, exponents, alone, sent):
     count = codes.shape[0]
-    width = (exponents.shape[0] - alone) * BLOCK
+    width = (alone if sent else exponents.shape[0] - alone) * BLOCK
     tile = min(count, 64)
     return pl.pallas_call(
-        functools.partial(scale_kernel, alone, tile),
+        functools.partial(scale_kernel, alone, tile, sent),
         out_shape=pltpu.VMEM((count, width), jnp.bfloat16),
         in_specs=[SMEM] + [pl.BlockSpec(memory_space=pl.ANY)] * 2,
         out_specs=VMEM,
@@ -235,52 +224,6 @@
         ),
         name="score",
     )(half, *in_vmem([*operands, *grads]))
-
-
-def received_kernel(pieces_given, runs, rows, half_ref, codes_ref, scales_ref, *refs):
-    *piece_refs, grads_ref, keep_ref, send_ref, buffer, sems = refs
-
-    def fetch(i):
-        _, start, width, _ = runs[i]
-        columns = pl.ds(start, width)
-        return pltpu.make_async_copy(codes_ref.at[:, columns], buffer.at[:, columns], sems.at[i])
-
-    for i in range(len(runs)):
-        fetch(i).start()
-    scales = by_example(scales_ref[...])
-    total = None
-    for i, (piece, start, width, at) in enumerate(runs):
-        fetch(i).wait()
-        for first in range(start, start + width, BLOCK):
-            columns = slice(first, first + BLOCK)
-            grads_ref[:, columns] = scaled(buffer[:, columns], scales, first // BLOCK)
-        term = dot(piece_refs[piece][:, at : at + width], grads_ref[:, start : start + width])
-        total = term if total is None else total + term
-    halves(half_ref[0], total, rows, keep_ref, send_ref)
-
-
-def score_received(half, rows, pieces, codes, scales):
-    runs = []
-    first = 0
-    for i, piece in enumerate(pieces):
-        width = min(piece.shape[1], codes.shape[1] - first)
-        for at in range(0, max(width, 0), RUN):
-            runs.append((i, first + at, min(RUN, width - at), at))
-        first += max(width, 0)
-    height = pieces[0].shape[0]
-    shape = pltpu.VMEM((height // rows, rows // 2, codes.shape[0]), jnp.float32)
-    return pl.pallas_call(
-        functools.partial(received_kernel, len(pieces), runs, rows),
-        out_shape=[pltpu.VMEM(codes.shape, codes.dtype), shape, shape],
-        in_specs=[SMEM, pl.BlockSpec(memory_space=pl.ANY)] + [VMEM] * (len(pieces) + 1),
-        out_specs=[VMEM] * 3,
-        scratch_shapes=[pltpu.VMEM(codes.shape, codes.dtype), pltpu.SemaphoreType.DMA((len(runs),))],
-        compiler_params=pltpu.CompilerParams(vmem_limit_bytes=16 << 20),
-        cost_estimate=pl.CostEstimate(
-            flops=2 * height * codes.size, bytes_accessed=2 * codes.size, transcendentals=0
-        ),
-        name="score_received",
-    )(half, in_hbm(codes), *in_vmem([scales, *pieces]))
 
 
 def place_kernel(rows, order_ref, ids_ref, *refs):
@@ -312,10 +255,16 @@
 
 
 def shards(fast, parts, total, queries, codes, exponents, example_ids):
-    part = lax.axis_index("groups")
+    slow = total // fast
     here = lax.axis_index("ex")
-    half = lax.axis_index("dim")[None]
-    slow = total // fast
+    order = jnp.stack([
+        lax.rem(here // fast + slow - s, slow) * fast + lax.rem(here % fast + fast - t, fast)
+        for s in range(slow)
+        for t in range(fast)
+    ]).astype(jnp.int32)
+    part, half, order = lax.optimization_barrier(
+        (lax.axis_index("groups")[None], lax.axis_index("dim")[None], order)
+    )
     rows = queries.shape[1]
     count = codes.shape[0]
     blocks = exponents.shape[1]
@@ -338,10 +287,9 @@
 
     swap = [(i, parts - 1 - i) for i in range(parts)]
     by_block = exponents.T
-    *chunks, sent, sent_scales = cut(part[None], queries, codes, by_block, alone, cuts)
-    theirs = lax.ppermute(sent, "groups", swap)
-    their_scales = lax.ppermute(sent_scales, "groups", swap)
-    ours = scale(part[None], codes, by_block, alone)
+    chunks = cut(part, queries, alone, cuts)
+    theirs = lax.ppermute(scale(part, codes, by_block, alone, True), "groups", swap)
+    ours = scale(part, codes, by_block, alone, False)
 
     def stack(arrays):
         return arrays if rows % 16 == 0 else [jnp.concatenate(arrays, axis=0)]
@@ -357,7 +305,7 @@
                 break
             tied = [step(chunk, slow, fast), *values] + held
             if c == CHUNKS - 1 and s == 0:
-                *tied, ours, their_scales = lax.optimization_barrier(tied + [ours, their_scales])
+                *tied, ours = lax.optimization_barrier(tied + [ours])
             else:
                 tied = lax.optimization_barrier(tied)
             chunk, values, held = tied[0], tied[1 : fast + 1], tied[fast + 1 :]
@@ -374,15 +322,11 @@
         ]
         return [share.reshape(-1, count) for share in shares]
 
-    theirs, *their_early = score_received(half, rows, early, theirs, their_scales)
+    early = [[held] for held in early]
+    their_early = score(half, rows, early, [theirs])
     theirs, *their_early = lax.optimization_barrier((theirs, *their_early))
-    shares = shares_of(*their_early, *score(half, rows, [[held] for held in early], [ours]))
+    shares = shares_of(*their_early, *score(half, rows, early, [ours]))
     shares += shares_of(*score(half, rows, late, [theirs, ours]))
-    order = jnp.stack([
-        lax.rem(here // fast + slow - s, slow) * fast + lax.rem(here % fast + fast - t, fast)
-        for s in range(slow)
-        for t in range(fast)
-    ]).astype(jnp.int32)
     return place(order, example_ids, shares, rows // 2)
 
 

time: 113 us -> 70.9 us (0.63)
  waiting for transfers between devices: 60.8 us -> 34.1 us
  local copies, waits for them, and re-layouts: 10.4 us -> 0.09 us
  Pallas kernels: 15.8 us -> 11.7 us
    ppermute x2 -> x1, waiting for transfers between devices: 35.8 us -> 0.01 us  [shards(): lax.ppermute(scale(part, codes, by_block, alone, True), 'groups', swap)]
    ppermute x14, waiting for transfers between devices: 18.2 us -> 30.9 us  [step(): return lax.ppermute(value, 'ex', pairs)]
    unnamed x34 -> x2, local copies, waits for them, and re-layouts: 10.3 us -> 0.01 us
    pallas_call x3, Pallas kernels: 9.85 us -> 6.06 us  [the longest x2 4.95 us: scale(): pl.pallas_call(functools.partial(scale_kernel, alone, tile, sent), out_sh...]
    ppermute x2, waiting for transfers between devices: 5.12 us -> 1.92 us  [shares_of(): lax.ppermute(their_send, ('groups', 'dim'), across)]
    ppermute x2, starting transfers between devices: 2.61 us -> 0.73 us  [shares_of(): lax.ppermute(their_send, ('groups', 'dim'), across)]
    pallas_call x2 -> x3, Pallas kernels: 3.83 us -> 3.49 us  [score(): pl.pallas_call(functools.partial(score_kernel, [len(arrays) for arrays in...]
    ppermute x2 -> x1, starting transfers between devices: 3.11 us -> 3.03 us  [shards(): lax.ppermute(scale(part, codes, by_block, alone, True), 'groups', swap)]
  transfers between devices with their start and end apart: 22 -> 21, of which waited for: 8 -> 11; matrix products, arithmetic and copies ran while one was open for 0% -> 0% of each run, Pallas kernels for 10% -> 11%
where the time goes in v6:
time: 70.9 us; the launch traced here: 70.7 us
  waiting for transfers between devices  34.1 us (48%)
  starting transfers between devices  24.7 us (35%)
  Pallas kernels  11.7 us (17%)
    ppermute x14, waiting for transfers between devices, step(): return lax.ppermute(value, 'ex', pairs)  30.9 us
    ppermute x14, starting transfers between devices, step(): return lax.ppermute(value, 'ex', pairs)  17.5 us
    pallas_call x2, Pallas kernels, scale(): pl.pallas_call(functools.partial(scale_kernel, alone, tile, sent), out_sh...  4.95 us
    pallas_call x3, Pallas kernels, score(): pl.pallas_call(functools.partial(score_kernel, [len(arrays) for arrays in...  3.49 us
    ppermute x1, starting transfers between devices, shards(): lax.ppermute(scale(part, codes, by_block, alone, True), 'groups', swap)  3.03 us
    ppermute x2, starting transfers between devices, shares_of(): lax.ppermute(their_keep, 'groups', swap)  2.09 us
    ppermute x2, waiting for transfers between devices, shares_of(): lax.ppermute(their_send, ('groups', 'dim'), across)  1.92 us
    pallas_call x1, Pallas kernels, place(): pl.pallas_call(functools.partial(place_kernel, rows), out_shape=jax.Shape...  1.89 us
  transfers between devices with their start and end apart: 21, of which 11 were waited for; matrix products, arithmetic and copies ran while one was open for 0% of the time, Pallas kernels for 11%

profile of v6, /device:TPU:0, one launch (start us, length us, event | category | flops | bytes accessed | tf_op | source)
XLA Modules:
  0.0 70.7 jit_solution(2096516803213421452)
XLA Ops:
  0.0 0.1 stack.35.order_ref
  0.1 2.3 %scale_codes.2 = bf16[256,3584]{1,0:T(8,128)(2,1)S(1)} custom-call(s32[1]{0:T(128)} %bitcast.part_ref, bf16[256,8192]{1,0:T(8,128)(2,1)} %codes_ref.3, s32[64,256]{1,0:T(8,128)} %bitcast.27), custom_call_target="tpu_custom_call" | custom-call | flops 2097152 | bytes 8388608 | tf_op jit(solution)/shard_map/scale_codes/pallas_call | solution.py:135
  2.4 3.0 %collective-permute-start = (bf16[256,3584]{1,0:T(8,128)(2,1)S(1)}, bf16[256,3584]{1,0:T(8,128)(2,1)S(1)}, u32[]{:S(2)}, u32[]{:S(2)}) collective-permute-start(bf16[256,3584]{1,0:T(8,128)(2,1)S(1)} %scale_codes.2), channel_id=1, source_target_pairs={{0,16},{16,0},{1,17},{17,1},{2,18},{18,2},{3,19},{19,3},{4,20},{20... | collective-permute-start | bytes 5505032 | tf_op jit(solution)/shard_map/ppermute | solution.py:291
  5.5 1.1 %cut_queries.1 = (bf16[64,2304]{1,0:T(8,128)(2,1)S(1)}, bf16[64,2304]{1,0:T(8,128)(2,1)S(1)}) custom-call(s32[1]{0:T(128)} %bitcast.part_ref, bf16[1,64,8192]{2,1,0:T(8,128)(2,1)} %queries_ref.1), custom_call_target="tpu_custom_call" | custom-call | bytes 1048576 | tf_op jit(solution)/shard_map/cut_queries/pallas_call | solution.py:83
  6.6 1.6 %collective-permute-start.7 = (bf16[64,2304]{1,0:T(8,128)(2,1)S(1)}, bf16[64,2304]{1,0:T(8,128)(2,1)S(1)}, u32[]{:S(2)}, u32[]{:S(2)}) collective-permute-start(bf16[64,2304]{1,0:T(8,128)(2,1)S(1)} %get-tuple-element.60.refs_0_), channel_id=1, source_target_pairs={{0,4},{2,6},{4,8},{6,10},{8,12},{10,14},{12,0},{14,2},{1,5},{3,7},... | collective-permute-start | bytes 884744 | tf_op jit(solution)/shard_map/ppermute | solution.py:280
  8.2 1.5 %collective-permute-start.8 = (bf16[64,2304]{1,0:T(8,128)(2,1)S(1)}, bf16[64,2304]{1,0:T(8,128)(2,1)S(1)}, u32[]{:S(2)}, u32[]{:S(2)}) collective-permute-start(bf16[64,2304]{1,0:T(8,128)(2,1)S(1)} %get-tuple-element.60.refs_0_), channel_id=1, source_target_pairs={{0,2},{2,0},{4,6},{6,4},{8,10},{10,8},{12,14},{14,12},{1,3},{3,1},... | collective-permute-start | bytes 884744 | tf_op jit(solution)/shard_map/ppermute | solution.py:280
  9.7 1.6 %collective-permute-start.1 = (bf16[64,2304]{1,0:T(8,128)(2,1)S(1)}, bf16[64,2304]{1,0:T(8,128)(2,1)S(1)}, u32[]{:S(2)}, u32[]{:S(2)}) collective-permute-start(bf16[64,2304]{1,0:T(8,128)(2,1)S(1)} %get-tuple-element.49.refs_0_), channel_id=1, source_target_pairs={{0,4},{2,6},{4,8},{6,10},{8,12},{10,14},{12,0},{14,2},{1,5},{3,7},... | collective-permute-start | bytes 884744 | tf_op jit(solution)/shard_map/ppermute | solution.py:280
  11.3 0.5 collective-permute-start.2
  11.8 2.6 %scale_codes.3.refs_2_.refs_5_ = bf16[256,4608]{1,0:T(8,128)(2,1)S(1)} custom-call(s32[1]{0:T(128)} %bitcast.part_ref, bf16[256,8192]{1,0:T(8,128)(2,1)} %codes_ref.3, s32[64,256]{1,0:T(8,128)} %bitcast.28), custom_call_target="tpu_custom_call" | custom-call | flops 2097152 | bytes 8388608 | tf_op jit(solution)/shard_map/scale_codes/pallas_call | solution.py:135
  14.4 3.9 %collective-permute-done.7.refs_1_ = bf16[64,2304]{1,0:T(8,128)(2,1)S(1)} collective-permute-done((bf16[64,2304]{1,0:T(8,128)(2,1)S(1)}, bf16[64,2304]{1,0:T(8,128)(2,1)S(1)}, u32[]{:S(2)}, u32[]{:S(2)}) %collective-permute-start.7) | collective-permute-done | bytes 294944 | tf_op jit(solution)/shard_map/ppermute | solution.py:280
  18.3 0.0 collective-permute-done.8.refs_1_
  18.3 1.5 %collective-permute-start.10 = (bf16[64,2304]{1,0:T(8,128)(2,1)S(1)}, bf16[64,2304]{1,0:T(8,128)(2,1)S(1)}, u32[]{:S(2)}, u32[]{:S(2)}) collective-permute-start(bf16[64,2304]{1,0:T(8,128)(2,1)S(1)} %collective-permute-done.7.refs_1_), channel_id=1, source_target_pairs={{0,2},{2,0},{4,6},{6,4},{8,10},{10,8},{12,14},{14,12},{1,3},{3,1},... | collective-permute-start | bytes 884744 | tf_op jit(solution)/shard_map/ppermute | solution.py:280
  19.8 1.4 %collective-permute-start.9 = (bf16[64,2304]{1,0:T(8,128)(2,1)S(1)}, bf16[64,2304]{1,0:T(8,128)(2,1)S(1)}, u32[]{:S(2)}, u32[]{:S(2)}) collective-permute-start(bf16[64,2304]{1,0:T(8,128)(2,1)S(1)} %collective-permute-done.7.refs_1_), channel_id=1, source_target_pairs={{0,4},{2,6},{4,8},{6,10},{8,12},{10,14},{12,0},{14,2},{1,5},{3,7},... | collective-permute-start | bytes 884744 | tf_op jit(solution)/shard_map/ppermute | solution.py:280
  21.2 3.5 %collective-permute-done.1.refs_1_ = bf16[64,2304]{1,0:T(8,128)(2,1)S(1)} collective-permute-done((bf16[64,2304]{1,0:T(8,128)(2,1)S(1)}, bf16[64,2304]{1,0:T(8,128)(2,1)S(1)}, u32[]{:S(2)}, u32[]{:S(2)}) %collective-permute-start.1) | collective-permute-done | bytes 294944 | tf_op jit(solution)/shard_map/ppermute | solution.py:280
  24.7 0.0 collective-permute-done.2.refs_1_
  24.7 1.4 %collective-permute-start.3 = (bf16[64,2304]{1,0:T(8,128)(2,1)S(1)}, bf16[64,2304]{1,0:T(8,128)(2,1)S(1)}, u32[]{:S(2)}, u32[]{:S(2)}) collective-permute-start(bf16[64,2304]{1,0:T(8,128)(2,1)S(1)} %collective-permute-done.1.refs_1_), channel_id=1, source_target_pairs={{0,4},{2,6},{4,8},{6,10},{8,12},{10,14},{12,0},{14,2},{1,5},{3,7},... | collective-permute-start | bytes 884744 | tf_op jit(solution)/shard_map/ppermute | solution.py:280
  26.0 1.5 %collective-permute-start.4 = (bf16[64,2304]{1,0:T(8,128)(2,1)S(1)}, bf16[64,2304]{1,0:T(8,128)(2,1)S(1)}, u32[]{:S(2)}, u32[]{:S(2)}) collective-permute-start(bf16[64,2304]{1,0:T(8,128)(2,1)S(1)} %collective-permute-done.1.refs_1_), channel_id=1, source_target_pairs={{0,2},{2,0},{4,6},{6,4},{8,10},{10,8},{12,14},{14,12},{1,3},{3,1},... | collective-permute-start | bytes 884744 | tf_op jit(solution)/shard_map/ppermute | solution.py:280
  27.6 3.2 %collective-permute-done.10.refs_2_ = bf16[64,2304]{1,0:T(8,128)(2,1)S(1)} collective-permute-done((bf16[64,2304]{1,0:T(8,128)(2,1)S(1)}, bf16[64,2304]{1,0:T(8,128)(2,1)S(1)}, u32[]{:S(2)}, u32[]{:S(2)}) %collective-permute-start.10) | collective-permute-done | bytes 294944 | tf_op jit(solution)/shard_map/ppermute | solution.py:280
  30.8 0.8 %collective-permute-done.9.refs_1_ = bf16[64,2304]{1,0:T(8,128)(2,1)S(1)} collective-permute-done((bf16[64,2304]{1,0:T(8,128)(2,1)S(1)}, bf16[64,2304]{1,0:T(8,128)(2,1)S(1)}, u32[]{:S(2)}, u32[]{:S(2)}) %collective-permute-start.9) | collective-permute-done | bytes 294944 | tf_op jit(solution)/shard_map/ppermute | solution.py:280
  31.6 0.8 %collective-permute-start.11 = (bf16[64,2304]{1,0:T(8,128)(2,1)S(1)}, bf16[64,2304]{1,0:T(8,128)(2,1)S(1)}, u32[]{:S(2)}, u32[]{:S(2)}) collective-permute-start(bf16[64,2304]{1,0:T(8,128)(2,1)S(1)} %collective-permute-done.9.refs_1_), channel_id=1, source_target_pairs={{0,4},{2,6},{4,8},{6,10},{8,12},{10,14},{12,0},{14,2},{1,5},{3,7},... | collective-permute-start | bytes 884744 | tf_op jit(solution)/shard_map/ppermute | solution.py:280
  32.4 1.5 %collective-permute-start.12 = (bf16[64,2304]{1,0:T(8,128)(2,1)S(1)}, bf16[64,2304]{1,0:T(8,128)(2,1)S(1)}, u32[]{:S(2)}, u32[]{:S(2)}) collective-permute-start(bf16[64,2304]{1,0:T(8,128)(2,1)S(1)} %collective-permute-done.9.refs_1_), channel_id=1, source_target_pairs={{0,2},{2,0},{4,6},{6,4},{8,10},{10,8},{12,14},{14,12},{1,3},{3,1},... | collective-permute-start | bytes 884744 | tf_op jit(solution)/shard_map/ppermute | solution.py:280
  33.9 4.0 %collective-permute-done.3.refs_1_ = bf16[64,2304]{1,0:T(8,128)(2,1)S(1)} collective-permute-done((bf16[64,2304]{1,0:T(8,128)(2,1)S(1)}, bf16[64,2304]{1,0:T(8,128)(2,1)S(1)}, u32[]{:S(2)}, u32[]{:S(2)}) %collective-permute-start.3) | collective-permute-done | bytes 294944 | tf_op jit(solution)/shard_map/ppermute | solution.py:280
  37.9 0.0 collective-permute-done.4.refs_2_
  37.9 0.8 %collective-permute-start.5 = (bf16[64,2304]{1,0:T(8,128)(2,1)S(1)}, bf16[64,2304]{1,0:T(8,128)(2,1)S(1)}, u32[]{:S(2)}, u32[]{:S(2)}) collective-permute-start(bf16[64,2304]{1,0:T(8,128)(2,1)S(1)} %collective-permute-done.3.refs_1_), channel_id=1, source_target_pairs={{0,4},{2,6},{4,8},{6,10},{8,12},{10,14},{12,0},{14,2},{1,5},{3,7},... | collective-permute-start | bytes 884744 | tf_op jit(solution)/shard_map/ppermute | solution.py:280
  38.7 1.5 %collective-permute-start.6 = (bf16[64,2304]{1,0:T(8,128)(2,1)S(1)}, bf16[64,2304]{1,0:T(8,128)(2,1)S(1)}, u32[]{:S(2)}, u32[]{:S(2)}) collective-permute-start(bf16[64,2304]{1,0:T(8,128)(2,1)S(1)} %collective-permute-done.3.refs_1_), channel_id=1, source_target_pairs={{0,2},{2,0},{4,6},{6,4},{8,10},{10,8},{12,14},{14,12},{1,3},{3,1},... | collective-permute-start | bytes 884744 | tf_op jit(solution)/shard_map/ppermute | solution.py:280
  40.3 4.0 %collective-permute-done.11.refs_2_ = bf16[64,2304]{1,0:T(8,128)(2,1)S(1)} collective-permute-done((bf16[64,2304]{1,0:T(8,128)(2,1)S(1)}, bf16[64,2304]{1,0:T(8,128)(2,1)S(1)}, u32[]{:S(2)}, u32[]{:S(2)}) %collective-permute-start.11) | collective-permute-done | bytes 294944 | tf_op jit(solution)/shard_map/ppermute | solution.py:280
  44.2 0.0 collective-permute-done.12.refs_2_
  44.2 4.3 %collective-permute-done.5.refs_0_ = bf16[64,2304]{1,0:T(8,128)(2,1)S(1)} collective-permute-done((bf16[64,2304]{1,0:T(8,128)(2,1)S(1)}, bf16[64,2304]{1,0:T(8,128)(2,1)S(1)}, u32[]{:S(2)}, u32[]{:S(2)}) %collective-permute-start.5) | collective-permute-done | bytes 294944 | tf_op jit(solution)/shard_map/ppermute | solution.py:280
  48.5 0.0 collective-permute-done.6.refs_2_
  48.5 1.5 %collective-permute-start.17 = (bf16[64,2304]{1,0:T(8,128)(2,1)S(1)}, bf16[64,2304]{1,0:T(8,128)(2,1)S(1)}, u32[]{:S(2)}, u32[]{:S(2)}) collective-permute-start(bf16[64,2304]{1,0:T(8,128)(2,1)S(1)} %collective-permute-done.11.refs_2_), channel_id=1, source_target_pairs={{0,2},{2,0},{4,6},{6,4},{8,10},{10,8},{12,14},{14,12},{1,3},{3,1},... | collective-permute-start | bytes 884744 | tf_op jit(solution)/shard_map/ppermute | solution.py:280
  50.0 0.5 collective-permute-start.16
  50.7 1.1 %score.4 = (f32[6,32,256]{2,1,0:T(8,128)S(1)}, f32[6,32,256]{2,1,0:T(8,128)S(1)}) custom-call(s32[1]{0:T(128)} %bitcast.1.half_ref, bf16[384,2304]{1,0:T(8,128)(2,1)S(1)} %stash.8.refs_0_, bf16[384,2304]{1,0:T(8,128)(2,1)S(1)} %stash.11.refs_1_, bf16[256,4608]{1,0:T(8,128)(2,1)S(1)} %scale_codes.3.refs_2_.refs_5_), custom_call_target="tpu_custom_call" | custom-call | flops 905969664 | bytes 2359296 | tf_op jit(solution)/shard_map/score/pallas_call | solution.py:216
  51.8 0.1 collective-permute-start.15
  51.9 0.0 collective-permute-done.refs_2_.refs_4_
  51.9 0.9 %score.3 = (f32[6,32,256]{2,1,0:T(8,128)S(1)}, f32[6,32,256]{2,1,0:T(8,128)S(1)}) custom-call(s32[1]{0:T(128)} %bitcast.1.half_ref, bf16[384,2304]{1,0:T(8,128)(2,1)S(1)} %stash.8.refs_0_, bf16[384,2304]{1,0:T(8,128)(2,1)S(1)} %stash.11.refs_1_, bf16[256,3584]{1,0:T(8,128)(2,1)S(1)} %collective-permute-done.refs_2_.refs_4_), custom_call_target="tpu_custom_call" | custom-call | flops 704643072 | bytes 1835008 | tf_op jit(solution)/shard_map/score/pallas_call | solution.py:216
  52.8 0.0 copy-start
  52.8 0.7 collective-permute-start.13
  53.5 1.5 %collective-permute-start.14 = (f32[6,32,256]{2,1,0:T(8,128)S(1)}, f32[6,32,256]{2,1,0:T(8,128)S(1)}, u32[]{:S(2)}, u32[]{:S(2)}) collective-permute-start(f32[6,32,256]{2,1,0:T(8,128)S(1)} %get-tuple-element.72), channel_id=1, source_target_pairs={{0,16},{16,0},{1,17},{17,1},{2,18},{18,2},{3,19},{19,3},{4,20},{20... | collective-permute-start | bytes 589832 | tf_op jit(solution)/shard_map/ppermute | solution.py:319
  55.0 3.5 %collective-permute-done.17.refs_3_ = bf16[64,2304]{1,0:T(8,128)(2,1)S(1)} collective-permute-done((bf16[64,2304]{1,0:T(8,128)(2,1)S(1)}, bf16[64,2304]{1,0:T(8,128)(2,1)S(1)}, u32[]{:S(2)}, u32[]{:S(2)}) %collective-permute-start.17) | collective-permute-done | bytes 294944 | tf_op jit(solution)/shard_map/ppermute | solution.py:280
  58.5 3.7 %collective-permute-done.16.refs_1_ = bf16[64,2304]{1,0:T(8,128)(2,1)S(1)} collective-permute-done((bf16[64,2304]{1,0:T(8,128)(2,1)S(1)}, bf16[64,2304]{1,0:T(8,128)(2,1)S(1)}, u32[]{:S(2)}, u32[]{:S(2)}) %collective-permute-start.16) | collective-permute-done | bytes 294944 | tf_op jit(solution)/shard_map/ppermute | solution.py:280
  62.2 1.5 %score.5 = (f32[2,32,256]{2,1,0:T(8,128)S(1)}, f32[2,32,256]{2,1,0:T(8,128)S(1)}, f32[2,32,256]{2,1,0:T(8,128)S(1)}, f32[2,32,256]{2,1,0:T(8,128)S(1)}) custom-call(s32[1]{0:T(128)} %bitcast.1.half_ref, bf16[64,2304]{1,0:T(8,128)(2,1)S(1)} %collective-permute-done.5.refs_0_, bf16[64,2304]{1,0:T(8,128)(2,1)S(1)} %collective-permute-done.16.refs_1_, ...), custom_call_target="tpu_custom_call" | custom-call | flops 536870912 | bytes 1835008 | tf_op jit(solution)/shard_map/score/pallas_call | solution.py:216
  63.7 0.1 collective-permute-start.18
  63.8 0.6 collective-permute-start.19
  64.4 0.0 collective-permute-done.15
  64.4 1.3 %collective-permute-start.20 = (f32[2,32,256]{2,1,0:T(8,128)S(1)}, f32[2,32,256]{2,1,0:T(8,128)S(1)}, u32[]{:S(2)}, u32[]{:S(2)}) collective-permute-start(f32[2,32,256]{2,1,0:T(8,128)S(1)} %get-tuple-element.81), channel_id=1, source_target_pairs={{0,1},{1,0},{2,3},{3,2},{4,5},{5,4},{6,7},{7,6},{8,9},{9,8},{10,11... | collective-permute-start | bytes 196616 | tf_op jit(solution)/shard_map/ppermute | solution.py:320
  65.6 1.9 %collective-permute-done.18 = f32[2,32,256]{2,1,0:T(8,128)S(1)} collective-permute-done((f32[2,32,256]{2,1,0:T(8,128)S(1)}, f32[2,32,256]{2,1,0:T(8,128)S(1)}, u32[]{:S(2)}, u32[]{:S(2)}) %collective-permute-start.18) | collective-permute-done | bytes 65568 | tf_op jit(solution)/shard_map/ppermute | solution.py:318
  67.6 1.2 %collective-permute-done.19 = f32[2,32,256]{2,1,0:T(8,128)S(1)} collective-permute-done((f32[2,32,256]{2,1,0:T(8,128)S(1)}, f32[2,32,256]{2,1,0:T(8,128)S(1)}, u32[]{:S(2)}, u32[]{:S(2)}) %collective-permute-start.19) | collective-permute-done | bytes 65568 | tf_op jit(solution)/shard_map/ppermute | solution.py:319
  68.8 0.0 collective-permute-done.20
  68.8 0.0 collective-permute-done.13
  68.8 0.0 collective-permute-done.14
  68.8 0.0 copy-done
  68.8 1.9 %place_scores.1 = f32[8,32,256]{2,1,0:T(8,128)} custom-call(s32[8]{0:T(128)S(1)} %stack.35.order_ref, s32[1,256]{1,0:T(1,128)S(1)} %copy-done, f32[192,256]{1,0:T(8,128)S(1)} %bitcast.21, f32[192,256]{1,0:T(8,128)S(1)} %bitcast.22, f32[192,256]{1,0:T(8,128)S(1)} %bitcast.20, f32[192,256]{1,0:T(8,128)S(1)} %bitcast.19, f32[64,256]{1,0:T(8,128)S(1)} %bitcast.24, ...), custom_call_target="tpu_custom_call" | custom-call | tf_op jit(solution)/shard_map/place_scores/pallas_call | solution.py:247
  (6 shorter events, 0.2 us)
Async XLA Ops:
  2.4 49.4 %collective-permute-start = (bf16[256,3584]{1,0:T(8,128)(2,1)S(1)}, bf16[256,3584]{1,0:T(8,128)(2,1)S(1)}, u32[]{:S(2)}, u32[]{:S(2)}) collective-permute-start(bf16[256,3584]{1,0:T(8,128)(2,1)S(1)} %scale_codes.2), channel_id=1, source_target_pairs={{0,16},{16,0},{1,17},{17,1},{2,18},{18,2},{3,19},{19,3},{4,20},{20... | collective-permute-start | bytes 5505032 | tf_op jit(solution)/shard_map/ppermute | solution.py:291
  6.6 11.8 %collective-permute-start.7 = (bf16[64,2304]{1,0:T(8,128)(2,1)S(1)}, bf16[64,2304]{1,0:T(8,128)(2,1)S(1)}, u32[]{:S(2)}, u32[]{:S(2)}) collective-permute-start(bf16[64,2304]{1,0:T(8,128)(2,1)S(1)} %get-tuple-element.60.refs_0_), channel_id=1, source_target_pairs={{0,4},{2,6},{4,8},{6,10},{8,12},{10,14},{12,0},{14,2},{1,5},{3,7},... | collective-permute-start | bytes 884744 | tf_op jit(solution)/shard_map/ppermute | solution.py:280
  8.2 10.2 %collective-permute-start.8 = (bf16[64,2304]{1,0:T(8,128)(2,1)S(1)}, bf16[64,2304]{1,0:T(8,128)(2,1)S(1)}, u32[]{:S(2)}, u32[]{:S(2)}) collective-permute-start(bf16[64,2304]{1,0:T(8,128)(2,1)S(1)} %get-tuple-element.60.refs_0_), channel_id=1, source_target_pairs={{0,2},{2,0},{4,6},{6,4},{8,10},{10,8},{12,14},{14,12},{1,3},{3,1},... | collective-permute-start | bytes 884744 | tf_op jit(solution)/shard_map/ppermute | solution.py:280
  9.7 15.0 %collective-permute-start.1 = (bf16[64,2304]{1,0:T(8,128)(2,1)S(1)}, bf16[64,2304]{1,0:T(8,128)(2,1)S(1)}, u32[]{:S(2)}, u32[]{:S(2)}) collective-permute-start(bf16[64,2304]{1,0:T(8,128)(2,1)S(1)} %get-tuple-element.49.refs_0_), channel_id=1, source_target_pairs={{0,4},{2,6},{4,8},{6,10},{8,12},{10,14},{12,0},{14,2},{1,5},{3,7},... | collective-permute-start | bytes 884744 | tf_op jit(solution)/shard_map/ppermute | solution.py:280
  11.3 13.4 %collective-permute-start.2 = (bf16[64,2304]{1,0:T(8,128)(2,1)S(1)}, bf16[64,2304]{1,0:T(8,128)(2,1)S(1)}, u32[]{:S(2)}, u32[]{:S(2)}) collective-permute-start(bf16[64,2304]{1,0:T(8,128)(2,1)S(1)} %get-tuple-element.49.refs_0_), channel_id=1, source_target_pairs={{0,2},{2,0},{4,6},{6,4},{8,10},{10,8},{12,14},{14,12},{1,3},{3,1},... | collective-permute-start | bytes 884744 | tf_op jit(solution)/shard_map/ppermute | solution.py:280
  18.3 12.4 %collective-permute-start.10 = (bf16[64,2304]{1,0:T(8,128)(2,1)S(1)}, bf16[64,2304]{1,0:T(8,128)(2,1)S(1)}, u32[]{:S(2)}, u32[]{:S(2)}) collective-permute-start(bf16[64,2304]{1,0:T(8,128)(2,1)S(1)} %collective-permute-done.7.refs_1_), channel_id=1, source_target_pairs={{0,2},{2,0},{4,6},{6,4},{8,10},{10,8},{12,14},{14,12},{1,3},{3,1},... | collective-permute-start | bytes 884744 | tf_op jit(solution)/shard_map/ppermute | solution.py:280
  19.8 11.7 %collective-permute-start.9 = (bf16[64,2304]{1,0:T(8,128)(2,1)S(1)}, bf16[64,2304]{1,0:T(8,128)(2,1)S(1)}, u32[]{:S(2)}, u32[]{:S(2)}) collective-permute-start(bf16[64,2304]{1,0:T(8,128)(2,1)S(1)} %collective-permute-done.7.refs_1_), channel_id=1, source_target_pairs={{0,4},{2,6},{4,8},{6,10},{8,12},{10,14},{12,0},{14,2},{1,5},{3,7},... | collective-permute-start | bytes 884744 | tf_op jit(solution)/shard_map/ppermute | solution.py:280
  24.7 13.2 %collective-permute-start.3 = (bf16[64,2304]{1,0:T(8,128)(2,1)S(1)}, bf16[64,2304]{1,0:T(8,128)(2,1)S(1)}, u32[]{:S(2)}, u32[]{:S(2)}) collective-permute-start(bf16[64,2304]{1,0:T(8,128)(2,1)S(1)} %collective-permute-done.1.refs_1_), channel_id=1, source_target_pairs={{0,4},{2,6},{4,8},{6,10},{8,12},{10,14},{12,0},{14,2},{1,5},{3,7},... | collective-permute-start | bytes 884744 | tf_op jit(solution)/shard_map/ppermute | solution.py:280
  26.0 11.9 %collective-permute-start.4 = (bf16[64,2304]{1,0:T(8,128)(2,1)S(1)}, bf16[64,2304]{1,0:T(8,128)(2,1)S(1)}, u32[]{:S(2)}, u32[]{:S(2)}) collective-permute-start(bf16[64,2304]{1,0:T(8,128)(2,1)S(1)} %collective-permute-done.1.refs_1_), channel_id=1, source_target_pairs={{0,2},{2,0},{4,6},{6,4},{8,10},{10,8},{12,14},{14,12},{1,3},{3,1},... | collective-permute-start | bytes 884744 | tf_op jit(solution)/shard_map/ppermute | solution.py:280
  31.6 12.6 %collective-permute-start.11 = (bf16[64,2304]{1,0:T(8,128)(2,1)S(1)}, bf16[64,2304]{1,0:T(8,128)(2,1)S(1)}, u32[]{:S(2)}, u32[]{:S(2)}) collective-permute-start(bf16[64,2304]{1,0:T(8,128)(2,1)S(1)} %collective-permute-done.9.refs_1_), channel_id=1, source_target_pairs={{0,4},{2,6},{4,8},{6,10},{8,12},{10,14},{12,0},{14,2},{1,5},{3,7},... | collective-permute-start | bytes 884744 | tf_op jit(solution)/shard_map/ppermute | solution.py:280
  32.4 11.9 %collective-permute-start.12 = (bf16[64,2304]{1,0:T(8,128)(2,1)S(1)}, bf16[64,2304]{1,0:T(8,128)(2,1)S(1)}, u32[]{:S(2)}, u32[]{:S(2)}) collective-permute-start(bf16[64,2304]{1,0:T(8,128)(2,1)S(1)} %collective-permute-done.9.refs_1_), channel_id=1, source_target_pairs={{0,2},{2,0},{4,6},{6,4},{8,10},{10,8},{12,14},{14,12},{1,3},{3,1},... | collective-permute-start | bytes 884744 | tf_op jit(solution)/shard_map/ppermute | solution.py:280
  37.9 10.6 %collective-permute-start.5 = (bf16[64,2304]{1,0:T(8,128)(2,1)S(1)}, bf16[64,2304]{1,0:T(8,128)(2,1)S(1)}, u32[]{:S(2)}, u32[]{:S(2)}) collective-permute-start(bf16[64,2304]{1,0:T(8,128)(2,1)S(1)} %collective-permute-done.3.refs_1_), channel_id=1, source_target_pairs={{0,4},{2,6},{4,8},{6,10},{8,12},{10,14},{12,0},{14,2},{1,5},{3,7},... | collective-permute-start | bytes 884744 | tf_op jit(solution)/shard_map/ppermute | solution.py:280
  38.7 9.9 %collective-permute-start.6 = (bf16[64,2304]{1,0:T(8,128)(2,1)S(1)}, bf16[64,2304]{1,0:T(8,128)(2,1)S(1)}, u32[]{:S(2)}, u32[]{:S(2)}) collective-permute-start(bf16[64,2304]{1,0:T(8,128)(2,1)S(1)} %collective-permute-done.3.refs_1_), channel_id=1, source_target_pairs={{0,2},{2,0},{4,6},{6,4},{8,10},{10,8},{12,14},{14,12},{1,3},{3,1},... | collective-permute-start | bytes 884744 | tf_op jit(solution)/shard_map/ppermute | solution.py:280
  48.5 9.9 %collective-permute-start.17 = (bf16[64,2304]{1,0:T(8,128)(2,1)S(1)}, bf16[64,2304]{1,0:T(8,128)(2,1)S(1)}, u32[]{:S(2)}, u32[]{:S(2)}) collective-permute-start(bf16[64,2304]{1,0:T(8,128)(2,1)S(1)} %collective-permute-done.11.refs_2_), channel_id=1, source_target_pairs={{0,2},{2,0},{4,6},{6,4},{8,10},{10,8},{12,14},{14,12},{1,3},{3,1},... | collective-permute-start | bytes 884744 | tf_op jit(solution)/shard_map/ppermute | solution.py:280
  50.0 12.2 %collective-permute-start.16 = (bf16[64,2304]{1,0:T(8,128)(2,1)S(1)}, bf16[64,2304]{1,0:T(8,128)(2,1)S(1)}, u32[]{:S(2)}, u32[]{:S(2)}) collective-permute-start(bf16[64,2304]{1,0:T(8,128)(2,1)S(1)} %collective-permute-done.5.refs_0_), channel_id=1, source_target_pairs={{0,2},{2,0},{4,6},{6,4},{8,10},{10,8},{12,14},{14,12},{1,3},{3,1},... | collective-permute-start | bytes 884744 | tf_op jit(solution)/shard_map/ppermute | solution.py:280
  51.8 12.6 %collective-permute-start.15 = (f32[6,32,256]{2,1,0:T(8,128)S(1)}, f32[6,32,256]{2,1,0:T(8,128)S(1)}, u32[]{:S(2)}, u32[]{:S(2)}) collective-permute-start(f32[6,32,256]{2,1,0:T(8,128)S(1)} %get-tuple-element.74), channel_id=1, source_target_pairs={{0,1},{1,0},{2,3},{3,2},{4,5},{5,4},{6,7},{7,6},{8,9},{9,8},{10,11... | collective-permute-start | bytes 589832 | tf_op jit(solution)/shard_map/ppermute | solution.py:320
  52.8 16.0 %copy-start = (s32[1,256]{1,0:T(1,128)S(1)}, s32[1,256]{1,0:T(1,128)}, u32[]{:S(2)}) copy-start(s32[1,256]{1,0:T(1,128)} %ids_ref.1) | copy-start | bytes 3076
  52.8 16.0 %collective-permute-start.13 = (f32[6,32,256]{2,1,0:T(8,128)S(1)}, f32[6,32,256]{2,1,0:T(8,128)S(1)}, u32[]{:S(2)}, u32[]{:S(2)}) collective-permute-start(f32[6,32,256]{2,1,0:T(8,128)S(1)} %get-tuple-element.71), channel_id=1, source_target_pairs={{0,17},{1,16},{16,1},{17,0},{2,19},{3,18},{18,3},{19,2},{4,21},{5,... | collective-permute-start | bytes 589832 | tf_op jit(solution)/shard_map/ppermute | solution.py:318
  53.5 15.3 %collective-permute-start.14 = (f32[6,32,256]{2,1,0:T(8,128)S(1)}, f32[6,32,256]{2,1,0:T(8,128)S(1)}, u32[]{:S(2)}, u32[]{:S(2)}) collective-permute-start(f32[6,32,256]{2,1,0:T(8,128)S(1)} %get-tuple-element.72), channel_id=1, source_target_pairs={{0,16},{16,0},{1,17},{17,1},{2,18},{18,2},{3,19},{19,3},{4,20},{20... | collective-permute-start | bytes 589832 | tf_op jit(solution)/shard_map/ppermute | solution.py:319
  63.7 3.8 %collective-permute-start.18 = (f32[2,32,256]{2,1,0:T(8,128)S(1)}, f32[2,32,256]{2,1,0:T(8,128)S(1)}, u32[]{:S(2)}, u32[]{:S(2)}) collective-permute-start(f32[2,32,256]{2,1,0:T(8,128)S(1)} %get-tuple-element.79), channel_id=1, source_target_pairs={{0,17},{1,16},{16,1},{17,0},{2,19},{3,18},{18,3},{19,2},{4,21},{5,... | collective-permute-start | bytes 196616 | tf_op jit(solution)/shard_map/ppermute | solution.py:318
  63.8 5.0 %collective-permute-start.19 = (f32[2,32,256]{2,1,0:T(8,128)S(1)}, f32[2,32,256]{2,1,0:T(8,128)S(1)}, u32[]{:S(2)}, u32[]{:S(2)}) collective-permute-start(f32[2,32,256]{2,1,0:T(8,128)S(1)} %get-tuple-element.80), channel_id=1, source_target_pairs={{0,16},{16,0},{1,17},{17,1},{2,18},{18,2},{3,19},{19,3},{4,20},{20... | collective-permute-start | bytes 196616 | tf_op jit(solution)/shard_map/ppermute | solution.py:319
  64.4 4.4 %collective-permute-start.20 = (f32[2,32,256]{2,1,0:T(8,128)S(1)}, f32[2,32,256]{2,1,0:T(8,128)S(1)}, u32[]{:S(2)}, u32[]{:S(2)}) collective-permute-start(f32[2,32,256]{2,1,0:T(8,128)S(1)} %get-tuple-element.81), channel_id=1, source_target_pairs={{0,1},{1,0},{2,3},{3,2},{4,5},{5,4},{6,7},{7,6},{8,9},{9,8},{10,11... | collective-permute-start | bytes 196616 | tf_op jit(solution)/shard_map/ppermute | solution.py:320

commit v7 on v6

--- a/solution.py
+++ b/solution.py
@@ -8,7 +8,7 @@
 from jax.sharding import PartitionSpec as P
 
 BLOCK = 128
-ALONE = 28
+ALONE = 30
 CHUNKS = 2
 VMEM = pl.BlockSpec(memory_space=pltpu.VMEM)
 SMEM = pl.BlockSpec(memory_space=pltpu.SMEM)
@@ -188,9 +188,8 @@
         send_ref[j] = jnp.where(half == 0, high, low)
 
 
-def product(pieces, grads_ref):
+def product(pieces, grads_ref, first):
     total = None
-    first = 0
     for refs in pieces:
         width = min(refs[0].shape[1], grads_ref.shape[1] - first)
         if width <= 0:
@@ -201,57 +200,81 @@
     return total
 
 
-def score_kernel(counts, grads_given, rows, half_ref, *refs):
+def score_kernel(counts, grads_given, first, rows, begun, half_ref, *refs):
     refs = list(refs)
     pieces = [[refs.pop(0) for _ in range(arrays)] for arrays in counts]
     grad_refs, outs = refs[:grads_given], refs[grads_given:]
+    base_refs, outs = (outs[:grads_given], outs[grads_given:]) if begun else (None, outs)
     for i, grads_ref in enumerate(grad_refs):
-        halves(half_ref[0], product(pieces, grads_ref), rows, *outs[2 * i : 2 * i + 2])
-
-
-def score(half, rows, pieces, grads):
-    operands = [array for arrays in pieces for array in arrays]
+        total = product(pieces, grads_ref, first)
+        if begun:
+            total = total + base_refs[i][...]
+        if rows:
+            halves(half_ref[0], total, rows, *outs[2 * i : 2 * i + 2])
+        else:
+            outs[i][...] = total
+
+
+def score(half, rows, pieces, grads, first=0, base=()):
+    operands = [array for arrays in pieces for array in arrays] + list(grads) + list(base)
     height = sum(array.shape[0] for array in pieces[0])
-    shape = pltpu.VMEM((height // rows, rows // 2, grads[0].shape[0]), jnp.float32)
-    return pl.pallas_call(
-        functools.partial(score_kernel, [len(arrays) for arrays in pieces], len(grads), rows),
-        out_shape=[shape] * (2 * len(grads)),
-        in_specs=[SMEM] + [VMEM] * (len(operands) + len(grads)),
-        out_specs=[VMEM] * (2 * len(grads)),
+    count = grads[0].shape[0]
+    if rows:
+        shapes = [pltpu.VMEM((height // rows, rows // 2, count), jnp.float32)] * (2 * len(grads))
+    else:
+        shapes = [pltpu.VMEM((height, count), jnp.float32)] * len(grads)
+    return pl.pallas_call(
+        functools.partial(score_kernel, [len(arrays) for arrays in pieces], len(grads), first, rows, bool(base)),
+        out_shape=shapes,
+        in_specs=[SMEM] + [VMEM] * len(operands),
+        out_specs=[VMEM] * len(shapes),
         compiler_params=pltpu.CompilerParams(vmem_limit_bytes=16 << 20),
         cost_estimate=pl.CostEstimate(
             flops=2 * height * sum(g.size for g in grads), bytes_accessed=2 * grads[0].size, transcendentals=0
         ),
         name="score",
-    )(half, *in_vmem([*operands, *grads]))
-
-
-def place_kernel(rows, order_ref, ids_ref, *refs):
-    *share_refs, out_ref = refs
+    )(half, *in_vmem(operands))
+
+
+def place_kernel(rows, first, order_ref, ids_ref, *refs):
+    *share_refs, out_ref, placed_ref, sems = refs
+    share_refs = share_refs[1:] if first else share_refs
     count = ids_ref.shape[1]
     slots = lax.broadcasted_iota(jnp.int32, (count, count), 0)
     table = (slots == jnp.broadcast_to(ids_ref[...], (count, count))).astype(jnp.float32)
-    j = 0
-    for first in range(0, len(share_refs), 4):
-        a, b, c, d = (ref[...] for ref in share_refs[first : first + 4])
+    copies = []
+    for at in range(0, len(share_refs), 4):
+        a, b, c, d = (ref[...] for ref in share_refs[at : at + 4])
         raw = (d + c) + (b + a)
         placed = lax.dot_general(
             raw, table, NT, precision=lax.Precision.HIGHEST, preferred_element_type=jnp.float32
         )
         for i in range(raw.shape[0] // rows):
-            out_ref[order_ref[j]] = placed[i * rows : (i + 1) * rows]
-            j += 1
-
-
-def place(order, ids, shares, rows):
-    return pl.pallas_call(
-        functools.partial(place_kernel, rows),
-        out_shape=jax.ShapeDtypeStruct((order.shape[0], rows, ids.shape[1]), jnp.float32),
-        in_specs=[SMEM] + [VMEM] * (len(shares) + 1),
-        out_specs=VMEM,
+            j = len(copies)
+            placed_ref[j] = placed[i * rows : (i + 1) * rows]
+            copies.append(
+                pltpu.make_async_copy(placed_ref.at[j], out_ref.at[order_ref[first + j]], sems.at[j])
+            )
+            copies[-1].start()
+    for copy in copies:
+        copy.wait()
+
+
+def place(order, ids, out, first, shares, rows):
+    count = ids.shape[1]
+    blocks = sum(share.shape[0] for share in shares[::4]) // rows
+    anywhere = pl.BlockSpec(memory_space=pl.ANY)
+    given = [in_hbm(out)] if first else []
+    return pl.pallas_call(
+        functools.partial(place_kernel, rows, first),
+        out_shape=pltpu.HBM((order.shape[0], rows, count), jnp.float32),
+        in_specs=[SMEM, VMEM] + [anywhere] * len(given) + [VMEM] * len(shares),
+        out_specs=anywhere,
+        input_output_aliases={2: 0} if given else {},
+        scratch_shapes=[pltpu.VMEM((blocks, rows, count), jnp.float32), pltpu.SemaphoreType.DMA((blocks,))],
         compiler_params=pltpu.CompilerParams(vmem_limit_bytes=16 << 20),
         name="place_scores",
-    )(order, ids, *in_vmem(shares))
+    )(order, ids, *given, *in_vmem(shares))
 
 
 def shards(fast, parts, total, queries, codes, exponents, example_ids):
@@ -294,23 +317,30 @@
     def stack(arrays):
         return arrays if rows % 16 == 0 else [jnp.concatenate(arrays, axis=0)]
 
-    early_rows = (slow - 1) * fast * rows
-    early, late = [], []
+    first_steps = max(slow - 2, 1)
+    early_rows = first_steps * fast * rows
+    early, middle, late = [], [], []
     for c, chunk in enumerate(chunks):
-        held = []
-        for s in range(slow):
-            values = along_fast(chunk)
-            if s == slow - 1:
-                late.append(stack(values))
-                break
-            tied = [step(chunk, slow, fast), *values] + held
+        held, between = [], []
+        for s in range(slow - 1):
+            tied = [step(chunk, slow, fast), *along_fast(chunk)] + held
             if c == CHUNKS - 1 and s == 0:
                 *tied, ours = lax.optimization_barrier(tied + [ours])
+            elif c == CHUNKS - 1 and s == slow - 2:
+                their_early = list(score(half, rows, early + [held], [theirs]))
+                *tied, keep, send = lax.optimization_barrier(tied + their_early)
+                their_early = [keep, send]
             else:
                 tied = lax.optimization_barrier(tied)
             chunk, values, held = tied[0], tied[1 : fast + 1], tied[fast + 1 :]
-            held = [stash(held[0] if s else None, stack(values), s * fast * rows, early_rows)]
-        early += held
+            if s < first_steps:
+                held = [stash(held[0] if s else None, stack(values), s * fast * rows, early_rows)]
+            else:
+                between += values
+        early.append(held)
+        middle.append(stack(between + [chunk]))
+        along = along_fast(chunk)[1:] if c < CHUNKS - 1 else [step(value, slow, fast) for value in values[1:]]
+        late.append(stack(along))
 
     def shares_of(their_keep, their_send, keep, send):
         across = [(i, 3 - i) for i in range(4)]
@@ -322,12 +352,13 @@
         ]
         return [share.reshape(-1, count) for share in shares]
 
-    early = [[held] for held in early]
-    their_early = score(half, rows, early, [theirs])
-    theirs, *their_early = lax.optimization_barrier((theirs, *their_early))
     shares = shares_of(*their_early, *score(half, rows, early, [ours]))
-    shares += shares_of(*score(half, rows, late, [theirs, ours]))
-    return place(order, example_ids, shares, rows // 2)
+    out = place(order, example_ids, None, 0, shares, rows // 2)
+    shares = shares_of(*score(half, rows, middle, [theirs, ours]))
+    begun = score(half, 0, late[:-1], [theirs, ours])
+    *begun, out = lax.optimization_barrier((*begun, out))
+    shares += shares_of(*score(half, rows, late[-1:], [theirs, ours], cuts[-2], begun))
+    return place(order, example_ids, out, first_steps * fast, shares, rows // 2)
 
 
 def solution(mesh):

time: 70.9 us -> 69.3 us (0.977)
  starting transfers between devices: 24.7 us -> 20.1 us
  Pallas kernels: 11.7 us -> 14 us
    ppermute x14, starting transfers between devices: 17.5 us -> 10.2 us  [step(): return lax.ppermute(value, 'ex', pairs)]
    ppermute x14, waiting for transfers between devices: 30.9 us -> 26.5 us  [step(): return lax.ppermute(value, 'ex', pairs)]
    ppermute x1, waiting for transfers between devices: 0.01 us -> 4.16 us  [shards(): lax.ppermute(scale(part, codes, by_block, alone, True), 'groups', swap)]
    ppermute x2 -> x3, starting transfers between devices: 2.09 us -> 4.9 us  [shares_of(): lax.ppermute(their_keep, 'groups', swap)]
    pallas_call x1 -> x2, Pallas kernels: 1.89 us -> 3.4 us  [place(): pl.pallas_call(functools.partial(place_kernel, rows, first), out_shape=pl...]
    ppermute x2 -> x3, waiting for transfers between devices: 1.21 us -> 2.55 us  [shares_of(): lax.ppermute(their_keep, 'groups', swap)]
    pallas_call x3 -> x5, Pallas kernels: 3.49 us -> 4.46 us  [score(): pl.pallas_call(functools.partial(score_kernel, [len(arrays) for arrays in...]
    ppermute x2 -> x3, starting transfers between devices: 1.35 us -> 0.38 us  [shares_of(): lax.ppermute(send, 'dim', [(0, 1), (1, 0)])]
  transfers between devices with their start and end apart: 21 -> 24, of which waited for: 11 -> 14; matrix products, arithmetic and copies ran while one was open for 0% -> 0% of each run, Pallas kernels for 11% -> 14%
where the time goes in v7:
time: 69.3 us; the launch traced here: 69.1 us
  waiting for transfers between devices  34.7 us (50%)
  starting transfers between devices  20.1 us (29%)
  Pallas kernels  14 us (20%)
    ppermute x14, waiting for transfers between devices, step(): return lax.ppermute(value, 'ex', pairs)  26.5 us
    ppermute x14, starting transfers between devices, step(): return lax.ppermute(value, 'ex', pairs)  10.2 us
    pallas_call x2, Pallas kernels, scale(): pl.pallas_call(functools.partial(scale_kernel, alone, tile, sent), out_sh...  4.95 us
    ppermute x3, starting transfers between devices, shares_of(): lax.ppermute(their_keep, 'groups', swap)  4.9 us
    pallas_call x5, Pallas kernels, score(): pl.pallas_call(functools.partial(score_kernel, [len(arrays) for arrays in...  4.46 us
    ppermute x1, waiting for transfers between devices, shards(): lax.ppermute(scale(part, codes, by_block, alone, True), 'groups', swap)  4.16 us
    pallas_call x2, Pallas kernels, place(): pl.pallas_call(functools.partial(place_kernel, rows, first), out_shape=pl...  3.4 us
    ppermute x1, starting transfers between devices, shards(): lax.ppermute(scale(part, codes, by_block, alone, True), 'groups', swap)  3.03 us
  transfers between devices with their start and end apart: 24, of which 14 were waited for; matrix products, arithmetic and copies ran while one was open for 0% of the time, Pallas kernels for 14%

profile of v7, /device:TPU:0, one launch (start us, length us, event | category | flops | bytes accessed | tf_op | source)
XLA Modules:
  0.0 69.1 jit_solution(1579678066897958310)
XLA Ops:
  0.0 0.1 stack.35.order_ref
  0.1 2.4 %scale_codes.2 = bf16[256,3840]{1,0:T(8,128)(2,1)S(1)} custom-call(s32[1]{0:T(128)} %bitcast.part_ref, bf16[256,8192]{1,0:T(8,128)(2,1)} %codes_ref.3, s32[64,256]{1,0:T(8,128)} %bitcast.35), custom_call_target="tpu_custom_call" | custom-call | flops 2097152 | bytes 8388608 | tf_op jit(solution)/shard_map/scale_codes/pallas_call | solution.py:135
  2.5 3.0 %collective-permute-start.7 = (bf16[256,3840]{1,0:T(8,128)(2,1)S(1)}, bf16[256,3840]{1,0:T(8,128)(2,1)S(1)}, u32[]{:S(2)}, u32[]{:S(2)}) collective-permute-start(bf16[256,3840]{1,0:T(8,128)(2,1)S(1)} %scale_codes.2), channel_id=1, source_target_pairs={{0,16},{16,0},{1,17},{17,1},{2,18},{18,2},{3,19},{19,3},{4,20},{20... | collective-permute-start | bytes 5898248 | tf_op jit(solution)/shard_map/ppermute | solution.py:314
  5.5 1.1 %cut_queries.1 = (bf16[64,2176]{1,0:T(8,128)(2,1)S(1)}, bf16[64,2176]{1,0:T(8,128)(2,1)S(1)}) custom-call(s32[1]{0:T(128)} %bitcast.part_ref, bf16[1,64,8192]{2,1,0:T(8,128)(2,1)} %queries_ref.1), custom_call_target="tpu_custom_call" | custom-call | bytes 1048576 | tf_op jit(solution)/shard_map/cut_queries/pallas_call | solution.py:83
  6.6 1.6 %collective-permute-start.1 = (bf16[64,2176]{1,0:T(8,128)(2,1)S(1)}, bf16[64,2176]{1,0:T(8,128)(2,1)S(1)}, u32[]{:S(2)}, u32[]{:S(2)}) collective-permute-start(bf16[64,2176]{1,0:T(8,128)(2,1)S(1)} %get-tuple-element.57.refs_0_), channel_id=1, source_target_pairs={{0,2},{2,0},{4,6},{6,4},{8,10},{10,8},{12,14},{14,12},{1,3},{3,1},... | collective-permute-start | bytes 835592 | tf_op jit(solution)/shard_map/ppermute | solution.py:303
  8.2 1.6 %collective-permute-start = (bf16[64,2176]{1,0:T(8,128)(2,1)S(1)}, bf16[64,2176]{1,0:T(8,128)(2,1)S(1)}, u32[]{:S(2)}, u32[]{:S(2)}) collective-permute-start(bf16[64,2176]{1,0:T(8,128)(2,1)S(1)} %get-tuple-element.57.refs_0_), channel_id=1, source_target_pairs={{0,4},{2,6},{4,8},{6,10},{8,12},{10,14},{12,0},{14,2},{1,5},{3,7},... | collective-permute-start | bytes 835592 | tf_op jit(solution)/shard_map/ppermute | solution.py:303
  9.7 0.5 collective-permute-start.9
  10.3 1.6 %collective-permute-start.8 = (bf16[64,2176]{1,0:T(8,128)(2,1)S(1)}, bf16[64,2176]{1,0:T(8,128)(2,1)S(1)}, u32[]{:S(2)}, u32[]{:S(2)}) collective-permute-start(bf16[64,2176]{1,0:T(8,128)(2,1)S(1)} %get-tuple-element.69.refs_0_), channel_id=1, source_target_pairs={{0,4},{2,6},{4,8},{6,10},{8,12},{10,14},{12,0},{14,2},{1,5},{3,7},... | collective-permute-start | bytes 835592 | tf_op jit(solution)/shard_map/ppermute | solution.py:303
  11.8 4.4 %collective-permute-done.1.refs_1_ = bf16[64,2176]{1,0:T(8,128)(2,1)S(1)} collective-permute-done((bf16[64,2176]{1,0:T(8,128)(2,1)S(1)}, bf16[64,2176]{1,0:T(8,128)(2,1)S(1)}, u32[]{:S(2)}, u32[]{:S(2)}) %collective-permute-start.1) | collective-permute-done | bytes 278560 | tf_op jit(solution)/shard_map/ppermute | solution.py:303
  16.2 3.3 %collective-permute-done.refs_1_ = bf16[64,2176]{1,0:T(8,128)(2,1)S(1)} collective-permute-done((bf16[64,2176]{1,0:T(8,128)(2,1)S(1)}, bf16[64,2176]{1,0:T(8,128)(2,1)S(1)}, u32[]{:S(2)}, u32[]{:S(2)}) %collective-permute-start) | collective-permute-done | bytes 278560 | tf_op jit(solution)/shard_map/ppermute | solution.py:303
  19.5 0.5 collective-permute-start.3
  20.1 0.0 collective-permute-start.2
  20.1 2.6 %scale_codes.3.refs_2_.refs_7_ = bf16[256,4352]{1,0:T(8,128)(2,1)S(1)} custom-call(s32[1]{0:T(128)} %bitcast.part_ref, bf16[256,8192]{1,0:T(8,128)(2,1)} %codes_ref.3, s32[64,256]{1,0:T(8,128)} %bitcast.36), custom_call_target="tpu_custom_call" | custom-call | flops 2097152 | bytes 8388608 | tf_op jit(solution)/shard_map/scale_codes/pallas_call | solution.py:135
  22.6 0.0 collective-permute-done.9.refs_1_
  22.6 2.9 %collective-permute-done.8.refs_1_ = bf16[64,2176]{1,0:T(8,128)(2,1)S(1)} collective-permute-done((bf16[64,2176]{1,0:T(8,128)(2,1)S(1)}, bf16[64,2176]{1,0:T(8,128)(2,1)S(1)}, u32[]{:S(2)}, u32[]{:S(2)}) %collective-permute-start.8) | collective-permute-done | bytes 278560 | tf_op jit(solution)/shard_map/ppermute | solution.py:303
  25.5 0.5 collective-permute-start.11
  26.0 0.0 collective-permute-start.10
  26.1 2.4 %collective-permute-done.3.refs_2_ = bf16[64,2176]{1,0:T(8,128)(2,1)S(1)} collective-permute-done((bf16[64,2176]{1,0:T(8,128)(2,1)S(1)}, bf16[64,2176]{1,0:T(8,128)(2,1)S(1)}, u32[]{:S(2)}, u32[]{:S(2)}) %collective-permute-start.3) | collective-permute-done | bytes 278560 | tf_op jit(solution)/shard_map/ppermute | solution.py:303
  28.5 2.9 %collective-permute-done.2.refs_0_ = bf16[64,2176]{1,0:T(8,128)(2,1)S(1)} collective-permute-done((bf16[64,2176]{1,0:T(8,128)(2,1)S(1)}, bf16[64,2176]{1,0:T(8,128)(2,1)S(1)}, u32[]{:S(2)}, u32[]{:S(2)}) %collective-permute-start.2) | collective-permute-done | bytes 278560 | tf_op jit(solution)/shard_map/ppermute | solution.py:303
  31.5 0.7 %collective-permute-start.5 = (bf16[64,2176]{1,0:T(8,128)(2,1)S(1)}, bf16[64,2176]{1,0:T(8,128)(2,1)S(1)}, u32[]{:S(2)}, u32[]{:S(2)}) collective-permute-start(bf16[64,2176]{1,0:T(8,128)(2,1)S(1)} %collective-permute-done.2.refs_0_), channel_id=1, source_target_pairs={{0,2},{2,0},{4,6},{6,4},{8,10},{10,8},{12,14},{14,12},{1,3},{3,1},... | collective-permute-start | bytes 835592 | tf_op jit(solution)/shard_map/ppermute | solution.py:303
  32.2 0.0 collective-permute-start.4
  32.3 2.3 %collective-permute-done.11.refs_2_ = bf16[64,2176]{1,0:T(8,128)(2,1)S(1)} collective-permute-done((bf16[64,2176]{1,0:T(8,128)(2,1)S(1)}, bf16[64,2176]{1,0:T(8,128)(2,1)S(1)}, u32[]{:S(2)}, u32[]{:S(2)}) %collective-permute-start.11) | collective-permute-done | bytes 278560 | tf_op jit(solution)/shard_map/ppermute | solution.py:303
  34.5 2.9 %collective-permute-done.10.refs_3_ = bf16[64,2176]{1,0:T(8,128)(2,1)S(1)} collective-permute-done((bf16[64,2176]{1,0:T(8,128)(2,1)S(1)}, bf16[64,2176]{1,0:T(8,128)(2,1)S(1)}, u32[]{:S(2)}, u32[]{:S(2)}) %collective-permute-start.10) | collective-permute-done | bytes 278560 | tf_op jit(solution)/shard_map/ppermute | solution.py:303
  37.4 0.7 %collective-permute-start.13 = (bf16[64,2176]{1,0:T(8,128)(2,1)S(1)}, bf16[64,2176]{1,0:T(8,128)(2,1)S(1)}, u32[]{:S(2)}, u32[]{:S(2)}) collective-permute-start(bf16[64,2176]{1,0:T(8,128)(2,1)S(1)} %collective-permute-done.10.refs_3_), channel_id=1, source_target_pairs={{0,2},{2,0},{4,6},{6,4},{8,10},{10,8},{12,14},{14,12},{1,3},{3,1},... | collective-permute-start | bytes 835592 | tf_op jit(solution)/shard_map/ppermute | solution.py:303
  38.2 0.0 collective-permute-start.12
  38.2 2.3 %collective-permute-done.5.refs_1_ = bf16[64,2176]{1,0:T(8,128)(2,1)S(1)} collective-permute-done((bf16[64,2176]{1,0:T(8,128)(2,1)S(1)}, bf16[64,2176]{1,0:T(8,128)(2,1)S(1)}, u32[]{:S(2)}, u32[]{:S(2)}) %collective-permute-start.5) | collective-permute-done | bytes 278560 | tf_op jit(solution)/shard_map/ppermute | solution.py:303
  40.5 3.1 %collective-permute-done.4.refs_2_ = bf16[64,2176]{1,0:T(8,128)(2,1)S(1)} collective-permute-done((bf16[64,2176]{1,0:T(8,128)(2,1)S(1)}, bf16[64,2176]{1,0:T(8,128)(2,1)S(1)}, u32[]{:S(2)}, u32[]{:S(2)}) %collective-permute-start.4) | collective-permute-done | bytes 278560 | tf_op jit(solution)/shard_map/ppermute | solution.py:303
  43.6 0.5 collective-permute-start.6
  44.2 4.2 %collective-permute-done.7.refs_1_.refs_2_.refs_6_ = bf16[256,3840]{1,0:T(8,128)(2,1)S(1)} collective-permute-done((bf16[256,3840]{1,0:T(8,128)(2,1)S(1)}, bf16[256,3840]{1,0:T(8,128)(2,1)S(1)}, u32[]{:S(2)}, u32[]{:S(2)}) %collective-permute-start.7) | collective-permute-done | bytes 1966112 | tf_op jit(solution)/shard_map/ppermute | solution.py:314
  48.3 0.7 %score.6 = (f32[4,32,256]{2,1,0:T(8,128)S(1)}, f32[4,32,256]{2,1,0:T(8,128)S(1)}) custom-call(s32[1]{0:T(128)} %bitcast.1.half_ref, bf16[256,2176]{1,0:T(8,128)(2,1)S(1)} %stash.5.refs_0_, bf16[256,2176]{1,0:T(8,128)(2,1)S(1)} %stash.7.refs_1_, bf16[256,3840]{1,0:T(8,128)(2,1)S(1)} %collective-permute-done.7.refs_1_.refs_2_.refs_6_), custom_call_target="tpu_custom_call" | custom-call | flops 503316480 | bytes 1966080 | tf_op jit(solution)/shard_map/score/pallas_call | solution.py:226
  49.1 0.0 collective-permute-done.13.refs_4_
  49.1 0.0 collective-permute-done.12.refs_5_
  49.1 1.8 %collective-permute-start.20 = (bf16[64,2176]{1,0:T(8,128)(2,1)S(1)}, bf16[64,2176]{1,0:T(8,128)(2,1)S(1)}, u32[]{:S(2)}, u32[]{:S(2)}) collective-permute-start(bf16[64,2176]{1,0:T(8,128)(2,1)S(1)} %collective-permute-done.13.refs_4_), channel_id=1, source_target_pairs={{0,4},{2,6},{4,8},{6,10},{8,12},{10,14},{12,0},{14,2},{1,5},{3,7},... | collective-permute-start | bytes 835592 | tf_op jit(solution)/shard_map/ppermute | solution.py:303
  50.9 0.0 collective-permute-start.14
  50.9 1.5 %collective-permute-start.15 = (f32[4,32,256]{2,1,0:T(8,128)S(1)}, f32[4,32,256]{2,1,0:T(8,128)S(1)}, u32[]{:S(2)}, u32[]{:S(2)}) collective-permute-start(f32[4,32,256]{2,1,0:T(8,128)S(1)} %get-tuple-element.79), channel_id=1, source_target_pairs={{0,16},{16,0},{1,17},{17,1},{2,18},{18,2},{3,19},{19,3},{4,20},{20... | collective-permute-start | bytes 393224 | tf_op jit(solution)/shard_map/ppermute | solution.py:349
  52.5 0.8 %score.7 = (f32[4,32,256]{2,1,0:T(8,128)S(1)}, f32[4,32,256]{2,1,0:T(8,128)S(1)}) custom-call(s32[1]{0:T(128)} %bitcast.1.half_ref, bf16[256,2176]{1,0:T(8,128)(2,1)S(1)} %stash.5.refs_0_, bf16[256,2176]{1,0:T(8,128)(2,1)S(1)} %stash.7.refs_1_, bf16[256,4352]{1,0:T(8,128)(2,1)S(1)} %scale_codes.3.refs_2_.refs_7_), custom_call_target="tpu_custom_call" | custom-call | flops 570425344 | bytes 2228224 | tf_op jit(solution)/shard_map/score/pallas_call | solution.py:226
  53.3 0.4 collective-permute-start.16
  53.6 1.5 %score.8 = (f32[3,32,256]{2,1,0:T(8,128)S(1)}, f32[3,32,256]{2,1,0:T(8,128)S(1)}, f32[3,32,256]{2,1,0:T(8,128)S(1)}, f32[3,32,256]{2,1,0:T(8,128)S(1)}) custom-call(s32[1]{0:T(128)} %bitcast.1.half_ref, bf16[64,2176]{1,0:T(8,128)(2,1)S(1)} %collective-permute-done.2.refs_0_, bf16[64,2176]{1,0:T(8,128)(2,1)S(1)} %collective-permute-done.5.refs_1_, ...), custom_call_target="tpu_custom_call" | custom-call | flops 805306368 | bytes 1966080 | tf_op jit(solution)/shard_map/score/pallas_call | solution.py:226
  55.1 0.0 collective-permute-done.6.refs_0_
  55.1 1.2 %collective-permute-start.17 = (f32[3,32,256]{2,1,0:T(8,128)S(1)}, f32[3,32,256]{2,1,0:T(8,128)S(1)}, u32[]{:S(2)}, u32[]{:S(2)}) collective-permute-start(f32[3,32,256]{2,1,0:T(8,128)S(1)} %get-tuple-element.89), channel_id=1, source_target_pairs={{0,17},{1,16},{16,1},{17,0},{2,19},{3,18},{18,3},{19,2},{4,21},{5,... | collective-permute-start | bytes 294920 | tf_op jit(solution)/shard_map/ppermute | solution.py:348
  56.4 0.3 collective-permute-done.14
  56.7 1.6 %collective-permute-start.18 = (f32[3,32,256]{2,1,0:T(8,128)S(1)}, f32[3,32,256]{2,1,0:T(8,128)S(1)}, u32[]{:S(2)}, u32[]{:S(2)}) collective-permute-start(f32[3,32,256]{2,1,0:T(8,128)S(1)} %get-tuple-element.90), channel_id=1, source_target_pairs={{0,16},{16,0},{1,17},{17,1},{2,18},{18,2},{3,19},{19,3},{4,20},{20... | collective-permute-start | bytes 294920 | tf_op jit(solution)/shard_map/ppermute | solution.py:349
  58.2 1.4 %collective-permute-done.15 = f32[4,32,256]{2,1,0:T(8,128)S(1)} collective-permute-done((f32[4,32,256]{2,1,0:T(8,128)S(1)}, f32[4,32,256]{2,1,0:T(8,128)S(1)}, u32[]{:S(2)}, u32[]{:S(2)}) %collective-permute-start.15) | collective-permute-done | bytes 131104 | tf_op jit(solution)/shard_map/ppermute | solution.py:349
  59.6 0.0 copy-start
  59.6 0.0 collective-permute-start.19
  59.6 0.8 %score.5 = (f32[64,256]{1,0:T(8,128)S(1)}, f32[64,256]{1,0:T(8,128)S(1)}) custom-call(s32[1]{0:T(128)} %bitcast.1.half_ref, bf16[64,2176]{1,0:T(8,128)(2,1)S(1)} %collective-permute-done.6.refs_0_, bf16[256,3840]{1,0:T(8,128)(2,1)S(1)} %collective-permute-done.7.refs_1_.refs_2_.refs_6_, bf16[256,4352]{1,0:T(8,128)(2,1)S(1)} %scale_codes.3.refs_2_.refs_7_), custom_call_target="tpu_custom_call" | custom-call | flops 268435456 | bytes 1966080 | tf_op jit(solution)/shard_map/score/pallas_call | solution.py:226
  60.4 0.0 collective-permute-done.16
  60.4 0.0 copy-done
  60.4 1.6 %place_scores.2.refs_0_ = f32[8,32,256]{2,1,0:T(8,128)} custom-call(s32[8]{0:T(128)S(1)} %stack.35.order_ref, s32[1,256]{1,0:T(1,128)S(1)} %copy-done, f32[128,256]{1,0:T(8,128)S(1)} %bitcast.23, f32[128,256]{1,0:T(8,128)S(1)} %bitcast.24, f32[128,256]{1,0:T(8,128)S(1)} %bitcast.26, f32[128,256]{1,0:T(8,128)S(1)} %bitcast.25), custom_call_target="tpu_custom_call" | custom-call | tf_op jit(solution)/shard_map/place_scores/pallas_call | solution.py:268
  62.0 0.0 collective-permute-done.20.refs_0_
  62.0 0.7 %score.9 = (f32[1,32,256]{2,1,0:T(8,128)S(1)}, f32[1,32,256]{2,1,0:T(8,128)S(1)}, f32[1,32,256]{2,1,0:T(8,128)S(1)}, f32[1,32,256]{2,1,0:T(8,128)S(1)}) custom-call(s32[1]{0:T(128)} %bitcast.1.half_ref, bf16[64,2176]{1,0:T(8,128)(2,1)S(1)} %collective-permute-done.20.refs_0_, bf16[256,3840]{1,0:T(8,128)(2,1)S(1)} %collective-permute-done.7.refs_1_.refs_2_.refs_6_, ...), custom_call_target="tpu_custom_call" | custom-call | flops 268435456 | bytes 1966080 | tf_op jit(solution)/shard_map/score/pallas_call | solution.py:226
  62.8 0.4 collective-permute-start.21
  63.2 1.8 %collective-permute-start.22 = (f32[1,32,256]{2,1,0:T(8,128)S(1)}, f32[1,32,256]{2,1,0:T(8,128)S(1)}, u32[]{:S(2)}, u32[]{:S(2)}) collective-permute-start(f32[1,32,256]{2,1,0:T(8,128)S(1)} %get-tuple-element.96), channel_id=1, source_target_pairs={{0,16},{16,0},{1,17},{17,1},{2,18},{18,2},{3,19},{19,3},{4,20},{20... | collective-permute-start | bytes 98312 | tf_op jit(solution)/shard_map/ppermute | solution.py:349
  65.0 0.0 collective-permute-done.17
  65.0 0.0 collective-permute-start.23
  65.0 0.0 collective-permute-done.18
  65.0 0.0 collective-permute-done.19
  65.0 1.2 %collective-permute-done.21 = f32[1,32,256]{2,1,0:T(8,128)S(1)} collective-permute-done((f32[1,32,256]{2,1,0:T(8,128)S(1)}, f32[1,32,256]{2,1,0:T(8,128)S(1)}, u32[]{:S(2)}, u32[]{:S(2)}) %collective-permute-start.21) | collective-permute-done | bytes 32800 | tf_op jit(solution)/shard_map/ppermute | solution.py:348
  66.2 1.2 %collective-permute-done.22 = f32[1,32,256]{2,1,0:T(8,128)S(1)} collective-permute-done((f32[1,32,256]{2,1,0:T(8,128)S(1)}, f32[1,32,256]{2,1,0:T(8,128)S(1)}, u32[]{:S(2)}, u32[]{:S(2)}) %collective-permute-start.22) | collective-permute-done | bytes 32800 | tf_op jit(solution)/shard_map/ppermute | solution.py:349
  67.3 0.0 collective-permute-done.23
  67.3 1.8 %place_scores.3 = f32[8,32,256]{2,1,0:T(8,128)} custom-call(s32[8]{0:T(128)S(1)} %stack.35.order_ref, s32[1,256]{1,0:T(1,128)S(1)} %copy-done, f32[8,32,256]{2,1,0:T(8,128)} %place_scores.2.refs_0_, f32[96,256]{1,0:T(8,128)S(1)} %bitcast.28, f32[96,256]{1,0:T(8,128)S(1)} %bitcast.29, f32[96,256]{1,0:T(8,128)S(1)} %bitcast.30, ...), custom_call_target="tpu_custom_call", output_to_operand_aliasing={{}: (2, {})} | custom-call | tf_op jit(solution)/shard_map/place_scores/pallas_call | solution.py:268
  (4 shorter events, 0.2 us)
Async XLA Ops:
  2.5 45.9 %collective-permute-start.7 = (bf16[256,3840]{1,0:T(8,128)(2,1)S(1)}, bf16[256,3840]{1,0:T(8,128)(2,1)S(1)}, u32[]{:S(2)}, u32[]{:S(2)}) collective-permute-start(bf16[256,3840]{1,0:T(8,128)(2,1)S(1)} %scale_codes.2), channel_id=1, source_target_pairs={{0,16},{16,0},{1,17},{17,1},{2,18},{18,2},{3,19},{19,3},{4,20},{20... | collective-permute-start | bytes 5898248 | tf_op jit(solution)/shard_map/ppermute | solution.py:314
  6.6 9.6 %collective-permute-start.1 = (bf16[64,2176]{1,0:T(8,128)(2,1)S(1)}, bf16[64,2176]{1,0:T(8,128)(2,1)S(1)}, u32[]{:S(2)}, u32[]{:S(2)}) collective-permute-start(bf16[64,2176]{1,0:T(8,128)(2,1)S(1)} %get-tuple-element.57.refs_0_), channel_id=1, source_target_pairs={{0,2},{2,0},{4,6},{6,4},{8,10},{10,8},{12,14},{14,12},{1,3},{3,1},... | collective-permute-start | bytes 835592 | tf_op jit(solution)/shard_map/ppermute | solution.py:303
  8.2 11.4 %collective-permute-start = (bf16[64,2176]{1,0:T(8,128)(2,1)S(1)}, bf16[64,2176]{1,0:T(8,128)(2,1)S(1)}, u32[]{:S(2)}, u32[]{:S(2)}) collective-permute-start(bf16[64,2176]{1,0:T(8,128)(2,1)S(1)} %get-tuple-element.57.refs_0_), channel_id=1, source_target_pairs={{0,4},{2,6},{4,8},{6,10},{8,12},{10,14},{12,0},{14,2},{1,5},{3,7},... | collective-permute-start | bytes 835592 | tf_op jit(solution)/shard_map/ppermute | solution.py:303
  9.7 12.9 %collective-permute-start.9 = (bf16[64,2176]{1,0:T(8,128)(2,1)S(1)}, bf16[64,2176]{1,0:T(8,128)(2,1)S(1)}, u32[]{:S(2)}, u32[]{:S(2)}) collective-permute-start(bf16[64,2176]{1,0:T(8,128)(2,1)S(1)} %get-tuple-element.69.refs_0_), channel_id=1, source_target_pairs={{0,2},{2,0},{4,6},{6,4},{8,10},{10,8},{12,14},{14,12},{1,3},{3,1},... | collective-permute-start | bytes 835592 | tf_op jit(solution)/shard_map/ppermute | solution.py:303
  10.3 15.2 %collective-permute-start.8 = (bf16[64,2176]{1,0:T(8,128)(2,1)S(1)}, bf16[64,2176]{1,0:T(8,128)(2,1)S(1)}, u32[]{:S(2)}, u32[]{:S(2)}) collective-permute-start(bf16[64,2176]{1,0:T(8,128)(2,1)S(1)} %get-tuple-element.69.refs_0_), channel_id=1, source_target_pairs={{0,4},{2,6},{4,8},{6,10},{8,12},{10,14},{12,0},{14,2},{1,5},{3,7},... | collective-permute-start | bytes 835592 | tf_op jit(solution)/shard_map/ppermute | solution.py:303
  19.5 9.0 %collective-permute-start.3 = (bf16[64,2176]{1,0:T(8,128)(2,1)S(1)}, bf16[64,2176]{1,0:T(8,128)(2,1)S(1)}, u32[]{:S(2)}, u32[]{:S(2)}) collective-permute-start(bf16[64,2176]{1,0:T(8,128)(2,1)S(1)} %collective-permute-done.refs_1_), channel_id=1, source_target_pairs={{0,2},{2,0},{4,6},{6,4},{8,10},{10,8},{12,14},{14,12},{1,3},{3,1},... | collective-permute-start | bytes 835592 | tf_op jit(solution)/shard_map/ppermute | solution.py:303
  20.1 11.4 %collective-permute-start.2 = (bf16[64,2176]{1,0:T(8,128)(2,1)S(1)}, bf16[64,2176]{1,0:T(8,128)(2,1)S(1)}, u32[]{:S(2)}, u32[]{:S(2)}) collective-permute-start(bf16[64,2176]{1,0:T(8,128)(2,1)S(1)} %collective-permute-done.refs_1_), channel_id=1, source_target_pairs={{0,4},{2,6},{4,8},{6,10},{8,12},{10,14},{12,0},{14,2},{1,5},{3,7},... | collective-permute-start | bytes 835592 | tf_op jit(solution)/shard_map/ppermute | solution.py:303
  25.5 9.0 %collective-permute-start.11 = (bf16[64,2176]{1,0:T(8,128)(2,1)S(1)}, bf16[64,2176]{1,0:T(8,128)(2,1)S(1)}, u32[]{:S(2)}, u32[]{:S(2)}) collective-permute-start(bf16[64,2176]{1,0:T(8,128)(2,1)S(1)} %collective-permute-done.8.refs_1_), channel_id=1, source_target_pairs={{0,2},{2,0},{4,6},{6,4},{8,10},{10,8},{12,14},{14,12},{1,3},{3,1},... | collective-permute-start | bytes 835592 | tf_op jit(solution)/shard_map/ppermute | solution.py:303
  26.0 11.4 %collective-permute-start.10 = (bf16[64,2176]{1,0:T(8,128)(2,1)S(1)}, bf16[64,2176]{1,0:T(8,128)(2,1)S(1)}, u32[]{:S(2)}, u32[]{:S(2)}) collective-permute-start(bf16[64,2176]{1,0:T(8,128)(2,1)S(1)} %collective-permute-done.8.refs_1_), channel_id=1, source_target_pairs={{0,4},{2,6},{4,8},{6,10},{8,12},{10,14},{12,0},{14,2},{1,5},{3,7},... | collective-permute-start | bytes 835592 | tf_op jit(solution)/shard_map/ppermute | solution.py:303
  31.5 9.0 %collective-permute-start.5 = (bf16[64,2176]{1,0:T(8,128)(2,1)S(1)}, bf16[64,2176]{1,0:T(8,128)(2,1)S(1)}, u32[]{:S(2)}, u32[]{:S(2)}) collective-permute-start(bf16[64,2176]{1,0:T(8,128)(2,1)S(1)} %collective-permute-done.2.refs_0_), channel_id=1, source_target_pairs={{0,2},{2,0},{4,6},{6,4},{8,10},{10,8},{12,14},{14,12},{1,3},{3,1},... | collective-permute-start | bytes 835592 | tf_op jit(solution)/shard_map/ppermute | solution.py:303
  32.2 11.4 %collective-permute-start.4 = (bf16[64,2176]{1,0:T(8,128)(2,1)S(1)}, bf16[64,2176]{1,0:T(8,128)(2,1)S(1)}, u32[]{:S(2)}, u32[]{:S(2)}) collective-permute-start(bf16[64,2176]{1,0:T(8,128)(2,1)S(1)} %collective-permute-done.2.refs_0_), channel_id=1, source_target_pairs={{0,4},{2,6},{4,8},{6,10},{8,12},{10,14},{12,0},{14,2},{1,5},{3,7},... | collective-permute-start | bytes 835592 | tf_op jit(solution)/shard_map/ppermute | solution.py:303
  37.4 11.6 %collective-permute-start.13 = (bf16[64,2176]{1,0:T(8,128)(2,1)S(1)}, bf16[64,2176]{1,0:T(8,128)(2,1)S(1)}, u32[]{:S(2)}, u32[]{:S(2)}) collective-permute-start(bf16[64,2176]{1,0:T(8,128)(2,1)S(1)} %collective-permute-done.10.refs_3_), channel_id=1, source_target_pairs={{0,2},{2,0},{4,6},{6,4},{8,10},{10,8},{12,14},{14,12},{1,3},{3,1},... | collective-permute-start | bytes 835592 | tf_op jit(solution)/shard_map/ppermute | solution.py:303
  38.2 10.9 %collective-permute-start.12 = (bf16[64,2176]{1,0:T(8,128)(2,1)S(1)}, bf16[64,2176]{1,0:T(8,128)(2,1)S(1)}, u32[]{:S(2)}, u32[]{:S(2)}) collective-permute-start(bf16[64,2176]{1,0:T(8,128)(2,1)S(1)} %collective-permute-done.10.refs_3_), channel_id=1, source_target_pairs={{0,4},{2,6},{4,8},{6,10},{8,12},{10,14},{12,0},{14,2},{1,5},{3,7},... | collective-permute-start | bytes 835592 | tf_op jit(solution)/shard_map/ppermute | solution.py:303
  43.6 11.5 %collective-permute-start.6 = (bf16[64,2176]{1,0:T(8,128)(2,1)S(1)}, bf16[64,2176]{1,0:T(8,128)(2,1)S(1)}, u32[]{:S(2)}, u32[]{:S(2)}) collective-permute-start(bf16[64,2176]{1,0:T(8,128)(2,1)S(1)} %collective-permute-done.4.refs_2_), channel_id=1, source_target_pairs={{0,2},{2,0},{4,6},{6,4},{8,10},{10,8},{12,14},{14,12},{1,3},{3,1},... | collective-permute-start | bytes 835592 | tf_op jit(solution)/shard_map/ppermute | solution.py:303
  49.1 12.9 %collective-permute-start.20 = (bf16[64,2176]{1,0:T(8,128)(2,1)S(1)}, bf16[64,2176]{1,0:T(8,128)(2,1)S(1)}, u32[]{:S(2)}, u32[]{:S(2)}) collective-permute-start(bf16[64,2176]{1,0:T(8,128)(2,1)S(1)} %collective-permute-done.13.refs_4_), channel_id=1, source_target_pairs={{0,4},{2,6},{4,8},{6,10},{8,12},{10,14},{12,0},{14,2},{1,5},{3,7},... | collective-permute-start | bytes 835592 | tf_op jit(solution)/shard_map/ppermute | solution.py:303
  50.9 5.7 %collective-permute-start.14 = (f32[4,32,256]{2,1,0:T(8,128)S(1)}, f32[4,32,256]{2,1,0:T(8,128)S(1)}, u32[]{:S(2)}, u32[]{:S(2)}) collective-permute-start(f32[4,32,256]{2,1,0:T(8,128)S(1)} %get-tuple-element.78), channel_id=1, source_target_pairs={{0,17},{1,16},{16,1},{17,0},{2,19},{3,18},{18,3},{19,2},{4,21},{5,... | collective-permute-start | bytes 393224 | tf_op jit(solution)/shard_map/ppermute | solution.py:348
  50.9 8.7 %collective-permute-start.15 = (f32[4,32,256]{2,1,0:T(8,128)S(1)}, f32[4,32,256]{2,1,0:T(8,128)S(1)}, u32[]{:S(2)}, u32[]{:S(2)}) collective-permute-start(f32[4,32,256]{2,1,0:T(8,128)S(1)} %get-tuple-element.79), channel_id=1, source_target_pairs={{0,16},{16,0},{1,17},{17,1},{2,18},{18,2},{3,19},{19,3},{4,20},{20... | collective-permute-start | bytes 393224 | tf_op jit(solution)/shard_map/ppermute | solution.py:349
  53.3 7.1 %collective-permute-start.16 = (f32[4,32,256]{2,1,0:T(8,128)S(1)}, f32[4,32,256]{2,1,0:T(8,128)S(1)}, u32[]{:S(2)}, u32[]{:S(2)}) collective-permute-start(f32[4,32,256]{2,1,0:T(8,128)S(1)} %get-tuple-element.81), channel_id=1, source_target_pairs={{0,1},{1,0},{2,3},{3,2},{4,5},{5,4},{6,7},{7,6},{8,9},{9,8},{10,11... | collective-permute-start | bytes 393224 | tf_op jit(solution)/shard_map/ppermute | solution.py:350
  55.1 9.8 %collective-permute-start.17 = (f32[3,32,256]{2,1,0:T(8,128)S(1)}, f32[3,32,256]{2,1,0:T(8,128)S(1)}, u32[]{:S(2)}, u32[]{:S(2)}) collective-permute-start(f32[3,32,256]{2,1,0:T(8,128)S(1)} %get-tuple-element.89), channel_id=1, source_target_pairs={{0,17},{1,16},{16,1},{17,0},{2,19},{3,18},{18,3},{19,2},{4,21},{5,... | collective-permute-start | bytes 294920 | tf_op jit(solution)/shard_map/ppermute | solution.py:348
  56.7 8.3 %collective-permute-start.18 = (f32[3,32,256]{2,1,0:T(8,128)S(1)}, f32[3,32,256]{2,1,0:T(8,128)S(1)}, u32[]{:S(2)}, u32[]{:S(2)}) collective-permute-start(f32[3,32,256]{2,1,0:T(8,128)S(1)} %get-tuple-element.90), channel_id=1, source_target_pairs={{0,16},{16,0},{1,17},{17,1},{2,18},{18,2},{3,19},{19,3},{4,20},{20... | collective-permute-start | bytes 294920 | tf_op jit(solution)/shard_map/ppermute | solution.py:349
  59.6 0.8 %copy-start = (s32[1,256]{1,0:T(1,128)S(1)}, s32[1,256]{1,0:T(1,128)}, u32[]{:S(2)}) copy-start(s32[1,256]{1,0:T(1,128)} %ids_ref.3) | copy-start | bytes 3076
  59.6 5.4 %collective-permute-start.19 = (f32[3,32,256]{2,1,0:T(8,128)S(1)}, f32[3,32,256]{2,1,0:T(8,128)S(1)}, u32[]{:S(2)}, u32[]{:S(2)}) collective-permute-start(f32[3,32,256]{2,1,0:T(8,128)S(1)} %get-tuple-element.91), channel_id=1, source_target_pairs={{0,1},{1,0},{2,3},{3,2},{4,5},{5,4},{6,7},{7,6},{8,9},{9,8},{10,11... | collective-permute-start | bytes 294920 | tf_op jit(solution)/shard_map/ppermute | solution.py:350
  62.8 3.4 %collective-permute-start.21 = (f32[1,32,256]{2,1,0:T(8,128)S(1)}, f32[1,32,256]{2,1,0:T(8,128)S(1)}, u32[]{:S(2)}, u32[]{:S(2)}) collective-permute-start(f32[1,32,256]{2,1,0:T(8,128)S(1)} %get-tuple-element.95), channel_id=1, source_target_pairs={{0,17},{1,16},{16,1},{17,0},{2,19},{3,18},{18,3},{19,2},{4,21},{5,... | collective-permute-start | bytes 98312 | tf_op jit(solution)/shard_map/ppermute | solution.py:348
  63.2 4.2 %collective-permute-start.22 = (f32[1,32,256]{2,1,0:T(8,128)S(1)}, f32[1,32,256]{2,1,0:T(8,128)S(1)}, u32[]{:S(2)}, u32[]{:S(2)}) collective-permute-start(f32[1,32,256]{2,1,0:T(8,128)S(1)} %get-tuple-element.96), channel_id=1, source_target_pairs={{0,16},{16,0},{1,17},{17,1},{2,18},{18,2},{3,19},{19,3},{4,20},{20... | collective-permute-start | bytes 98312 | tf_op jit(solution)/shard_map/ppermute | solution.py:349
  65.0 2.4 %collective-permute-start.23 = (f32[1,32,256]{2,1,0:T(8,128)S(1)}, f32[1,32,256]{2,1,0:T(8,128)S(1)}, u32[]{:S(2)}, u32[]{:S(2)}) collective-permute-start(f32[1,32,256]{2,1,0:T(8,128)S(1)} %get-tuple-element.97), channel_id=1, source_target_pairs={{0,1},{1,0},{2,3},{3,2},{4,5},{5,4},{6,7},{7,6},{8,9},{9,8},{10,11... | collective-permute-start | bytes 98312 | tf_op jit(solution)/shard_map/ppermute | solution.py:350

commit v8 on v7

--- a/solution.py
+++ b/solution.py
@@ -8,7 +8,8 @@
 from jax.sharding import PartitionSpec as P
 
 BLOCK = 128
-ALONE = 30
+ALONE = 29
+LATE_WEIGHT = 10
 CHUNKS = 2
 VMEM = pl.BlockSpec(memory_space=pltpu.VMEM)
 SMEM = pl.BlockSpec(memory_space=pltpu.SMEM)
@@ -52,11 +53,34 @@
     return jnp.concatenate([scales, pad], axis=0).T
 
 
-def cut_kernel(alone, blocks, cuts, part_ref, queries_ref, *refs):
-    *chunk_refs, sems = refs
-    first = pl.multiple_of(part_ref[0] * (blocks - alone) * BLOCK, BLOCK)
+def scale_tiles(codes_ref, begin, buffer, sems, scales, order, out_ref):
+    tiles, tile, width = buffer.shape
+
+    def fetch(i):
+        start = pl.multiple_of(begin * BLOCK, BLOCK)
+        return pltpu.make_async_copy(
+            codes_ref.at[pl.ds(i * tile, tile), pl.ds(start, width)], buffer.at[i], sems.at[i]
+        )
+
+    for i in range(tiles):
+        fetch(i).start()
+    scales = scales()
+    for i in range(tiles):
+        fetch(i).wait()
+        rows = slice(i * tile, (i + 1) * tile)
+        for block, at in enumerate(order):
+            columns = pl.ds(pl.multiple_of(at * BLOCK, BLOCK), BLOCK)
+            out_ref[rows, block * BLOCK : (block + 1) * BLOCK] = scaled(buffer[i, :, columns], scales[rows], block)
+
+
+def cut_kernel(alone, cuts, part_ref, queries_ref, codes_ref, exponents_ref, *refs):
+    *chunk_refs, sent_ref, buffer, powers, code_sems, sems = refs
+    part = part_ref[0]
+    blocks = exponents_ref.shape[0]
+    far = blocks - alone
+    first = pl.multiple_of(part * far * BLOCK, BLOCK)
     wide = alone * BLOCK
-    copies = []
+    copies = [(exponents_ref, powers)]
     for out_ref, start, stop in zip(chunk_refs, cuts[:-1], cuts[1:]):
         if start < wide:
             width = min(stop, wide) - start
@@ -71,69 +95,66 @@
                 out_ref.at[:, pl.ds(begin - start, stop - begin)],
             ))
     copies = [pltpu.make_async_copy(a, b, sems.at[i]) for i, (a, b) in enumerate(copies)]
-    for copy in copies:
-        copy.start()
-    for copy in copies:
+    copies[0].start()
+
+    def scales():
+        for copy in copies[1:]:
+            copy.start()
+        copies[0].wait()
+        near, away = powers[0:alone, :], powers[far:blocks, :]
+        return by_example(scales_of(jnp.where(part == 0, away, near)))
+
+    scale_tiles(codes_ref, (1 - part) * far, buffer, code_sems, scales, range(alone), sent_ref)
+    for copy in copies[1:]:
         copy.wait()
 
 
-def cut(part, queries, alone, cuts):
+def cut(part, queries, codes, exponents, alone, cuts):
     rows = queries.shape[1]
+    count = codes.shape[0]
+    wide = alone * BLOCK
+    tile = min(count, 64)
     chunks = len(cuts) - 1
     return pl.pallas_call(
-        functools.partial(cut_kernel, alone, queries.shape[2] // BLOCK, cuts),
-        out_shape=[pltpu.VMEM((rows, b - a), jnp.bfloat16) for a, b in zip(cuts[:-1], cuts[1:])],
-        in_specs=[SMEM, pl.BlockSpec(memory_space=pl.ANY)],
-        out_specs=[VMEM] * chunks,
-        scratch_shapes=[pltpu.SemaphoreType.DMA((2 * chunks,))],
-        compiler_params=pltpu.CompilerParams(vmem_limit_bytes=16 << 20),
-        cost_estimate=pl.CostEstimate(flops=0, bytes_accessed=2 * queries.size, transcendentals=0),
+        functools.partial(cut_kernel, alone, cuts),
+        out_shape=[pltpu.VMEM((rows, b - a), jnp.bfloat16) for a, b in zip(cuts[:-1], cuts[1:])]
+        + [pltpu.VMEM((count, wide), jnp.bfloat16)],
+        in_specs=[SMEM] + [pl.BlockSpec(memory_space=pl.ANY)] * 3,
+        out_specs=[VMEM] * (chunks + 1),
+        scratch_shapes=[
+            pltpu.VMEM((count // tile, tile, wide), jnp.bfloat16),
+            pltpu.VMEM(exponents.shape, exponents.dtype),
+            pltpu.SemaphoreType.DMA((count // tile,)),
+            pltpu.SemaphoreType.DMA((2 * chunks + 1,)),
+        ],
+        compiler_params=pltpu.CompilerParams(vmem_limit_bytes=16 << 20),
+        cost_estimate=pl.CostEstimate(flops=codes.size, bytes_accessed=2 * codes.size, transcendentals=0),
         name="cut_queries",
-    )(part, in_hbm(queries))
-
-
-def scale_kernel(alone, tile, sent, part_ref, codes_ref, exponents_ref, out_ref, buffer, powers, sems, powers_sem):
+    )(part, in_hbm(queries), in_hbm(codes), in_hbm(exponents))
+
+
+def scale_kernel(alone, part_ref, codes_ref, exponents_ref, out_ref, buffer, powers, code_sems, sem):
     part = part_ref[0]
     blocks = exponents_ref.shape[0]
     far = blocks - alone
-    shared = far - alone
-    tiles, _, width = buffer.shape
-    begin = (1 - part) * far if sent else part * alone
-
-    def fetch(i):
-        start = pl.multiple_of(begin * BLOCK, BLOCK)
-        return pltpu.make_async_copy(
-            codes_ref.at[pl.ds(i * tile, tile), pl.ds(start, width)], buffer.at[i], sems.at[i]
-        )
-
-    powers_copy = pltpu.make_async_copy(exponents_ref, powers, powers_sem)
-    powers_copy.start()
-    for i in range(tiles):
-        fetch(i).start()
-    powers_copy.wait()
-    near, away = powers[0:alone, :], powers[far:blocks, :]
-    if sent:
-        scales = by_example(scales_of(jnp.where(part == 0, away, near)))
-    else:
-        own = jnp.where(part == 0, near, away)
-        scales = by_example(scales_of(jnp.concatenate([own, powers[alone:far, :]], axis=0)))
-    for i in range(tiles):
-        fetch(i).wait()
-        rows = slice(i * tile, (i + 1) * tile)
-        for block in range(width // BLOCK):
-            at = block
-            if not sent:
-                at = block + part * shared if block < alone else block - part * alone
-            columns = pl.ds(pl.multiple_of(at * BLOCK, BLOCK), BLOCK)
-            out_ref[rows, block * BLOCK : (block + 1) * BLOCK] = scaled(buffer[i, :, columns], scales[rows], block)
-
-
-def scale(part, codes, exponents, alone, sent):
+    copy = pltpu.make_async_copy(exponents_ref, powers, sem)
+    copy.start()
+
+    def scales():
+        copy.wait()
+        own = jnp.where(part == 0, powers[0:alone, :], powers[far:blocks, :])
+        return by_example(scales_of(jnp.concatenate([own, powers[alone:far, :]], axis=0)))
+
+    order = [i + part * (far - alone) if i < alone else i - part * alone for i in range(far)]
+    scale_tiles(codes_ref, part * alone, buffer, code_sems, scales, order, out_ref)
+
+
+def scale(part, codes, exponents, alone):
     count = codes.shape[0]
-    width = (alone if sent else exponents.shape[0] - alone) * BLOCK
+    width = (exponents.shape[0] - alone) * BLOCK
     tile = min(count, 64)
     return pl.pallas_call(
-        functools.partial(scale_kernel, alone, tile, sent),
+        functools.partial(scale_kernel, alone),
         out_shape=pltpu.VMEM((count, width), jnp.bfloat16),
         in_specs=[SMEM] + [pl.BlockSpec(memory_space=pl.ANY)] * 2,
         out_specs=VMEM,
@@ -215,7 +236,7 @@
             outs[i][...] = total
 
 
-def score(half, rows, pieces, grads, first=0, base=()):
+def score(half, rows, pieces, grads, first=0, base=(), weight=1):
     operands = [array for arrays in pieces for array in arrays] + list(grads) + list(base)
     height = sum(array.shape[0] for array in pieces[0])
     count = grads[0].shape[0]
@@ -230,43 +251,56 @@
         out_specs=[VMEM] * len(shapes),
         compiler_params=pltpu.CompilerParams(vmem_limit_bytes=16 << 20),
         cost_estimate=pl.CostEstimate(
-            flops=2 * height * sum(g.size for g in grads), bytes_accessed=2 * grads[0].size, transcendentals=0
+            flops=2 * height * sum(g.size for g in grads) * weight, bytes_accessed=2 * grads[0].size, transcendentals=0
         ),
         name="score",
     )(half, *in_vmem(operands))
 
 
-def place_kernel(rows, first, order_ref, ids_ref, *refs):
+def add_kernel(a_ref, b_ref, out_ref):
+    out_ref[...] = a_ref[...] + b_ref[...]
+
+
+def add(a, b):
+    return pl.pallas_call(
+        add_kernel,
+        out_shape=pltpu.VMEM(a.shape, a.dtype),
+        in_specs=[VMEM, VMEM],
+        out_specs=VMEM,
+        compiler_params=pltpu.CompilerParams(vmem_limit_bytes=16 << 20),
+        name="add",
+    )(*in_vmem([a, b]))
+
+
+def place_kernel(first, order_ref, ids_ref, *refs):
     *share_refs, out_ref, placed_ref, sems = refs
     share_refs = share_refs[1:] if first else share_refs
-    count = ids_ref.shape[1]
+    blocks, rows, count = placed_ref.shape
     slots = lax.broadcasted_iota(jnp.int32, (count, count), 0)
-    table = (slots == jnp.broadcast_to(ids_ref[...], (count, count))).astype(jnp.float32)
+    table = (slots == jnp.broadcast_to(ids_ref[...], (count, count))).astype(jnp.float32).astype(jnp.bfloat16)
+    raw = functools.reduce(jnp.add, [ref[...] for ref in share_refs])
+    high = raw.astype(jnp.bfloat16)
+    rest = raw - high.astype(jnp.float32)
+    middle = rest.astype(jnp.bfloat16)
+    low = (rest - middle.astype(jnp.float32)).astype(jnp.bfloat16)
+    placed = (dot(high, table) + dot(middle, table)) + dot(low, table)
     copies = []
-    for at in range(0, len(share_refs), 4):
-        a, b, c, d = (ref[...] for ref in share_refs[at : at + 4])
-        raw = (d + c) + (b + a)
-        placed = lax.dot_general(
-            raw, table, NT, precision=lax.Precision.HIGHEST, preferred_element_type=jnp.float32
-        )
-        for i in range(raw.shape[0] // rows):
-            j = len(copies)
-            placed_ref[j] = placed[i * rows : (i + 1) * rows]
-            copies.append(
-                pltpu.make_async_copy(placed_ref.at[j], out_ref.at[order_ref[first + j]], sems.at[j])
-            )
-            copies[-1].start()
+    for j in range(blocks):
+        placed_ref[j] = placed[j * rows : (j + 1) * rows]
+        copies.append(pltpu.make_async_copy(placed_ref.at[j], out_ref.at[order_ref[first + j]], sems.at[j]))
+        copies[-1].start()
     for copy in copies:
         copy.wait()
 
 
 def place(order, ids, out, first, shares, rows):
     count = ids.shape[1]
-    blocks = sum(share.shape[0] for share in shares[::4]) // rows
+    shares = [share.reshape(-1, count) for share in shares]
+    blocks = shares[0].shape[0] // rows
     anywhere = pl.BlockSpec(memory_space=pl.ANY)
     given = [in_hbm(out)] if first else []
     return pl.pallas_call(
-        functools.partial(place_kernel, rows, first),
+        functools.partial(place_kernel, first),
         out_shape=pltpu.HBM((order.shape[0], rows, count), jnp.float32),
         in_specs=[SMEM, VMEM] + [anywhere] * len(given) + [VMEM] * len(shares),
         out_specs=anywhere,
@@ -310,55 +344,52 @@
 
     swap = [(i, parts - 1 - i) for i in range(parts)]
     by_block = exponents.T
-    chunks = cut(part, queries, alone, cuts)
-    theirs = lax.ppermute(scale(part, codes, by_block, alone, True), "groups", swap)
-    ours = scale(part, codes, by_block, alone, False)
+    *chunks, sent = cut(part, queries, codes, by_block, alone, cuts)
+    theirs = lax.ppermute(sent, "groups", swap)
+    ours = scale(part, codes, by_block, alone)
 
     def stack(arrays):
         return arrays if rows % 16 == 0 else [jnp.concatenate(arrays, axis=0)]
 
-    first_steps = max(slow - 2, 1)
-    early_rows = first_steps * fast * rows
-    early, middle, late = [], [], []
+    kept_rows = (slow - 2) * fast * rows
+    early, late = [], []
     for c, chunk in enumerate(chunks):
-        held, between = [], []
+        held = []
         for s in range(slow - 1):
             tied = [step(chunk, slow, fast), *along_fast(chunk)] + held
             if c == CHUNKS - 1 and s == 0:
                 *tied, ours = lax.optimization_barrier(tied + [ours])
-            elif c == CHUNKS - 1 and s == slow - 2:
-                their_early = list(score(half, rows, early + [held], [theirs]))
-                *tied, keep, send = lax.optimization_barrier(tied + their_early)
-                their_early = [keep, send]
             else:
                 tied = lax.optimization_barrier(tied)
             chunk, values, held = tied[0], tied[1 : fast + 1], tied[fast + 1 :]
-            if s < first_steps:
-                held = [stash(held[0] if s else None, stack(values), s * fast * rows, early_rows)]
-            else:
-                between += values
-        early.append(held)
-        middle.append(stack(between + [chunk]))
+            if s < slow - 2:
+                held = [stash(held[0] if s else None, stack(values), s * fast * rows, kept_rows)]
+        early.append(held + stack(values + [chunk]))
         along = along_fast(chunk)[1:] if c < CHUNKS - 1 else [step(value, slow, fast) for value in values[1:]]
         late.append(stack(along))
 
-    def shares_of(their_keep, their_send, keep, send):
-        across = [(i, 3 - i) for i in range(4)]
-        shares = [
-            lax.ppermute(their_send, ("groups", "dim"), across),
-            lax.ppermute(their_keep, "groups", swap),
-            lax.ppermute(send, "dim", [(0, 1), (1, 0)]),
-            keep,
-        ]
-        return [share.reshape(-1, count) for share in shares]
-
-    shares = shares_of(*their_early, *score(half, rows, early, [ours]))
+    def over_dim(value):
+        return lax.ppermute(value, "dim", [(0, 1), (1, 0)])
+
+    keep, send = score(half, rows, early, [theirs])
+    added, theirs = lax.optimization_barrier((add(keep, over_dim(send)), theirs))
+    given = lax.ppermute(added, "groups", swap)
+    keep, send = score(half, rows, early, [ours])
+    shares = [given, keep, over_dim(send)]
+
+    begun = score(half, 0, late[:-1], [theirs, ours])
+    last = score(half, rows, late[-1:], [theirs, ours], cuts[-2], begun, LATE_WEIGHT)
+    *last, shares[1] = lax.optimization_barrier((*last, shares[1]))
     out = place(order, example_ids, None, 0, shares, rows // 2)
-    shares = shares_of(*score(half, rows, middle, [theirs, ours]))
-    begun = score(half, 0, late[:-1], [theirs, ours])
-    *begun, out = lax.optimization_barrier((*begun, out))
-    shares += shares_of(*score(half, rows, late[-1:], [theirs, ours], cuts[-2], begun))
-    return place(order, example_ids, out, first_steps * fast, shares, rows // 2)
+    their_keep, their_send, keep, send = last
+    across = [(i, 3 - i) for i in range(4)]
+    shares = [
+        lax.ppermute(their_send, ("groups", "dim"), across),
+        lax.ppermute(their_keep, "groups", swap),
+        over_dim(send),
+        keep,
+    ]
+    return place(order, example_ids, out, total - fast + 1, shares, rows // 2)
 
 
 def solution(mesh):

time: 69.3 us -> 63.2 us (0.912)
  waiting for transfers between devices: 34.7 us -> 25.8 us
  starting transfers between devices: 20.1 us -> 25.3 us
  Pallas kernels: 14 us -> 11.7 us
    ppermute x14, starting transfers between devices: 10.2 us -> 19.1 us  [step(): return lax.ppermute(value, 'ex', pairs)]
    ppermute x10 -> x7, waiting for transfers between devices: 8.19 us -> 0.6 us  [the longest x1 0.58 us: shards(): lax.ppermute(their_keep, 'groups', swap)]
    ppermute x10 -> x7, starting transfers between devices: 9.96 us -> 6.13 us  [the longest x1 3.03 us: shards(): theirs = lax.ppermute(sent, 'groups', swap)]
    pallas_call x5, Pallas kernels: 9.41 us -> 7.71 us  [the longest x2 3 us: place(): pl.pallas_call(functools.partial(place_kernel, first), out_shape=pltpu.HB...]
    ppermute x14, waiting for transfers between devices: 26.5 us -> 25.2 us  [step(): return lax.ppermute(value, 'ex', pairs)]
    pallas_call x5 -> x4, Pallas kernels: 4.46 us -> 3.86 us  [score(): pl.pallas_call(functools.partial(score_kernel, [len(arrays) for arrays in...]
  transfers between devices with their start and end apart: 24 -> 21, of which waited for: 14 -> 8; matrix products, arithmetic and copies ran while one was open for 0% -> 0% of each run, Pallas kernels for 14% -> 13%
where the time goes in v8:
time: 63.2 us; the launch traced here: 63 us
  waiting for transfers between devices  25.8 us (41%)
  starting transfers between devices  25.3 us (40%)
  Pallas kernels  11.7 us (19%)
    ppermute x14, waiting for transfers between devices, step(): return lax.ppermute(value, 'ex', pairs)  25.2 us
    ppermute x14, starting transfers between devices, step(): return lax.ppermute(value, 'ex', pairs)  19.1 us
    pallas_call x4, Pallas kernels, score(): pl.pallas_call(functools.partial(score_kernel, [len(arrays) for arrays in...  3.86 us
    ppermute x1, starting transfers between devices, shards(): theirs = lax.ppermute(sent, 'groups', swap)  3.03 us
    pallas_call x2, Pallas kernels, place(): pl.pallas_call(functools.partial(place_kernel, first), out_shape=pltpu.HB...  3 us
    pallas_call x1, Pallas kernels, scale(): pl.pallas_call(functools.partial(scale_kernel, alone), out_shape=pltpu.VM...  2.6 us
    pallas_call x1, Pallas kernels, cut(): pl.pallas_call(functools.partial(cut_kernel, alone, cuts), out_shape=[plt...  2.09 us
    ppermute x3, starting transfers between devices, over_dim(): return lax.ppermute(value, 'dim', [(0, 1), (1, 0)])  1.9 us
  transfers between devices with their start and end apart: 21, of which 8 were waited for; matrix products, arithmetic and copies ran while one was open for 0% of the time, Pallas kernels for 13%

profile of v8, /device:TPU:0, one launch (start us, length us, event | category | flops | bytes accessed | tf_op | source)
XLA Modules:
  0.0 63.0 jit_solution(2584571842495544861)
XLA Ops:
  0.0 0.1 stack.35.order_ref
  0.1 2.1 %cut_queries.1 = (bf16[64,2176]{1,0:T(8,128)(2,1)S(1)}, bf16[64,2304]{1,0:T(8,128)(2,1)S(1)}, bf16[256,3712]{1,0:T(8,128)(2,1)S(1)}) custom-call(s32[1]{0:T(128)} %bitcast.part_ref, bf16[1,64,8192]{2,1,0:T(8,128)(2,1)} %queries_ref.1, bf16[256,8192]{1,0:T(8,128)(2,1)} %codes_ref.3, s32[64,256]{1,0:T(8,128)} %bitcast.25), custom_call_target="tpu_custom_call" | custom-call | flops 2097152 | bytes 4194304 | tf_op jit(solution)/shard_map/cut_queries/pallas_call | solution.py:118
  2.2 3.0 %collective-permute-start.12 = (bf16[256,3712]{1,0:T(8,128)(2,1)S(1)}, bf16[256,3712]{1,0:T(8,128)(2,1)S(1)}, u32[]{:S(2)}, u32[]{:S(2)}) collective-permute-start(bf16[256,3712]{1,0:T(8,128)(2,1)S(1)} %get-tuple-element.78), channel_id=1, source_target_pairs={{0,16},{16,0},{1,17},{17,1},{2,18},{18,2},{3,19},{19,3},{4,20},{20... | collective-permute-start | bytes 5701640 | tf_op jit(solution)/shard_map/ppermute | solution.py:348
  5.2 1.6 %collective-permute-start.6 = (bf16[64,2304]{1,0:T(8,128)(2,1)S(1)}, bf16[64,2304]{1,0:T(8,128)(2,1)S(1)}, u32[]{:S(2)}, u32[]{:S(2)}) collective-permute-start(bf16[64,2304]{1,0:T(8,128)(2,1)S(1)} %get-tuple-element.68.refs_0_), channel_id=1, source_target_pairs={{0,4},{2,6},{4,8},{6,10},{8,12},{10,14},{12,0},{14,2},{1,5},{3,7},... | collective-permute-start | bytes 884744 | tf_op jit(solution)/shard_map/ppermute | solution.py:337
  6.8 1.5 %collective-permute-start.7 = (bf16[64,2304]{1,0:T(8,128)(2,1)S(1)}, bf16[64,2304]{1,0:T(8,128)(2,1)S(1)}, u32[]{:S(2)}, u32[]{:S(2)}) collective-permute-start(bf16[64,2304]{1,0:T(8,128)(2,1)S(1)} %get-tuple-element.68.refs_0_), channel_id=1, source_target_pairs={{0,2},{2,0},{4,6},{6,4},{8,10},{10,8},{12,14},{14,12},{1,3},{3,1},... | collective-permute-start | bytes 884744 | tf_op jit(solution)/shard_map/ppermute | solution.py:337
  8.3 1.6 %collective-permute-start = (bf16[64,2176]{1,0:T(8,128)(2,1)S(1)}, bf16[64,2176]{1,0:T(8,128)(2,1)S(1)}, u32[]{:S(2)}, u32[]{:S(2)}) collective-permute-start(bf16[64,2176]{1,0:T(8,128)(2,1)S(1)} %get-tuple-element.56.refs_0_), channel_id=1, source_target_pairs={{0,4},{2,6},{4,8},{6,10},{8,12},{10,14},{12,0},{14,2},{1,5},{3,7},... | collective-permute-start | bytes 835592 | tf_op jit(solution)/shard_map/ppermute | solution.py:337
  9.9 0.5 collective-permute-start.1
  10.4 2.6 %scale_codes.1.refs_2_.refs_8_ = bf16[256,4480]{1,0:T(8,128)(2,1)S(1)} custom-call(s32[1]{0:T(128)} %bitcast.part_ref, bf16[256,8192]{1,0:T(8,128)(2,1)} %codes_ref.3, s32[64,256]{1,0:T(8,128)} %bitcast.26), custom_call_target="tpu_custom_call" | custom-call | flops 2097152 | bytes 8388608 | tf_op jit(solution)/shard_map/scale_codes/pallas_call | solution.py:156
  13.0 3.9 %collective-permute-done.6.refs_1_ = bf16[64,2304]{1,0:T(8,128)(2,1)S(1)} collective-permute-done((bf16[64,2304]{1,0:T(8,128)(2,1)S(1)}, bf16[64,2304]{1,0:T(8,128)(2,1)S(1)}, u32[]{:S(2)}, u32[]{:S(2)}) %collective-permute-start.6) | collective-permute-done | bytes 294944 | tf_op jit(solution)/shard_map/ppermute | solution.py:337
  16.9 0.0 collective-permute-done.7.refs_1_
  16.9 1.4 %collective-permute-start.8 = (bf16[64,2304]{1,0:T(8,128)(2,1)S(1)}, bf16[64,2304]{1,0:T(8,128)(2,1)S(1)}, u32[]{:S(2)}, u32[]{:S(2)}) collective-permute-start(bf16[64,2304]{1,0:T(8,128)(2,1)S(1)} %collective-permute-done.6.refs_1_), channel_id=1, source_target_pairs={{0,4},{2,6},{4,8},{6,10},{8,12},{10,14},{12,0},{14,2},{1,5},{3,7},... | collective-permute-start | bytes 884744 | tf_op jit(solution)/shard_map/ppermute | solution.py:337
  18.3 1.5 %collective-permute-start.9 = (bf16[64,2304]{1,0:T(8,128)(2,1)S(1)}, bf16[64,2304]{1,0:T(8,128)(2,1)S(1)}, u32[]{:S(2)}, u32[]{:S(2)}) collective-permute-start(bf16[64,2304]{1,0:T(8,128)(2,1)S(1)} %collective-permute-done.6.refs_1_), channel_id=1, source_target_pairs={{0,2},{2,0},{4,6},{6,4},{8,10},{10,8},{12,14},{14,12},{1,3},{3,1},... | collective-permute-start | bytes 884744 | tf_op jit(solution)/shard_map/ppermute | solution.py:337
  19.8 3.1 %collective-permute-done.refs_1_ = bf16[64,2176]{1,0:T(8,128)(2,1)S(1)} collective-permute-done((bf16[64,2176]{1,0:T(8,128)(2,1)S(1)}, bf16[64,2176]{1,0:T(8,128)(2,1)S(1)}, u32[]{:S(2)}, u32[]{:S(2)}) %collective-permute-start) | collective-permute-done | bytes 278560 | tf_op jit(solution)/shard_map/ppermute | solution.py:337
  22.9 0.0 collective-permute-done.1.refs_1_
  22.9 1.4 %collective-permute-start.2 = (bf16[64,2176]{1,0:T(8,128)(2,1)S(1)}, bf16[64,2176]{1,0:T(8,128)(2,1)S(1)}, u32[]{:S(2)}, u32[]{:S(2)}) collective-permute-start(bf16[64,2176]{1,0:T(8,128)(2,1)S(1)} %collective-permute-done.refs_1_), channel_id=1, source_target_pairs={{0,4},{2,6},{4,8},{6,10},{8,12},{10,14},{12,0},{14,2},{1,5},{3,7},... | collective-permute-start | bytes 835592 | tf_op jit(solution)/shard_map/ppermute | solution.py:337
  24.3 1.5 %collective-permute-start.3 = (bf16[64,2176]{1,0:T(8,128)(2,1)S(1)}, bf16[64,2176]{1,0:T(8,128)(2,1)S(1)}, u32[]{:S(2)}, u32[]{:S(2)}) collective-permute-start(bf16[64,2176]{1,0:T(8,128)(2,1)S(1)} %collective-permute-done.refs_1_), channel_id=1, source_target_pairs={{0,2},{2,0},{4,6},{6,4},{8,10},{10,8},{12,14},{14,12},{1,3},{3,1},... | collective-permute-start | bytes 835592 | tf_op jit(solution)/shard_map/ppermute | solution.py:337
  25.8 3.4 %collective-permute-done.8.refs_5_ = bf16[64,2304]{1,0:T(8,128)(2,1)S(1)} collective-permute-done((bf16[64,2304]{1,0:T(8,128)(2,1)S(1)}, bf16[64,2304]{1,0:T(8,128)(2,1)S(1)}, u32[]{:S(2)}, u32[]{:S(2)}) %collective-permute-start.8) | collective-permute-done | bytes 294944 | tf_op jit(solution)/shard_map/ppermute | solution.py:337
  29.2 0.0 collective-permute-done.9.refs_2_
  29.2 1.4 %collective-permute-start.10 = (bf16[64,2304]{1,0:T(8,128)(2,1)S(1)}, bf16[64,2304]{1,0:T(8,128)(2,1)S(1)}, u32[]{:S(2)}, u32[]{:S(2)}) collective-permute-start(bf16[64,2304]{1,0:T(8,128)(2,1)S(1)} %collective-permute-done.8.refs_5_), channel_id=1, source_target_pairs={{0,4},{2,6},{4,8},{6,10},{8,12},{10,14},{12,0},{14,2},{1,5},{3,7},... | collective-permute-start | bytes 884744 | tf_op jit(solution)/shard_map/ppermute | solution.py:337
  30.6 1.5 %collective-permute-start.11 = (bf16[64,2304]{1,0:T(8,128)(2,1)S(1)}, bf16[64,2304]{1,0:T(8,128)(2,1)S(1)}, u32[]{:S(2)}, u32[]{:S(2)}) collective-permute-start(bf16[64,2304]{1,0:T(8,128)(2,1)S(1)} %collective-permute-done.8.refs_5_), channel_id=1, source_target_pairs={{0,2},{2,0},{4,6},{6,4},{8,10},{10,8},{12,14},{14,12},{1,3},{3,1},... | collective-permute-start | bytes 884744 | tf_op jit(solution)/shard_map/ppermute | solution.py:337
  32.1 3.1 %collective-permute-done.2.refs_1_ = bf16[64,2176]{1,0:T(8,128)(2,1)S(1)} collective-permute-done((bf16[64,2176]{1,0:T(8,128)(2,1)S(1)}, bf16[64,2176]{1,0:T(8,128)(2,1)S(1)}, u32[]{:S(2)}, u32[]{:S(2)}) %collective-permute-start.2) | collective-permute-done | bytes 278560 | tf_op jit(solution)/shard_map/ppermute | solution.py:337
  35.2 0.0 collective-permute-done.3.refs_2_
  35.2 1.4 %collective-permute-start.4 = (bf16[64,2176]{1,0:T(8,128)(2,1)S(1)}, bf16[64,2176]{1,0:T(8,128)(2,1)S(1)}, u32[]{:S(2)}, u32[]{:S(2)}) collective-permute-start(bf16[64,2176]{1,0:T(8,128)(2,1)S(1)} %collective-permute-done.2.refs_1_), channel_id=1, source_target_pairs={{0,4},{2,6},{4,8},{6,10},{8,12},{10,14},{12,0},{14,2},{1,5},{3,7},... | collective-permute-start | bytes 835592 | tf_op jit(solution)/shard_map/ppermute | solution.py:337
  36.6 1.5 %collective-permute-start.5 = (bf16[64,2176]{1,0:T(8,128)(2,1)S(1)}, bf16[64,2176]{1,0:T(8,128)(2,1)S(1)}, u32[]{:S(2)}, u32[]{:S(2)}) collective-permute-start(bf16[64,2176]{1,0:T(8,128)(2,1)S(1)} %collective-permute-done.2.refs_1_), channel_id=1, source_target_pairs={{0,2},{2,0},{4,6},{6,4},{8,10},{10,8},{12,14},{14,12},{1,3},{3,1},... | collective-permute-start | bytes 835592 | tf_op jit(solution)/shard_map/ppermute | solution.py:337
  38.2 7.9 %collective-permute-done.4.refs_3_ = bf16[64,2176]{1,0:T(8,128)(2,1)S(1)} collective-permute-done((bf16[64,2176]{1,0:T(8,128)(2,1)S(1)}, bf16[64,2176]{1,0:T(8,128)(2,1)S(1)}, u32[]{:S(2)}, u32[]{:S(2)}) %collective-permute-start.4) | collective-permute-done | bytes 278560 | tf_op jit(solution)/shard_map/ppermute | solution.py:337
  46.1 0.0 collective-permute-done.5.refs_2_
  46.1 1.5 %collective-permute-start.16 = (bf16[64,2176]{1,0:T(8,128)(2,1)S(1)}, bf16[64,2176]{1,0:T(8,128)(2,1)S(1)}, u32[]{:S(2)}, u32[]{:S(2)}) collective-permute-start(bf16[64,2176]{1,0:T(8,128)(2,1)S(1)} %collective-permute-done.4.refs_3_), channel_id=1, source_target_pairs={{0,2},{2,0},{4,6},{6,4},{8,10},{10,8},{12,14},{14,12},{1,3},{3,1},... | collective-permute-start | bytes 835592 | tf_op jit(solution)/shard_map/ppermute | solution.py:337
  47.6 0.0 collective-permute-done.10.refs_7_
  47.6 0.0 collective-permute-done.11.refs_6_
  47.6 1.0 %collective-permute-start.15 = (bf16[64,2304]{1,0:T(8,128)(2,1)S(1)}, bf16[64,2304]{1,0:T(8,128)(2,1)S(1)}, u32[]{:S(2)}, u32[]{:S(2)}) collective-permute-start(bf16[64,2304]{1,0:T(8,128)(2,1)S(1)} %collective-permute-done.11.refs_6_), channel_id=1, source_target_pairs={{0,4},{2,6},{4,8},{6,10},{8,12},{10,14},{12,0},{14,2},{1,5},{3,7},... | collective-permute-start | bytes 884744 | tf_op jit(solution)/shard_map/ppermute | solution.py:337
  48.6 0.0 collective-permute-done.12.refs_8_.refs_1_
  48.6 1.1 %score.4 = (f32[7,32,256]{2,1,0:T(8,128)S(1)}, f32[7,32,256]{2,1,0:T(8,128)S(1)}) custom-call(s32[1]{0:T(128)} %bitcast.1.half_ref, bf16[256,2176]{1,0:T(8,128)(2,1)S(1)} %stash.5.refs_0_, bf16[64,2176]{1,0:T(8,128)(2,1)S(1)} %collective-permute-done.2.refs_1_, bf16[64,2176]{1,0:T(8,128)(2,1)S(1)} %collective-permute-done.5.refs_2_, ...), custom_call_target="tpu_custom_call" | custom-call | flops 851443712 | bytes 1900544 | tf_op jit(solution)/shard_map/score/pallas_call | solution.py:247
  49.7 0.1 collective-permute-start.13
  49.8 1.3 %score.7 = (f32[7,32,256]{2,1,0:T(8,128)S(1)}, f32[7,32,256]{2,1,0:T(8,128)S(1)}) custom-call(s32[1]{0:T(128)} %bitcast.1.half_ref, bf16[256,2176]{1,0:T(8,128)(2,1)S(1)} %stash.5.refs_0_, bf16[64,2176]{1,0:T(8,128)(2,1)S(1)} %collective-permute-done.2.refs_1_, bf16[64,2176]{1,0:T(8,128)(2,1)S(1)} %collective-permute-done.5.refs_2_, ...), custom_call_target="tpu_custom_call" | custom-call | flops 1027604480 | bytes 2293760 | tf_op jit(solution)/shard_map/score/pallas_call | solution.py:247
  51.1 0.6 collective-permute-start.17
  51.6 0.0 collective-permute-done.13.b_ref
  51.6 0.6 collective-permute-start.14
  52.2 1.2 %collective-permute-done.16.refs_0_ = bf16[64,2176]{1,0:T(8,128)(2,1)S(1)} collective-permute-done((bf16[64,2176]{1,0:T(8,128)(2,1)S(1)}, bf16[64,2176]{1,0:T(8,128)(2,1)S(1)}, u32[]{:S(2)}, u32[]{:S(2)}) %collective-permute-start.16) | collective-permute-done | bytes 278560 | tf_op jit(solution)/shard_map/ppermute | solution.py:337
  53.4 0.8 %score.5 = (f32[64,256]{1,0:T(8,128)S(1)}, f32[64,256]{1,0:T(8,128)S(1)}) custom-call(s32[1]{0:T(128)} %bitcast.1.half_ref, bf16[64,2176]{1,0:T(8,128)(2,1)S(1)} %collective-permute-done.16.refs_0_, bf16[256,3712]{1,0:T(8,128)(2,1)S(1)} %collective-permute-done.12.refs_8_.refs_1_, bf16[256,4480]{1,0:T(8,128)(2,1)S(1)} %scale_codes.1.refs_2_.refs_8_), custom_call_target="tpu_custom_call" | custom-call | flops 268435456 | bytes 1900544 | tf_op jit(solution)/shard_map/score/pallas_call | solution.py:247
  54.2 2.6 %collective-permute-done.15.refs_0_ = bf16[64,2304]{1,0:T(8,128)(2,1)S(1)} collective-permute-done((bf16[64,2304]{1,0:T(8,128)(2,1)S(1)}, bf16[64,2304]{1,0:T(8,128)(2,1)S(1)}, u32[]{:S(2)}, u32[]{:S(2)}) %collective-permute-start.15) | collective-permute-done | bytes 294944 | tf_op jit(solution)/shard_map/ppermute | solution.py:337
  56.7 0.0 copy-start
  56.7 0.7 %score.6 = (f32[1,32,256]{2,1,0:T(8,128)S(1)}, f32[1,32,256]{2,1,0:T(8,128)S(1)}, f32[1,32,256]{2,1,0:T(8,128)S(1)}, f32[1,32,256]{2,1,0:T(8,128)S(1)}) custom-call(s32[1]{0:T(128)} %bitcast.1.half_ref, bf16[64,2304]{1,0:T(8,128)(2,1)S(1)} %collective-permute-done.15.refs_0_, bf16[256,3712]{1,0:T(8,128)(2,1)S(1)} %collective-permute-done.12.refs_8_.refs_1_, ...), custom_call_target="tpu_custom_call" | custom-call | flops 2684354560 | bytes 1900544 | tf_op jit(solution)/shard_map/score/pallas_call | solution.py:247
  57.5 0.1 collective-permute-start.18
  57.5 0.6 collective-permute-start.19
  58.1 1.3 %collective-permute-start.20 = (f32[1,32,256]{2,1,0:T(8,128)S(1)}, f32[1,32,256]{2,1,0:T(8,128)S(1)}, u32[]{:S(2)}, u32[]{:S(2)}) collective-permute-start(f32[1,32,256]{2,1,0:T(8,128)S(1)} %get-tuple-element.95), channel_id=1, source_target_pairs={{0,1},{1,0},{2,3},{3,2},{4,5},{5,4},{6,7},{7,6},{8,9},{9,8},{10,11... | collective-permute-start | bytes 98312 | tf_op jit(solution)/shard_map/ppermute | solution.py:372
  59.4 0.0 collective-permute-done.17
  59.4 0.0 collective-permute-done.14
  59.4 0.0 copy-done
  59.4 1.6 %place_scores.2.refs_0_ = f32[8,32,256]{2,1,0:T(8,128)} custom-call(s32[8]{0:T(128)S(1)} %stack.35.order_ref, s32[1,256]{1,0:T(1,128)S(1)} %copy-done, f32[224,256]{1,0:T(8,128)S(1)} %bitcast.20, f32[224,256]{1,0:T(8,128)S(1)} %bitcast.18, f32[224,256]{1,0:T(8,128)S(1)} %bitcast.19), custom_call_target="tpu_custom_call" | custom-call | tf_op jit(solution)/shard_map/place_scores/pallas_call | solution.py:302
  61.0 0.0 collective-permute-done.18
  61.0 0.6 collective-permute-done.19
  61.6 0.0 collective-permute-done.20
  61.6 1.4 %place_scores.3 = f32[8,32,256]{2,1,0:T(8,128)} custom-call(s32[8]{0:T(128)S(1)} %stack.35.order_ref, s32[1,256]{1,0:T(1,128)S(1)} %copy-done, f32[8,32,256]{2,1,0:T(8,128)} %place_scores.2.refs_0_, f32[32,256]{1,0:T(8,128)S(1)} %bitcast.22, f32[32,256]{1,0:T(8,128)S(1)} %bitcast.23, f32[32,256]{1,0:T(8,128)S(1)} %bitcast.24, ...), custom_call_target="tpu_custom_call", output_to_operand_aliasing={{}: (2, {})} | custom-call | tf_op jit(solution)/shard_map/place_scores/pallas_call | solution.py:302
  (5 shorter events, 0.2 us)
Async XLA Ops:
  2.2 46.4 %collective-permute-start.12 = (bf16[256,3712]{1,0:T(8,128)(2,1)S(1)}, bf16[256,3712]{1,0:T(8,128)(2,1)S(1)}, u32[]{:S(2)}, u32[]{:S(2)}) collective-permute-start(bf16[256,3712]{1,0:T(8,128)(2,1)S(1)} %get-tuple-element.78), channel_id=1, source_target_pairs={{0,16},{16,0},{1,17},{17,1},{2,18},{18,2},{3,19},{19,3},{4,20},{20... | collective-permute-start | bytes 5701640 | tf_op jit(solution)/shard_map/ppermute | solution.py:348
  5.2 11.7 %collective-permute-start.6 = (bf16[64,2304]{1,0:T(8,128)(2,1)S(1)}, bf16[64,2304]{1,0:T(8,128)(2,1)S(1)}, u32[]{:S(2)}, u32[]{:S(2)}) collective-permute-start(bf16[64,2304]{1,0:T(8,128)(2,1)S(1)} %get-tuple-element.68.refs_0_), channel_id=1, source_target_pairs={{0,4},{2,6},{4,8},{6,10},{8,12},{10,14},{12,0},{14,2},{1,5},{3,7},... | collective-permute-start | bytes 884744 | tf_op jit(solution)/shard_map/ppermute | solution.py:337
  6.8 10.2 %collective-permute-start.7 = (bf16[64,2304]{1,0:T(8,128)(2,1)S(1)}, bf16[64,2304]{1,0:T(8,128)(2,1)S(1)}, u32[]{:S(2)}, u32[]{:S(2)}) collective-permute-start(bf16[64,2304]{1,0:T(8,128)(2,1)S(1)} %get-tuple-element.68.refs_0_), channel_id=1, source_target_pairs={{0,2},{2,0},{4,6},{6,4},{8,10},{10,8},{12,14},{14,12},{1,3},{3,1},... | collective-permute-start | bytes 884744 | tf_op jit(solution)/shard_map/ppermute | solution.py:337
  8.3 14.6 %collective-permute-start = (bf16[64,2176]{1,0:T(8,128)(2,1)S(1)}, bf16[64,2176]{1,0:T(8,128)(2,1)S(1)}, u32[]{:S(2)}, u32[]{:S(2)}) collective-permute-start(bf16[64,2176]{1,0:T(8,128)(2,1)S(1)} %get-tuple-element.56.refs_0_), channel_id=1, source_target_pairs={{0,4},{2,6},{4,8},{6,10},{8,12},{10,14},{12,0},{14,2},{1,5},{3,7},... | collective-permute-start | bytes 835592 | tf_op jit(solution)/shard_map/ppermute | solution.py:337
  9.9 13.1 %collective-permute-start.1 = (bf16[64,2176]{1,0:T(8,128)(2,1)S(1)}, bf16[64,2176]{1,0:T(8,128)(2,1)S(1)}, u32[]{:S(2)}, u32[]{:S(2)}) collective-permute-start(bf16[64,2176]{1,0:T(8,128)(2,1)S(1)} %get-tuple-element.56.refs_0_), channel_id=1, source_target_pairs={{0,2},{2,0},{4,6},{6,4},{8,10},{10,8},{12,14},{14,12},{1,3},{3,1},... | collective-permute-start | bytes 835592 | tf_op jit(solution)/shard_map/ppermute | solution.py:337
  16.9 12.3 %collective-permute-start.8 = (bf16[64,2304]{1,0:T(8,128)(2,1)S(1)}, bf16[64,2304]{1,0:T(8,128)(2,1)S(1)}, u32[]{:S(2)}, u32[]{:S(2)}) collective-permute-start(bf16[64,2304]{1,0:T(8,128)(2,1)S(1)} %collective-permute-done.6.refs_1_), channel_id=1, source_target_pairs={{0,4},{2,6},{4,8},{6,10},{8,12},{10,14},{12,0},{14,2},{1,5},{3,7},... | collective-permute-start | bytes 884744 | tf_op jit(solution)/shard_map/ppermute | solution.py:337
  18.3 10.9 %collective-permute-start.9 = (bf16[64,2304]{1,0:T(8,128)(2,1)S(1)}, bf16[64,2304]{1,0:T(8,128)(2,1)S(1)}, u32[]{:S(2)}, u32[]{:S(2)}) collective-permute-start(bf16[64,2304]{1,0:T(8,128)(2,1)S(1)} %collective-permute-done.6.refs_1_), channel_id=1, source_target_pairs={{0,2},{2,0},{4,6},{6,4},{8,10},{10,8},{12,14},{14,12},{1,3},{3,1},... | collective-permute-start | bytes 884744 | tf_op jit(solution)/shard_map/ppermute | solution.py:337
  22.9 12.3 %collective-permute-start.2 = (bf16[64,2176]{1,0:T(8,128)(2,1)S(1)}, bf16[64,2176]{1,0:T(8,128)(2,1)S(1)}, u32[]{:S(2)}, u32[]{:S(2)}) collective-permute-start(bf16[64,2176]{1,0:T(8,128)(2,1)S(1)} %collective-permute-done.refs_1_), channel_id=1, source_target_pairs={{0,4},{2,6},{4,8},{6,10},{8,12},{10,14},{12,0},{14,2},{1,5},{3,7},... | collective-permute-start | bytes 835592 | tf_op jit(solution)/shard_map/ppermute | solution.py:337
  24.3 10.9 %collective-permute-start.3 = (bf16[64,2176]{1,0:T(8,128)(2,1)S(1)}, bf16[64,2176]{1,0:T(8,128)(2,1)S(1)}, u32[]{:S(2)}, u32[]{:S(2)}) collective-permute-start(bf16[64,2176]{1,0:T(8,128)(2,1)S(1)} %collective-permute-done.refs_1_), channel_id=1, source_target_pairs={{0,2},{2,0},{4,6},{6,4},{8,10},{10,8},{12,14},{14,12},{1,3},{3,1},... | collective-permute-start | bytes 835592 | tf_op jit(solution)/shard_map/ppermute | solution.py:337
  29.2 18.4 %collective-permute-start.10 = (bf16[64,2304]{1,0:T(8,128)(2,1)S(1)}, bf16[64,2304]{1,0:T(8,128)(2,1)S(1)}, u32[]{:S(2)}, u32[]{:S(2)}) collective-permute-start(bf16[64,2304]{1,0:T(8,128)(2,1)S(1)} %collective-permute-done.8.refs_5_), channel_id=1, source_target_pairs={{0,4},{2,6},{4,8},{6,10},{8,12},{10,14},{12,0},{14,2},{1,5},{3,7},... | collective-permute-start | bytes 884744 | tf_op jit(solution)/shard_map/ppermute | solution.py:337
  30.6 17.0 %collective-permute-start.11 = (bf16[64,2304]{1,0:T(8,128)(2,1)S(1)}, bf16[64,2304]{1,0:T(8,128)(2,1)S(1)}, u32[]{:S(2)}, u32[]{:S(2)}) collective-permute-start(bf16[64,2304]{1,0:T(8,128)(2,1)S(1)} %collective-permute-done.8.refs_5_), channel_id=1, source_target_pairs={{0,2},{2,0},{4,6},{6,4},{8,10},{10,8},{12,14},{14,12},{1,3},{3,1},... | collective-permute-start | bytes 884744 | tf_op jit(solution)/shard_map/ppermute | solution.py:337
  35.2 10.9 %collective-permute-start.4 = (bf16[64,2176]{1,0:T(8,128)(2,1)S(1)}, bf16[64,2176]{1,0:T(8,128)(2,1)S(1)}, u32[]{:S(2)}, u32[]{:S(2)}) collective-permute-start(bf16[64,2176]{1,0:T(8,128)(2,1)S(1)} %collective-permute-done.2.refs_1_), channel_id=1, source_target_pairs={{0,4},{2,6},{4,8},{6,10},{8,12},{10,14},{12,0},{14,2},{1,5},{3,7},... | collective-permute-start | bytes 835592 | tf_op jit(solution)/shard_map/ppermute | solution.py:337
  36.6 9.5 %collective-permute-start.5 = (bf16[64,2176]{1,0:T(8,128)(2,1)S(1)}, bf16[64,2176]{1,0:T(8,128)(2,1)S(1)}, u32[]{:S(2)}, u32[]{:S(2)}) collective-permute-start(bf16[64,2176]{1,0:T(8,128)(2,1)S(1)} %collective-permute-done.2.refs_1_), channel_id=1, source_target_pairs={{0,2},{2,0},{4,6},{6,4},{8,10},{10,8},{12,14},{14,12},{1,3},{3,1},... | collective-permute-start | bytes 835592 | tf_op jit(solution)/shard_map/ppermute | solution.py:337
  46.1 7.3 %collective-permute-start.16 = (bf16[64,2176]{1,0:T(8,128)(2,1)S(1)}, bf16[64,2176]{1,0:T(8,128)(2,1)S(1)}, u32[]{:S(2)}, u32[]{:S(2)}) collective-permute-start(bf16[64,2176]{1,0:T(8,128)(2,1)S(1)} %collective-permute-done.4.refs_3_), channel_id=1, source_target_pairs={{0,2},{2,0},{4,6},{6,4},{8,10},{10,8},{12,14},{14,12},{1,3},{3,1},... | collective-permute-start | bytes 835592 | tf_op jit(solution)/shard_map/ppermute | solution.py:337
  47.6 9.1 %collective-permute-start.15 = (bf16[64,2304]{1,0:T(8,128)(2,1)S(1)}, bf16[64,2304]{1,0:T(8,128)(2,1)S(1)}, u32[]{:S(2)}, u32[]{:S(2)}) collective-permute-start(bf16[64,2304]{1,0:T(8,128)(2,1)S(1)} %collective-permute-done.11.refs_6_), channel_id=1, source_target_pairs={{0,4},{2,6},{4,8},{6,10},{8,12},{10,14},{12,0},{14,2},{1,5},{3,7},... | collective-permute-start | bytes 884744 | tf_op jit(solution)/shard_map/ppermute | solution.py:337
  49.7 1.9 %collective-permute-start.13 = (f32[7,32,256]{2,1,0:T(8,128)S(1)}, f32[7,32,256]{2,1,0:T(8,128)S(1)}, u32[]{:S(2)}, u32[]{:S(2)}) collective-permute-start(f32[7,32,256]{2,1,0:T(8,128)S(1)} %get-tuple-element.80), channel_id=1, source_target_pairs={{0,1},{1,0},{2,3},{3,2},{4,5},{5,4},{6,7},{7,6},{8,9},{9,8},{10,11... | collective-permute-start | bytes 688136 | tf_op jit(solution)/shard_map/ppermute | solution.py:372
  51.1 8.3 %collective-permute-start.17 = (f32[7,32,256]{2,1,0:T(8,128)S(1)}, f32[7,32,256]{2,1,0:T(8,128)S(1)}, u32[]{:S(2)}, u32[]{:S(2)}) collective-permute-start(f32[7,32,256]{2,1,0:T(8,128)S(1)} %get-tuple-element.92), channel_id=1, source_target_pairs={{0,1},{1,0},{2,3},{3,2},{4,5},{5,4},{6,7},{7,6},{8,9},{9,8},{10,11... | collective-permute-start | bytes 688136 | tf_op jit(solution)/shard_map/ppermute | solution.py:372
  51.6 7.8 %collective-permute-start.14 = (f32[7,32,256]{2,1,0:T(8,128)S(1)}, f32[7,32,256]{2,1,0:T(8,128)S(1)}, u32[]{:S(2)}, u32[]{:S(2)}) collective-permute-start(f32[7,32,256]{2,1,0:T(8,128)S(1)} %add.80), channel_id=1, source_target_pairs={{0,16},{16,0},{1,17},{17,1},{2,18},{18,2},{3,19},{19,3},{4,20},{20... | collective-permute-start | bytes 688136 | tf_op jit(solution)/shard_map/ppermute | solution.py:376
  56.7 2.7 %copy-start = (s32[1,256]{1,0:T(1,128)S(1)}, s32[1,256]{1,0:T(1,128)}, u32[]{:S(2)}) copy-start(s32[1,256]{1,0:T(1,128)} %ids_ref.3) | copy-start | bytes 3076
  57.5 3.5 %collective-permute-start.18 = (f32[1,32,256]{2,1,0:T(8,128)S(1)}, f32[1,32,256]{2,1,0:T(8,128)S(1)}, u32[]{:S(2)}, u32[]{:S(2)}) collective-permute-start(f32[1,32,256]{2,1,0:T(8,128)S(1)} %get-tuple-element.93), channel_id=1, source_target_pairs={{0,17},{1,16},{16,1},{17,0},{2,19},{3,18},{18,3},{19,2},{4,21},{5,... | collective-permute-start | bytes 98312 | tf_op jit(solution)/shard_map/ppermute | solution.py:387
  57.5 4.0 %collective-permute-start.19 = (f32[1,32,256]{2,1,0:T(8,128)S(1)}, f32[1,32,256]{2,1,0:T(8,128)S(1)}, u32[]{:S(2)}, u32[]{:S(2)}) collective-permute-start(f32[1,32,256]{2,1,0:T(8,128)S(1)} %get-tuple-element.94), channel_id=1, source_target_pairs={{0,16},{16,0},{1,17},{17,1},{2,18},{18,2},{3,19},{19,3},{4,20},{20... | collective-permute-start | bytes 98312 | tf_op jit(solution)/shard_map/ppermute | solution.py:388
  58.1 3.5 %collective-permute-start.20 = (f32[1,32,256]{2,1,0:T(8,128)S(1)}, f32[1,32,256]{2,1,0:T(8,128)S(1)}, u32[]{:S(2)}, u32[]{:S(2)}) collective-permute-start(f32[1,32,256]{2,1,0:T(8,128)S(1)} %get-tuple-element.95), channel_id=1, source_target_pairs={{0,1},{1,0},{2,3},{3,2},{4,5},{5,4},{6,7},{7,6},{8,9},{9,8},{10,11... | collective-permute-start | bytes 98312 | tf_op jit(solution)/shard_map/ppermute | solution.py:372

commit v9 on v8

--- a/solution.py
+++ b/solution.py
@@ -10,6 +10,7 @@
 BLOCK = 128
 ALONE = 29
 LATE_WEIGHT = 10
+LEAD = 0
 CHUNKS = 2
 VMEM = pl.BlockSpec(memory_space=pltpu.VMEM)
 SMEM = pl.BlockSpec(memory_space=pltpu.SMEM)
@@ -272,43 +273,34 @@
     )(*in_vmem([a, b]))
 
 
-def place_kernel(first, order_ref, ids_ref, *refs):
-    *share_refs, out_ref, placed_ref, sems = refs
-    share_refs = share_refs[1:] if first else share_refs
-    blocks, rows, count = placed_ref.shape
+def place_kernel(groups, order_ref, ids_ref, *refs):
+    *share_refs, out_ref = refs
+    share_refs = list(share_refs)
+    _, rows, count = out_ref.shape
     slots = lax.broadcasted_iota(jnp.int32, (count, count), 0)
     table = (slots == jnp.broadcast_to(ids_ref[...], (count, count))).astype(jnp.float32).astype(jnp.bfloat16)
-    raw = functools.reduce(jnp.add, [ref[...] for ref in share_refs])
+    raw = [functools.reduce(jnp.add, [share_refs.pop(0)[...] for _ in range(shares)]) for shares in groups]
+    raw = jnp.concatenate(raw, axis=0)
     high = raw.astype(jnp.bfloat16)
     rest = raw - high.astype(jnp.float32)
     middle = rest.astype(jnp.bfloat16)
     low = (rest - middle.astype(jnp.float32)).astype(jnp.bfloat16)
     placed = (dot(high, table) + dot(middle, table)) + dot(low, table)
-    copies = []
-    for j in range(blocks):
-        placed_ref[j] = placed[j * rows : (j + 1) * rows]
-        copies.append(pltpu.make_async_copy(placed_ref.at[j], out_ref.at[order_ref[first + j]], sems.at[j]))
-        copies[-1].start()
-    for copy in copies:
-        copy.wait()
-
-
-def place(order, ids, out, first, shares, rows):
+    for j in range(raw.shape[0] // rows):
+        out_ref[order_ref[j]] = placed[j * rows : (j + 1) * rows]
+
+
+def place(order, ids, groups, rows):
     count = ids.shape[1]
-    shares = [share.reshape(-1, count) for share in shares]
-    blocks = shares[0].shape[0] // rows
-    anywhere = pl.BlockSpec(memory_space=pl.ANY)
-    given = [in_hbm(out)] if first else []
-    return pl.pallas_call(
-        functools.partial(place_kernel, first),
-        out_shape=pltpu.HBM((order.shape[0], rows, count), jnp.float32),
-        in_specs=[SMEM, VMEM] + [anywhere] * len(given) + [VMEM] * len(shares),
-        out_specs=anywhere,
-        input_output_aliases={2: 0} if given else {},
-        scratch_shapes=[pltpu.VMEM((blocks, rows, count), jnp.float32), pltpu.SemaphoreType.DMA((blocks,))],
+    shares = [share.reshape(-1, count) for group in groups for share in group]
+    return pl.pallas_call(
+        functools.partial(place_kernel, [len(group) for group in groups]),
+        out_shape=jax.ShapeDtypeStruct((order.shape[0], rows, count), jnp.float32),
+        in_specs=[SMEM, VMEM] + [VMEM] * len(shares),
+        out_specs=VMEM,
         compiler_params=pltpu.CompilerParams(vmem_limit_bytes=16 << 20),
         name="place_scores",
-    )(order, ids, *given, *in_vmem(shares))
+    )(order, ids, *in_vmem(shares))
 
 
 def shards(fast, parts, total, queries, codes, exponents, example_ids):
@@ -327,7 +319,7 @@
     blocks = exponents.shape[1]
     alone = blocks * ALONE // 64
     held = blocks - alone
-    cuts = [i * held // CHUNKS * BLOCK for i in range(CHUNKS + 1)]
+    cuts = [-(-i * held // CHUNKS) * BLOCK for i in range(CHUNKS + 1)]
 
     def step(value, length, stride):
         pairs = [
@@ -352,44 +344,49 @@
         return arrays if rows % 16 == 0 else [jnp.concatenate(arrays, axis=0)]
 
     kept_rows = (slow - 2) * fast * rows
-    early, late = [], []
-    for c, chunk in enumerate(chunks):
-        held = []
-        for s in range(slow - 1):
-            tied = [step(chunk, slow, fast), *along_fast(chunk)] + held
-            if c == CHUNKS - 1 and s == 0:
+    early, late = [None] * CHUNKS, [None] * CHUNKS
+    held = [[] for _ in range(CHUNKS)]
+    for s in range(slow - 1):
+        for c in (LEAD, 1 - LEAD):
+            tied = [step(chunks[c], slow, fast), *along_fast(chunks[c])] + held[c]
+            if s == 0 and c == LEAD:
                 *tied, ours = lax.optimization_barrier(tied + [ours])
+            elif s == slow - 2 and c != LEAD:
+                begun_own = score(half, 0, early[LEAD:LEAD + 1], [ours], cuts[LEAD])
+                *tied, begun_own = lax.optimization_barrier(tied + list(begun_own))
             else:
                 tied = lax.optimization_barrier(tied)
-            chunk, values, held = tied[0], tied[1 : fast + 1], tied[fast + 1 :]
+            chunks[c], values, kept = tied[0], tied[1 : fast + 1], tied[fast + 1 :]
             if s < slow - 2:
-                held = [stash(held[0] if s else None, stack(values), s * fast * rows, kept_rows)]
-        early.append(held + stack(values + [chunk]))
-        along = along_fast(chunk)[1:] if c < CHUNKS - 1 else [step(value, slow, fast) for value in values[1:]]
-        late.append(stack(along))
+                held[c] = [stash(kept[0] if s else None, stack(values), s * fast * rows, kept_rows)]
+                continue
+            early[c] = kept + stack(values + [chunks[c]])
+            late[c] = stack(
+                along_fast(chunks[c])[1:] if c == LEAD else [step(value, slow, fast) for value in values[1:]]
+            )
 
     def over_dim(value):
         return lax.ppermute(value, "dim", [(0, 1), (1, 0)])
 
+    lead, trail = slice(LEAD, LEAD + 1), slice(1 - LEAD, 2 - LEAD)
     keep, send = score(half, rows, early, [theirs])
     added, theirs = lax.optimization_barrier((add(keep, over_dim(send)), theirs))
     given = lax.ppermute(added, "groups", swap)
-    keep, send = score(half, rows, early, [ours])
+    keep, send = score(half, rows, early[trail], [ours], cuts[1 - LEAD], [begun_own])
     shares = [given, keep, over_dim(send)]
 
-    begun = score(half, 0, late[:-1], [theirs, ours])
-    last = score(half, rows, late[-1:], [theirs, ours], cuts[-2], begun, LATE_WEIGHT)
-    *last, shares[1] = lax.optimization_barrier((*last, shares[1]))
-    out = place(order, example_ids, None, 0, shares, rows // 2)
-    their_keep, their_send, keep, send = last
+    begun = score(half, 0, late[lead], [theirs, ours], cuts[LEAD])
+    their_keep, their_send, own_keep, own_send = score(
+        half, rows, late[trail], [theirs, ours], cuts[1 - LEAD], begun, LATE_WEIGHT
+    )
     across = [(i, 3 - i) for i in range(4)]
-    shares = [
+    last = [
         lax.ppermute(their_send, ("groups", "dim"), across),
         lax.ppermute(their_keep, "groups", swap),
-        over_dim(send),
-        keep,
+        over_dim(own_send),
+        own_keep,
     ]
-    return place(order, example_ids, out, total - fast + 1, shares, rows // 2)
+    return place(order, example_ids, [shares, last], rows // 2)
 
 
 def solution(mesh):

time: 63.2 us -> 62.4 us (0.987)
  Pallas kernels: 11.7 us -> 10.5 us
    ppermute x14, waiting for transfers between devices: 25.2 us -> 23.1 us  [step(): return lax.ppermute(value, 'ex', pairs)]
    ppermute x1, waiting for transfers between devices: 0.01 us -> 1.71 us  [shards(): lax.ppermute(their_send, ('groups', 'dim'), across)]
    pallas_call x2 -> x1, Pallas kernels: 3 us -> 1.58 us  [place(): pl.pallas_call(functools.partial(place_kernel, [len(group) for group in g...]
    pallas_call x4 -> x5, Pallas kernels: 3.86 us -> 4.01 us  [score(): pl.pallas_call(functools.partial(score_kernel, [len(arrays) for arrays in...]
  transfers between devices with their start and end apart: 21 -> 21, of which waited for: 8 -> 11; matrix products, arithmetic and copies ran while one was open for 0% -> 0% of each run, Pallas kernels for 13% -> 11%
where the time goes in v9:
time: 62.4 us; the launch traced here: 62.2 us
  starting transfers between devices  25.9 us (42%)
  waiting for transfers between devices  25.7 us (41%)
  Pallas kernels  10.5 us (17%)
    ppermute x14, waiting for transfers between devices, step(): return lax.ppermute(value, 'ex', pairs)  23.1 us
    ppermute x14, starting transfers between devices, step(): return lax.ppermute(value, 'ex', pairs)  19.7 us
    pallas_call x5, Pallas kernels, score(): pl.pallas_call(functools.partial(score_kernel, [len(arrays) for arrays in...  4.01 us
    ppermute x1, starting transfers between devices, shards(): theirs = lax.ppermute(sent, 'groups', swap)  3.03 us
    pallas_call x1, Pallas kernels, scale(): pl.pallas_call(functools.partial(scale_kernel, alone), out_shape=pltpu.VM...  2.6 us
    pallas_call x1, Pallas kernels, cut(): pl.pallas_call(functools.partial(cut_kernel, alone, cuts), out_shape=[plt...  2.09 us
    ppermute x3, starting transfers between devices, over_dim(): return lax.ppermute(value, 'dim', [(0, 1), (1, 0)])  1.91 us
    ppermute x1, waiting for transfers between devices, shards(): lax.ppermute(their_send, ('groups', 'dim'), across)  1.71 us
  transfers between devices with their start and end apart: 21, of which 11 were waited for; matrix products, arithmetic and copies ran while one was open for 0% of the time, Pallas kernels for 11%

profile of v9, /device:TPU:0, one launch (start us, length us, event | category | flops | bytes accessed | tf_op | source)
XLA Modules:
  0.0 62.2 jit_solution(5354991710249541817)
XLA Ops:
  0.0 0.1 stack.35.order_ref
  0.1 2.1 %cut_queries.1 = (bf16[64,2304]{1,0:T(8,128)(2,1)S(1)}, bf16[64,2176]{1,0:T(8,128)(2,1)S(1)}, bf16[256,3712]{1,0:T(8,128)(2,1)S(1)}) custom-call(s32[1]{0:T(128)} %bitcast.part_ref, bf16[1,64,8192]{2,1,0:T(8,128)(2,1)} %queries_ref.1, bf16[256,8192]{1,0:T(8,128)(2,1)} %codes_ref.3, s32[64,256]{1,0:T(8,128)} %bitcast.25), custom_call_target="tpu_custom_call" | custom-call | flops 2097152 | bytes 4194304 | tf_op jit(solution)/shard_map/cut_queries/pallas_call | solution.py:119
  2.2 3.0 %collective-permute-start.12 = (bf16[256,3712]{1,0:T(8,128)(2,1)S(1)}, bf16[256,3712]{1,0:T(8,128)(2,1)S(1)}, u32[]{:S(2)}, u32[]{:S(2)}) collective-permute-start(bf16[256,3712]{1,0:T(8,128)(2,1)S(1)} %get-tuple-element.75), channel_id=1, source_target_pairs={{0,16},{16,0},{1,17},{17,1},{2,18},{18,2},{3,19},{19,3},{4,20},{20... | collective-permute-start | bytes 5701640 | tf_op jit(solution)/shard_map/ppermute | solution.py:340
  5.2 1.6 %collective-permute-start = (bf16[64,2304]{1,0:T(8,128)(2,1)S(1)}, bf16[64,2304]{1,0:T(8,128)(2,1)S(1)}, u32[]{:S(2)}, u32[]{:S(2)}) collective-permute-start(bf16[64,2304]{1,0:T(8,128)(2,1)S(1)} %get-tuple-element.52.refs_0_), channel_id=1, source_target_pairs={{0,4},{2,6},{4,8},{6,10},{8,12},{10,14},{12,0},{14,2},{1,5},{3,7},... | collective-permute-start | bytes 884744 | tf_op jit(solution)/shard_map/ppermute | solution.py:329
  6.8 1.5 %collective-permute-start.1 = (bf16[64,2304]{1,0:T(8,128)(2,1)S(1)}, bf16[64,2304]{1,0:T(8,128)(2,1)S(1)}, u32[]{:S(2)}, u32[]{:S(2)}) collective-permute-start(bf16[64,2304]{1,0:T(8,128)(2,1)S(1)} %get-tuple-element.52.refs_0_), channel_id=1, source_target_pairs={{0,2},{2,0},{4,6},{6,4},{8,10},{10,8},{12,14},{14,12},{1,3},{3,1},... | collective-permute-start | bytes 884744 | tf_op jit(solution)/shard_map/ppermute | solution.py:329
  8.3 1.6 %collective-permute-start.6 = (bf16[64,2176]{1,0:T(8,128)(2,1)S(1)}, bf16[64,2176]{1,0:T(8,128)(2,1)S(1)}, u32[]{:S(2)}, u32[]{:S(2)}) collective-permute-start(bf16[64,2176]{1,0:T(8,128)(2,1)S(1)} %get-tuple-element.64.refs_0_), channel_id=1, source_target_pairs={{0,4},{2,6},{4,8},{6,10},{8,12},{10,14},{12,0},{14,2},{1,5},{3,7},... | collective-permute-start | bytes 835592 | tf_op jit(solution)/shard_map/ppermute | solution.py:329
  9.9 0.5 collective-permute-start.7
  10.4 2.6 %scale_codes.1.refs_4_.refs_2_ = bf16[256,4480]{1,0:T(8,128)(2,1)S(1)} custom-call(s32[1]{0:T(128)} %bitcast.part_ref, bf16[256,8192]{1,0:T(8,128)(2,1)} %codes_ref.3, s32[64,256]{1,0:T(8,128)} %bitcast.26), custom_call_target="tpu_custom_call" | custom-call | flops 2097152 | bytes 8388608 | tf_op jit(solution)/shard_map/scale_codes/pallas_call | solution.py:157
  13.0 3.9 %collective-permute-done.refs_1_ = bf16[64,2304]{1,0:T(8,128)(2,1)S(1)} collective-permute-done((bf16[64,2304]{1,0:T(8,128)(2,1)S(1)}, bf16[64,2304]{1,0:T(8,128)(2,1)S(1)}, u32[]{:S(2)}, u32[]{:S(2)}) %collective-permute-start) | collective-permute-done | bytes 294944 | tf_op jit(solution)/shard_map/ppermute | solution.py:329
  16.9 0.0 collective-permute-done.1.refs_1_
  16.9 1.4 %collective-permute-start.2 = (bf16[64,2304]{1,0:T(8,128)(2,1)S(1)}, bf16[64,2304]{1,0:T(8,128)(2,1)S(1)}, u32[]{:S(2)}, u32[]{:S(2)}) collective-permute-start(bf16[64,2304]{1,0:T(8,128)(2,1)S(1)} %collective-permute-done.refs_1_), channel_id=1, source_target_pairs={{0,4},{2,6},{4,8},{6,10},{8,12},{10,14},{12,0},{14,2},{1,5},{3,7},... | collective-permute-start | bytes 884744 | tf_op jit(solution)/shard_map/ppermute | solution.py:329
  18.3 1.5 %collective-permute-start.3 = (bf16[64,2304]{1,0:T(8,128)(2,1)S(1)}, bf16[64,2304]{1,0:T(8,128)(2,1)S(1)}, u32[]{:S(2)}, u32[]{:S(2)}) collective-permute-start(bf16[64,2304]{1,0:T(8,128)(2,1)S(1)} %collective-permute-done.refs_1_), channel_id=1, source_target_pairs={{0,2},{2,0},{4,6},{6,4},{8,10},{10,8},{12,14},{14,12},{1,3},{3,1},... | collective-permute-start | bytes 884744 | tf_op jit(solution)/shard_map/ppermute | solution.py:329
  19.8 3.1 %collective-permute-done.6.refs_1_ = bf16[64,2176]{1,0:T(8,128)(2,1)S(1)} collective-permute-done((bf16[64,2176]{1,0:T(8,128)(2,1)S(1)}, bf16[64,2176]{1,0:T(8,128)(2,1)S(1)}, u32[]{:S(2)}, u32[]{:S(2)}) %collective-permute-start.6) | collective-permute-done | bytes 278560 | tf_op jit(solution)/shard_map/ppermute | solution.py:329
  22.9 0.0 collective-permute-done.7.refs_1_
  22.9 1.4 %collective-permute-start.8 = (bf16[64,2176]{1,0:T(8,128)(2,1)S(1)}, bf16[64,2176]{1,0:T(8,128)(2,1)S(1)}, u32[]{:S(2)}, u32[]{:S(2)}) collective-permute-start(bf16[64,2176]{1,0:T(8,128)(2,1)S(1)} %collective-permute-done.6.refs_1_), channel_id=1, source_target_pairs={{0,4},{2,6},{4,8},{6,10},{8,12},{10,14},{12,0},{14,2},{1,5},{3,7},... | collective-permute-start | bytes 835592 | tf_op jit(solution)/shard_map/ppermute | solution.py:329
  24.3 1.5 %collective-permute-start.9 = (bf16[64,2176]{1,0:T(8,128)(2,1)S(1)}, bf16[64,2176]{1,0:T(8,128)(2,1)S(1)}, u32[]{:S(2)}, u32[]{:S(2)}) collective-permute-start(bf16[64,2176]{1,0:T(8,128)(2,1)S(1)} %collective-permute-done.6.refs_1_), channel_id=1, source_target_pairs={{0,2},{2,0},{4,6},{6,4},{8,10},{10,8},{12,14},{14,12},{1,3},{3,1},... | collective-permute-start | bytes 835592 | tf_op jit(solution)/shard_map/ppermute | solution.py:329
  25.8 3.4 %collective-permute-done.2.refs_1_ = bf16[64,2304]{1,0:T(8,128)(2,1)S(1)} collective-permute-done((bf16[64,2304]{1,0:T(8,128)(2,1)S(1)}, bf16[64,2304]{1,0:T(8,128)(2,1)S(1)}, u32[]{:S(2)}, u32[]{:S(2)}) %collective-permute-start.2) | collective-permute-done | bytes 294944 | tf_op jit(solution)/shard_map/ppermute | solution.py:329
  29.2 0.0 collective-permute-done.3.refs_2_
  29.2 1.4 %collective-permute-start.4 = (bf16[64,2304]{1,0:T(8,128)(2,1)S(1)}, bf16[64,2304]{1,0:T(8,128)(2,1)S(1)}, u32[]{:S(2)}, u32[]{:S(2)}) collective-permute-start(bf16[64,2304]{1,0:T(8,128)(2,1)S(1)} %collective-permute-done.2.refs_1_), channel_id=1, source_target_pairs={{0,4},{2,6},{4,8},{6,10},{8,12},{10,14},{12,0},{14,2},{1,5},{3,7},... | collective-permute-start | bytes 884744 | tf_op jit(solution)/shard_map/ppermute | solution.py:329
  30.6 1.5 %collective-permute-start.5 = (bf16[64,2304]{1,0:T(8,128)(2,1)S(1)}, bf16[64,2304]{1,0:T(8,128)(2,1)S(1)}, u32[]{:S(2)}, u32[]{:S(2)}) collective-permute-start(bf16[64,2304]{1,0:T(8,128)(2,1)S(1)} %collective-permute-done.2.refs_1_), channel_id=1, source_target_pairs={{0,2},{2,0},{4,6},{6,4},{8,10},{10,8},{12,14},{14,12},{1,3},{3,1},... | collective-permute-start | bytes 884744 | tf_op jit(solution)/shard_map/ppermute | solution.py:329
  32.1 3.1 %collective-permute-done.8.refs_5_.refs_1_ = bf16[64,2176]{1,0:T(8,128)(2,1)S(1)} collective-permute-done((bf16[64,2176]{1,0:T(8,128)(2,1)S(1)}, bf16[64,2176]{1,0:T(8,128)(2,1)S(1)}, u32[]{:S(2)}, u32[]{:S(2)}) %collective-permute-start.8) | collective-permute-done | bytes 278560 | tf_op jit(solution)/shard_map/ppermute | solution.py:329
  35.2 0.0 collective-permute-done.9.refs_2_
  35.2 1.4 %collective-permute-start.10 = (bf16[64,2176]{1,0:T(8,128)(2,1)S(1)}, bf16[64,2176]{1,0:T(8,128)(2,1)S(1)}, u32[]{:S(2)}, u32[]{:S(2)}) collective-permute-start(bf16[64,2176]{1,0:T(8,128)(2,1)S(1)} %collective-permute-done.8.refs_5_.refs_1_), channel_id=1, source_target_pairs={{0,4},{2,6},{4,8},{6,10},{8,12},{10,14},{12,0},{14,2},{1,5},{3,7},... | collective-permute-start | bytes 835592 | tf_op jit(solution)/shard_map/ppermute | solution.py:329
  36.6 1.5 %collective-permute-start.11 = (bf16[64,2176]{1,0:T(8,128)(2,1)S(1)}, bf16[64,2176]{1,0:T(8,128)(2,1)S(1)}, u32[]{:S(2)}, u32[]{:S(2)}) collective-permute-start(bf16[64,2176]{1,0:T(8,128)(2,1)S(1)} %collective-permute-done.8.refs_5_.refs_1_), channel_id=1, source_target_pairs={{0,2},{2,0},{4,6},{6,4},{8,10},{10,8},{12,14},{14,12},{1,3},{3,1},... | collective-permute-start | bytes 835592 | tf_op jit(solution)/shard_map/ppermute | solution.py:329
  38.2 3.4 %collective-permute-done.4.refs_3_ = bf16[64,2304]{1,0:T(8,128)(2,1)S(1)} collective-permute-done((bf16[64,2304]{1,0:T(8,128)(2,1)S(1)}, bf16[64,2304]{1,0:T(8,128)(2,1)S(1)}, u32[]{:S(2)}, u32[]{:S(2)}) %collective-permute-start.4) | collective-permute-done | bytes 294944 | tf_op jit(solution)/shard_map/ppermute | solution.py:329
  41.5 0.0 collective-permute-done.5.refs_2_
  41.5 1.5 %collective-permute-start.17 = (bf16[64,2304]{1,0:T(8,128)(2,1)S(1)}, bf16[64,2304]{1,0:T(8,128)(2,1)S(1)}, u32[]{:S(2)}, u32[]{:S(2)}) collective-permute-start(bf16[64,2304]{1,0:T(8,128)(2,1)S(1)} %collective-permute-done.4.refs_3_), channel_id=1, source_target_pairs={{0,2},{2,0},{4,6},{6,4},{8,10},{10,8},{12,14},{14,12},{1,3},{3,1},... | collective-permute-start | bytes 884744 | tf_op jit(solution)/shard_map/ppermute | solution.py:329
  43.0 0.7 %score.5.refs_5_ = f32[448,256]{1,0:T(8,128)S(1)} custom-call(s32[1]{0:T(128)} %bitcast.1.half_ref, bf16[256,2304]{1,0:T(8,128)(2,1)S(1)} %stash.5.refs_0_, bf16[64,2304]{1,0:T(8,128)(2,1)S(1)} %collective-permute-done.2.refs_1_, bf16[64,2304]{1,0:T(8,128)(2,1)S(1)} %collective-permute-done.5.refs_2_, bf16[64,2304]{1,0:T(8,128)(2,1)S(1)} %collective-permute-done.4.refs_3_, ...), custom_call_target="tpu_custom_call" | custom-call | flops 1027604480 | bytes 2293760 | tf_op jit(solution)/shard_map/score/pallas_call | solution.py:248
  43.7 2.3 %collective-permute-done.10.refs_7_.refs_3_ = bf16[64,2176]{1,0:T(8,128)(2,1)S(1)} collective-permute-done((bf16[64,2176]{1,0:T(8,128)(2,1)S(1)}, bf16[64,2176]{1,0:T(8,128)(2,1)S(1)}, u32[]{:S(2)}, u32[]{:S(2)}) %collective-permute-start.10) | collective-permute-done | bytes 278560 | tf_op jit(solution)/shard_map/ppermute | solution.py:329
  46.1 1.2 %collective-permute-done.11.refs_6_.refs_2_ = bf16[64,2176]{1,0:T(8,128)(2,1)S(1)} collective-permute-done((bf16[64,2176]{1,0:T(8,128)(2,1)S(1)}, bf16[64,2176]{1,0:T(8,128)(2,1)S(1)}, u32[]{:S(2)}, u32[]{:S(2)}) %collective-permute-start.11) | collective-permute-done | bytes 278560 | tf_op jit(solution)/shard_map/ppermute | solution.py:329
  47.3 1.6 %collective-permute-start.16 = (bf16[64,2176]{1,0:T(8,128)(2,1)S(1)}, bf16[64,2176]{1,0:T(8,128)(2,1)S(1)}, u32[]{:S(2)}, u32[]{:S(2)}) collective-permute-start(bf16[64,2176]{1,0:T(8,128)(2,1)S(1)} %collective-permute-done.11.refs_6_.refs_2_), channel_id=1, source_target_pairs={{0,4},{2,6},{4,8},{6,10},{8,12},{10,14},{12,0},{14,2},{1,5},{3,7},... | collective-permute-start | bytes 835592 | tf_op jit(solution)/shard_map/ppermute | solution.py:329
  48.9 0.0 collective-permute-done.12.refs_8_.refs_1_
  48.9 1.1 %score.6 = (f32[7,32,256]{2,1,0:T(8,128)S(1)}, f32[7,32,256]{2,1,0:T(8,128)S(1)}) custom-call(s32[1]{0:T(128)} %bitcast.1.half_ref, bf16[256,2304]{1,0:T(8,128)(2,1)S(1)} %stash.5.refs_0_, bf16[64,2304]{1,0:T(8,128)(2,1)S(1)} %collective-permute-done.2.refs_1_, bf16[64,2304]{1,0:T(8,128)(2,1)S(1)} %collective-permute-done.5.refs_2_, ...), custom_call_target="tpu_custom_call" | custom-call | flops 851443712 | bytes 1900544 | tf_op jit(solution)/shard_map/score/pallas_call | solution.py:248
  49.9 0.1 collective-permute-start.13
  50.0 0.7 %score.7 = (f32[7,32,256]{2,1,0:T(8,128)S(1)}, f32[7,32,256]{2,1,0:T(8,128)S(1)}) custom-call(s32[1]{0:T(128)} %bitcast.1.half_ref, bf16[256,2176]{1,0:T(8,128)(2,1)S(1)} %stash.7.refs_4_.refs_0_, bf16[64,2176]{1,0:T(8,128)(2,1)S(1)} %collective-permute-done.8.refs_5_.refs_1_, bf16[64,2176]{1,0:T(8,128)(2,1)S(1)} %collective-permute-done.11.refs_6_.refs_2_, ...), custom_call_target="tpu_custom_call" | custom-call | flops 1027604480 | bytes 2293760 | tf_op jit(solution)/shard_map/score/pallas_call | solution.py:248
  50.8 0.6 collective-permute-start.15
  51.3 0.2 collective-permute-done.13.b_ref
  51.5 0.6 collective-permute-start.14
  52.1 0.0 collective-permute-done.17.refs_0_
  52.1 0.8 %score.8 = (f32[64,256]{1,0:T(8,128)S(1)}, f32[64,256]{1,0:T(8,128)S(1)}) custom-call(s32[1]{0:T(128)} %bitcast.1.half_ref, bf16[64,2304]{1,0:T(8,128)(2,1)S(1)} %collective-permute-done.17.refs_0_, bf16[256,3712]{1,0:T(8,128)(2,1)S(1)} %collective-permute-done.12.refs_8_.refs_1_, bf16[256,4480]{1,0:T(8,128)(2,1)S(1)} %scale_codes.1.refs_4_.refs_2_), custom_call_target="tpu_custom_call" | custom-call | flops 268435456 | bytes 1900544 | tf_op jit(solution)/shard_map/score/pallas_call | solution.py:248
  52.9 2.7 %collective-permute-done.16.refs_0_ = bf16[64,2176]{1,0:T(8,128)(2,1)S(1)} collective-permute-done((bf16[64,2176]{1,0:T(8,128)(2,1)S(1)}, bf16[64,2176]{1,0:T(8,128)(2,1)S(1)}, u32[]{:S(2)}, u32[]{:S(2)}) %collective-permute-start.16) | collective-permute-done | bytes 278560 | tf_op jit(solution)/shard_map/ppermute | solution.py:329
  55.6 0.0 copy-start
  55.6 0.7 %score.9 = (f32[1,32,256]{2,1,0:T(8,128)S(1)}, f32[1,32,256]{2,1,0:T(8,128)S(1)}, f32[1,32,256]{2,1,0:T(8,128)S(1)}, f32[1,32,256]{2,1,0:T(8,128)S(1)}) custom-call(s32[1]{0:T(128)} %bitcast.1.half_ref, bf16[64,2176]{1,0:T(8,128)(2,1)S(1)} %collective-permute-done.16.refs_0_, bf16[256,3712]{1,0:T(8,128)(2,1)S(1)} %collective-permute-done.12.refs_8_.refs_1_, ...), custom_call_target="tpu_custom_call" | custom-call | flops 2684354560 | bytes 1900544 | tf_op jit(solution)/shard_map/score/pallas_call | solution.py:248
  56.3 0.1 collective-permute-start.18
  56.4 0.6 collective-permute-start.19
  57.0 1.3 %collective-permute-start.20 = (f32[1,32,256]{2,1,0:T(8,128)S(1)}, f32[1,32,256]{2,1,0:T(8,128)S(1)}, u32[]{:S(2)}, u32[]{:S(2)}) collective-permute-start(f32[1,32,256]{2,1,0:T(8,128)S(1)} %get-tuple-element.87), channel_id=1, source_target_pairs={{0,1},{1,0},{2,3},{3,2},{4,5},{5,4},{6,7},{7,6},{8,9},{9,8},{10,11... | collective-permute-start | bytes 98312 | tf_op jit(solution)/shard_map/ppermute | solution.py:369
  58.2 0.0 collective-permute-done.15
  58.2 1.7 %collective-permute-done.18 = f32[1,32,256]{2,1,0:T(8,128)S(1)} collective-permute-done((f32[1,32,256]{2,1,0:T(8,128)S(1)}, f32[1,32,256]{2,1,0:T(8,128)S(1)}, u32[]{:S(2)}, u32[]{:S(2)}) %collective-permute-start.18) | collective-permute-done | bytes 32800 | tf_op jit(solution)/shard_map/ppermute | solution.py:384
  59.9 0.7 %collective-permute-done.19 = f32[1,32,256]{2,1,0:T(8,128)S(1)} collective-permute-done((f32[1,32,256]{2,1,0:T(8,128)S(1)}, f32[1,32,256]{2,1,0:T(8,128)S(1)}, u32[]{:S(2)}, u32[]{:S(2)}) %collective-permute-start.19) | collective-permute-done | bytes 32800 | tf_op jit(solution)/shard_map/ppermute | solution.py:385
  60.6 0.0 collective-permute-done.20
  60.7 0.0 collective-permute-done.14
  60.7 0.0 copy-done
  60.7 1.6 %place_scores.1 = f32[8,32,256]{2,1,0:T(8,128)} custom-call(s32[8]{0:T(128)S(1)} %stack.35.order_ref, s32[1,256]{1,0:T(1,128)S(1)} %copy-done, f32[224,256]{1,0:T(8,128)S(1)} %bitcast.20, f32[224,256]{1,0:T(8,128)S(1)} %bitcast.18, f32[224,256]{1,0:T(8,128)S(1)} %bitcast.19, f32[32,256]{1,0:T(8,128)S(1)} %bitcast.22, f32[32,256]{1,0:T(8,128)S(1)} %bitcast.23, ...), custom_call_target="tpu_custom_call" | custom-call | tf_op jit(solution)/shard_map/place_scores/pallas_call | solution.py:296
  (5 shorter events, 0.2 us)
Async XLA Ops:
  2.2 46.7 %collective-permute-start.12 = (bf16[256,3712]{1,0:T(8,128)(2,1)S(1)}, bf16[256,3712]{1,0:T(8,128)(2,1)S(1)}, u32[]{:S(2)}, u32[]{:S(2)}) collective-permute-start(bf16[256,3712]{1,0:T(8,128)(2,1)S(1)} %get-tuple-element.75), channel_id=1, source_target_pairs={{0,16},{16,0},{1,17},{17,1},{2,18},{18,2},{3,19},{19,3},{4,20},{20... | collective-permute-start | bytes 5701640 | tf_op jit(solution)/shard_map/ppermute | solution.py:340
  5.2 11.7 %collective-permute-start = (bf16[64,2304]{1,0:T(8,128)(2,1)S(1)}, bf16[64,2304]{1,0:T(8,128)(2,1)S(1)}, u32[]{:S(2)}, u32[]{:S(2)}) collective-permute-start(bf16[64,2304]{1,0:T(8,128)(2,1)S(1)} %get-tuple-element.52.refs_0_), channel_id=1, source_target_pairs={{0,4},{2,6},{4,8},{6,10},{8,12},{10,14},{12,0},{14,2},{1,5},{3,7},... | collective-permute-start | bytes 884744 | tf_op jit(solution)/shard_map/ppermute | solution.py:329
  6.8 10.2 %collective-permute-start.1 = (bf16[64,2304]{1,0:T(8,128)(2,1)S(1)}, bf16[64,2304]{1,0:T(8,128)(2,1)S(1)}, u32[]{:S(2)}, u32[]{:S(2)}) collective-permute-start(bf16[64,2304]{1,0:T(8,128)(2,1)S(1)} %get-tuple-element.52.refs_0_), channel_id=1, source_target_pairs={{0,2},{2,0},{4,6},{6,4},{8,10},{10,8},{12,14},{14,12},{1,3},{3,1},... | collective-permute-start | bytes 884744 | tf_op jit(solution)/shard_map/ppermute | solution.py:329
  8.3 14.6 %collective-permute-start.6 = (bf16[64,2176]{1,0:T(8,128)(2,1)S(1)}, bf16[64,2176]{1,0:T(8,128)(2,1)S(1)}, u32[]{:S(2)}, u32[]{:S(2)}) collective-permute-start(bf16[64,2176]{1,0:T(8,128)(2,1)S(1)} %get-tuple-element.64.refs_0_), channel_id=1, source_target_pairs={{0,4},{2,6},{4,8},{6,10},{8,12},{10,14},{12,0},{14,2},{1,5},{3,7},... | collective-permute-start | bytes 835592 | tf_op jit(solution)/shard_map/ppermute | solution.py:329
  9.9 13.1 %collective-permute-start.7 = (bf16[64,2176]{1,0:T(8,128)(2,1)S(1)}, bf16[64,2176]{1,0:T(8,128)(2,1)S(1)}, u32[]{:S(2)}, u32[]{:S(2)}) collective-permute-start(bf16[64,2176]{1,0:T(8,128)(2,1)S(1)} %get-tuple-element.64.refs_0_), channel_id=1, source_target_pairs={{0,2},{2,0},{4,6},{6,4},{8,10},{10,8},{12,14},{14,12},{1,3},{3,1},... | collective-permute-start | bytes 835592 | tf_op jit(solution)/shard_map/ppermute | solution.py:329
  16.9 12.3 %collective-permute-start.2 = (bf16[64,2304]{1,0:T(8,128)(2,1)S(1)}, bf16[64,2304]{1,0:T(8,128)(2,1)S(1)}, u32[]{:S(2)}, u32[]{:S(2)}) collective-permute-start(bf16[64,2304]{1,0:T(8,128)(2,1)S(1)} %collective-permute-done.refs_1_), channel_id=1, source_target_pairs={{0,4},{2,6},{4,8},{6,10},{8,12},{10,14},{12,0},{14,2},{1,5},{3,7},... | collective-permute-start | bytes 884744 | tf_op jit(solution)/shard_map/ppermute | solution.py:329
  18.3 10.9 %collective-permute-start.3 = (bf16[64,2304]{1,0:T(8,128)(2,1)S(1)}, bf16[64,2304]{1,0:T(8,128)(2,1)S(1)}, u32[]{:S(2)}, u32[]{:S(2)}) collective-permute-start(bf16[64,2304]{1,0:T(8,128)(2,1)S(1)} %collective-permute-done.refs_1_), channel_id=1, source_target_pairs={{0,2},{2,0},{4,6},{6,4},{8,10},{10,8},{12,14},{14,12},{1,3},{3,1},... | collective-permute-start | bytes 884744 | tf_op jit(solution)/shard_map/ppermute | solution.py:329
  22.9 12.3 %collective-permute-start.8 = (bf16[64,2176]{1,0:T(8,128)(2,1)S(1)}, bf16[64,2176]{1,0:T(8,128)(2,1)S(1)}, u32[]{:S(2)}, u32[]{:S(2)}) collective-permute-start(bf16[64,2176]{1,0:T(8,128)(2,1)S(1)} %collective-permute-done.6.refs_1_), channel_id=1, source_target_pairs={{0,4},{2,6},{4,8},{6,10},{8,12},{10,14},{12,0},{14,2},{1,5},{3,7},... | collective-permute-start | bytes 835592 | tf_op jit(solution)/shard_map/ppermute | solution.py:329
  24.3 10.9 %collective-permute-start.9 = (bf16[64,2176]{1,0:T(8,128)(2,1)S(1)}, bf16[64,2176]{1,0:T(8,128)(2,1)S(1)}, u32[]{:S(2)}, u32[]{:S(2)}) collective-permute-start(bf16[64,2176]{1,0:T(8,128)(2,1)S(1)} %collective-permute-done.6.refs_1_), channel_id=1, source_target_pairs={{0,2},{2,0},{4,6},{6,4},{8,10},{10,8},{12,14},{14,12},{1,3},{3,1},... | collective-permute-start | bytes 835592 | tf_op jit(solution)/shard_map/ppermute | solution.py:329
  29.2 12.3 %collective-permute-start.4 = (bf16[64,2304]{1,0:T(8,128)(2,1)S(1)}, bf16[64,2304]{1,0:T(8,128)(2,1)S(1)}, u32[]{:S(2)}, u32[]{:S(2)}) collective-permute-start(bf16[64,2304]{1,0:T(8,128)(2,1)S(1)} %collective-permute-done.2.refs_1_), channel_id=1, source_target_pairs={{0,4},{2,6},{4,8},{6,10},{8,12},{10,14},{12,0},{14,2},{1,5},{3,7},... | collective-permute-start | bytes 884744 | tf_op jit(solution)/shard_map/ppermute | solution.py:329
  30.6 10.9 %collective-permute-start.5 = (bf16[64,2304]{1,0:T(8,128)(2,1)S(1)}, bf16[64,2304]{1,0:T(8,128)(2,1)S(1)}, u32[]{:S(2)}, u32[]{:S(2)}) collective-permute-start(bf16[64,2304]{1,0:T(8,128)(2,1)S(1)} %collective-permute-done.2.refs_1_), channel_id=1, source_target_pairs={{0,2},{2,0},{4,6},{6,4},{8,10},{10,8},{12,14},{14,12},{1,3},{3,1},... | collective-permute-start | bytes 884744 | tf_op jit(solution)/shard_map/ppermute | solution.py:329
  35.2 10.9 %collective-permute-start.10 = (bf16[64,2176]{1,0:T(8,128)(2,1)S(1)}, bf16[64,2176]{1,0:T(8,128)(2,1)S(1)}, u32[]{:S(2)}, u32[]{:S(2)}) collective-permute-start(bf16[64,2176]{1,0:T(8,128)(2,1)S(1)} %collective-permute-done.8.refs_5_.refs_1_), channel_id=1, source_target_pairs={{0,4},{2,6},{4,8},{6,10},{8,12},{10,14},{12,0},{14,2},{1,5},{3,7},... | collective-permute-start | bytes 835592 | tf_op jit(solution)/shard_map/ppermute | solution.py:329
  36.6 10.7 %collective-permute-start.11 = (bf16[64,2176]{1,0:T(8,128)(2,1)S(1)}, bf16[64,2176]{1,0:T(8,128)(2,1)S(1)}, u32[]{:S(2)}, u32[]{:S(2)}) collective-permute-start(bf16[64,2176]{1,0:T(8,128)(2,1)S(1)} %collective-permute-done.8.refs_5_.refs_1_), channel_id=1, source_target_pairs={{0,2},{2,0},{4,6},{6,4},{8,10},{10,8},{12,14},{14,12},{1,3},{3,1},... | collective-permute-start | bytes 835592 | tf_op jit(solution)/shard_map/ppermute | solution.py:329
  41.5 10.6 %collective-permute-start.17 = (bf16[64,2304]{1,0:T(8,128)(2,1)S(1)}, bf16[64,2304]{1,0:T(8,128)(2,1)S(1)}, u32[]{:S(2)}, u32[]{:S(2)}) collective-permute-start(bf16[64,2304]{1,0:T(8,128)(2,1)S(1)} %collective-permute-done.4.refs_3_), channel_id=1, source_target_pairs={{0,2},{2,0},{4,6},{6,4},{8,10},{10,8},{12,14},{14,12},{1,3},{3,1},... | collective-permute-start | bytes 884744 | tf_op jit(solution)/shard_map/ppermute | solution.py:329
  47.3 8.3 %collective-permute-start.16 = (bf16[64,2176]{1,0:T(8,128)(2,1)S(1)}, bf16[64,2176]{1,0:T(8,128)(2,1)S(1)}, u32[]{:S(2)}, u32[]{:S(2)}) collective-permute-start(bf16[64,2176]{1,0:T(8,128)(2,1)S(1)} %collective-permute-done.11.refs_6_.refs_2_), channel_id=1, source_target_pairs={{0,4},{2,6},{4,8},{6,10},{8,12},{10,14},{12,0},{14,2},{1,5},{3,7},... | collective-permute-start | bytes 835592 | tf_op jit(solution)/shard_map/ppermute | solution.py:329
  49.9 1.6 %collective-permute-start.13 = (f32[7,32,256]{2,1,0:T(8,128)S(1)}, f32[7,32,256]{2,1,0:T(8,128)S(1)}, u32[]{:S(2)}, u32[]{:S(2)}) collective-permute-start(f32[7,32,256]{2,1,0:T(8,128)S(1)} %get-tuple-element.77), channel_id=1, source_target_pairs={{0,1},{1,0},{2,3},{3,2},{4,5},{5,4},{6,7},{7,6},{8,9},{9,8},{10,11... | collective-permute-start | bytes 688136 | tf_op jit(solution)/shard_map/ppermute | solution.py:369
  50.8 7.5 %collective-permute-start.15 = (f32[7,32,256]{2,1,0:T(8,128)S(1)}, f32[7,32,256]{2,1,0:T(8,128)S(1)}, u32[]{:S(2)}, u32[]{:S(2)}) collective-permute-start(f32[7,32,256]{2,1,0:T(8,128)S(1)} %get-tuple-element.81), channel_id=1, source_target_pairs={{0,1},{1,0},{2,3},{3,2},{4,5},{5,4},{6,7},{7,6},{8,9},{9,8},{10,11... | collective-permute-start | bytes 688136 | tf_op jit(solution)/shard_map/ppermute | solution.py:369
  51.5 9.1 %collective-permute-start.14 = (f32[7,32,256]{2,1,0:T(8,128)S(1)}, f32[7,32,256]{2,1,0:T(8,128)S(1)}, u32[]{:S(2)}, u32[]{:S(2)}) collective-permute-start(f32[7,32,256]{2,1,0:T(8,128)S(1)} %add.80), channel_id=1, source_target_pairs={{0,16},{16,0},{1,17},{17,1},{2,18},{18,2},{3,19},{19,3},{4,20},{20... | collective-permute-start | bytes 688136 | tf_op jit(solution)/shard_map/ppermute | solution.py:374
  55.6 5.0 %copy-start = (s32[1,256]{1,0:T(1,128)S(1)}, s32[1,256]{1,0:T(1,128)}, u32[]{:S(2)}) copy-start(s32[1,256]{1,0:T(1,128)} %ids_ref.1) | copy-start | bytes 3076
  56.3 3.6 %collective-permute-start.18 = (f32[1,32,256]{2,1,0:T(8,128)S(1)}, f32[1,32,256]{2,1,0:T(8,128)S(1)}, u32[]{:S(2)}, u32[]{:S(2)}) collective-permute-start(f32[1,32,256]{2,1,0:T(8,128)S(1)} %get-tuple-element.85), channel_id=1, source_target_pairs={{0,17},{1,16},{16,1},{17,0},{2,19},{3,18},{18,3},{19,2},{4,21},{5,... | collective-permute-start | bytes 98312 | tf_op jit(solution)/shard_map/ppermute | solution.py:384
  56.4 4.3 %collective-permute-start.19 = (f32[1,32,256]{2,1,0:T(8,128)S(1)}, f32[1,32,256]{2,1,0:T(8,128)S(1)}, u32[]{:S(2)}, u32[]{:S(2)}) collective-permute-start(f32[1,32,256]{2,1,0:T(8,128)S(1)} %get-tuple-element.86), channel_id=1, source_target_pairs={{0,16},{16,0},{1,17},{17,1},{2,18},{18,2},{3,19},{19,3},{4,20},{20... | collective-permute-start | bytes 98312 | tf_op jit(solution)/shard_map/ppermute | solution.py:385
  57.0 3.7 %collective-permute-start.20 = (f32[1,32,256]{2,1,0:T(8,128)S(1)}, f32[1,32,256]{2,1,0:T(8,128)S(1)}, u32[]{:S(2)}, u32[]{:S(2)}) collective-permute-start(f32[1,32,256]{2,1,0:T(8,128)S(1)} %get-tuple-element.87), channel_id=1, source_target_pairs={{0,1},{1,0},{2,3},{3,2},{4,5},{5,4},{6,7},{7,6},{8,9},{9,8},{10,11... | collective-permute-start | bytes 98312 | tf_op jit(solution)/shard_map/ppermute | solution.py:369

commit v10 on v9

--- a/solution.py
+++ b/solution.py
@@ -8,8 +8,9 @@
 from jax.sharding import PartitionSpec as P
 
 BLOCK = 128
-ALONE = 29
+ALONE = 28
 LATE_WEIGHT = 10
+BEGUN_WEIGHT = 10
 LEAD = 0
 CHUNKS = 2
 VMEM = pl.BlockSpec(memory_space=pltpu.VMEM)
@@ -276,10 +277,15 @@
 def place_kernel(groups, order_ref, ids_ref, *refs):
     *share_refs, out_ref = refs
     share_refs = list(share_refs)
+
+    def stacked_share(arrays):
+        given = [share_refs.pop(0)[...] for _ in range(arrays)]
+        return jnp.concatenate(given, axis=0) if arrays > 1 else given[0]
+
     _, rows, count = out_ref.shape
     slots = lax.broadcasted_iota(jnp.int32, (count, count), 0)
     table = (slots == jnp.broadcast_to(ids_ref[...], (count, count))).astype(jnp.float32).astype(jnp.bfloat16)
-    raw = [functools.reduce(jnp.add, [share_refs.pop(0)[...] for _ in range(shares)]) for shares in groups]
+    raw = [functools.reduce(jnp.add, [stacked_share(arrays) for arrays in shares]) for shares in groups]
     raw = jnp.concatenate(raw, axis=0)
     high = raw.astype(jnp.bfloat16)
     rest = raw - high.astype(jnp.float32)
@@ -292,9 +298,9 @@
 
 def place(order, ids, groups, rows):
     count = ids.shape[1]
-    shares = [share.reshape(-1, count) for group in groups for share in group]
-    return pl.pallas_call(
-        functools.partial(place_kernel, [len(group) for group in groups]),
+    shares = [array.reshape(-1, count) for group in groups for share in group for array in share]
+    return pl.pallas_call(
+        functools.partial(place_kernel, [[len(share) for share in group] for group in groups]),
         out_shape=jax.ShapeDtypeStruct((order.shape[0], rows, count), jnp.float32),
         in_specs=[SMEM, VMEM] + [VMEM] * len(shares),
         out_specs=VMEM,
@@ -344,49 +350,58 @@
         return arrays if rows % 16 == 0 else [jnp.concatenate(arrays, axis=0)]
 
     kept_rows = (slow - 2) * fast * rows
-    early, late = [None] * CHUNKS, [None] * CHUNKS
+    first, second, last = ([None] * CHUNKS for _ in range(3))
     held = [[] for _ in range(CHUNKS)]
+    lead, trail = slice(LEAD, LEAD + 1), slice(1 - LEAD, 2 - LEAD)
     for s in range(slow - 1):
         for c in (LEAD, 1 - LEAD):
+            if s == slow - 2:
+                first[c] = held[c] + [chunks[c]]
             tied = [step(chunks[c], slow, fast), *along_fast(chunks[c])] + held[c]
             if s == 0 and c == LEAD:
                 *tied, ours = lax.optimization_barrier(tied + [ours])
             elif s == slow - 2 and c != LEAD:
-                begun_own = score(half, 0, early[LEAD:LEAD + 1], [ours], cuts[LEAD])
-                *tied, begun_own = lax.optimization_barrier(tied + list(begun_own))
+                begun_own = score(half, 0, [first[LEAD] + second[LEAD]], [ours], cuts[LEAD])
+                ready, *begun_own = lax.optimization_barrier((chunks[LEAD], *begun_own))
+                last[LEAD] = stack(along_fast(ready)[1:])
+                their_first = score(half, rows, first, [theirs])
+                *tied, keep, send = lax.optimization_barrier(tied + list(their_first))
+                their_first = keep, send
             else:
                 tied = lax.optimization_barrier(tied)
             chunks[c], values, kept = tied[0], tied[1 : fast + 1], tied[fast + 1 :]
             if s < slow - 2:
                 held[c] = [stash(kept[0] if s else None, stack(values), s * fast * rows, kept_rows)]
                 continue
-            early[c] = kept + stack(values + [chunks[c]])
-            late[c] = stack(
-                along_fast(chunks[c])[1:] if c == LEAD else [step(value, slow, fast) for value in values[1:]]
-            )
+            second[c] = stack(values[1:] + [chunks[c]])
+            if c != LEAD:
+                last[c] = stack([step(value, slow, fast) for value in values[1:]])
 
     def over_dim(value):
         return lax.ppermute(value, "dim", [(0, 1), (1, 0)])
 
-    lead, trail = slice(LEAD, LEAD + 1), slice(1 - LEAD, 2 - LEAD)
-    keep, send = score(half, rows, early, [theirs])
+    keep, send = their_first
     added, theirs = lax.optimization_barrier((add(keep, over_dim(send)), theirs))
-    given = lax.ppermute(added, "groups", swap)
-    keep, send = score(half, rows, early[trail], [ours], cuts[1 - LEAD], [begun_own])
-    shares = [given, keep, over_dim(send)]
-
-    begun = score(half, 0, late[lead], [theirs, ours], cuts[LEAD])
+    given = [lax.ppermute(added, "groups", swap)]
+    keep, send = score(half, rows, second, [theirs])
+    added, *begun_own = lax.optimization_barrier((add(keep, over_dim(send)), *begun_own))
+    given.append(lax.ppermute(added, "groups", swap))
+    early = [a + b for a, b in zip(first, second)]
+    keep, send = score(half, rows, early[trail], [ours], cuts[1 - LEAD], begun_own)
+    shares = [given, [keep], [over_dim(send)]]
+
+    begun = score(half, 0, last[lead], [theirs, ours], cuts[LEAD], (), BEGUN_WEIGHT)
     their_keep, their_send, own_keep, own_send = score(
-        half, rows, late[trail], [theirs, ours], cuts[1 - LEAD], begun, LATE_WEIGHT
+        half, rows, last[trail], [theirs, ours], cuts[1 - LEAD], begun, LATE_WEIGHT
     )
     across = [(i, 3 - i) for i in range(4)]
-    last = [
-        lax.ppermute(their_send, ("groups", "dim"), across),
-        lax.ppermute(their_keep, "groups", swap),
-        over_dim(own_send),
-        own_keep,
+    late = [
+        [lax.ppermute(their_send, ("groups", "dim"), across)],
+        [lax.ppermute(their_keep, "groups", swap)],
+        [over_dim(own_send)],
+        [own_keep],
     ]
-    return place(order, example_ids, [shares, last], rows // 2)
+    return place(order, example_ids, [shares, late], rows // 2)
 
 
 def solution(mesh):

time: 62.4 us -> 66.3 us (1.062)
  waiting for transfers between devices: 25.7 us -> 29 us
    ppermute x14, waiting for transfers between devices: 23.1 us -> 25.9 us  [step(): return lax.ppermute(value, 'ex', pairs)]
    ppermute x3 -> x4, starting transfers between devices: 1.91 us -> 0.65 us  [over_dim(): return lax.ppermute(value, 'dim', [(0, 1), (1, 0)])]
    ppermute x1, starting transfers between devices: 0.57 us -> 1.34 us  [shards(): lax.ppermute(their_keep, 'groups', swap)]
    ppermute x1, waiting for transfers between devices: 0.01 us -> 0.67 us  [shards(): theirs = lax.ppermute(sent, 'groups', swap)]
    pallas_call x5 -> x6, Pallas kernels: 4.01 us -> 4.43 us  [score(): pl.pallas_call(functools.partial(score_kernel, [len(arrays) for arrays in...]
  transfers between devices with their start and end apart: 21 -> 23, of which waited for: 11 -> 12; matrix products, arithmetic and copies ran while one was open for 0% -> 0% of each run, Pallas kernels for 11% -> 11%
where the time goes in v10:
time: 66.3 us; the launch traced here: 66.2 us
  waiting for transfers between devices  29 us (44%)
  starting transfers between devices  26 us (39%)
  Pallas kernels  10.9 us (16%)
    ppermute x14, waiting for transfers between devices, step(): return lax.ppermute(value, 'ex', pairs)  25.9 us
    ppermute x14, starting transfers between devices, step(): return lax.ppermute(value, 'ex', pairs)  19.8 us
    pallas_call x6, Pallas kernels, score(): pl.pallas_call(functools.partial(score_kernel, [len(arrays) for arrays in...  4.43 us
    ppermute x1, starting transfers between devices, shards(): theirs = lax.ppermute(sent, 'groups', swap)  3.03 us
    pallas_call x1, Pallas kernels, scale(): pl.pallas_call(functools.partial(scale_kernel, alone), out_shape=pltpu.VM...  2.63 us
    pallas_call x1, Pallas kernels, cut(): pl.pallas_call(functools.partial(cut_kernel, alone, cuts), out_shape=[plt...  2.06 us
    ppermute x1, waiting for transfers between devices, shards(): lax.ppermute(their_send, ('groups', 'dim'), across)  1.73 us
    pallas_call x1, Pallas kernels, place(): pl.pallas_call(functools.partial(place_kernel, [[len(share) for share in...  1.58 us
  transfers between devices with their start and end apart: 23, of which 12 were waited for; matrix products, arithmetic and copies ran while one was open for 0% of the time, Pallas kernels for 11%

profile of v10, /device:TPU:0, one launch (start us, length us, event | category | flops | bytes accessed | tf_op | source)
XLA Modules:
  0.0 66.2 jit_solution(7650366627917183134)
XLA Ops:
  0.0 0.1 stack.35.order_ref
  0.1 2.1 %cut_queries.1 = (bf16[64,2304]{1,0:T(8,128)(2,1)S(1)}, bf16[64,2304]{1,0:T(8,128)(2,1)S(1)}, bf16[256,3584]{1,0:T(8,128)(2,1)S(1)}) custom-call(s32[1]{0:T(128)} %bitcast.part_ref, bf16[1,64,8192]{2,1,0:T(8,128)(2,1)} %queries_ref.1, bf16[256,8192]{1,0:T(8,128)(2,1)} %codes_ref.3, s32[64,256]{1,0:T(8,128)} %bitcast.27), custom_call_target="tpu_custom_call" | custom-call | flops 2097152 | bytes 4194304 | tf_op jit(solution)/shard_map/cut_queries/pallas_call | solution.py:120
  2.2 3.0 %collective-permute-start.10 = (bf16[256,3584]{1,0:T(8,128)(2,1)S(1)}, bf16[256,3584]{1,0:T(8,128)(2,1)S(1)}, u32[]{:S(2)}, u32[]{:S(2)}) collective-permute-start(bf16[256,3584]{1,0:T(8,128)(2,1)S(1)} %get-tuple-element.69), channel_id=1, source_target_pairs={{0,16},{16,0},{1,17},{17,1},{2,18},{18,2},{3,19},{19,3},{4,20},{20... | collective-permute-start | bytes 5505032 | tf_op jit(solution)/shard_map/ppermute | solution.py:346
  5.2 1.6 %collective-permute-start.6 = (bf16[64,2304]{1,0:T(8,128)(2,1)S(1)}, bf16[64,2304]{1,0:T(8,128)(2,1)S(1)}, u32[]{:S(2)}, u32[]{:S(2)}) collective-permute-start(bf16[64,2304]{1,0:T(8,128)(2,1)S(1)} %get-tuple-element.63.refs_0_), channel_id=1, source_target_pairs={{0,4},{2,6},{4,8},{6,10},{8,12},{10,14},{12,0},{14,2},{1,5},{3,7},... | collective-permute-start | bytes 884744 | tf_op jit(solution)/shard_map/ppermute | solution.py:335
  6.8 1.5 %collective-permute-start.7 = (bf16[64,2304]{1,0:T(8,128)(2,1)S(1)}, bf16[64,2304]{1,0:T(8,128)(2,1)S(1)}, u32[]{:S(2)}, u32[]{:S(2)}) collective-permute-start(bf16[64,2304]{1,0:T(8,128)(2,1)S(1)} %get-tuple-element.63.refs_0_), channel_id=1, source_target_pairs={{0,2},{2,0},{4,6},{6,4},{8,10},{10,8},{12,14},{14,12},{1,3},{3,1},... | collective-permute-start | bytes 884744 | tf_op jit(solution)/shard_map/ppermute | solution.py:335
  8.3 1.6 %collective-permute-start = (bf16[64,2304]{1,0:T(8,128)(2,1)S(1)}, bf16[64,2304]{1,0:T(8,128)(2,1)S(1)}, u32[]{:S(2)}, u32[]{:S(2)}) collective-permute-start(bf16[64,2304]{1,0:T(8,128)(2,1)S(1)} %get-tuple-element.54.refs_0_), channel_id=1, source_target_pairs={{0,4},{2,6},{4,8},{6,10},{8,12},{10,14},{12,0},{14,2},{1,5},{3,7},... | collective-permute-start | bytes 884744 | tf_op jit(solution)/shard_map/ppermute | solution.py:335
  9.8 0.5 collective-permute-start.1
  10.4 2.6 %scale_codes.1.refs_4_.refs_2_ = bf16[256,4608]{1,0:T(8,128)(2,1)S(1)} custom-call(s32[1]{0:T(128)} %bitcast.part_ref, bf16[256,8192]{1,0:T(8,128)(2,1)} %codes_ref.3, s32[64,256]{1,0:T(8,128)} %bitcast.28), custom_call_target="tpu_custom_call" | custom-call | flops 2097152 | bytes 8388608 | tf_op jit(solution)/shard_map/scale_codes/pallas_call | solution.py:158
  13.0 3.9 %collective-permute-done.6.refs_1_ = bf16[64,2304]{1,0:T(8,128)(2,1)S(1)} collective-permute-done((bf16[64,2304]{1,0:T(8,128)(2,1)S(1)}, bf16[64,2304]{1,0:T(8,128)(2,1)S(1)}, u32[]{:S(2)}, u32[]{:S(2)}) %collective-permute-start.6) | collective-permute-done | bytes 294944 | tf_op jit(solution)/shard_map/ppermute | solution.py:335
  16.9 0.0 collective-permute-done.7.refs_1_
  16.9 1.4 %collective-permute-start.8 = (bf16[64,2304]{1,0:T(8,128)(2,1)S(1)}, bf16[64,2304]{1,0:T(8,128)(2,1)S(1)}, u32[]{:S(2)}, u32[]{:S(2)}) collective-permute-start(bf16[64,2304]{1,0:T(8,128)(2,1)S(1)} %collective-permute-done.6.refs_1_), channel_id=1, source_target_pairs={{0,4},{2,6},{4,8},{6,10},{8,12},{10,14},{12,0},{14,2},{1,5},{3,7},... | collective-permute-start | bytes 884744 | tf_op jit(solution)/shard_map/ppermute | solution.py:335
  18.3 1.5 %collective-permute-start.9 = (bf16[64,2304]{1,0:T(8,128)(2,1)S(1)}, bf16[64,2304]{1,0:T(8,128)(2,1)S(1)}, u32[]{:S(2)}, u32[]{:S(2)}) collective-permute-start(bf16[64,2304]{1,0:T(8,128)(2,1)S(1)} %collective-permute-done.6.refs_1_), channel_id=1, source_target_pairs={{0,2},{2,0},{4,6},{6,4},{8,10},{10,8},{12,14},{14,12},{1,3},{3,1},... | collective-permute-start | bytes 884744 | tf_op jit(solution)/shard_map/ppermute | solution.py:335
  19.8 3.5 %collective-permute-done.refs_1_ = bf16[64,2304]{1,0:T(8,128)(2,1)S(1)} collective-permute-done((bf16[64,2304]{1,0:T(8,128)(2,1)S(1)}, bf16[64,2304]{1,0:T(8,128)(2,1)S(1)}, u32[]{:S(2)}, u32[]{:S(2)}) %collective-permute-start) | collective-permute-done | bytes 294944 | tf_op jit(solution)/shard_map/ppermute | solution.py:335
  23.2 0.0 collective-permute-done.1.refs_1_
  23.2 1.4 %collective-permute-start.2 = (bf16[64,2304]{1,0:T(8,128)(2,1)S(1)}, bf16[64,2304]{1,0:T(8,128)(2,1)S(1)}, u32[]{:S(2)}, u32[]{:S(2)}) collective-permute-start(bf16[64,2304]{1,0:T(8,128)(2,1)S(1)} %collective-permute-done.refs_1_), channel_id=1, source_target_pairs={{0,4},{2,6},{4,8},{6,10},{8,12},{10,14},{12,0},{14,2},{1,5},{3,7},... | collective-permute-start | bytes 884744 | tf_op jit(solution)/shard_map/ppermute | solution.py:335
  24.6 1.5 %collective-permute-start.3 = (bf16[64,2304]{1,0:T(8,128)(2,1)S(1)}, bf16[64,2304]{1,0:T(8,128)(2,1)S(1)}, u32[]{:S(2)}, u32[]{:S(2)}) collective-permute-start(bf16[64,2304]{1,0:T(8,128)(2,1)S(1)} %collective-permute-done.refs_1_), channel_id=1, source_target_pairs={{0,2},{2,0},{4,6},{6,4},{8,10},{10,8},{12,14},{14,12},{1,3},{3,1},... | collective-permute-start | bytes 884744 | tf_op jit(solution)/shard_map/ppermute | solution.py:335
  26.1 3.4 %collective-permute-done.8.refs_1_ = bf16[64,2304]{1,0:T(8,128)(2,1)S(1)} collective-permute-done((bf16[64,2304]{1,0:T(8,128)(2,1)S(1)}, bf16[64,2304]{1,0:T(8,128)(2,1)S(1)}, u32[]{:S(2)}, u32[]{:S(2)}) %collective-permute-start.8) | collective-permute-done | bytes 294944 | tf_op jit(solution)/shard_map/ppermute | solution.py:335
  29.6 0.0 collective-permute-done.9.refs_2_
  29.6 1.4 %collective-permute-start.13 = (bf16[64,2304]{1,0:T(8,128)(2,1)S(1)}, bf16[64,2304]{1,0:T(8,128)(2,1)S(1)}, u32[]{:S(2)}, u32[]{:S(2)}) collective-permute-start(bf16[64,2304]{1,0:T(8,128)(2,1)S(1)} %collective-permute-done.8.refs_1_), channel_id=1, source_target_pairs={{0,4},{2,6},{4,8},{6,10},{8,12},{10,14},{12,0},{14,2},{1,5},{3,7},... | collective-permute-start | bytes 884744 | tf_op jit(solution)/shard_map/ppermute | solution.py:335
  30.9 1.5 %collective-permute-start.14 = (bf16[64,2304]{1,0:T(8,128)(2,1)S(1)}, bf16[64,2304]{1,0:T(8,128)(2,1)S(1)}, u32[]{:S(2)}, u32[]{:S(2)}) collective-permute-start(bf16[64,2304]{1,0:T(8,128)(2,1)S(1)} %collective-permute-done.8.refs_1_), channel_id=1, source_target_pairs={{0,2},{2,0},{4,6},{6,4},{8,10},{10,8},{12,14},{14,12},{1,3},{3,1},... | collective-permute-start | bytes 884744 | tf_op jit(solution)/shard_map/ppermute | solution.py:335
  32.5 3.4 %collective-permute-done.2.refs_3_.refs_1_ = bf16[64,2304]{1,0:T(8,128)(2,1)S(1)} collective-permute-done((bf16[64,2304]{1,0:T(8,128)(2,1)S(1)}, bf16[64,2304]{1,0:T(8,128)(2,1)S(1)}, u32[]{:S(2)}, u32[]{:S(2)}) %collective-permute-start.2) | collective-permute-done | bytes 294944 | tf_op jit(solution)/shard_map/ppermute | solution.py:335
  35.9 0.0 collective-permute-done.3.refs_2_
  35.9 1.4 %collective-permute-start.4 = (bf16[64,2304]{1,0:T(8,128)(2,1)S(1)}, bf16[64,2304]{1,0:T(8,128)(2,1)S(1)}, u32[]{:S(2)}, u32[]{:S(2)}) collective-permute-start(bf16[64,2304]{1,0:T(8,128)(2,1)S(1)} %collective-permute-done.2.refs_3_.refs_1_), channel_id=1, source_target_pairs={{0,4},{2,6},{4,8},{6,10},{8,12},{10,14},{12,0},{14,2},{1,5},{3,7},... | collective-permute-start | bytes 884744 | tf_op jit(solution)/shard_map/ppermute | solution.py:335
  37.2 1.5 %collective-permute-start.5 = (bf16[64,2304]{1,0:T(8,128)(2,1)S(1)}, bf16[64,2304]{1,0:T(8,128)(2,1)S(1)}, u32[]{:S(2)}, u32[]{:S(2)}) collective-permute-start(bf16[64,2304]{1,0:T(8,128)(2,1)S(1)} %collective-permute-done.2.refs_3_.refs_1_), channel_id=1, source_target_pairs={{0,2},{2,0},{4,6},{6,4},{8,10},{10,8},{12,14},{14,12},{1,3},{3,1},... | collective-permute-start | bytes 884744 | tf_op jit(solution)/shard_map/ppermute | solution.py:335
  38.8 3.4 %collective-permute-done.13.refs_1_.refs_3_ = bf16[64,2304]{1,0:T(8,128)(2,1)S(1)} collective-permute-done((bf16[64,2304]{1,0:T(8,128)(2,1)S(1)}, bf16[64,2304]{1,0:T(8,128)(2,1)S(1)}, u32[]{:S(2)}, u32[]{:S(2)}) %collective-permute-start.13) | collective-permute-done | bytes 294944 | tf_op jit(solution)/shard_map/ppermute | solution.py:335
  42.2 0.0 collective-permute-done.14.refs_0_.refs_2_
  42.2 0.7 %score.8.refs_5_ = f32[448,256]{1,0:T(8,128)S(1)} custom-call(s32[1]{0:T(128)} %bitcast.1.half_ref, bf16[256,2304]{1,0:T(8,128)(2,1)S(1)} %stash.7.refs_0_, bf16[64,2304]{1,0:T(8,128)(2,1)S(1)} %collective-permute-done.8.refs_1_, bf16[64,2304]{1,0:T(8,128)(2,1)S(1)} %collective-permute-done.14.refs_0_.refs_2_, ...), custom_call_target="tpu_custom_call" | custom-call | flops 1056964608 | bytes 2359296 | tf_op jit(solution)/shard_map/score/pallas_call | solution.py:249
  42.9 1.6 %collective-permute-start.19 = (bf16[64,2304]{1,0:T(8,128)(2,1)S(1)}, bf16[64,2304]{1,0:T(8,128)(2,1)S(1)}, u32[]{:S(2)}, u32[]{:S(2)}) collective-permute-start(bf16[64,2304]{1,0:T(8,128)(2,1)S(1)} %collective-permute-done.13.refs_1_.refs_3_), channel_id=1, source_target_pairs={{0,2},{2,0},{4,6},{6,4},{8,10},{10,8},{12,14},{14,12},{1,3},{3,1},... | collective-permute-start | bytes 884744 | tf_op jit(solution)/shard_map/ppermute | solution.py:335
  44.5 0.7 %collective-permute-done.10.refs_4_.refs_1_ = bf16[256,3584]{1,0:T(8,128)(2,1)S(1)} collective-permute-done((bf16[256,3584]{1,0:T(8,128)(2,1)S(1)}, bf16[256,3584]{1,0:T(8,128)(2,1)S(1)}, u32[]{:S(2)}, u32[]{:S(2)}) %collective-permute-start.10) | collective-permute-done | bytes 1835040 | tf_op jit(solution)/shard_map/ppermute | solution.py:346
  45.2 0.8 %score.6 = (f32[5,32,256]{2,1,0:T(8,128)S(1)}, f32[5,32,256]{2,1,0:T(8,128)S(1)}) custom-call(s32[1]{0:T(128)} %bitcast.1.half_ref, bf16[256,2304]{1,0:T(8,128)(2,1)S(1)} %stash.7.refs_0_, bf16[64,2304]{1,0:T(8,128)(2,1)S(1)} %collective-permute-done.8.refs_1_, bf16[256,2304]{1,0:T(8,128)(2,1)S(1)} %stash.5.refs_2_.refs_0_, ...), custom_call_target="tpu_custom_call" | custom-call | flops 587202560 | bytes 1835008 | tf_op jit(solution)/shard_map/score/pallas_call | solution.py:249
  46.0 1.1 %collective-permute-done.4.refs_3_ = bf16[64,2304]{1,0:T(8,128)(2,1)S(1)} collective-permute-done((bf16[64,2304]{1,0:T(8,128)(2,1)S(1)}, bf16[64,2304]{1,0:T(8,128)(2,1)S(1)}, u32[]{:S(2)}, u32[]{:S(2)}) %collective-permute-start.4) | collective-permute-done | bytes 294944 | tf_op jit(solution)/shard_map/ppermute | solution.py:335
  47.1 1.2 %collective-permute-done.5.refs_2_ = bf16[64,2304]{1,0:T(8,128)(2,1)S(1)} collective-permute-done((bf16[64,2304]{1,0:T(8,128)(2,1)S(1)}, bf16[64,2304]{1,0:T(8,128)(2,1)S(1)}, u32[]{:S(2)}, u32[]{:S(2)}) %collective-permute-start.5) | collective-permute-done | bytes 294944 | tf_op jit(solution)/shard_map/ppermute | solution.py:335
  48.3 0.0 collective-permute-start.11
  48.3 1.6 %collective-permute-start.18 = (bf16[64,2304]{1,0:T(8,128)(2,1)S(1)}, bf16[64,2304]{1,0:T(8,128)(2,1)S(1)}, u32[]{:S(2)}, u32[]{:S(2)}) collective-permute-start(bf16[64,2304]{1,0:T(8,128)(2,1)S(1)} %collective-permute-done.5.refs_2_), channel_id=1, source_target_pairs={{0,4},{2,6},{4,8},{6,10},{8,12},{10,14},{12,0},{14,2},{1,5},{3,7},... | collective-permute-start | bytes 884744 | tf_op jit(solution)/shard_map/ppermute | solution.py:335
  49.9 0.0 collective-permute-done.11.b_ref
  49.9 0.6 collective-permute-start.12
  50.5 0.7 %score.7 = (f32[2,32,256]{2,1,0:T(8,128)S(1)}, f32[2,32,256]{2,1,0:T(8,128)S(1)}) custom-call(s32[1]{0:T(128)} %bitcast.1.half_ref, bf16[64,2304]{1,0:T(8,128)(2,1)S(1)} %collective-permute-done.14.refs_0_.refs_2_, bf16[64,2304]{1,0:T(8,128)(2,1)S(1)} %collective-permute-done.13.refs_1_.refs_3_, bf16[64,2304]{1,0:T(8,128)(2,1)S(1)} %collective-permute-done.5.refs_2_, ...), custom_call_target="tpu_custom_call" | custom-call | flops 234881024 | bytes 1835008 | tf_op jit(solution)/shard_map/score/pallas_call | solution.py:249
  51.2 0.1 collective-permute-start.15
  51.3 1.6 %collective-permute-done.19.refs_0_ = bf16[64,2304]{1,0:T(8,128)(2,1)S(1)} collective-permute-done((bf16[64,2304]{1,0:T(8,128)(2,1)S(1)}, bf16[64,2304]{1,0:T(8,128)(2,1)S(1)}, u32[]{:S(2)}, u32[]{:S(2)}) %collective-permute-start.19) | collective-permute-done | bytes 294944 | tf_op jit(solution)/shard_map/ppermute | solution.py:335
  52.9 0.8 %score.10 = (f32[64,256]{1,0:T(8,128)S(1)}, f32[64,256]{1,0:T(8,128)S(1)}) custom-call(s32[1]{0:T(128)} %bitcast.1.half_ref, bf16[64,2304]{1,0:T(8,128)(2,1)S(1)} %collective-permute-done.19.refs_0_, bf16[256,3584]{1,0:T(8,128)(2,1)S(1)} %collective-permute-done.10.refs_4_.refs_1_, bf16[256,4608]{1,0:T(8,128)(2,1)S(1)} %scale_codes.1.refs_4_.refs_2_), custom_call_target="tpu_custom_call" | custom-call | flops 2684354560 | bytes 1835008 | tf_op jit(solution)/shard_map/score/pallas_call | solution.py:249
  53.7 0.0 collective-permute-done.15.b_ref
  53.7 0.6 collective-permute-start.16
  54.3 0.7 %score.9 = (f32[7,32,256]{2,1,0:T(8,128)S(1)}, f32[7,32,256]{2,1,0:T(8,128)S(1)}) custom-call(s32[1]{0:T(128)} %bitcast.1.half_ref, bf16[256,2304]{1,0:T(8,128)(2,1)S(1)} %stash.5.refs_2_.refs_0_, bf16[64,2304]{1,0:T(8,128)(2,1)S(1)} %collective-permute-done.2.refs_3_.refs_1_, bf16[64,2304]{1,0:T(8,128)(2,1)S(1)} %collective-permute-done.5.refs_2_, ...), custom_call_target="tpu_custom_call" | custom-call | flops 1056964608 | bytes 2359296 | tf_op jit(solution)/shard_map/score/pallas_call | solution.py:249
  55.0 0.1 collective-permute-start.17
  55.1 4.4 %collective-permute-done.18.refs_0_ = bf16[64,2304]{1,0:T(8,128)(2,1)S(1)} collective-permute-done((bf16[64,2304]{1,0:T(8,128)(2,1)S(1)}, bf16[64,2304]{1,0:T(8,128)(2,1)S(1)}, u32[]{:S(2)}, u32[]{:S(2)}) %collective-permute-start.18) | collective-permute-done | bytes 294944 | tf_op jit(solution)/shard_map/ppermute | solution.py:335
  59.5 0.0 copy-start
  59.5 0.7 %score.11 = (f32[1,32,256]{2,1,0:T(8,128)S(1)}, f32[1,32,256]{2,1,0:T(8,128)S(1)}, f32[1,32,256]{2,1,0:T(8,128)S(1)}, f32[1,32,256]{2,1,0:T(8,128)S(1)}) custom-call(s32[1]{0:T(128)} %bitcast.1.half_ref, bf16[64,2304]{1,0:T(8,128)(2,1)S(1)} %collective-permute-done.18.refs_0_, bf16[256,3584]{1,0:T(8,128)(2,1)S(1)} %collective-permute-done.10.refs_4_.refs_1_, ...), custom_call_target="tpu_custom_call" | custom-call | flops 2684354560 | bytes 1835008 | tf_op jit(solution)/shard_map/score/pallas_call | solution.py:249
  60.2 0.1 collective-permute-start.20
  60.3 1.3 %collective-permute-start.21 = (f32[1,32,256]{2,1,0:T(8,128)S(1)}, f32[1,32,256]{2,1,0:T(8,128)S(1)}, u32[]{:S(2)}, u32[]{:S(2)}) collective-permute-start(f32[1,32,256]{2,1,0:T(8,128)S(1)} %get-tuple-element.92), channel_id=1, source_target_pairs={{0,16},{16,0},{1,17},{17,1},{2,18},{18,2},{3,19},{19,3},{4,20},{20... | collective-permute-start | bytes 98312 | tf_op jit(solution)/shard_map/ppermute | solution.py:400
  61.6 0.0 collective-permute-done.16
  61.6 0.5 collective-permute-start.22
  62.1 1.7 %collective-permute-done.20 = f32[1,32,256]{2,1,0:T(8,128)S(1)} collective-permute-done((f32[1,32,256]{2,1,0:T(8,128)S(1)}, f32[1,32,256]{2,1,0:T(8,128)S(1)}, u32[]{:S(2)}, u32[]{:S(2)}) %collective-permute-start.20) | collective-permute-done | bytes 32800 | tf_op jit(solution)/shard_map/ppermute | solution.py:399
  63.9 0.7 %collective-permute-done.21 = f32[1,32,256]{2,1,0:T(8,128)S(1)} collective-permute-done((f32[1,32,256]{2,1,0:T(8,128)S(1)}, f32[1,32,256]{2,1,0:T(8,128)S(1)}, u32[]{:S(2)}, u32[]{:S(2)}) %collective-permute-start.21) | collective-permute-done | bytes 32800 | tf_op jit(solution)/shard_map/ppermute | solution.py:400
  64.6 0.0 collective-permute-done.22
  64.6 0.0 collective-permute-done.12
  64.6 0.0 collective-permute-done.17
  64.6 0.0 copy-done
  64.6 1.6 %place_scores.1 = f32[8,32,256]{2,1,0:T(8,128)} custom-call(s32[8]{0:T(128)S(1)} %stack.35.order_ref, s32[1,256]{1,0:T(1,128)S(1)} %copy-done, f32[160,256]{1,0:T(8,128)S(1)} %bitcast.21, f32[64,256]{1,0:T(8,128)S(1)} %bitcast.22, f32[224,256]{1,0:T(8,128)S(1)} %bitcast.19, f32[224,256]{1,0:T(8,128)S(1)} %bitcast.20, f32[32,256]{1,0:T(8,128)S(1)} %bitcast.24, ...), custom_call_target="tpu_custom_call" | custom-call | tf_op jit(solution)/shard_map/place_scores/pallas_call | solution.py:302
  (6 shorter events, 0.2 us)
Async XLA Ops:
  2.2 43.0 %collective-permute-start.10 = (bf16[256,3584]{1,0:T(8,128)(2,1)S(1)}, bf16[256,3584]{1,0:T(8,128)(2,1)S(1)}, u32[]{:S(2)}, u32[]{:S(2)}) collective-permute-start(bf16[256,3584]{1,0:T(8,128)(2,1)S(1)} %get-tuple-element.69), channel_id=1, source_target_pairs={{0,16},{16,0},{1,17},{17,1},{2,18},{18,2},{3,19},{19,3},{4,20},{20... | collective-permute-start | bytes 5505032 | tf_op jit(solution)/shard_map/ppermute | solution.py:346
  5.2 11.7 %collective-permute-start.6 = (bf16[64,2304]{1,0:T(8,128)(2,1)S(1)}, bf16[64,2304]{1,0:T(8,128)(2,1)S(1)}, u32[]{:S(2)}, u32[]{:S(2)}) collective-permute-start(bf16[64,2304]{1,0:T(8,128)(2,1)S(1)} %get-tuple-element.63.refs_0_), channel_id=1, source_target_pairs={{0,4},{2,6},{4,8},{6,10},{8,12},{10,14},{12,0},{14,2},{1,5},{3,7},... | collective-permute-start | bytes 884744 | tf_op jit(solution)/shard_map/ppermute | solution.py:335
  6.8 10.2 %collective-permute-start.7 = (bf16[64,2304]{1,0:T(8,128)(2,1)S(1)}, bf16[64,2304]{1,0:T(8,128)(2,1)S(1)}, u32[]{:S(2)}, u32[]{:S(2)}) collective-permute-start(bf16[64,2304]{1,0:T(8,128)(2,1)S(1)} %get-tuple-element.63.refs_0_), channel_id=1, source_target_pairs={{0,2},{2,0},{4,6},{6,4},{8,10},{10,8},{12,14},{14,12},{1,3},{3,1},... | collective-permute-start | bytes 884744 | tf_op jit(solution)/shard_map/ppermute | solution.py:335
  8.3 15.0 %collective-permute-start = (bf16[64,2304]{1,0:T(8,128)(2,1)S(1)}, bf16[64,2304]{1,0:T(8,128)(2,1)S(1)}, u32[]{:S(2)}, u32[]{:S(2)}) collective-permute-start(bf16[64,2304]{1,0:T(8,128)(2,1)S(1)} %get-tuple-element.54.refs_0_), channel_id=1, source_target_pairs={{0,4},{2,6},{4,8},{6,10},{8,12},{10,14},{12,0},{14,2},{1,5},{3,7},... | collective-permute-start | bytes 884744 | tf_op jit(solution)/shard_map/ppermute | solution.py:335
  9.8 13.4 %collective-permute-start.1 = (bf16[64,2304]{1,0:T(8,128)(2,1)S(1)}, bf16[64,2304]{1,0:T(8,128)(2,1)S(1)}, u32[]{:S(2)}, u32[]{:S(2)}) collective-permute-start(bf16[64,2304]{1,0:T(8,128)(2,1)S(1)} %get-tuple-element.54.refs_0_), channel_id=1, source_target_pairs={{0,2},{2,0},{4,6},{6,4},{8,10},{10,8},{12,14},{14,12},{1,3},{3,1},... | collective-permute-start | bytes 884744 | tf_op jit(solution)/shard_map/ppermute | solution.py:335
  16.9 12.6 %collective-permute-start.8 = (bf16[64,2304]{1,0:T(8,128)(2,1)S(1)}, bf16[64,2304]{1,0:T(8,128)(2,1)S(1)}, u32[]{:S(2)}, u32[]{:S(2)}) collective-permute-start(bf16[64,2304]{1,0:T(8,128)(2,1)S(1)} %collective-permute-done.6.refs_1_), channel_id=1, source_target_pairs={{0,4},{2,6},{4,8},{6,10},{8,12},{10,14},{12,0},{14,2},{1,5},{3,7},... | collective-permute-start | bytes 884744 | tf_op jit(solution)/shard_map/ppermute | solution.py:335
  18.3 11.3 %collective-permute-start.9 = (bf16[64,2304]{1,0:T(8,128)(2,1)S(1)}, bf16[64,2304]{1,0:T(8,128)(2,1)S(1)}, u32[]{:S(2)}, u32[]{:S(2)}) collective-permute-start(bf16[64,2304]{1,0:T(8,128)(2,1)S(1)} %collective-permute-done.6.refs_1_), channel_id=1, source_target_pairs={{0,2},{2,0},{4,6},{6,4},{8,10},{10,8},{12,14},{14,12},{1,3},{3,1},... | collective-permute-start | bytes 884744 | tf_op jit(solution)/shard_map/ppermute | solution.py:335
  23.2 12.6 %collective-permute-start.2 = (bf16[64,2304]{1,0:T(8,128)(2,1)S(1)}, bf16[64,2304]{1,0:T(8,128)(2,1)S(1)}, u32[]{:S(2)}, u32[]{:S(2)}) collective-permute-start(bf16[64,2304]{1,0:T(8,128)(2,1)S(1)} %collective-permute-done.refs_1_), channel_id=1, source_target_pairs={{0,4},{2,6},{4,8},{6,10},{8,12},{10,14},{12,0},{14,2},{1,5},{3,7},... | collective-permute-start | bytes 884744 | tf_op jit(solution)/shard_map/ppermute | solution.py:335
  24.6 11.3 %collective-permute-start.3 = (bf16[64,2304]{1,0:T(8,128)(2,1)S(1)}, bf16[64,2304]{1,0:T(8,128)(2,1)S(1)}, u32[]{:S(2)}, u32[]{:S(2)}) collective-permute-start(bf16[64,2304]{1,0:T(8,128)(2,1)S(1)} %collective-permute-done.refs_1_), channel_id=1, source_target_pairs={{0,2},{2,0},{4,6},{6,4},{8,10},{10,8},{12,14},{14,12},{1,3},{3,1},... | collective-permute-start | bytes 884744 | tf_op jit(solution)/shard_map/ppermute | solution.py:335
  29.6 12.6 %collective-permute-start.13 = (bf16[64,2304]{1,0:T(8,128)(2,1)S(1)}, bf16[64,2304]{1,0:T(8,128)(2,1)S(1)}, u32[]{:S(2)}, u32[]{:S(2)}) collective-permute-start(bf16[64,2304]{1,0:T(8,128)(2,1)S(1)} %collective-permute-done.8.refs_1_), channel_id=1, source_target_pairs={{0,4},{2,6},{4,8},{6,10},{8,12},{10,14},{12,0},{14,2},{1,5},{3,7},... | collective-permute-start | bytes 884744 | tf_op jit(solution)/shard_map/ppermute | solution.py:335
  30.9 11.3 %collective-permute-start.14 = (bf16[64,2304]{1,0:T(8,128)(2,1)S(1)}, bf16[64,2304]{1,0:T(8,128)(2,1)S(1)}, u32[]{:S(2)}, u32[]{:S(2)}) collective-permute-start(bf16[64,2304]{1,0:T(8,128)(2,1)S(1)} %collective-permute-done.8.refs_1_), channel_id=1, source_target_pairs={{0,2},{2,0},{4,6},{6,4},{8,10},{10,8},{12,14},{14,12},{1,3},{3,1},... | collective-permute-start | bytes 884744 | tf_op jit(solution)/shard_map/ppermute | solution.py:335
  35.9 11.2 %collective-permute-start.4 = (bf16[64,2304]{1,0:T(8,128)(2,1)S(1)}, bf16[64,2304]{1,0:T(8,128)(2,1)S(1)}, u32[]{:S(2)}, u32[]{:S(2)}) collective-permute-start(bf16[64,2304]{1,0:T(8,128)(2,1)S(1)} %collective-permute-done.2.refs_3_.refs_1_), channel_id=1, source_target_pairs={{0,4},{2,6},{4,8},{6,10},{8,12},{10,14},{12,0},{14,2},{1,5},{3,7},... | collective-permute-start | bytes 884744 | tf_op jit(solution)/shard_map/ppermute | solution.py:335
  37.2 11.1 %collective-permute-start.5 = (bf16[64,2304]{1,0:T(8,128)(2,1)S(1)}, bf16[64,2304]{1,0:T(8,128)(2,1)S(1)}, u32[]{:S(2)}, u32[]{:S(2)}) collective-permute-start(bf16[64,2304]{1,0:T(8,128)(2,1)S(1)} %collective-permute-done.2.refs_3_.refs_1_), channel_id=1, source_target_pairs={{0,2},{2,0},{4,6},{6,4},{8,10},{10,8},{12,14},{14,12},{1,3},{3,1},... | collective-permute-start | bytes 884744 | tf_op jit(solution)/shard_map/ppermute | solution.py:335
  42.9 9.9 %collective-permute-start.19 = (bf16[64,2304]{1,0:T(8,128)(2,1)S(1)}, bf16[64,2304]{1,0:T(8,128)(2,1)S(1)}, u32[]{:S(2)}, u32[]{:S(2)}) collective-permute-start(bf16[64,2304]{1,0:T(8,128)(2,1)S(1)} %collective-permute-done.13.refs_1_.refs_3_), channel_id=1, source_target_pairs={{0,2},{2,0},{4,6},{6,4},{8,10},{10,8},{12,14},{14,12},{1,3},{3,1},... | collective-permute-start | bytes 884744 | tf_op jit(solution)/shard_map/ppermute | solution.py:335
  48.3 1.6 %collective-permute-start.11 = (f32[5,32,256]{2,1,0:T(8,128)S(1)}, f32[5,32,256]{2,1,0:T(8,128)S(1)}, u32[]{:S(2)}, u32[]{:S(2)}) collective-permute-start(f32[5,32,256]{2,1,0:T(8,128)S(1)} %get-tuple-element.73), channel_id=1, source_target_pairs={{0,1},{1,0},{2,3},{3,2},{4,5},{5,4},{6,7},{7,6},{8,9},{9,8},{10,11... | collective-permute-start | bytes 491528 | tf_op jit(solution)/shard_map/ppermute | solution.py:381
  48.3 11.2 %collective-permute-start.18 = (bf16[64,2304]{1,0:T(8,128)(2,1)S(1)}, bf16[64,2304]{1,0:T(8,128)(2,1)S(1)}, u32[]{:S(2)}, u32[]{:S(2)}) collective-permute-start(bf16[64,2304]{1,0:T(8,128)(2,1)S(1)} %collective-permute-done.5.refs_2_), channel_id=1, source_target_pairs={{0,4},{2,6},{4,8},{6,10},{8,12},{10,14},{12,0},{14,2},{1,5},{3,7},... | collective-permute-start | bytes 884744 | tf_op jit(solution)/shard_map/ppermute | solution.py:335
  49.9 14.7 %collective-permute-start.12 = (f32[5,32,256]{2,1,0:T(8,128)S(1)}, f32[5,32,256]{2,1,0:T(8,128)S(1)}, u32[]{:S(2)}, u32[]{:S(2)}) collective-permute-start(f32[5,32,256]{2,1,0:T(8,128)S(1)} %add.81), channel_id=1, source_target_pairs={{0,16},{16,0},{1,17},{17,1},{2,18},{18,2},{3,19},{19,3},{4,20},{20... | collective-permute-start | bytes 491528 | tf_op jit(solution)/shard_map/ppermute | solution.py:385
  51.2 2.5 %collective-permute-start.15 = (f32[2,32,256]{2,1,0:T(8,128)S(1)}, f32[2,32,256]{2,1,0:T(8,128)S(1)}, u32[]{:S(2)}, u32[]{:S(2)}) collective-permute-start(f32[2,32,256]{2,1,0:T(8,128)S(1)} %get-tuple-element.81), channel_id=1, source_target_pairs={{0,1},{1,0},{2,3},{3,2},{4,5},{5,4},{6,7},{7,6},{8,9},{9,8},{10,11... | collective-permute-start | bytes 196616 | tf_op jit(solution)/shard_map/ppermute | solution.py:381
  53.7 7.9 %collective-permute-start.16 = (f32[2,32,256]{2,1,0:T(8,128)S(1)}, f32[2,32,256]{2,1,0:T(8,128)S(1)}, u32[]{:S(2)}, u32[]{:S(2)}) collective-permute-start(f32[2,32,256]{2,1,0:T(8,128)S(1)} %add.82), channel_id=1, source_target_pairs={{0,16},{16,0},{1,17},{17,1},{2,18},{18,2},{3,19},{19,3},{4,20},{20... | collective-permute-start | bytes 196616 | tf_op jit(solution)/shard_map/ppermute | solution.py:388
  55.0 9.5 %collective-permute-start.17 = (f32[7,32,256]{2,1,0:T(8,128)S(1)}, f32[7,32,256]{2,1,0:T(8,128)S(1)}, u32[]{:S(2)}, u32[]{:S(2)}) collective-permute-start(f32[7,32,256]{2,1,0:T(8,128)S(1)} %get-tuple-element.87), channel_id=1, source_target_pairs={{0,1},{1,0},{2,3},{3,2},{4,5},{5,4},{6,7},{7,6},{8,9},{9,8},{10,11... | collective-permute-start | bytes 688136 | tf_op jit(solution)/shard_map/ppermute | solution.py:381
  59.5 5.0 %copy-start = (s32[1,256]{1,0:T(1,128)S(1)}, s32[1,256]{1,0:T(1,128)}, u32[]{:S(2)}) copy-start(s32[1,256]{1,0:T(1,128)} %ids_ref.1) | copy-start | bytes 3076
  60.2 3.7 %collective-permute-start.20 = (f32[1,32,256]{2,1,0:T(8,128)S(1)}, f32[1,32,256]{2,1,0:T(8,128)S(1)}, u32[]{:S(2)}, u32[]{:S(2)}) collective-permute-start(f32[1,32,256]{2,1,0:T(8,128)S(1)} %get-tuple-element.91), channel_id=1, source_target_pairs={{0,17},{1,16},{16,1},{17,0},{2,19},{3,18},{18,3},{19,2},{4,21},{5,... | collective-permute-start | bytes 98312 | tf_op jit(solution)/shard_map/ppermute | solution.py:399
  60.3 4.3 %collective-permute-start.21 = (f32[1,32,256]{2,1,0:T(8,128)S(1)}, f32[1,32,256]{2,1,0:T(8,128)S(1)}, u32[]{:S(2)}, u32[]{:S(2)}) collective-permute-start(f32[1,32,256]{2,1,0:T(8,128)S(1)} %get-tuple-element.92), channel_id=1, source_target_pairs={{0,16},{16,0},{1,17},{17,1},{2,18},{18,2},{3,19},{19,3},{4,20},{20... | collective-permute-start | bytes 98312 | tf_op jit(solution)/shard_map/ppermute | solution.py:400
  61.6 2.9 %collective-permute-start.22 = (f32[1,32,256]{2,1,0:T(8,128)S(1)}, f32[1,32,256]{2,1,0:T(8,128)S(1)}, u32[]{:S(2)}, u32[]{:S(2)}) collective-permute-start(f32[1,32,256]{2,1,0:T(8,128)S(1)} %get-tuple-element.93), channel_id=1, source_target_pairs={{0,1},{1,0},{2,3},{3,2},{4,5},{5,4},{6,7},{7,6},{8,9},{9,8},{10,11... | collective-permute-start | bytes 98312 | tf_op jit(solution)/shard_map/ppermute | solution.py:381

commit v11 on v9

--- a/solution.py
+++ b/solution.py
@@ -9,8 +9,9 @@
 
 BLOCK = 128
 ALONE = 29
-LATE_WEIGHT = 10
+LATE_WEIGHT = 30
 LEAD = 0
+LEAD_PART = 19
 CHUNKS = 2
 VMEM = pl.BlockSpec(memory_space=pltpu.VMEM)
 SMEM = pl.BlockSpec(memory_space=pltpu.SMEM)
@@ -319,7 +320,7 @@
     blocks = exponents.shape[1]
     alone = blocks * ALONE // 64
     held = blocks - alone
-    cuts = [-(-i * held // CHUNKS) * BLOCK for i in range(CHUNKS + 1)]
+    cuts = [0, held * LEAD_PART // 35 * BLOCK, held * BLOCK]
 
     def step(value, length, stride):
         pairs = [
@@ -352,8 +353,10 @@
             if s == 0 and c == LEAD:
                 *tied, ours = lax.optimization_barrier(tied + [ours])
             elif s == slow - 2 and c != LEAD:
-                begun_own = score(half, 0, early[LEAD:LEAD + 1], [ours], cuts[LEAD])
-                *tied, begun_own = lax.optimization_barrier(tied + list(begun_own))
+                begun_own = score(half, 0, early[LEAD : LEAD + 1], [ours], cuts[LEAD])
+                ready, *begun_own = lax.optimization_barrier((chunks[LEAD], *begun_own))
+                late[LEAD] = stack(along_fast(ready)[1:])
+                *tied, begun_own = lax.optimization_barrier(tied + begun_own)
             else:
                 tied = lax.optimization_barrier(tied)
             chunks[c], values, kept = tied[0], tied[1 : fast + 1], tied[fast + 1 :]
@@ -361,9 +364,8 @@
                 held[c] = [stash(kept[0] if s else None, stack(values), s * fast * rows, kept_rows)]
                 continue
             early[c] = kept + stack(values + [chunks[c]])
-            late[c] = stack(
-                along_fast(chunks[c])[1:] if c == LEAD else [step(value, slow, fast) for value in values[1:]]
-            )
+            if c != LEAD:
+                late[c] = stack([step(value, slow, fast) for value in values[1:]])
 
     def over_dim(value):
         return lax.ppermute(value, "dim", [(0, 1), (1, 0)])

time: 62.4 us -> 62.4 us (level)
  transfers between devices with their start and end apart: 21 -> 21, of which waited for: 11 -> 12; matrix products, arithmetic and copies ran while one was open for 0% -> 0% of each run, Pallas kernels for 11% -> 11%
where the time goes in v11:
time: 62.4 us; the launch traced here: 62.3 us
  starting transfers between devices  25.9 us (42%)
  waiting for transfers between devices  25.6 us (41%)
  Pallas kernels  10.5 us (17%)
    ppermute x14, waiting for transfers between devices, step(): return lax.ppermute(value, 'ex', pairs)  22.8 us
    ppermute x14, starting transfers between devices, step(): return lax.ppermute(value, 'ex', pairs)  19.8 us
    pallas_call x5, Pallas kernels, score(): pl.pallas_call(functools.partial(score_kernel, [len(arrays) for arrays in...  4.07 us
    ppermute x1, starting transfers between devices, shards(): theirs = lax.ppermute(sent, 'groups', swap)  3.03 us
    pallas_call x1, Pallas kernels, scale(): pl.pallas_call(functools.partial(scale_kernel, alone), out_shape=pltpu.VM...  2.6 us
    pallas_call x1, Pallas kernels, cut(): pl.pallas_call(functools.partial(cut_kernel, alone, cuts), out_shape=[plt...  2.09 us
    ppermute x3, starting transfers between devices, over_dim(): return lax.ppermute(value, 'dim', [(0, 1), (1, 0)])  1.91 us
    ppermute x1, waiting for transfers between devices, shards(): lax.ppermute(their_send, ('groups', 'dim'), across)  1.89 us
  transfers between devices with their start and end apart: 21, of which 12 were waited for; matrix products, arithmetic and copies ran while one was open for 0% of the time, Pallas kernels for 11%

profile of v11, /device:TPU:0, one launch (start us, length us, event | category | flops | bytes accessed | tf_op | source)
XLA Modules:
  0.0 62.3 jit_solution(13208879623990247450)
XLA Ops:
  0.0 0.1 stack.35.order_ref
  0.1 2.1 %cut_queries.1 = (bf16[64,2432]{1,0:T(8,128)(2,1)S(1)}, bf16[64,2048]{1,0:T(8,128)(2,1)S(1)}, bf16[256,3712]{1,0:T(8,128)(2,1)S(1)}) custom-call(s32[1]{0:T(128)} %bitcast.part_ref, bf16[1,64,8192]{2,1,0:T(8,128)(2,1)} %queries_ref.1, bf16[256,8192]{1,0:T(8,128)(2,1)} %codes_ref.3, s32[64,256]{1,0:T(8,128)} %bitcast.25), custom_call_target="tpu_custom_call" | custom-call | flops 2097152 | bytes 4194304 | tf_op jit(solution)/shard_map/cut_queries/pallas_call | solution.py:120
  2.2 3.0 %collective-permute-start.12 = (bf16[256,3712]{1,0:T(8,128)(2,1)S(1)}, bf16[256,3712]{1,0:T(8,128)(2,1)S(1)}, u32[]{:S(2)}, u32[]{:S(2)}) collective-permute-start(bf16[256,3712]{1,0:T(8,128)(2,1)S(1)} %get-tuple-element.78), channel_id=1, source_target_pairs={{0,16},{16,0},{1,17},{17,1},{2,18},{18,2},{3,19},{19,3},{4,20},{20... | collective-permute-start | bytes 5701640 | tf_op jit(solution)/shard_map/ppermute | solution.py:341
  5.2 1.6 %collective-permute-start = (bf16[64,2432]{1,0:T(8,128)(2,1)S(1)}, bf16[64,2432]{1,0:T(8,128)(2,1)S(1)}, u32[]{:S(2)}, u32[]{:S(2)}) collective-permute-start(bf16[64,2432]{1,0:T(8,128)(2,1)S(1)} %get-tuple-element.54.refs_0_), channel_id=1, source_target_pairs={{0,4},{2,6},{4,8},{6,10},{8,12},{10,14},{12,0},{14,2},{1,5},{3,7},... | collective-permute-start | bytes 933896 | tf_op jit(solution)/shard_map/ppermute | solution.py:330
  6.8 1.5 %collective-permute-start.1 = (bf16[64,2432]{1,0:T(8,128)(2,1)S(1)}, bf16[64,2432]{1,0:T(8,128)(2,1)S(1)}, u32[]{:S(2)}, u32[]{:S(2)}) collective-permute-start(bf16[64,2432]{1,0:T(8,128)(2,1)S(1)} %get-tuple-element.54.refs_0_), channel_id=1, source_target_pairs={{0,2},{2,0},{4,6},{6,4},{8,10},{10,8},{12,14},{14,12},{1,3},{3,1},... | collective-permute-start | bytes 933896 | tf_op jit(solution)/shard_map/ppermute | solution.py:330
  8.3 1.6 %collective-permute-start.6 = (bf16[64,2048]{1,0:T(8,128)(2,1)S(1)}, bf16[64,2048]{1,0:T(8,128)(2,1)S(1)}, u32[]{:S(2)}, u32[]{:S(2)}) collective-permute-start(bf16[64,2048]{1,0:T(8,128)(2,1)S(1)} %get-tuple-element.66.refs_0_), channel_id=1, source_target_pairs={{0,4},{2,6},{4,8},{6,10},{8,12},{10,14},{12,0},{14,2},{1,5},{3,7},... | collective-permute-start | bytes 786440 | tf_op jit(solution)/shard_map/ppermute | solution.py:330
  9.9 0.5 collective-permute-start.7
  10.4 2.6 %scale_codes.1.refs_4_.refs_2_ = bf16[256,4480]{1,0:T(8,128)(2,1)S(1)} custom-call(s32[1]{0:T(128)} %bitcast.part_ref, bf16[256,8192]{1,0:T(8,128)(2,1)} %codes_ref.3, s32[64,256]{1,0:T(8,128)} %bitcast.26), custom_call_target="tpu_custom_call" | custom-call | flops 2097152 | bytes 8388608 | tf_op jit(solution)/shard_map/scale_codes/pallas_call | solution.py:158
  13.0 4.3 %collective-permute-done.refs_1_ = bf16[64,2432]{1,0:T(8,128)(2,1)S(1)} collective-permute-done((bf16[64,2432]{1,0:T(8,128)(2,1)S(1)}, bf16[64,2432]{1,0:T(8,128)(2,1)S(1)}, u32[]{:S(2)}, u32[]{:S(2)}) %collective-permute-start) | collective-permute-done | bytes 311328 | tf_op jit(solution)/shard_map/ppermute | solution.py:330
  17.3 0.0 collective-permute-done.1.refs_1_
  17.3 1.4 %collective-permute-start.2 = (bf16[64,2432]{1,0:T(8,128)(2,1)S(1)}, bf16[64,2432]{1,0:T(8,128)(2,1)S(1)}, u32[]{:S(2)}, u32[]{:S(2)}) collective-permute-start(bf16[64,2432]{1,0:T(8,128)(2,1)S(1)} %collective-permute-done.refs_1_), channel_id=1, source_target_pairs={{0,4},{2,6},{4,8},{6,10},{8,12},{10,14},{12,0},{14,2},{1,5},{3,7},... | collective-permute-start | bytes 933896 | tf_op jit(solution)/shard_map/ppermute | solution.py:330
  18.7 1.5 %collective-permute-start.3 = (bf16[64,2432]{1,0:T(8,128)(2,1)S(1)}, bf16[64,2432]{1,0:T(8,128)(2,1)S(1)}, u32[]{:S(2)}, u32[]{:S(2)}) collective-permute-start(bf16[64,2432]{1,0:T(8,128)(2,1)S(1)} %collective-permute-done.refs_1_), channel_id=1, source_target_pairs={{0,2},{2,0},{4,6},{6,4},{8,10},{10,8},{12,14},{14,12},{1,3},{3,1},... | collective-permute-start | bytes 933896 | tf_op jit(solution)/shard_map/ppermute | solution.py:330
  20.2 2.7 %collective-permute-done.6.refs_1_ = bf16[64,2048]{1,0:T(8,128)(2,1)S(1)} collective-permute-done((bf16[64,2048]{1,0:T(8,128)(2,1)S(1)}, bf16[64,2048]{1,0:T(8,128)(2,1)S(1)}, u32[]{:S(2)}, u32[]{:S(2)}) %collective-permute-start.6) | collective-permute-done | bytes 262176 | tf_op jit(solution)/shard_map/ppermute | solution.py:330
  22.9 0.0 collective-permute-done.7.refs_1_
  22.9 1.4 %collective-permute-start.8 = (bf16[64,2048]{1,0:T(8,128)(2,1)S(1)}, bf16[64,2048]{1,0:T(8,128)(2,1)S(1)}, u32[]{:S(2)}, u32[]{:S(2)}) collective-permute-start(bf16[64,2048]{1,0:T(8,128)(2,1)S(1)} %collective-permute-done.6.refs_1_), channel_id=1, source_target_pairs={{0,4},{2,6},{4,8},{6,10},{8,12},{10,14},{12,0},{14,2},{1,5},{3,7},... | collective-permute-start | bytes 786440 | tf_op jit(solution)/shard_map/ppermute | solution.py:330
  24.3 1.5 %collective-permute-start.9 = (bf16[64,2048]{1,0:T(8,128)(2,1)S(1)}, bf16[64,2048]{1,0:T(8,128)(2,1)S(1)}, u32[]{:S(2)}, u32[]{:S(2)}) collective-permute-start(bf16[64,2048]{1,0:T(8,128)(2,1)S(1)} %collective-permute-done.6.refs_1_), channel_id=1, source_target_pairs={{0,2},{2,0},{4,6},{6,4},{8,10},{10,8},{12,14},{14,12},{1,3},{3,1},... | collective-permute-start | bytes 786440 | tf_op jit(solution)/shard_map/ppermute | solution.py:330
  25.8 3.8 %collective-permute-done.2.refs_1_ = bf16[64,2432]{1,0:T(8,128)(2,1)S(1)} collective-permute-done((bf16[64,2432]{1,0:T(8,128)(2,1)S(1)}, bf16[64,2432]{1,0:T(8,128)(2,1)S(1)}, u32[]{:S(2)}, u32[]{:S(2)}) %collective-permute-start.2) | collective-permute-done | bytes 311328 | tf_op jit(solution)/shard_map/ppermute | solution.py:330
  29.6 0.0 collective-permute-done.3.refs_2_
  29.6 1.4 %collective-permute-start.4 = (bf16[64,2432]{1,0:T(8,128)(2,1)S(1)}, bf16[64,2432]{1,0:T(8,128)(2,1)S(1)}, u32[]{:S(2)}, u32[]{:S(2)}) collective-permute-start(bf16[64,2432]{1,0:T(8,128)(2,1)S(1)} %collective-permute-done.2.refs_1_), channel_id=1, source_target_pairs={{0,4},{2,6},{4,8},{6,10},{8,12},{10,14},{12,0},{14,2},{1,5},{3,7},... | collective-permute-start | bytes 933896 | tf_op jit(solution)/shard_map/ppermute | solution.py:330
  31.0 1.5 %collective-permute-start.5 = (bf16[64,2432]{1,0:T(8,128)(2,1)S(1)}, bf16[64,2432]{1,0:T(8,128)(2,1)S(1)}, u32[]{:S(2)}, u32[]{:S(2)}) collective-permute-start(bf16[64,2432]{1,0:T(8,128)(2,1)S(1)} %collective-permute-done.2.refs_1_), channel_id=1, source_target_pairs={{0,2},{2,0},{4,6},{6,4},{8,10},{10,8},{12,14},{14,12},{1,3},{3,1},... | collective-permute-start | bytes 933896 | tf_op jit(solution)/shard_map/ppermute | solution.py:330
  32.5 2.7 %collective-permute-done.8.refs_5_.refs_1_ = bf16[64,2048]{1,0:T(8,128)(2,1)S(1)} collective-permute-done((bf16[64,2048]{1,0:T(8,128)(2,1)S(1)}, bf16[64,2048]{1,0:T(8,128)(2,1)S(1)}, u32[]{:S(2)}, u32[]{:S(2)}) %collective-permute-start.8) | collective-permute-done | bytes 262176 | tf_op jit(solution)/shard_map/ppermute | solution.py:330
  35.2 0.0 collective-permute-done.9.refs_2_
  35.2 1.4 %collective-permute-start.10 = (bf16[64,2048]{1,0:T(8,128)(2,1)S(1)}, bf16[64,2048]{1,0:T(8,128)(2,1)S(1)}, u32[]{:S(2)}, u32[]{:S(2)}) collective-permute-start(bf16[64,2048]{1,0:T(8,128)(2,1)S(1)} %collective-permute-done.8.refs_5_.refs_1_), channel_id=1, source_target_pairs={{0,4},{2,6},{4,8},{6,10},{8,12},{10,14},{12,0},{14,2},{1,5},{3,7},... | collective-permute-start | bytes 786440 | tf_op jit(solution)/shard_map/ppermute | solution.py:330
  36.6 1.5 %collective-permute-start.11 = (bf16[64,2048]{1,0:T(8,128)(2,1)S(1)}, bf16[64,2048]{1,0:T(8,128)(2,1)S(1)}, u32[]{:S(2)}, u32[]{:S(2)}) collective-permute-start(bf16[64,2048]{1,0:T(8,128)(2,1)S(1)} %collective-permute-done.8.refs_5_.refs_1_), channel_id=1, source_target_pairs={{0,2},{2,0},{4,6},{6,4},{8,10},{10,8},{12,14},{14,12},{1,3},{3,1},... | collective-permute-start | bytes 786440 | tf_op jit(solution)/shard_map/ppermute | solution.py:330
  38.1 3.8 %collective-permute-done.4.refs_3_ = bf16[64,2432]{1,0:T(8,128)(2,1)S(1)} collective-permute-done((bf16[64,2432]{1,0:T(8,128)(2,1)S(1)}, bf16[64,2432]{1,0:T(8,128)(2,1)S(1)}, u32[]{:S(2)}, u32[]{:S(2)}) %collective-permute-start.4) | collective-permute-done | bytes 311328 | tf_op jit(solution)/shard_map/ppermute | solution.py:330
  41.9 0.0 collective-permute-done.5.refs_2_
  41.9 0.8 %score.5.refs_5_ = f32[448,256]{1,0:T(8,128)S(1)} custom-call(s32[1]{0:T(128)} %bitcast.1.half_ref, bf16[256,2432]{1,0:T(8,128)(2,1)S(1)} %stash.5.refs_0_, bf16[64,2432]{1,0:T(8,128)(2,1)S(1)} %collective-permute-done.2.refs_1_, bf16[64,2432]{1,0:T(8,128)(2,1)S(1)} %collective-permute-done.5.refs_2_, bf16[64,2432]{1,0:T(8,128)(2,1)S(1)} %collective-permute-done.4.refs_3_, ...), custom_call_target="tpu_custom_call" | custom-call | flops 1027604480 | bytes 2293760 | tf_op jit(solution)/shard_map/score/pallas_call | solution.py:249
  42.7 1.6 %collective-permute-start.17 = (bf16[64,2432]{1,0:T(8,128)(2,1)S(1)}, bf16[64,2432]{1,0:T(8,128)(2,1)S(1)}, u32[]{:S(2)}, u32[]{:S(2)}) collective-permute-start(bf16[64,2432]{1,0:T(8,128)(2,1)S(1)} %collective-permute-done.4.refs_3_), channel_id=1, source_target_pairs={{0,2},{2,0},{4,6},{6,4},{8,10},{10,8},{12,14},{14,12},{1,3},{3,1},... | collective-permute-start | bytes 933896 | tf_op jit(solution)/shard_map/ppermute | solution.py:330
  44.3 1.8 %collective-permute-done.10.refs_7_.refs_3_ = bf16[64,2048]{1,0:T(8,128)(2,1)S(1)} collective-permute-done((bf16[64,2048]{1,0:T(8,128)(2,1)S(1)}, bf16[64,2048]{1,0:T(8,128)(2,1)S(1)}, u32[]{:S(2)}, u32[]{:S(2)}) %collective-permute-start.10) | collective-permute-done | bytes 262176 | tf_op jit(solution)/shard_map/ppermute | solution.py:330
  46.1 1.2 %collective-permute-done.11.refs_6_.refs_2_ = bf16[64,2048]{1,0:T(8,128)(2,1)S(1)} collective-permute-done((bf16[64,2048]{1,0:T(8,128)(2,1)S(1)}, bf16[64,2048]{1,0:T(8,128)(2,1)S(1)}, u32[]{:S(2)}, u32[]{:S(2)}) %collective-permute-start.11) | collective-permute-done | bytes 262176 | tf_op jit(solution)/shard_map/ppermute | solution.py:330
  47.3 1.6 %collective-permute-start.16 = (bf16[64,2048]{1,0:T(8,128)(2,1)S(1)}, bf16[64,2048]{1,0:T(8,128)(2,1)S(1)}, u32[]{:S(2)}, u32[]{:S(2)}) collective-permute-start(bf16[64,2048]{1,0:T(8,128)(2,1)S(1)} %collective-permute-done.11.refs_6_.refs_2_), channel_id=1, source_target_pairs={{0,4},{2,6},{4,8},{6,10},{8,12},{10,14},{12,0},{14,2},{1,5},{3,7},... | collective-permute-start | bytes 786440 | tf_op jit(solution)/shard_map/ppermute | solution.py:330
  48.9 0.0 collective-permute-done.12.refs_8_.refs_1_
  48.9 1.1 %score.6 = (f32[7,32,256]{2,1,0:T(8,128)S(1)}, f32[7,32,256]{2,1,0:T(8,128)S(1)}) custom-call(s32[1]{0:T(128)} %bitcast.1.half_ref, bf16[256,2432]{1,0:T(8,128)(2,1)S(1)} %stash.5.refs_0_, bf16[64,2432]{1,0:T(8,128)(2,1)S(1)} %collective-permute-done.2.refs_1_, bf16[64,2432]{1,0:T(8,128)(2,1)S(1)} %collective-permute-done.5.refs_2_, ...), custom_call_target="tpu_custom_call" | custom-call | flops 851443712 | bytes 1900544 | tf_op jit(solution)/shard_map/score/pallas_call | solution.py:249
  50.0 0.1 collective-permute-start.13
  50.1 0.7 %score.7 = (f32[7,32,256]{2,1,0:T(8,128)S(1)}, f32[7,32,256]{2,1,0:T(8,128)S(1)}) custom-call(s32[1]{0:T(128)} %bitcast.1.half_ref, bf16[256,2048]{1,0:T(8,128)(2,1)S(1)} %stash.7.refs_4_.refs_0_, bf16[64,2048]{1,0:T(8,128)(2,1)S(1)} %collective-permute-done.8.refs_5_.refs_1_, bf16[64,2048]{1,0:T(8,128)(2,1)S(1)} %collective-permute-done.11.refs_6_.refs_2_, ...), custom_call_target="tpu_custom_call" | custom-call | flops 1027604480 | bytes 2293760 | tf_op jit(solution)/shard_map/score/pallas_call | solution.py:249
  50.7 0.6 collective-permute-start.15
  51.3 0.2 collective-permute-done.13.b_ref
  51.6 0.6 collective-permute-start.14
  52.1 0.1 collective-permute-done.17.refs_0_
  52.2 0.9 %score.8 = (f32[64,256]{1,0:T(8,128)S(1)}, f32[64,256]{1,0:T(8,128)S(1)}) custom-call(s32[1]{0:T(128)} %bitcast.1.half_ref, bf16[64,2432]{1,0:T(8,128)(2,1)S(1)} %collective-permute-done.17.refs_0_, bf16[256,3712]{1,0:T(8,128)(2,1)S(1)} %collective-permute-done.12.refs_8_.refs_1_, bf16[256,4480]{1,0:T(8,128)(2,1)S(1)} %scale_codes.1.refs_4_.refs_2_), custom_call_target="tpu_custom_call" | custom-call | flops 268435456 | bytes 1900544 | tf_op jit(solution)/shard_map/score/pallas_call | solution.py:249
  53.1 2.4 %collective-permute-done.16.refs_0_ = bf16[64,2048]{1,0:T(8,128)(2,1)S(1)} collective-permute-done((bf16[64,2048]{1,0:T(8,128)(2,1)S(1)}, bf16[64,2048]{1,0:T(8,128)(2,1)S(1)}, u32[]{:S(2)}, u32[]{:S(2)}) %collective-permute-start.16) | collective-permute-done | bytes 262176 | tf_op jit(solution)/shard_map/ppermute | solution.py:330
  55.5 0.0 copy-start
  55.5 0.7 %score.9 = (f32[1,32,256]{2,1,0:T(8,128)S(1)}, f32[1,32,256]{2,1,0:T(8,128)S(1)}, f32[1,32,256]{2,1,0:T(8,128)S(1)}, f32[1,32,256]{2,1,0:T(8,128)S(1)}) custom-call(s32[1]{0:T(128)} %bitcast.1.half_ref, bf16[64,2048]{1,0:T(8,128)(2,1)S(1)} %collective-permute-done.16.refs_0_, bf16[256,3712]{1,0:T(8,128)(2,1)S(1)} %collective-permute-done.12.refs_8_.refs_1_, ...), custom_call_target="tpu_custom_call" | custom-call | flops 8053063680 | bytes 1900544 | tf_op jit(solution)/shard_map/score/pallas_call | solution.py:249
  56.1 0.1 collective-permute-start.18
  56.2 0.6 collective-permute-start.19
  56.8 1.3 %collective-permute-start.20 = (f32[1,32,256]{2,1,0:T(8,128)S(1)}, f32[1,32,256]{2,1,0:T(8,128)S(1)}, u32[]{:S(2)}, u32[]{:S(2)}) collective-permute-start(f32[1,32,256]{2,1,0:T(8,128)S(1)} %get-tuple-element.91), channel_id=1, source_target_pairs={{0,1},{1,0},{2,3},{3,2},{4,5},{5,4},{6,7},{7,6},{8,9},{9,8},{10,11... | collective-permute-start | bytes 98312 | tf_op jit(solution)/shard_map/ppermute | solution.py:371
  58.0 0.0 collective-permute-done.15
  58.0 1.9 %collective-permute-done.18 = f32[1,32,256]{2,1,0:T(8,128)S(1)} collective-permute-done((f32[1,32,256]{2,1,0:T(8,128)S(1)}, f32[1,32,256]{2,1,0:T(8,128)S(1)}, u32[]{:S(2)}, u32[]{:S(2)}) %collective-permute-start.18) | collective-permute-done | bytes 32800 | tf_op jit(solution)/shard_map/ppermute | solution.py:386
  59.9 0.8 %collective-permute-done.19 = f32[1,32,256]{2,1,0:T(8,128)S(1)} collective-permute-done((f32[1,32,256]{2,1,0:T(8,128)S(1)}, f32[1,32,256]{2,1,0:T(8,128)S(1)}, u32[]{:S(2)}, u32[]{:S(2)}) %collective-permute-start.19) | collective-permute-done | bytes 32800 | tf_op jit(solution)/shard_map/ppermute | solution.py:387
  60.7 0.0 collective-permute-done.20
  60.7 0.0 collective-permute-done.14
  60.7 0.0 copy-done
  60.7 1.6 %place_scores.1 = f32[8,32,256]{2,1,0:T(8,128)} custom-call(s32[8]{0:T(128)S(1)} %stack.35.order_ref, s32[1,256]{1,0:T(1,128)S(1)} %copy-done, f32[224,256]{1,0:T(8,128)S(1)} %bitcast.20, f32[224,256]{1,0:T(8,128)S(1)} %bitcast.18, f32[224,256]{1,0:T(8,128)S(1)} %bitcast.19, f32[32,256]{1,0:T(8,128)S(1)} %bitcast.22, f32[32,256]{1,0:T(8,128)S(1)} %bitcast.23, ...), custom_call_target="tpu_custom_call" | custom-call | tf_op jit(solution)/shard_map/place_scores/pallas_call | solution.py:297
  (5 shorter events, 0.2 us)
Async XLA Ops:
  2.2 46.7 %collective-permute-start.12 = (bf16[256,3712]{1,0:T(8,128)(2,1)S(1)}, bf16[256,3712]{1,0:T(8,128)(2,1)S(1)}, u32[]{:S(2)}, u32[]{:S(2)}) collective-permute-start(bf16[256,3712]{1,0:T(8,128)(2,1)S(1)} %get-tuple-element.78), channel_id=1, source_target_pairs={{0,16},{16,0},{1,17},{17,1},{2,18},{18,2},{3,19},{19,3},{4,20},{20... | collective-permute-start | bytes 5701640 | tf_op jit(solution)/shard_map/ppermute | solution.py:341
  5.2 12.1 %collective-permute-start = (bf16[64,2432]{1,0:T(8,128)(2,1)S(1)}, bf16[64,2432]{1,0:T(8,128)(2,1)S(1)}, u32[]{:S(2)}, u32[]{:S(2)}) collective-permute-start(bf16[64,2432]{1,0:T(8,128)(2,1)S(1)} %get-tuple-element.54.refs_0_), channel_id=1, source_target_pairs={{0,4},{2,6},{4,8},{6,10},{8,12},{10,14},{12,0},{14,2},{1,5},{3,7},... | collective-permute-start | bytes 933896 | tf_op jit(solution)/shard_map/ppermute | solution.py:330
  6.8 10.5 %collective-permute-start.1 = (bf16[64,2432]{1,0:T(8,128)(2,1)S(1)}, bf16[64,2432]{1,0:T(8,128)(2,1)S(1)}, u32[]{:S(2)}, u32[]{:S(2)}) collective-permute-start(bf16[64,2432]{1,0:T(8,128)(2,1)S(1)} %get-tuple-element.54.refs_0_), channel_id=1, source_target_pairs={{0,2},{2,0},{4,6},{6,4},{8,10},{10,8},{12,14},{14,12},{1,3},{3,1},... | collective-permute-start | bytes 933896 | tf_op jit(solution)/shard_map/ppermute | solution.py:330
  8.3 14.6 %collective-permute-start.6 = (bf16[64,2048]{1,0:T(8,128)(2,1)S(1)}, bf16[64,2048]{1,0:T(8,128)(2,1)S(1)}, u32[]{:S(2)}, u32[]{:S(2)}) collective-permute-start(bf16[64,2048]{1,0:T(8,128)(2,1)S(1)} %get-tuple-element.66.refs_0_), channel_id=1, source_target_pairs={{0,4},{2,6},{4,8},{6,10},{8,12},{10,14},{12,0},{14,2},{1,5},{3,7},... | collective-permute-start | bytes 786440 | tf_op jit(solution)/shard_map/ppermute | solution.py:330
  9.9 13.1 %collective-permute-start.7 = (bf16[64,2048]{1,0:T(8,128)(2,1)S(1)}, bf16[64,2048]{1,0:T(8,128)(2,1)S(1)}, u32[]{:S(2)}, u32[]{:S(2)}) collective-permute-start(bf16[64,2048]{1,0:T(8,128)(2,1)S(1)} %get-tuple-element.66.refs_0_), channel_id=1, source_target_pairs={{0,2},{2,0},{4,6},{6,4},{8,10},{10,8},{12,14},{14,12},{1,3},{3,1},... | collective-permute-start | bytes 786440 | tf_op jit(solution)/shard_map/ppermute | solution.py:330
  17.3 12.3 %collective-permute-start.2 = (bf16[64,2432]{1,0:T(8,128)(2,1)S(1)}, bf16[64,2432]{1,0:T(8,128)(2,1)S(1)}, u32[]{:S(2)}, u32[]{:S(2)}) collective-permute-start(bf16[64,2432]{1,0:T(8,128)(2,1)S(1)} %collective-permute-done.refs_1_), channel_id=1, source_target_pairs={{0,4},{2,6},{4,8},{6,10},{8,12},{10,14},{12,0},{14,2},{1,5},{3,7},... | collective-permute-start | bytes 933896 | tf_op jit(solution)/shard_map/ppermute | solution.py:330
  18.7 10.9 %collective-permute-start.3 = (bf16[64,2432]{1,0:T(8,128)(2,1)S(1)}, bf16[64,2432]{1,0:T(8,128)(2,1)S(1)}, u32[]{:S(2)}, u32[]{:S(2)}) collective-permute-start(bf16[64,2432]{1,0:T(8,128)(2,1)S(1)} %collective-permute-done.refs_1_), channel_id=1, source_target_pairs={{0,2},{2,0},{4,6},{6,4},{8,10},{10,8},{12,14},{14,12},{1,3},{3,1},... | collective-permute-start | bytes 933896 | tf_op jit(solution)/shard_map/ppermute | solution.py:330
  22.9 12.3 %collective-permute-start.8 = (bf16[64,2048]{1,0:T(8,128)(2,1)S(1)}, bf16[64,2048]{1,0:T(8,128)(2,1)S(1)}, u32[]{:S(2)}, u32[]{:S(2)}) collective-permute-start(bf16[64,2048]{1,0:T(8,128)(2,1)S(1)} %collective-permute-done.6.refs_1_), channel_id=1, source_target_pairs={{0,4},{2,6},{4,8},{6,10},{8,12},{10,14},{12,0},{14,2},{1,5},{3,7},... | collective-permute-start | bytes 786440 | tf_op jit(solution)/shard_map/ppermute | solution.py:330
  24.3 10.9 %collective-permute-start.9 = (bf16[64,2048]{1,0:T(8,128)(2,1)S(1)}, bf16[64,2048]{1,0:T(8,128)(2,1)S(1)}, u32[]{:S(2)}, u32[]{:S(2)}) collective-permute-start(bf16[64,2048]{1,0:T(8,128)(2,1)S(1)} %collective-permute-done.6.refs_1_), channel_id=1, source_target_pairs={{0,2},{2,0},{4,6},{6,4},{8,10},{10,8},{12,14},{14,12},{1,3},{3,1},... | collective-permute-start | bytes 786440 | tf_op jit(solution)/shard_map/ppermute | solution.py:330
  29.6 12.3 %collective-permute-start.4 = (bf16[64,2432]{1,0:T(8,128)(2,1)S(1)}, bf16[64,2432]{1,0:T(8,128)(2,1)S(1)}, u32[]{:S(2)}, u32[]{:S(2)}) collective-permute-start(bf16[64,2432]{1,0:T(8,128)(2,1)S(1)} %collective-permute-done.2.refs_1_), channel_id=1, source_target_pairs={{0,4},{2,6},{4,8},{6,10},{8,12},{10,14},{12,0},{14,2},{1,5},{3,7},... | collective-permute-start | bytes 933896 | tf_op jit(solution)/shard_map/ppermute | solution.py:330
  31.0 10.9 %collective-permute-start.5 = (bf16[64,2432]{1,0:T(8,128)(2,1)S(1)}, bf16[64,2432]{1,0:T(8,128)(2,1)S(1)}, u32[]{:S(2)}, u32[]{:S(2)}) collective-permute-start(bf16[64,2432]{1,0:T(8,128)(2,1)S(1)} %collective-permute-done.2.refs_1_), channel_id=1, source_target_pairs={{0,2},{2,0},{4,6},{6,4},{8,10},{10,8},{12,14},{14,12},{1,3},{3,1},... | collective-permute-start | bytes 933896 | tf_op jit(solution)/shard_map/ppermute | solution.py:330
  35.2 10.9 %collective-permute-start.10 = (bf16[64,2048]{1,0:T(8,128)(2,1)S(1)}, bf16[64,2048]{1,0:T(8,128)(2,1)S(1)}, u32[]{:S(2)}, u32[]{:S(2)}) collective-permute-start(bf16[64,2048]{1,0:T(8,128)(2,1)S(1)} %collective-permute-done.8.refs_5_.refs_1_), channel_id=1, source_target_pairs={{0,4},{2,6},{4,8},{6,10},{8,12},{10,14},{12,0},{14,2},{1,5},{3,7},... | collective-permute-start | bytes 786440 | tf_op jit(solution)/shard_map/ppermute | solution.py:330
  36.6 10.7 %collective-permute-start.11 = (bf16[64,2048]{1,0:T(8,128)(2,1)S(1)}, bf16[64,2048]{1,0:T(8,128)(2,1)S(1)}, u32[]{:S(2)}, u32[]{:S(2)}) collective-permute-start(bf16[64,2048]{1,0:T(8,128)(2,1)S(1)} %collective-permute-done.8.refs_5_.refs_1_), channel_id=1, source_target_pairs={{0,2},{2,0},{4,6},{6,4},{8,10},{10,8},{12,14},{14,12},{1,3},{3,1},... | collective-permute-start | bytes 786440 | tf_op jit(solution)/shard_map/ppermute | solution.py:330
  42.7 9.5 %collective-permute-start.17 = (bf16[64,2432]{1,0:T(8,128)(2,1)S(1)}, bf16[64,2432]{1,0:T(8,128)(2,1)S(1)}, u32[]{:S(2)}, u32[]{:S(2)}) collective-permute-start(bf16[64,2432]{1,0:T(8,128)(2,1)S(1)} %collective-permute-done.4.refs_3_), channel_id=1, source_target_pairs={{0,2},{2,0},{4,6},{6,4},{8,10},{10,8},{12,14},{14,12},{1,3},{3,1},... | collective-permute-start | bytes 933896 | tf_op jit(solution)/shard_map/ppermute | solution.py:330
  47.3 8.2 %collective-permute-start.16 = (bf16[64,2048]{1,0:T(8,128)(2,1)S(1)}, bf16[64,2048]{1,0:T(8,128)(2,1)S(1)}, u32[]{:S(2)}, u32[]{:S(2)}) collective-permute-start(bf16[64,2048]{1,0:T(8,128)(2,1)S(1)} %collective-permute-done.11.refs_6_.refs_2_), channel_id=1, source_target_pairs={{0,4},{2,6},{4,8},{6,10},{8,12},{10,14},{12,0},{14,2},{1,5},{3,7},... | collective-permute-start | bytes 786440 | tf_op jit(solution)/shard_map/ppermute | solution.py:330
  50.0 1.6 %collective-permute-start.13 = (f32[7,32,256]{2,1,0:T(8,128)S(1)}, f32[7,32,256]{2,1,0:T(8,128)S(1)}, u32[]{:S(2)}, u32[]{:S(2)}) collective-permute-start(f32[7,32,256]{2,1,0:T(8,128)S(1)} %get-tuple-element.80), channel_id=1, source_target_pairs={{0,1},{1,0},{2,3},{3,2},{4,5},{5,4},{6,7},{7,6},{8,9},{9,8},{10,11... | collective-permute-start | bytes 688136 | tf_op jit(solution)/shard_map/ppermute | solution.py:371
  50.7 7.3 %collective-permute-start.15 = (f32[7,32,256]{2,1,0:T(8,128)S(1)}, f32[7,32,256]{2,1,0:T(8,128)S(1)}, u32[]{:S(2)}, u32[]{:S(2)}) collective-permute-start(f32[7,32,256]{2,1,0:T(8,128)S(1)} %get-tuple-element.84), channel_id=1, source_target_pairs={{0,1},{1,0},{2,3},{3,2},{4,5},{5,4},{6,7},{7,6},{8,9},{9,8},{10,11... | collective-permute-start | bytes 688136 | tf_op jit(solution)/shard_map/ppermute | solution.py:371
  51.6 9.1 %collective-permute-start.14 = (f32[7,32,256]{2,1,0:T(8,128)S(1)}, f32[7,32,256]{2,1,0:T(8,128)S(1)}, u32[]{:S(2)}, u32[]{:S(2)}) collective-permute-start(f32[7,32,256]{2,1,0:T(8,128)S(1)} %add.80), channel_id=1, source_target_pairs={{0,16},{16,0},{1,17},{17,1},{2,18},{18,2},{3,19},{19,3},{4,20},{20... | collective-permute-start | bytes 688136 | tf_op jit(solution)/shard_map/ppermute | solution.py:376
  55.5 5.2 %copy-start = (s32[1,256]{1,0:T(1,128)S(1)}, s32[1,256]{1,0:T(1,128)}, u32[]{:S(2)}) copy-start(s32[1,256]{1,0:T(1,128)} %ids_ref.1) | copy-start | bytes 3076
  56.1 3.8 %collective-permute-start.18 = (f32[1,32,256]{2,1,0:T(8,128)S(1)}, f32[1,32,256]{2,1,0:T(8,128)S(1)}, u32[]{:S(2)}, u32[]{:S(2)}) collective-permute-start(f32[1,32,256]{2,1,0:T(8,128)S(1)} %get-tuple-element.89), channel_id=1, source_target_pairs={{0,17},{1,16},{16,1},{17,0},{2,19},{3,18},{18,3},{19,2},{4,21},{5,... | collective-permute-start | bytes 98312 | tf_op jit(solution)/shard_map/ppermute | solution.py:386
  56.2 4.5 %collective-permute-start.19 = (f32[1,32,256]{2,1,0:T(8,128)S(1)}, f32[1,32,256]{2,1,0:T(8,128)S(1)}, u32[]{:S(2)}, u32[]{:S(2)}) collective-permute-start(f32[1,32,256]{2,1,0:T(8,128)S(1)} %get-tuple-element.90), channel_id=1, source_target_pairs={{0,16},{16,0},{1,17},{17,1},{2,18},{18,2},{3,19},{19,3},{4,20},{20... | collective-permute-start | bytes 98312 | tf_op jit(solution)/shard_map/ppermute | solution.py:387
  56.8 3.9 %collective-permute-start.20 = (f32[1,32,256]{2,1,0:T(8,128)S(1)}, f32[1,32,256]{2,1,0:T(8,128)S(1)}, u32[]{:S(2)}, u32[]{:S(2)}) collective-permute-start(f32[1,32,256]{2,1,0:T(8,128)S(1)} %get-tuple-element.91), channel_id=1, source_target_pairs={{0,1},{1,0},{2,3},{3,2},{4,5},{5,4},{6,7},{7,6},{8,9},{9,8},{10,11... | collective-permute-start | bytes 98312 | tf_op jit(solution)/shard_map/ppermute | solution.py:371

commit v12 on v11

--- a/solution.py
+++ b/solution.py
@@ -381,13 +381,8 @@
     their_keep, their_send, own_keep, own_send = score(
         half, rows, late[trail], [theirs, ours], cuts[1 - LEAD], begun, LATE_WEIGHT
     )
-    across = [(i, 3 - i) for i in range(4)]
-    last = [
-        lax.ppermute(their_send, ("groups", "dim"), across),
-        lax.ppermute(their_keep, "groups", swap),
-        over_dim(own_send),
-        own_keep,
-    ]
+    given = lax.ppermute(add(their_keep, over_dim(their_send)), "groups", swap)
+    last = [given, own_keep, over_dim(own_send)]
     return place(order, example_ids, [shares, last], rows // 2)
 
 

time: 62.4 us -> 63 us (level)
  waiting for transfers between devices: 25.6 us -> 27.1 us
  starting transfers between devices: 25.9 us -> 25.1 us
    ppermute x2 -> x1, waiting for transfers between devices: 2.64 us -> 3.4 us  [shards(): given = lax.ppermute(add(their_keep, over_dim(their_send)), 'groups', swap)]
    ppermute x3 -> x4, starting transfers between devices: 1.91 us -> 1.18 us  [over_dim(): return lax.ppermute(value, 'dim', [(0, 1), (1, 0)])]
    ppermute x3 -> x4, waiting for transfers between devices: 0.24 us -> 0.93 us  [over_dim(): return lax.ppermute(value, 'dim', [(0, 1), (1, 0)])]
where the time goes in v12:
time: 63 us; the launch traced here: 62.9 us
  waiting for transfers between devices  27.1 us (43%)
  starting transfers between devices  25.1 us (40%)
  Pallas kernels  10.5 us (17%)
    ppermute x14, waiting for transfers between devices, step(): return lax.ppermute(value, 'ex', pairs)  22.8 us
    ppermute x14, starting transfers between devices, step(): return lax.ppermute(value, 'ex', pairs)  19.8 us
    pallas_call x5, Pallas kernels, score(): pl.pallas_call(functools.partial(score_kernel, [len(arrays) for arrays in...  4.07 us
    ppermute x1, waiting for transfers between devices, shards(): given = lax.ppermute(add(their_keep, over_dim(their_send)), 'groups', swap)  3.4 us
    ppermute x1, starting transfers between devices, shards(): theirs = lax.ppermute(sent, 'groups', swap)  3.03 us
    pallas_call x1, Pallas kernels, scale(): pl.pallas_call(functools.partial(scale_kernel, alone), out_shape=pltpu.VM...  2.6 us
    pallas_call x1, Pallas kernels, cut(): pl.pallas_call(functools.partial(cut_kernel, alone, cuts), out_shape=[plt...  2.09 us
    pallas_call x1, Pallas kernels, place(): pl.pallas_call(functools.partial(place_kernel, [len(group) for group in g...  1.57 us
  transfers between devices with their start and end apart: 21, of which 12 were waited for; matrix products, arithmetic and copies ran while one was open for 0% of the time, Pallas kernels for 11%

profile of v12, /device:TPU:0, one launch (start us, length us, event | category | flops | bytes accessed | tf_op | source)
XLA Modules:
  0.0 62.9 jit_solution(7358593798648773841)
XLA Ops:
  0.0 0.1 stack.35.order_ref
  0.1 2.1 %cut_queries.1 = (bf16[64,2432]{1,0:T(8,128)(2,1)S(1)}, bf16[64,2048]{1,0:T(8,128)(2,1)S(1)}, bf16[256,3712]{1,0:T(8,128)(2,1)S(1)}) custom-call(s32[1]{0:T(128)} %bitcast.part_ref, bf16[1,64,8192]{2,1,0:T(8,128)(2,1)} %queries_ref.1, bf16[256,8192]{1,0:T(8,128)(2,1)} %codes_ref.3, s32[64,256]{1,0:T(8,128)} %bitcast.23), custom_call_target="tpu_custom_call" | custom-call | flops 2097152 | bytes 4194304 | tf_op jit(solution)/shard_map/cut_queries/pallas_call | solution.py:120
  2.2 3.0 %collective-permute-start.12 = (bf16[256,3712]{1,0:T(8,128)(2,1)S(1)}, bf16[256,3712]{1,0:T(8,128)(2,1)S(1)}, u32[]{:S(2)}, u32[]{:S(2)}) collective-permute-start(bf16[256,3712]{1,0:T(8,128)(2,1)S(1)} %get-tuple-element.78), channel_id=1, source_target_pairs={{0,16},{16,0},{1,17},{17,1},{2,18},{18,2},{3,19},{19,3},{4,20},{20... | collective-permute-start | bytes 5701640 | tf_op jit(solution)/shard_map/ppermute | solution.py:341
  5.2 1.6 %collective-permute-start = (bf16[64,2432]{1,0:T(8,128)(2,1)S(1)}, bf16[64,2432]{1,0:T(8,128)(2,1)S(1)}, u32[]{:S(2)}, u32[]{:S(2)}) collective-permute-start(bf16[64,2432]{1,0:T(8,128)(2,1)S(1)} %get-tuple-element.54.refs_0_), channel_id=1, source_target_pairs={{0,4},{2,6},{4,8},{6,10},{8,12},{10,14},{12,0},{14,2},{1,5},{3,7},... | collective-permute-start | bytes 933896 | tf_op jit(solution)/shard_map/ppermute | solution.py:330
  6.8 1.5 %collective-permute-start.1 = (bf16[64,2432]{1,0:T(8,128)(2,1)S(1)}, bf16[64,2432]{1,0:T(8,128)(2,1)S(1)}, u32[]{:S(2)}, u32[]{:S(2)}) collective-permute-start(bf16[64,2432]{1,0:T(8,128)(2,1)S(1)} %get-tuple-element.54.refs_0_), channel_id=1, source_target_pairs={{0,2},{2,0},{4,6},{6,4},{8,10},{10,8},{12,14},{14,12},{1,3},{3,1},... | collective-permute-start | bytes 933896 | tf_op jit(solution)/shard_map/ppermute | solution.py:330
  8.3 1.6 %collective-permute-start.6 = (bf16[64,2048]{1,0:T(8,128)(2,1)S(1)}, bf16[64,2048]{1,0:T(8,128)(2,1)S(1)}, u32[]{:S(2)}, u32[]{:S(2)}) collective-permute-start(bf16[64,2048]{1,0:T(8,128)(2,1)S(1)} %get-tuple-element.66.refs_0_), channel_id=1, source_target_pairs={{0,4},{2,6},{4,8},{6,10},{8,12},{10,14},{12,0},{14,2},{1,5},{3,7},... | collective-permute-start | bytes 786440 | tf_op jit(solution)/shard_map/ppermute | solution.py:330
  9.9 0.5 collective-permute-start.7
  10.4 2.6 %scale_codes.1.refs_4_.refs_2_ = bf16[256,4480]{1,0:T(8,128)(2,1)S(1)} custom-call(s32[1]{0:T(128)} %bitcast.part_ref, bf16[256,8192]{1,0:T(8,128)(2,1)} %codes_ref.3, s32[64,256]{1,0:T(8,128)} %bitcast.24), custom_call_target="tpu_custom_call" | custom-call | flops 2097152 | bytes 8388608 | tf_op jit(solution)/shard_map/scale_codes/pallas_call | solution.py:158
  13.0 4.3 %collective-permute-done.refs_1_ = bf16[64,2432]{1,0:T(8,128)(2,1)S(1)} collective-permute-done((bf16[64,2432]{1,0:T(8,128)(2,1)S(1)}, bf16[64,2432]{1,0:T(8,128)(2,1)S(1)}, u32[]{:S(2)}, u32[]{:S(2)}) %collective-permute-start) | collective-permute-done | bytes 311328 | tf_op jit(solution)/shard_map/ppermute | solution.py:330
  17.3 0.0 collective-permute-done.1.refs_1_
  17.3 1.4 %collective-permute-start.2 = (bf16[64,2432]{1,0:T(8,128)(2,1)S(1)}, bf16[64,2432]{1,0:T(8,128)(2,1)S(1)}, u32[]{:S(2)}, u32[]{:S(2)}) collective-permute-start(bf16[64,2432]{1,0:T(8,128)(2,1)S(1)} %collective-permute-done.refs_1_), channel_id=1, source_target_pairs={{0,4},{2,6},{4,8},{6,10},{8,12},{10,14},{12,0},{14,2},{1,5},{3,7},... | collective-permute-start | bytes 933896 | tf_op jit(solution)/shard_map/ppermute | solution.py:330
  18.7 1.5 %collective-permute-start.3 = (bf16[64,2432]{1,0:T(8,128)(2,1)S(1)}, bf16[64,2432]{1,0:T(8,128)(2,1)S(1)}, u32[]{:S(2)}, u32[]{:S(2)}) collective-permute-start(bf16[64,2432]{1,0:T(8,128)(2,1)S(1)} %collective-permute-done.refs_1_), channel_id=1, source_target_pairs={{0,2},{2,0},{4,6},{6,4},{8,10},{10,8},{12,14},{14,12},{1,3},{3,1},... | collective-permute-start | bytes 933896 | tf_op jit(solution)/shard_map/ppermute | solution.py:330
  20.2 2.7 %collective-permute-done.6.refs_1_ = bf16[64,2048]{1,0:T(8,128)(2,1)S(1)} collective-permute-done((bf16[64,2048]{1,0:T(8,128)(2,1)S(1)}, bf16[64,2048]{1,0:T(8,128)(2,1)S(1)}, u32[]{:S(2)}, u32[]{:S(2)}) %collective-permute-start.6) | collective-permute-done | bytes 262176 | tf_op jit(solution)/shard_map/ppermute | solution.py:330
  22.9 0.0 collective-permute-done.7.refs_1_
  22.9 1.4 %collective-permute-start.8 = (bf16[64,2048]{1,0:T(8,128)(2,1)S(1)}, bf16[64,2048]{1,0:T(8,128)(2,1)S(1)}, u32[]{:S(2)}, u32[]{:S(2)}) collective-permute-start(bf16[64,2048]{1,0:T(8,128)(2,1)S(1)} %collective-permute-done.6.refs_1_), channel_id=1, source_target_pairs={{0,4},{2,6},{4,8},{6,10},{8,12},{10,14},{12,0},{14,2},{1,5},{3,7},... | collective-permute-start | bytes 786440 | tf_op jit(solution)/shard_map/ppermute | solution.py:330
  24.3 1.5 %collective-permute-start.9 = (bf16[64,2048]{1,0:T(8,128)(2,1)S(1)}, bf16[64,2048]{1,0:T(8,128)(2,1)S(1)}, u32[]{:S(2)}, u32[]{:S(2)}) collective-permute-start(bf16[64,2048]{1,0:T(8,128)(2,1)S(1)} %collective-permute-done.6.refs_1_), channel_id=1, source_target_pairs={{0,2},{2,0},{4,6},{6,4},{8,10},{10,8},{12,14},{14,12},{1,3},{3,1},... | collective-permute-start | bytes 786440 | tf_op jit(solution)/shard_map/ppermute | solution.py:330
  25.8 3.8 %collective-permute-done.2.refs_1_ = bf16[64,2432]{1,0:T(8,128)(2,1)S(1)} collective-permute-done((bf16[64,2432]{1,0:T(8,128)(2,1)S(1)}, bf16[64,2432]{1,0:T(8,128)(2,1)S(1)}, u32[]{:S(2)}, u32[]{:S(2)}) %collective-permute-start.2) | collective-permute-done | bytes 311328 | tf_op jit(solution)/shard_map/ppermute | solution.py:330
  29.6 0.0 collective-permute-done.3.refs_2_
  29.6 1.4 %collective-permute-start.4 = (bf16[64,2432]{1,0:T(8,128)(2,1)S(1)}, bf16[64,2432]{1,0:T(8,128)(2,1)S(1)}, u32[]{:S(2)}, u32[]{:S(2)}) collective-permute-start(bf16[64,2432]{1,0:T(8,128)(2,1)S(1)} %collective-permute-done.2.refs_1_), channel_id=1, source_target_pairs={{0,4},{2,6},{4,8},{6,10},{8,12},{10,14},{12,0},{14,2},{1,5},{3,7},... | collective-permute-start | bytes 933896 | tf_op jit(solution)/shard_map/ppermute | solution.py:330
  31.0 1.5 %collective-permute-start.5 = (bf16[64,2432]{1,0:T(8,128)(2,1)S(1)}, bf16[64,2432]{1,0:T(8,128)(2,1)S(1)}, u32[]{:S(2)}, u32[]{:S(2)}) collective-permute-start(bf16[64,2432]{1,0:T(8,128)(2,1)S(1)} %collective-permute-done.2.refs_1_), channel_id=1, source_target_pairs={{0,2},{2,0},{4,6},{6,4},{8,10},{10,8},{12,14},{14,12},{1,3},{3,1},... | collective-permute-start | bytes 933896 | tf_op jit(solution)/shard_map/ppermute | solution.py:330
  32.5 2.7 %collective-permute-done.8.refs_5_.refs_1_ = bf16[64,2048]{1,0:T(8,128)(2,1)S(1)} collective-permute-done((bf16[64,2048]{1,0:T(8,128)(2,1)S(1)}, bf16[64,2048]{1,0:T(8,128)(2,1)S(1)}, u32[]{:S(2)}, u32[]{:S(2)}) %collective-permute-start.8) | collective-permute-done | bytes 262176 | tf_op jit(solution)/shard_map/ppermute | solution.py:330
  35.2 0.0 collective-permute-done.9.refs_2_
  35.2 1.4 %collective-permute-start.10 = (bf16[64,2048]{1,0:T(8,128)(2,1)S(1)}, bf16[64,2048]{1,0:T(8,128)(2,1)S(1)}, u32[]{:S(2)}, u32[]{:S(2)}) collective-permute-start(bf16[64,2048]{1,0:T(8,128)(2,1)S(1)} %collective-permute-done.8.refs_5_.refs_1_), channel_id=1, source_target_pairs={{0,4},{2,6},{4,8},{6,10},{8,12},{10,14},{12,0},{14,2},{1,5},{3,7},... | collective-permute-start | bytes 786440 | tf_op jit(solution)/shard_map/ppermute | solution.py:330
  36.6 1.5 %collective-permute-start.11 = (bf16[64,2048]{1,0:T(8,128)(2,1)S(1)}, bf16[64,2048]{1,0:T(8,128)(2,1)S(1)}, u32[]{:S(2)}, u32[]{:S(2)}) collective-permute-start(bf16[64,2048]{1,0:T(8,128)(2,1)S(1)} %collective-permute-done.8.refs_5_.refs_1_), channel_id=1, source_target_pairs={{0,2},{2,0},{4,6},{6,4},{8,10},{10,8},{12,14},{14,12},{1,3},{3,1},... | collective-permute-start | bytes 786440 | tf_op jit(solution)/shard_map/ppermute | solution.py:330
  38.1 3.8 %collective-permute-done.4.refs_3_ = bf16[64,2432]{1,0:T(8,128)(2,1)S(1)} collective-permute-done((bf16[64,2432]{1,0:T(8,128)(2,1)S(1)}, bf16[64,2432]{1,0:T(8,128)(2,1)S(1)}, u32[]{:S(2)}, u32[]{:S(2)}) %collective-permute-start.4) | collective-permute-done | bytes 311328 | tf_op jit(solution)/shard_map/ppermute | solution.py:330
  41.9 0.0 collective-permute-done.5.refs_2_
  41.9 0.8 %score.5.refs_5_ = f32[448,256]{1,0:T(8,128)S(1)} custom-call(s32[1]{0:T(128)} %bitcast.1.half_ref, bf16[256,2432]{1,0:T(8,128)(2,1)S(1)} %stash.5.refs_0_, bf16[64,2432]{1,0:T(8,128)(2,1)S(1)} %collective-permute-done.2.refs_1_, bf16[64,2432]{1,0:T(8,128)(2,1)S(1)} %collective-permute-done.5.refs_2_, bf16[64,2432]{1,0:T(8,128)(2,1)S(1)} %collective-permute-done.4.refs_3_, ...), custom_call_target="tpu_custom_call" | custom-call | flops 1027604480 | bytes 2293760 | tf_op jit(solution)/shard_map/score/pallas_call | solution.py:249
  42.7 1.6 %collective-permute-start.17 = (bf16[64,2432]{1,0:T(8,128)(2,1)S(1)}, bf16[64,2432]{1,0:T(8,128)(2,1)S(1)}, u32[]{:S(2)}, u32[]{:S(2)}) collective-permute-start(bf16[64,2432]{1,0:T(8,128)(2,1)S(1)} %collective-permute-done.4.refs_3_), channel_id=1, source_target_pairs={{0,2},{2,0},{4,6},{6,4},{8,10},{10,8},{12,14},{14,12},{1,3},{3,1},... | collective-permute-start | bytes 933896 | tf_op jit(solution)/shard_map/ppermute | solution.py:330
  44.3 1.8 %collective-permute-done.10.refs_7_.refs_3_ = bf16[64,2048]{1,0:T(8,128)(2,1)S(1)} collective-permute-done((bf16[64,2048]{1,0:T(8,128)(2,1)S(1)}, bf16[64,2048]{1,0:T(8,128)(2,1)S(1)}, u32[]{:S(2)}, u32[]{:S(2)}) %collective-permute-start.10) | collective-permute-done | bytes 262176 | tf_op jit(solution)/shard_map/ppermute | solution.py:330
  46.1 1.2 %collective-permute-done.11.refs_6_.refs_2_ = bf16[64,2048]{1,0:T(8,128)(2,1)S(1)} collective-permute-done((bf16[64,2048]{1,0:T(8,128)(2,1)S(1)}, bf16[64,2048]{1,0:T(8,128)(2,1)S(1)}, u32[]{:S(2)}, u32[]{:S(2)}) %collective-permute-start.11) | collective-permute-done | bytes 262176 | tf_op jit(solution)/shard_map/ppermute | solution.py:330
  47.3 1.6 %collective-permute-start.16 = (bf16[64,2048]{1,0:T(8,128)(2,1)S(1)}, bf16[64,2048]{1,0:T(8,128)(2,1)S(1)}, u32[]{:S(2)}, u32[]{:S(2)}) collective-permute-start(bf16[64,2048]{1,0:T(8,128)(2,1)S(1)} %collective-permute-done.11.refs_6_.refs_2_), channel_id=1, source_target_pairs={{0,4},{2,6},{4,8},{6,10},{8,12},{10,14},{12,0},{14,2},{1,5},{3,7},... | collective-permute-start | bytes 786440 | tf_op jit(solution)/shard_map/ppermute | solution.py:330
  48.9 0.0 collective-permute-done.12.refs_8_.refs_1_
  48.9 1.1 %score.6 = (f32[7,32,256]{2,1,0:T(8,128)S(1)}, f32[7,32,256]{2,1,0:T(8,128)S(1)}) custom-call(s32[1]{0:T(128)} %bitcast.1.half_ref, bf16[256,2432]{1,0:T(8,128)(2,1)S(1)} %stash.5.refs_0_, bf16[64,2432]{1,0:T(8,128)(2,1)S(1)} %collective-permute-done.2.refs_1_, bf16[64,2432]{1,0:T(8,128)(2,1)S(1)} %collective-permute-done.5.refs_2_, ...), custom_call_target="tpu_custom_call" | custom-call | flops 851443712 | bytes 1900544 | tf_op jit(solution)/shard_map/score/pallas_call | solution.py:249
  50.0 0.1 collective-permute-start.13
  50.1 0.7 %score.7 = (f32[7,32,256]{2,1,0:T(8,128)S(1)}, f32[7,32,256]{2,1,0:T(8,128)S(1)}) custom-call(s32[1]{0:T(128)} %bitcast.1.half_ref, bf16[256,2048]{1,0:T(8,128)(2,1)S(1)} %stash.7.refs_4_.refs_0_, bf16[64,2048]{1,0:T(8,128)(2,1)S(1)} %collective-permute-done.8.refs_5_.refs_1_, bf16[64,2048]{1,0:T(8,128)(2,1)S(1)} %collective-permute-done.11.refs_6_.refs_2_, ...), custom_call_target="tpu_custom_call" | custom-call | flops 1027604480 | bytes 2293760 | tf_op jit(solution)/shard_map/score/pallas_call | solution.py:249
  50.7 0.6 collective-permute-start.15
  51.3 0.2 collective-permute-done.13.b_ref
  51.6 0.6 collective-permute-start.14
  52.1 0.1 collective-permute-done.17.refs_0_
  52.2 0.9 %score.8 = (f32[64,256]{1,0:T(8,128)S(1)}, f32[64,256]{1,0:T(8,128)S(1)}) custom-call(s32[1]{0:T(128)} %bitcast.1.half_ref, bf16[64,2432]{1,0:T(8,128)(2,1)S(1)} %collective-permute-done.17.refs_0_, bf16[256,3712]{1,0:T(8,128)(2,1)S(1)} %collective-permute-done.12.refs_8_.refs_1_, bf16[256,4480]{1,0:T(8,128)(2,1)S(1)} %scale_codes.1.refs_4_.refs_2_), custom_call_target="tpu_custom_call" | custom-call | flops 268435456 | bytes 1900544 | tf_op jit(solution)/shard_map/score/pallas_call | solution.py:249
  53.1 2.4 %collective-permute-done.16.refs_0_ = bf16[64,2048]{1,0:T(8,128)(2,1)S(1)} collective-permute-done((bf16[64,2048]{1,0:T(8,128)(2,1)S(1)}, bf16[64,2048]{1,0:T(8,128)(2,1)S(1)}, u32[]{:S(2)}, u32[]{:S(2)}) %collective-permute-start.16) | collective-permute-done | bytes 262176 | tf_op jit(solution)/shard_map/ppermute | solution.py:330
  55.5 0.0 copy-start
  55.5 0.7 %score.9 = (f32[1,32,256]{2,1,0:T(8,128)S(1)}, f32[1,32,256]{2,1,0:T(8,128)S(1)}, f32[1,32,256]{2,1,0:T(8,128)S(1)}, f32[1,32,256]{2,1,0:T(8,128)S(1)}) custom-call(s32[1]{0:T(128)} %bitcast.1.half_ref, bf16[64,2048]{1,0:T(8,128)(2,1)S(1)} %collective-permute-done.16.refs_0_, bf16[256,3712]{1,0:T(8,128)(2,1)S(1)} %collective-permute-done.12.refs_8_.refs_1_, ...), custom_call_target="tpu_custom_call" | custom-call | flops 8053063680 | bytes 1900544 | tf_op jit(solution)/shard_map/score/pallas_call | solution.py:249
  56.1 0.1 collective-permute-start.18
  56.2 0.5 collective-permute-start.20
  56.7 0.7 %collective-permute-done.18.b_ref = f32[1,32,256]{2,1,0:T(8,128)S(1)} collective-permute-done((f32[1,32,256]{2,1,0:T(8,128)S(1)}, f32[1,32,256]{2,1,0:T(8,128)S(1)}, u32[]{:S(2)}, u32[]{:S(2)}) %collective-permute-start.18) | collective-permute-done | bytes 32800 | tf_op jit(solution)/shard_map/ppermute | solution.py:371
  57.4 0.5 collective-permute-start.19
  57.9 0.0 collective-permute-done.15
  57.9 0.0 collective-permute-done.20
  57.9 3.4 %collective-permute-done.19 = f32[1,32,256]{2,1,0:T(8,128)S(1)} collective-permute-done((f32[1,32,256]{2,1,0:T(8,128)S(1)}, f32[1,32,256]{2,1,0:T(8,128)S(1)}, u32[]{:S(2)}, u32[]{:S(2)}) %collective-permute-start.19) | collective-permute-done | bytes 32800 | tf_op jit(solution)/shard_map/ppermute | solution.py:384
  61.3 0.0 collective-permute-done.14
  61.3 0.0 copy-done
  61.3 1.6 %place_scores.1 = f32[8,32,256]{2,1,0:T(8,128)} custom-call(s32[8]{0:T(128)S(1)} %stack.35.order_ref, s32[1,256]{1,0:T(1,128)S(1)} %copy-done, f32[224,256]{1,0:T(8,128)S(1)} %bitcast.19, f32[224,256]{1,0:T(8,128)S(1)} %bitcast.17, f32[224,256]{1,0:T(8,128)S(1)} %bitcast.18, f32[32,256]{1,0:T(8,128)S(1)} %bitcast.22, f32[32,256]{1,0:T(8,128)S(1)} %bitcast.20, ...), custom_call_target="tpu_custom_call" | custom-call | tf_op jit(solution)/shard_map/place_scores/pallas_call | solution.py:297
  (6 shorter events, 0.2 us)
Async XLA Ops:
  2.2 46.7 %collective-permute-start.12 = (bf16[256,3712]{1,0:T(8,128)(2,1)S(1)}, bf16[256,3712]{1,0:T(8,128)(2,1)S(1)}, u32[]{:S(2)}, u32[]{:S(2)}) collective-permute-start(bf16[256,3712]{1,0:T(8,128)(2,1)S(1)} %get-tuple-element.78), channel_id=1, source_target_pairs={{0,16},{16,0},{1,17},{17,1},{2,18},{18,2},{3,19},{19,3},{4,20},{20... | collective-permute-start | bytes 5701640 | tf_op jit(solution)/shard_map/ppermute | solution.py:341
  5.2 12.1 %collective-permute-start = (bf16[64,2432]{1,0:T(8,128)(2,1)S(1)}, bf16[64,2432]{1,0:T(8,128)(2,1)S(1)}, u32[]{:S(2)}, u32[]{:S(2)}) collective-permute-start(bf16[64,2432]{1,0:T(8,128)(2,1)S(1)} %get-tuple-element.54.refs_0_), channel_id=1, source_target_pairs={{0,4},{2,6},{4,8},{6,10},{8,12},{10,14},{12,0},{14,2},{1,5},{3,7},... | collective-permute-start | bytes 933896 | tf_op jit(solution)/shard_map/ppermute | solution.py:330
  6.8 10.5 %collective-permute-start.1 = (bf16[64,2432]{1,0:T(8,128)(2,1)S(1)}, bf16[64,2432]{1,0:T(8,128)(2,1)S(1)}, u32[]{:S(2)}, u32[]{:S(2)}) collective-permute-start(bf16[64,2432]{1,0:T(8,128)(2,1)S(1)} %get-tuple-element.54.refs_0_), channel_id=1, source_target_pairs={{0,2},{2,0},{4,6},{6,4},{8,10},{10,8},{12,14},{14,12},{1,3},{3,1},... | collective-permute-start | bytes 933896 | tf_op jit(solution)/shard_map/ppermute | solution.py:330
  8.3 14.6 %collective-permute-start.6 = (bf16[64,2048]{1,0:T(8,128)(2,1)S(1)}, bf16[64,2048]{1,0:T(8,128)(2,1)S(1)}, u32[]{:S(2)}, u32[]{:S(2)}) collective-permute-start(bf16[64,2048]{1,0:T(8,128)(2,1)S(1)} %get-tuple-element.66.refs_0_), channel_id=1, source_target_pairs={{0,4},{2,6},{4,8},{6,10},{8,12},{10,14},{12,0},{14,2},{1,5},{3,7},... | collective-permute-start | bytes 786440 | tf_op jit(solution)/shard_map/ppermute | solution.py:330
  9.9 13.1 %collective-permute-start.7 = (bf16[64,2048]{1,0:T(8,128)(2,1)S(1)}, bf16[64,2048]{1,0:T(8,128)(2,1)S(1)}, u32[]{:S(2)}, u32[]{:S(2)}) collective-permute-start(bf16[64,2048]{1,0:T(8,128)(2,1)S(1)} %get-tuple-element.66.refs_0_), channel_id=1, source_target_pairs={{0,2},{2,0},{4,6},{6,4},{8,10},{10,8},{12,14},{14,12},{1,3},{3,1},... | collective-permute-start | bytes 786440 | tf_op jit(solution)/shard_map/ppermute | solution.py:330
  17.3 12.3 %collective-permute-start.2 = (bf16[64,2432]{1,0:T(8,128)(2,1)S(1)}, bf16[64,2432]{1,0:T(8,128)(2,1)S(1)}, u32[]{:S(2)}, u32[]{:S(2)}) collective-permute-start(bf16[64,2432]{1,0:T(8,128)(2,1)S(1)} %collective-permute-done.refs_1_), channel_id=1, source_target_pairs={{0,4},{2,6},{4,8},{6,10},{8,12},{10,14},{12,0},{14,2},{1,5},{3,7},... | collective-permute-start | bytes 933896 | tf_op jit(solution)/shard_map/ppermute | solution.py:330
  18.7 10.9 %collective-permute-start.3 = (bf16[64,2432]{1,0:T(8,128)(2,1)S(1)}, bf16[64,2432]{1,0:T(8,128)(2,1)S(1)}, u32[]{:S(2)}, u32[]{:S(2)}) collective-permute-start(bf16[64,2432]{1,0:T(8,128)(2,1)S(1)} %collective-permute-done.refs_1_), channel_id=1, source_target_pairs={{0,2},{2,0},{4,6},{6,4},{8,10},{10,8},{12,14},{14,12},{1,3},{3,1},... | collective-permute-start | bytes 933896 | tf_op jit(solution)/shard_map/ppermute | solution.py:330
  22.9 12.3 %collective-permute-start.8 = (bf16[64,2048]{1,0:T(8,128)(2,1)S(1)}, bf16[64,2048]{1,0:T(8,128)(2,1)S(1)}, u32[]{:S(2)}, u32[]{:S(2)}) collective-permute-start(bf16[64,2048]{1,0:T(8,128)(2,1)S(1)} %collective-permute-done.6.refs_1_), channel_id=1, source_target_pairs={{0,4},{2,6},{4,8},{6,10},{8,12},{10,14},{12,0},{14,2},{1,5},{3,7},... | collective-permute-start | bytes 786440 | tf_op jit(solution)/shard_map/ppermute | solution.py:330
  24.3 10.9 %collective-permute-start.9 = (bf16[64,2048]{1,0:T(8,128)(2,1)S(1)}, bf16[64,2048]{1,0:T(8,128)(2,1)S(1)}, u32[]{:S(2)}, u32[]{:S(2)}) collective-permute-start(bf16[64,2048]{1,0:T(8,128)(2,1)S(1)} %collective-permute-done.6.refs_1_), channel_id=1, source_target_pairs={{0,2},{2,0},{4,6},{6,4},{8,10},{10,8},{12,14},{14,12},{1,3},{3,1},... | collective-permute-start | bytes 786440 | tf_op jit(solution)/shard_map/ppermute | solution.py:330
  29.6 12.3 %collective-permute-start.4 = (bf16[64,2432]{1,0:T(8,128)(2,1)S(1)}, bf16[64,2432]{1,0:T(8,128)(2,1)S(1)}, u32[]{:S(2)}, u32[]{:S(2)}) collective-permute-start(bf16[64,2432]{1,0:T(8,128)(2,1)S(1)} %collective-permute-done.2.refs_1_), channel_id=1, source_target_pairs={{0,4},{2,6},{4,8},{6,10},{8,12},{10,14},{12,0},{14,2},{1,5},{3,7},... | collective-permute-start | bytes 933896 | tf_op jit(solution)/shard_map/ppermute | solution.py:330
  31.0 10.9 %collective-permute-start.5 = (bf16[64,2432]{1,0:T(8,128)(2,1)S(1)}, bf16[64,2432]{1,0:T(8,128)(2,1)S(1)}, u32[]{:S(2)}, u32[]{:S(2)}) collective-permute-start(bf16[64,2432]{1,0:T(8,128)(2,1)S(1)} %collective-permute-done.2.refs_1_), channel_id=1, source_target_pairs={{0,2},{2,0},{4,6},{6,4},{8,10},{10,8},{12,14},{14,12},{1,3},{3,1},... | collective-permute-start | bytes 933896 | tf_op jit(solution)/shard_map/ppermute | solution.py:330
  35.2 10.9 %collective-permute-start.10 = (bf16[64,2048]{1,0:T(8,128)(2,1)S(1)}, bf16[64,2048]{1,0:T(8,128)(2,1)S(1)}, u32[]{:S(2)}, u32[]{:S(2)}) collective-permute-start(bf16[64,2048]{1,0:T(8,128)(2,1)S(1)} %collective-permute-done.8.refs_5_.refs_1_), channel_id=1, source_target_pairs={{0,4},{2,6},{4,8},{6,10},{8,12},{10,14},{12,0},{14,2},{1,5},{3,7},... | collective-permute-start | bytes 786440 | tf_op jit(solution)/shard_map/ppermute | solution.py:330
  36.6 10.7 %collective-permute-start.11 = (bf16[64,2048]{1,0:T(8,128)(2,1)S(1)}, bf16[64,2048]{1,0:T(8,128)(2,1)S(1)}, u32[]{:S(2)}, u32[]{:S(2)}) collective-permute-start(bf16[64,2048]{1,0:T(8,128)(2,1)S(1)} %collective-permute-done.8.refs_5_.refs_1_), channel_id=1, source_target_pairs={{0,2},{2,0},{4,6},{6,4},{8,10},{10,8},{12,14},{14,12},{1,3},{3,1},... | collective-permute-start | bytes 786440 | tf_op jit(solution)/shard_map/ppermute | solution.py:330
  42.7 9.5 %collective-permute-start.17 = (bf16[64,2432]{1,0:T(8,128)(2,1)S(1)}, bf16[64,2432]{1,0:T(8,128)(2,1)S(1)}, u32[]{:S(2)}, u32[]{:S(2)}) collective-permute-start(bf16[64,2432]{1,0:T(8,128)(2,1)S(1)} %collective-permute-done.4.refs_3_), channel_id=1, source_target_pairs={{0,2},{2,0},{4,6},{6,4},{8,10},{10,8},{12,14},{14,12},{1,3},{3,1},... | collective-permute-start | bytes 933896 | tf_op jit(solution)/shard_map/ppermute | solution.py:330
  47.3 8.2 %collective-permute-start.16 = (bf16[64,2048]{1,0:T(8,128)(2,1)S(1)}, bf16[64,2048]{1,0:T(8,128)(2,1)S(1)}, u32[]{:S(2)}, u32[]{:S(2)}) collective-permute-start(bf16[64,2048]{1,0:T(8,128)(2,1)S(1)} %collective-permute-done.11.refs_6_.refs_2_), channel_id=1, source_target_pairs={{0,4},{2,6},{4,8},{6,10},{8,12},{10,14},{12,0},{14,2},{1,5},{3,7},... | collective-permute-start | bytes 786440 | tf_op jit(solution)/shard_map/ppermute | solution.py:330
  50.0 1.6 %collective-permute-start.13 = (f32[7,32,256]{2,1,0:T(8,128)S(1)}, f32[7,32,256]{2,1,0:T(8,128)S(1)}, u32[]{:S(2)}, u32[]{:S(2)}) collective-permute-start(f32[7,32,256]{2,1,0:T(8,128)S(1)} %get-tuple-element.80), channel_id=1, source_target_pairs={{0,1},{1,0},{2,3},{3,2},{4,5},{5,4},{6,7},{7,6},{8,9},{9,8},{10,11... | collective-permute-start | bytes 688136 | tf_op jit(solution)/shard_map/ppermute | solution.py:371
  50.7 7.2 %collective-permute-start.15 = (f32[7,32,256]{2,1,0:T(8,128)S(1)}, f32[7,32,256]{2,1,0:T(8,128)S(1)}, u32[]{:S(2)}, u32[]{:S(2)}) collective-permute-start(f32[7,32,256]{2,1,0:T(8,128)S(1)} %get-tuple-element.84), channel_id=1, source_target_pairs={{0,1},{1,0},{2,3},{3,2},{4,5},{5,4},{6,7},{7,6},{8,9},{9,8},{10,11... | collective-permute-start | bytes 688136 | tf_op jit(solution)/shard_map/ppermute | solution.py:371
  51.6 9.7 %collective-permute-start.14 = (f32[7,32,256]{2,1,0:T(8,128)S(1)}, f32[7,32,256]{2,1,0:T(8,128)S(1)}, u32[]{:S(2)}, u32[]{:S(2)}) collective-permute-start(f32[7,32,256]{2,1,0:T(8,128)S(1)} %add.81), channel_id=1, source_target_pairs={{0,16},{16,0},{1,17},{17,1},{2,18},{18,2},{3,19},{19,3},{4,20},{20... | collective-permute-start | bytes 688136 | tf_op jit(solution)/shard_map/ppermute | solution.py:376
  55.5 5.8 %copy-start = (s32[1,256]{1,0:T(1,128)S(1)}, s32[1,256]{1,0:T(1,128)}, u32[]{:S(2)}) copy-start(s32[1,256]{1,0:T(1,128)} %ids_ref.1) | copy-start | bytes 3076
  56.1 1.3 %collective-permute-start.18 = (f32[1,32,256]{2,1,0:T(8,128)S(1)}, f32[1,32,256]{2,1,0:T(8,128)S(1)}, u32[]{:S(2)}, u32[]{:S(2)}) collective-permute-start(f32[1,32,256]{2,1,0:T(8,128)S(1)} %get-tuple-element.90), channel_id=1, source_target_pairs={{0,1},{1,0},{2,3},{3,2},{4,5},{5,4},{6,7},{7,6},{8,9},{9,8},{10,11... | collective-permute-start | bytes 98312 | tf_op jit(solution)/shard_map/ppermute | solution.py:371
  56.2 1.7 %collective-permute-start.20 = (f32[1,32,256]{2,1,0:T(8,128)S(1)}, f32[1,32,256]{2,1,0:T(8,128)S(1)}, u32[]{:S(2)}, u32[]{:S(2)}) collective-permute-start(f32[1,32,256]{2,1,0:T(8,128)S(1)} %get-tuple-element.92), channel_id=1, source_target_pairs={{0,1},{1,0},{2,3},{3,2},{4,5},{5,4},{6,7},{7,6},{8,9},{9,8},{10,11... | collective-permute-start | bytes 98312 | tf_op jit(solution)/shard_map/ppermute | solution.py:371
  57.4 3.9 %collective-permute-start.19 = (f32[1,32,256]{2,1,0:T(8,128)S(1)}, f32[1,32,256]{2,1,0:T(8,128)S(1)}, u32[]{:S(2)}, u32[]{:S(2)}) collective-permute-start(f32[1,32,256]{2,1,0:T(8,128)S(1)} %add.82), channel_id=1, source_target_pairs={{0,16},{16,0},{1,17},{17,1},{2,18},{18,2},{3,19},{19,3},{4,20},{20... | collective-permute-start | bytes 98312 | tf_op jit(solution)/shard_map/ppermute | solution.py:384

commit v13 on v12

--- a/solution.py
+++ b/solution.py
@@ -8,7 +8,7 @@
 from jax.sharding import PartitionSpec as P
 
 BLOCK = 128
-ALONE = 29
+ALONE = 30
 LATE_WEIGHT = 30
 LEAD = 0
 LEAD_PART = 19
@@ -354,9 +354,8 @@
                 *tied, ours = lax.optimization_barrier(tied + [ours])
             elif s == slow - 2 and c != LEAD:
                 begun_own = score(half, 0, early[LEAD : LEAD + 1], [ours], cuts[LEAD])
-                ready, *begun_own = lax.optimization_barrier((chunks[LEAD], *begun_own))
-                late[LEAD] = stack(along_fast(ready)[1:])
-                *tied, begun_own = lax.optimization_barrier(tied + begun_own)
+                late[LEAD] = stack(along_fast(chunks[LEAD])[1:])
+                *tied, begun_own = lax.optimization_barrier(tied + list(begun_own))
             else:
                 tied = lax.optimization_barrier(tied)
             chunks[c], values, kept = tied[0], tied[1 : fast + 1], tied[fast + 1 :]

time: 63 us -> 62 us (0.984)
  waiting for transfers between devices: 27.1 us -> 25 us
  starting transfers between devices: 25.1 us -> 26.3 us
    ppermute x14, waiting for transfers between devices: 22.8 us -> 20.5 us  [step(): return lax.ppermute(value, 'ex', pairs)]
    ppermute x1, starting transfers between devices: 0.57 us -> 1.81 us  [shards(): given = lax.ppermute(added, 'groups', swap)]
where the time goes in v13:
time: 62 us; the launch traced here: 61.9 us
  starting transfers between devices  26.3 us (42%)
  waiting for transfers between devices  25 us (40%)
  Pallas kernels  10.4 us (17%)
    ppermute x14, waiting for transfers between devices, step(): return lax.ppermute(value, 'ex', pairs)  20.5 us
    ppermute x14, starting transfers between devices, step(): return lax.ppermute(value, 'ex', pairs)  19.7 us
    pallas_call x5, Pallas kernels, score(): pl.pallas_call(functools.partial(score_kernel, [len(arrays) for arrays in...  3.98 us
    ppermute x1, waiting for transfers between devices, shards(): given = lax.ppermute(add(their_keep, over_dim(their_send)), 'groups', swap)  3.4 us
    ppermute x1, starting transfers between devices, shards(): theirs = lax.ppermute(sent, 'groups', swap)  3.03 us
    pallas_call x1, Pallas kernels, scale(): pl.pallas_call(functools.partial(scale_kernel, alone), out_shape=pltpu.VM...  2.55 us
    pallas_call x1, Pallas kernels, cut(): pl.pallas_call(functools.partial(cut_kernel, alone, cuts), out_shape=[plt...  2.12 us
    ppermute x1, starting transfers between devices, shards(): given = lax.ppermute(added, 'groups', swap)  1.81 us
  transfers between devices with their start and end apart: 21, of which 12 were waited for; matrix products, arithmetic and copies ran while one was open for 0% of the time, Pallas kernels for 11%

profile of v13, /device:TPU:0, one launch (start us, length us, event | category | flops | bytes accessed | tf_op | source)
XLA Modules:
  0.0 61.9 jit_solution(4496590519088385095)
XLA Ops:
  0.0 0.1 stack.35.order_ref
  0.1 2.1 %cut_queries.1 = (bf16[64,2304]{1,0:T(8,128)(2,1)S(1)}, bf16[64,2048]{1,0:T(8,128)(2,1)S(1)}, bf16[256,3840]{1,0:T(8,128)(2,1)S(1)}) custom-call(s32[1]{0:T(128)} %bitcast.part_ref, bf16[1,64,8192]{2,1,0:T(8,128)(2,1)} %queries_ref.1, bf16[256,8192]{1,0:T(8,128)(2,1)} %codes_ref.3, s32[64,256]{1,0:T(8,128)} %bitcast.23), custom_call_target="tpu_custom_call" | custom-call | flops 2097152 | bytes 4194304 | tf_op jit(solution)/shard_map/cut_queries/pallas_call | solution.py:120
  2.2 3.0 %collective-permute-start.12 = (bf16[256,3840]{1,0:T(8,128)(2,1)S(1)}, bf16[256,3840]{1,0:T(8,128)(2,1)S(1)}, u32[]{:S(2)}, u32[]{:S(2)}) collective-permute-start(bf16[256,3840]{1,0:T(8,128)(2,1)S(1)} %get-tuple-element.75), channel_id=1, source_target_pairs={{0,16},{16,0},{1,17},{17,1},{2,18},{18,2},{3,19},{19,3},{4,20},{20... | collective-permute-start | bytes 5898248 | tf_op jit(solution)/shard_map/ppermute | solution.py:341
  5.2 1.6 %collective-permute-start = (bf16[64,2304]{1,0:T(8,128)(2,1)S(1)}, bf16[64,2304]{1,0:T(8,128)(2,1)S(1)}, u32[]{:S(2)}, u32[]{:S(2)}) collective-permute-start(bf16[64,2304]{1,0:T(8,128)(2,1)S(1)} %get-tuple-element.52.refs_0_), channel_id=1, source_target_pairs={{0,4},{2,6},{4,8},{6,10},{8,12},{10,14},{12,0},{14,2},{1,5},{3,7},... | collective-permute-start | bytes 884744 | tf_op jit(solution)/shard_map/ppermute | solution.py:330
  6.8 1.5 %collective-permute-start.1 = (bf16[64,2304]{1,0:T(8,128)(2,1)S(1)}, bf16[64,2304]{1,0:T(8,128)(2,1)S(1)}, u32[]{:S(2)}, u32[]{:S(2)}) collective-permute-start(bf16[64,2304]{1,0:T(8,128)(2,1)S(1)} %get-tuple-element.52.refs_0_), channel_id=1, source_target_pairs={{0,2},{2,0},{4,6},{6,4},{8,10},{10,8},{12,14},{14,12},{1,3},{3,1},... | collective-permute-start | bytes 884744 | tf_op jit(solution)/shard_map/ppermute | solution.py:330
  8.3 1.6 %collective-permute-start.6 = (bf16[64,2048]{1,0:T(8,128)(2,1)S(1)}, bf16[64,2048]{1,0:T(8,128)(2,1)S(1)}, u32[]{:S(2)}, u32[]{:S(2)}) collective-permute-start(bf16[64,2048]{1,0:T(8,128)(2,1)S(1)} %get-tuple-element.64.refs_0_), channel_id=1, source_target_pairs={{0,4},{2,6},{4,8},{6,10},{8,12},{10,14},{12,0},{14,2},{1,5},{3,7},... | collective-permute-start | bytes 786440 | tf_op jit(solution)/shard_map/ppermute | solution.py:330
  9.9 0.5 collective-permute-start.7
  10.4 2.6 %scale_codes.1.refs_4_.refs_2_ = bf16[256,4352]{1,0:T(8,128)(2,1)S(1)} custom-call(s32[1]{0:T(128)} %bitcast.part_ref, bf16[256,8192]{1,0:T(8,128)(2,1)} %codes_ref.3, s32[64,256]{1,0:T(8,128)} %bitcast.24), custom_call_target="tpu_custom_call" | custom-call | flops 2097152 | bytes 8388608 | tf_op jit(solution)/shard_map/scale_codes/pallas_call | solution.py:158
  13.0 4.0 %collective-permute-done.refs_1_ = bf16[64,2304]{1,0:T(8,128)(2,1)S(1)} collective-permute-done((bf16[64,2304]{1,0:T(8,128)(2,1)S(1)}, bf16[64,2304]{1,0:T(8,128)(2,1)S(1)}, u32[]{:S(2)}, u32[]{:S(2)}) %collective-permute-start) | collective-permute-done | bytes 294944 | tf_op jit(solution)/shard_map/ppermute | solution.py:330
  17.0 0.0 collective-permute-done.1.refs_1_
  17.0 1.4 %collective-permute-start.2 = (bf16[64,2304]{1,0:T(8,128)(2,1)S(1)}, bf16[64,2304]{1,0:T(8,128)(2,1)S(1)}, u32[]{:S(2)}, u32[]{:S(2)}) collective-permute-start(bf16[64,2304]{1,0:T(8,128)(2,1)S(1)} %collective-permute-done.refs_1_), channel_id=1, source_target_pairs={{0,4},{2,6},{4,8},{6,10},{8,12},{10,14},{12,0},{14,2},{1,5},{3,7},... | collective-permute-start | bytes 884744 | tf_op jit(solution)/shard_map/ppermute | solution.py:330
  18.3 1.5 %collective-permute-start.3 = (bf16[64,2304]{1,0:T(8,128)(2,1)S(1)}, bf16[64,2304]{1,0:T(8,128)(2,1)S(1)}, u32[]{:S(2)}, u32[]{:S(2)}) collective-permute-start(bf16[64,2304]{1,0:T(8,128)(2,1)S(1)} %collective-permute-done.refs_1_), channel_id=1, source_target_pairs={{0,2},{2,0},{4,6},{6,4},{8,10},{10,8},{12,14},{14,12},{1,3},{3,1},... | collective-permute-start | bytes 884744 | tf_op jit(solution)/shard_map/ppermute | solution.py:330
  19.8 2.7 %collective-permute-done.6.refs_1_ = bf16[64,2048]{1,0:T(8,128)(2,1)S(1)} collective-permute-done((bf16[64,2048]{1,0:T(8,128)(2,1)S(1)}, bf16[64,2048]{1,0:T(8,128)(2,1)S(1)}, u32[]{:S(2)}, u32[]{:S(2)}) %collective-permute-start.6) | collective-permute-done | bytes 262176 | tf_op jit(solution)/shard_map/ppermute | solution.py:330
  22.6 0.0 collective-permute-done.7.refs_1_
  22.6 1.4 %collective-permute-start.8 = (bf16[64,2048]{1,0:T(8,128)(2,1)S(1)}, bf16[64,2048]{1,0:T(8,128)(2,1)S(1)}, u32[]{:S(2)}, u32[]{:S(2)}) collective-permute-start(bf16[64,2048]{1,0:T(8,128)(2,1)S(1)} %collective-permute-done.6.refs_1_), channel_id=1, source_target_pairs={{0,4},{2,6},{4,8},{6,10},{8,12},{10,14},{12,0},{14,2},{1,5},{3,7},... | collective-permute-start | bytes 786440 | tf_op jit(solution)/shard_map/ppermute | solution.py:330
  24.0 1.5 %collective-permute-start.9 = (bf16[64,2048]{1,0:T(8,128)(2,1)S(1)}, bf16[64,2048]{1,0:T(8,128)(2,1)S(1)}, u32[]{:S(2)}, u32[]{:S(2)}) collective-permute-start(bf16[64,2048]{1,0:T(8,128)(2,1)S(1)} %collective-permute-done.6.refs_1_), channel_id=1, source_target_pairs={{0,2},{2,0},{4,6},{6,4},{8,10},{10,8},{12,14},{14,12},{1,3},{3,1},... | collective-permute-start | bytes 786440 | tf_op jit(solution)/shard_map/ppermute | solution.py:330
  25.5 3.4 %collective-permute-done.2.refs_1_ = bf16[64,2304]{1,0:T(8,128)(2,1)S(1)} collective-permute-done((bf16[64,2304]{1,0:T(8,128)(2,1)S(1)}, bf16[64,2304]{1,0:T(8,128)(2,1)S(1)}, u32[]{:S(2)}, u32[]{:S(2)}) %collective-permute-start.2) | collective-permute-done | bytes 294944 | tf_op jit(solution)/shard_map/ppermute | solution.py:330
  28.9 0.0 collective-permute-done.3.refs_2_
  28.9 1.4 %collective-permute-start.4 = (bf16[64,2304]{1,0:T(8,128)(2,1)S(1)}, bf16[64,2304]{1,0:T(8,128)(2,1)S(1)}, u32[]{:S(2)}, u32[]{:S(2)}) collective-permute-start(bf16[64,2304]{1,0:T(8,128)(2,1)S(1)} %collective-permute-done.2.refs_1_), channel_id=1, source_target_pairs={{0,4},{2,6},{4,8},{6,10},{8,12},{10,14},{12,0},{14,2},{1,5},{3,7},... | collective-permute-start | bytes 884744 | tf_op jit(solution)/shard_map/ppermute | solution.py:330
  30.3 1.5 %collective-permute-start.5 = (bf16[64,2304]{1,0:T(8,128)(2,1)S(1)}, bf16[64,2304]{1,0:T(8,128)(2,1)S(1)}, u32[]{:S(2)}, u32[]{:S(2)}) collective-permute-start(bf16[64,2304]{1,0:T(8,128)(2,1)S(1)} %collective-permute-done.2.refs_1_), channel_id=1, source_target_pairs={{0,2},{2,0},{4,6},{6,4},{8,10},{10,8},{12,14},{14,12},{1,3},{3,1},... | collective-permute-start | bytes 884744 | tf_op jit(solution)/shard_map/ppermute | solution.py:330
  31.8 2.7 %collective-permute-done.8.refs_5_.refs_1_ = bf16[64,2048]{1,0:T(8,128)(2,1)S(1)} collective-permute-done((bf16[64,2048]{1,0:T(8,128)(2,1)S(1)}, bf16[64,2048]{1,0:T(8,128)(2,1)S(1)}, u32[]{:S(2)}, u32[]{:S(2)}) %collective-permute-start.8) | collective-permute-done | bytes 262176 | tf_op jit(solution)/shard_map/ppermute | solution.py:330
  34.5 0.0 collective-permute-done.9.refs_2_
  34.5 1.4 %collective-permute-start.10 = (bf16[64,2048]{1,0:T(8,128)(2,1)S(1)}, bf16[64,2048]{1,0:T(8,128)(2,1)S(1)}, u32[]{:S(2)}, u32[]{:S(2)}) collective-permute-start(bf16[64,2048]{1,0:T(8,128)(2,1)S(1)} %collective-permute-done.8.refs_5_.refs_1_), channel_id=1, source_target_pairs={{0,4},{2,6},{4,8},{6,10},{8,12},{10,14},{12,0},{14,2},{1,5},{3,7},... | collective-permute-start | bytes 786440 | tf_op jit(solution)/shard_map/ppermute | solution.py:330
  35.9 1.5 %collective-permute-start.11 = (bf16[64,2048]{1,0:T(8,128)(2,1)S(1)}, bf16[64,2048]{1,0:T(8,128)(2,1)S(1)}, u32[]{:S(2)}, u32[]{:S(2)}) collective-permute-start(bf16[64,2048]{1,0:T(8,128)(2,1)S(1)} %collective-permute-done.8.refs_5_.refs_1_), channel_id=1, source_target_pairs={{0,2},{2,0},{4,6},{6,4},{8,10},{10,8},{12,14},{14,12},{1,3},{3,1},... | collective-permute-start | bytes 786440 | tf_op jit(solution)/shard_map/ppermute | solution.py:330
  37.5 3.4 %collective-permute-done.4.refs_3_ = bf16[64,2304]{1,0:T(8,128)(2,1)S(1)} collective-permute-done((bf16[64,2304]{1,0:T(8,128)(2,1)S(1)}, bf16[64,2304]{1,0:T(8,128)(2,1)S(1)}, u32[]{:S(2)}, u32[]{:S(2)}) %collective-permute-start.4) | collective-permute-done | bytes 294944 | tf_op jit(solution)/shard_map/ppermute | solution.py:330
  40.8 0.0 collective-permute-done.5.refs_2_
  40.8 1.5 %collective-permute-start.17 = (bf16[64,2304]{1,0:T(8,128)(2,1)S(1)}, bf16[64,2304]{1,0:T(8,128)(2,1)S(1)}, u32[]{:S(2)}, u32[]{:S(2)}) collective-permute-start(bf16[64,2304]{1,0:T(8,128)(2,1)S(1)} %collective-permute-done.4.refs_3_), channel_id=1, source_target_pairs={{0,2},{2,0},{4,6},{6,4},{8,10},{10,8},{12,14},{14,12},{1,3},{3,1},... | collective-permute-start | bytes 884744 | tf_op jit(solution)/shard_map/ppermute | solution.py:330
  42.3 0.7 %score.5.refs_5_ = f32[448,256]{1,0:T(8,128)S(1)} custom-call(s32[1]{0:T(128)} %bitcast.1.half_ref, bf16[256,2304]{1,0:T(8,128)(2,1)S(1)} %stash.5.refs_0_, bf16[64,2304]{1,0:T(8,128)(2,1)S(1)} %collective-permute-done.2.refs_1_, bf16[64,2304]{1,0:T(8,128)(2,1)S(1)} %collective-permute-done.5.refs_2_, bf16[64,2304]{1,0:T(8,128)(2,1)S(1)} %collective-permute-done.4.refs_3_, ...), custom_call_target="tpu_custom_call" | custom-call | flops 998244352 | bytes 2228224 | tf_op jit(solution)/shard_map/score/pallas_call | solution.py:249
  43.1 2.0 %collective-permute-done.10.refs_7_.refs_3_ = bf16[64,2048]{1,0:T(8,128)(2,1)S(1)} collective-permute-done((bf16[64,2048]{1,0:T(8,128)(2,1)S(1)}, bf16[64,2048]{1,0:T(8,128)(2,1)S(1)}, u32[]{:S(2)}, u32[]{:S(2)}) %collective-permute-start.10) | collective-permute-done | bytes 262176 | tf_op jit(solution)/shard_map/ppermute | solution.py:330
  45.1 1.2 %collective-permute-done.11.refs_6_.refs_2_ = bf16[64,2048]{1,0:T(8,128)(2,1)S(1)} collective-permute-done((bf16[64,2048]{1,0:T(8,128)(2,1)S(1)}, bf16[64,2048]{1,0:T(8,128)(2,1)S(1)}, u32[]{:S(2)}, u32[]{:S(2)}) %collective-permute-start.11) | collective-permute-done | bytes 262176 | tf_op jit(solution)/shard_map/ppermute | solution.py:330
  46.3 1.6 %collective-permute-start.16 = (bf16[64,2048]{1,0:T(8,128)(2,1)S(1)}, bf16[64,2048]{1,0:T(8,128)(2,1)S(1)}, u32[]{:S(2)}, u32[]{:S(2)}) collective-permute-start(bf16[64,2048]{1,0:T(8,128)(2,1)S(1)} %collective-permute-done.11.refs_6_.refs_2_), channel_id=1, source_target_pairs={{0,4},{2,6},{4,8},{6,10},{8,12},{10,14},{12,0},{14,2},{1,5},{3,7},... | collective-permute-start | bytes 786440 | tf_op jit(solution)/shard_map/ppermute | solution.py:330
  47.8 0.2 collective-permute-done.12.refs_8_.refs_1_
  48.1 1.1 %score.6 = (f32[7,32,256]{2,1,0:T(8,128)S(1)}, f32[7,32,256]{2,1,0:T(8,128)S(1)}) custom-call(s32[1]{0:T(128)} %bitcast.1.half_ref, bf16[256,2304]{1,0:T(8,128)(2,1)S(1)} %stash.5.refs_0_, bf16[64,2304]{1,0:T(8,128)(2,1)S(1)} %collective-permute-done.2.refs_1_, bf16[64,2304]{1,0:T(8,128)(2,1)S(1)} %collective-permute-done.5.refs_2_, ...), custom_call_target="tpu_custom_call" | custom-call | flops 880803840 | bytes 1966080 | tf_op jit(solution)/shard_map/score/pallas_call | solution.py:249
  49.2 0.1 collective-permute-start.13
  49.2 0.7 %score.7 = (f32[7,32,256]{2,1,0:T(8,128)S(1)}, f32[7,32,256]{2,1,0:T(8,128)S(1)}) custom-call(s32[1]{0:T(128)} %bitcast.1.half_ref, bf16[256,2048]{1,0:T(8,128)(2,1)S(1)} %stash.7.refs_4_.refs_0_, bf16[64,2048]{1,0:T(8,128)(2,1)S(1)} %collective-permute-done.8.refs_5_.refs_1_, bf16[64,2048]{1,0:T(8,128)(2,1)S(1)} %collective-permute-done.11.refs_6_.refs_2_, ...), custom_call_target="tpu_custom_call" | custom-call | flops 998244352 | bytes 2228224 | tf_op jit(solution)/shard_map/score/pallas_call | solution.py:249
  49.9 0.6 collective-permute-start.15
  50.5 0.2 collective-permute-done.13.b_ref
  50.7 1.8 %collective-permute-start.14 = (f32[7,32,256]{2,1,0:T(8,128)S(1)}, f32[7,32,256]{2,1,0:T(8,128)S(1)}, u32[]{:S(2)}, u32[]{:S(2)}) collective-permute-start(f32[7,32,256]{2,1,0:T(8,128)S(1)} %add.81), channel_id=1, source_target_pairs={{0,16},{16,0},{1,17},{17,1},{2,18},{18,2},{3,19},{19,3},{4,20},{20... | collective-permute-start | bytes 688136 | tf_op jit(solution)/shard_map/ppermute | solution.py:375
  52.6 0.0 collective-permute-done.17.refs_0_
  52.6 0.8 %score.8 = (f32[64,256]{1,0:T(8,128)S(1)}, f32[64,256]{1,0:T(8,128)S(1)}) custom-call(s32[1]{0:T(128)} %bitcast.1.half_ref, bf16[64,2304]{1,0:T(8,128)(2,1)S(1)} %collective-permute-done.17.refs_0_, bf16[256,3840]{1,0:T(8,128)(2,1)S(1)} %collective-permute-done.12.refs_8_.refs_1_, bf16[256,4352]{1,0:T(8,128)(2,1)S(1)} %scale_codes.1.refs_4_.refs_2_), custom_call_target="tpu_custom_call" | custom-call | flops 268435456 | bytes 1966080 | tf_op jit(solution)/shard_map/score/pallas_call | solution.py:249
  53.4 1.1 %collective-permute-done.16.refs_0_ = bf16[64,2048]{1,0:T(8,128)(2,1)S(1)} collective-permute-done((bf16[64,2048]{1,0:T(8,128)(2,1)S(1)}, bf16[64,2048]{1,0:T(8,128)(2,1)S(1)}, u32[]{:S(2)}, u32[]{:S(2)}) %collective-permute-start.16) | collective-permute-done | bytes 262176 | tf_op jit(solution)/shard_map/ppermute | solution.py:330
  54.4 0.0 copy-start
  54.4 0.7 %score.9 = (f32[1,32,256]{2,1,0:T(8,128)S(1)}, f32[1,32,256]{2,1,0:T(8,128)S(1)}, f32[1,32,256]{2,1,0:T(8,128)S(1)}, f32[1,32,256]{2,1,0:T(8,128)S(1)}) custom-call(s32[1]{0:T(128)} %bitcast.1.half_ref, bf16[64,2048]{1,0:T(8,128)(2,1)S(1)} %collective-permute-done.16.refs_0_, bf16[256,3840]{1,0:T(8,128)(2,1)S(1)} %collective-permute-done.12.refs_8_.refs_1_, ...), custom_call_target="tpu_custom_call" | custom-call | flops 8053063680 | bytes 1966080 | tf_op jit(solution)/shard_map/score/pallas_call | solution.py:249
  55.1 0.1 collective-permute-start.18
  55.2 0.5 collective-permute-start.20
  55.7 0.7 %collective-permute-done.18.b_ref = f32[1,32,256]{2,1,0:T(8,128)S(1)} collective-permute-done((f32[1,32,256]{2,1,0:T(8,128)S(1)}, f32[1,32,256]{2,1,0:T(8,128)S(1)}, u32[]{:S(2)}, u32[]{:S(2)}) %collective-permute-start.18) | collective-permute-done | bytes 32800 | tf_op jit(solution)/shard_map/ppermute | solution.py:370
  56.4 0.5 collective-permute-start.19
  56.9 0.0 collective-permute-done.15
  56.9 0.0 collective-permute-done.20
  56.9 3.4 %collective-permute-done.19 = f32[1,32,256]{2,1,0:T(8,128)S(1)} collective-permute-done((f32[1,32,256]{2,1,0:T(8,128)S(1)}, f32[1,32,256]{2,1,0:T(8,128)S(1)}, u32[]{:S(2)}, u32[]{:S(2)}) %collective-permute-start.19) | collective-permute-done | bytes 32800 | tf_op jit(solution)/shard_map/ppermute | solution.py:383
  60.3 0.0 collective-permute-done.14
  60.3 0.0 copy-done
  60.3 1.6 %place_scores.1 = f32[8,32,256]{2,1,0:T(8,128)} custom-call(s32[8]{0:T(128)S(1)} %stack.35.order_ref, s32[1,256]{1,0:T(1,128)S(1)} %copy-done, f32[224,256]{1,0:T(8,128)S(1)} %bitcast.19, f32[224,256]{1,0:T(8,128)S(1)} %bitcast.17, f32[224,256]{1,0:T(8,128)S(1)} %bitcast.18, f32[32,256]{1,0:T(8,128)S(1)} %bitcast.22, f32[32,256]{1,0:T(8,128)S(1)} %bitcast.20, ...), custom_call_target="tpu_custom_call" | custom-call | tf_op jit(solution)/shard_map/place_scores/pallas_call | solution.py:297
  (6 shorter events, 0.2 us)
Async XLA Ops:
  2.2 45.9 %collective-permute-start.12 = (bf16[256,3840]{1,0:T(8,128)(2,1)S(1)}, bf16[256,3840]{1,0:T(8,128)(2,1)S(1)}, u32[]{:S(2)}, u32[]{:S(2)}) collective-permute-start(bf16[256,3840]{1,0:T(8,128)(2,1)S(1)} %get-tuple-element.75), channel_id=1, source_target_pairs={{0,16},{16,0},{1,17},{17,1},{2,18},{18,2},{3,19},{19,3},{4,20},{20... | collective-permute-start | bytes 5898248 | tf_op jit(solution)/shard_map/ppermute | solution.py:341
  5.2 11.7 %collective-permute-start = (bf16[64,2304]{1,0:T(8,128)(2,1)S(1)}, bf16[64,2304]{1,0:T(8,128)(2,1)S(1)}, u32[]{:S(2)}, u32[]{:S(2)}) collective-permute-start(bf16[64,2304]{1,0:T(8,128)(2,1)S(1)} %get-tuple-element.52.refs_0_), channel_id=1, source_target_pairs={{0,4},{2,6},{4,8},{6,10},{8,12},{10,14},{12,0},{14,2},{1,5},{3,7},... | collective-permute-start | bytes 884744 | tf_op jit(solution)/shard_map/ppermute | solution.py:330
  6.8 10.2 %collective-permute-start.1 = (bf16[64,2304]{1,0:T(8,128)(2,1)S(1)}, bf16[64,2304]{1,0:T(8,128)(2,1)S(1)}, u32[]{:S(2)}, u32[]{:S(2)}) collective-permute-start(bf16[64,2304]{1,0:T(8,128)(2,1)S(1)} %get-tuple-element.52.refs_0_), channel_id=1, source_target_pairs={{0,2},{2,0},{4,6},{6,4},{8,10},{10,8},{12,14},{14,12},{1,3},{3,1},... | collective-permute-start | bytes 884744 | tf_op jit(solution)/shard_map/ppermute | solution.py:330
  8.3 14.3 %collective-permute-start.6 = (bf16[64,2048]{1,0:T(8,128)(2,1)S(1)}, bf16[64,2048]{1,0:T(8,128)(2,1)S(1)}, u32[]{:S(2)}, u32[]{:S(2)}) collective-permute-start(bf16[64,2048]{1,0:T(8,128)(2,1)S(1)} %get-tuple-element.64.refs_0_), channel_id=1, source_target_pairs={{0,4},{2,6},{4,8},{6,10},{8,12},{10,14},{12,0},{14,2},{1,5},{3,7},... | collective-permute-start | bytes 786440 | tf_op jit(solution)/shard_map/ppermute | solution.py:330
  9.9 12.7 %collective-permute-start.7 = (bf16[64,2048]{1,0:T(8,128)(2,1)S(1)}, bf16[64,2048]{1,0:T(8,128)(2,1)S(1)}, u32[]{:S(2)}, u32[]{:S(2)}) collective-permute-start(bf16[64,2048]{1,0:T(8,128)(2,1)S(1)} %get-tuple-element.64.refs_0_), channel_id=1, source_target_pairs={{0,2},{2,0},{4,6},{6,4},{8,10},{10,8},{12,14},{14,12},{1,3},{3,1},... | collective-permute-start | bytes 786440 | tf_op jit(solution)/shard_map/ppermute | solution.py:330
  17.0 11.9 %collective-permute-start.2 = (bf16[64,2304]{1,0:T(8,128)(2,1)S(1)}, bf16[64,2304]{1,0:T(8,128)(2,1)S(1)}, u32[]{:S(2)}, u32[]{:S(2)}) collective-permute-start(bf16[64,2304]{1,0:T(8,128)(2,1)S(1)} %collective-permute-done.refs_1_), channel_id=1, source_target_pairs={{0,4},{2,6},{4,8},{6,10},{8,12},{10,14},{12,0},{14,2},{1,5},{3,7},... | collective-permute-start | bytes 884744 | tf_op jit(solution)/shard_map/ppermute | solution.py:330
  18.3 10.6 %collective-permute-start.3 = (bf16[64,2304]{1,0:T(8,128)(2,1)S(1)}, bf16[64,2304]{1,0:T(8,128)(2,1)S(1)}, u32[]{:S(2)}, u32[]{:S(2)}) collective-permute-start(bf16[64,2304]{1,0:T(8,128)(2,1)S(1)} %collective-permute-done.refs_1_), channel_id=1, source_target_pairs={{0,2},{2,0},{4,6},{6,4},{8,10},{10,8},{12,14},{14,12},{1,3},{3,1},... | collective-permute-start | bytes 884744 | tf_op jit(solution)/shard_map/ppermute | solution.py:330
  22.6 11.9 %collective-permute-start.8 = (bf16[64,2048]{1,0:T(8,128)(2,1)S(1)}, bf16[64,2048]{1,0:T(8,128)(2,1)S(1)}, u32[]{:S(2)}, u32[]{:S(2)}) collective-permute-start(bf16[64,2048]{1,0:T(8,128)(2,1)S(1)} %collective-permute-done.6.refs_1_), channel_id=1, source_target_pairs={{0,4},{2,6},{4,8},{6,10},{8,12},{10,14},{12,0},{14,2},{1,5},{3,7},... | collective-permute-start | bytes 786440 | tf_op jit(solution)/shard_map/ppermute | solution.py:330
  24.0 10.6 %collective-permute-start.9 = (bf16[64,2048]{1,0:T(8,128)(2,1)S(1)}, bf16[64,2048]{1,0:T(8,128)(2,1)S(1)}, u32[]{:S(2)}, u32[]{:S(2)}) collective-permute-start(bf16[64,2048]{1,0:T(8,128)(2,1)S(1)} %collective-permute-done.6.refs_1_), channel_id=1, source_target_pairs={{0,2},{2,0},{4,6},{6,4},{8,10},{10,8},{12,14},{14,12},{1,3},{3,1},... | collective-permute-start | bytes 786440 | tf_op jit(solution)/shard_map/ppermute | solution.py:330
  28.9 11.9 %collective-permute-start.4 = (bf16[64,2304]{1,0:T(8,128)(2,1)S(1)}, bf16[64,2304]{1,0:T(8,128)(2,1)S(1)}, u32[]{:S(2)}, u32[]{:S(2)}) collective-permute-start(bf16[64,2304]{1,0:T(8,128)(2,1)S(1)} %collective-permute-done.2.refs_1_), channel_id=1, source_target_pairs={{0,4},{2,6},{4,8},{6,10},{8,12},{10,14},{12,0},{14,2},{1,5},{3,7},... | collective-permute-start | bytes 884744 | tf_op jit(solution)/shard_map/ppermute | solution.py:330
  30.3 10.6 %collective-permute-start.5 = (bf16[64,2304]{1,0:T(8,128)(2,1)S(1)}, bf16[64,2304]{1,0:T(8,128)(2,1)S(1)}, u32[]{:S(2)}, u32[]{:S(2)}) collective-permute-start(bf16[64,2304]{1,0:T(8,128)(2,1)S(1)} %collective-permute-done.2.refs_1_), channel_id=1, source_target_pairs={{0,2},{2,0},{4,6},{6,4},{8,10},{10,8},{12,14},{14,12},{1,3},{3,1},... | collective-permute-start | bytes 884744 | tf_op jit(solution)/shard_map/ppermute | solution.py:330
  34.5 10.5 %collective-permute-start.10 = (bf16[64,2048]{1,0:T(8,128)(2,1)S(1)}, bf16[64,2048]{1,0:T(8,128)(2,1)S(1)}, u32[]{:S(2)}, u32[]{:S(2)}) collective-permute-start(bf16[64,2048]{1,0:T(8,128)(2,1)S(1)} %collective-permute-done.8.refs_5_.refs_1_), channel_id=1, source_target_pairs={{0,4},{2,6},{4,8},{6,10},{8,12},{10,14},{12,0},{14,2},{1,5},{3,7},... | collective-permute-start | bytes 786440 | tf_op jit(solution)/shard_map/ppermute | solution.py:330
  35.9 10.4 %collective-permute-start.11 = (bf16[64,2048]{1,0:T(8,128)(2,1)S(1)}, bf16[64,2048]{1,0:T(8,128)(2,1)S(1)}, u32[]{:S(2)}, u32[]{:S(2)}) collective-permute-start(bf16[64,2048]{1,0:T(8,128)(2,1)S(1)} %collective-permute-done.8.refs_5_.refs_1_), channel_id=1, source_target_pairs={{0,2},{2,0},{4,6},{6,4},{8,10},{10,8},{12,14},{14,12},{1,3},{3,1},... | collective-permute-start | bytes 786440 | tf_op jit(solution)/shard_map/ppermute | solution.py:330
  40.8 11.7 %collective-permute-start.17 = (bf16[64,2304]{1,0:T(8,128)(2,1)S(1)}, bf16[64,2304]{1,0:T(8,128)(2,1)S(1)}, u32[]{:S(2)}, u32[]{:S(2)}) collective-permute-start(bf16[64,2304]{1,0:T(8,128)(2,1)S(1)} %collective-permute-done.4.refs_3_), channel_id=1, source_target_pairs={{0,2},{2,0},{4,6},{6,4},{8,10},{10,8},{12,14},{14,12},{1,3},{3,1},... | collective-permute-start | bytes 884744 | tf_op jit(solution)/shard_map/ppermute | solution.py:330
  46.3 8.2 %collective-permute-start.16 = (bf16[64,2048]{1,0:T(8,128)(2,1)S(1)}, bf16[64,2048]{1,0:T(8,128)(2,1)S(1)}, u32[]{:S(2)}, u32[]{:S(2)}) collective-permute-start(bf16[64,2048]{1,0:T(8,128)(2,1)S(1)} %collective-permute-done.11.refs_6_.refs_2_), channel_id=1, source_target_pairs={{0,4},{2,6},{4,8},{6,10},{8,12},{10,14},{12,0},{14,2},{1,5},{3,7},... | collective-permute-start | bytes 786440 | tf_op jit(solution)/shard_map/ppermute | solution.py:330
  49.2 1.6 %collective-permute-start.13 = (f32[7,32,256]{2,1,0:T(8,128)S(1)}, f32[7,32,256]{2,1,0:T(8,128)S(1)}, u32[]{:S(2)}, u32[]{:S(2)}) collective-permute-start(f32[7,32,256]{2,1,0:T(8,128)S(1)} %get-tuple-element.77), channel_id=1, source_target_pairs={{0,1},{1,0},{2,3},{3,2},{4,5},{5,4},{6,7},{7,6},{8,9},{9,8},{10,11... | collective-permute-start | bytes 688136 | tf_op jit(solution)/shard_map/ppermute | solution.py:370
  49.9 7.0 %collective-permute-start.15 = (f32[7,32,256]{2,1,0:T(8,128)S(1)}, f32[7,32,256]{2,1,0:T(8,128)S(1)}, u32[]{:S(2)}, u32[]{:S(2)}) collective-permute-start(f32[7,32,256]{2,1,0:T(8,128)S(1)} %get-tuple-element.81), channel_id=1, source_target_pairs={{0,1},{1,0},{2,3},{3,2},{4,5},{5,4},{6,7},{7,6},{8,9},{9,8},{10,11... | collective-permute-start | bytes 688136 | tf_op jit(solution)/shard_map/ppermute | solution.py:370
  50.7 9.6 %collective-permute-start.14 = (f32[7,32,256]{2,1,0:T(8,128)S(1)}, f32[7,32,256]{2,1,0:T(8,128)S(1)}, u32[]{:S(2)}, u32[]{:S(2)}) collective-permute-start(f32[7,32,256]{2,1,0:T(8,128)S(1)} %add.81), channel_id=1, source_target_pairs={{0,16},{16,0},{1,17},{17,1},{2,18},{18,2},{3,19},{19,3},{4,20},{20... | collective-permute-start | bytes 688136 | tf_op jit(solution)/shard_map/ppermute | solution.py:375
  54.4 5.9 %copy-start = (s32[1,256]{1,0:T(1,128)S(1)}, s32[1,256]{1,0:T(1,128)}, u32[]{:S(2)}) copy-start(s32[1,256]{1,0:T(1,128)} %ids_ref.1) | copy-start | bytes 3076
  55.1 1.3 %collective-permute-start.18 = (f32[1,32,256]{2,1,0:T(8,128)S(1)}, f32[1,32,256]{2,1,0:T(8,128)S(1)}, u32[]{:S(2)}, u32[]{:S(2)}) collective-permute-start(f32[1,32,256]{2,1,0:T(8,128)S(1)} %get-tuple-element.86), channel_id=1, source_target_pairs={{0,1},{1,0},{2,3},{3,2},{4,5},{5,4},{6,7},{7,6},{8,9},{9,8},{10,11... | collective-permute-start | bytes 98312 | tf_op jit(solution)/shard_map/ppermute | solution.py:370
  55.2 1.7 %collective-permute-start.20 = (f32[1,32,256]{2,1,0:T(8,128)S(1)}, f32[1,32,256]{2,1,0:T(8,128)S(1)}, u32[]{:S(2)}, u32[]{:S(2)}) collective-permute-start(f32[1,32,256]{2,1,0:T(8,128)S(1)} %get-tuple-element.88), channel_id=1, source_target_pairs={{0,1},{1,0},{2,3},{3,2},{4,5},{5,4},{6,7},{7,6},{8,9},{9,8},{10,11... | collective-permute-start | bytes 98312 | tf_op jit(solution)/shard_map/ppermute | solution.py:370
  56.4 3.9 %collective-permute-start.19 = (f32[1,32,256]{2,1,0:T(8,128)S(1)}, f32[1,32,256]{2,1,0:T(8,128)S(1)}, u32[]{:S(2)}, u32[]{:S(2)}) collective-permute-start(f32[1,32,256]{2,1,0:T(8,128)S(1)} %add.82), channel_id=1, source_target_pairs={{0,16},{16,0},{1,17},{17,1},{2,18},{18,2},{3,19},{19,3},{4,20},{20... | collective-permute-start | bytes 98312 | tf_op jit(solution)/shard_map/ppermute | solution.py:383

commit v14 on v13

--- a/solution.py
+++ b/solution.py
@@ -43,7 +43,7 @@
 
 
 def scaled(codes, scales, at):
-    return codes * scales[:, at : at + 1].astype(jnp.bfloat16)
+    return codes * scales[:, at : at + 1]
 
 
 def scales_of(exponents):
@@ -52,7 +52,7 @@
 
 def by_example(scales):
     pad = jnp.zeros((-scales.shape[0] % 8, scales.shape[1]), scales.dtype)
-    return jnp.concatenate([scales, pad], axis=0).T
+    return jnp.concatenate([scales, pad], axis=0).T.astype(jnp.bfloat16)
 
 
 def scale_tiles(codes_ref, begin, buffer, sems, scales, order, out_ref):
@@ -115,7 +115,7 @@
     rows = queries.shape[1]
     count = codes.shape[0]
     wide = alone * BLOCK
-    tile = min(count, 64)
+    tile = min(count, 32)
     chunks = len(cuts) - 1
     return pl.pallas_call(
         functools.partial(cut_kernel, alone, cuts),

time: 62 us -> 62.8 us (1.013)
  Pallas kernels: 10.4 us -> 11.1 us
    pallas_call x1, Pallas kernels: 2.12 us -> 2.83 us  [cut(): pl.pallas_call(functools.partial(cut_kernel, alone, cuts), out_shape=[plt...]
where the time goes in v14:
time: 62.8 us; the launch traced here: 62.6 us
  starting transfers between devices  26.2 us (42%)
  waiting for transfers between devices  25 us (40%)
  Pallas kernels  11.1 us (18%)
    ppermute x14, waiting for transfers between devices, step(): return lax.ppermute(value, 'ex', pairs)  20.5 us
    ppermute x14, starting transfers between devices, step(): return lax.ppermute(value, 'ex', pairs)  19.7 us
    pallas_call x5, Pallas kernels, score(): pl.pallas_call(functools.partial(score_kernel, [len(arrays) for arrays in...  3.98 us
    ppermute x1, waiting for transfers between devices, shards(): given = lax.ppermute(add(their_keep, over_dim(their_send)), 'groups', swap)  3.4 us
    ppermute x1, starting transfers between devices, shards(): theirs = lax.ppermute(sent, 'groups', swap)  3.03 us
    pallas_call x1, Pallas kernels, cut(): pl.pallas_call(functools.partial(cut_kernel, alone, cuts), out_shape=[plt...  2.83 us
    pallas_call x1, Pallas kernels, scale(): pl.pallas_call(functools.partial(scale_kernel, alone), out_shape=pltpu.VM...  2.55 us
    ppermute x1, starting transfers between devices, shards(): given = lax.ppermute(added, 'groups', swap)  1.8 us
  transfers between devices with their start and end apart: 21, of which 12 were waited for; matrix products, arithmetic and copies ran while one was open for 0% of the time, Pallas kernels for 11%

profile of v14, /device:TPU:0, one launch (start us, length us, event | category | flops | bytes accessed | tf_op | source)
XLA Modules:
  0.0 62.6 jit_solution(18027712933089845521)
XLA Ops:
  0.0 0.1 stack.35.order_ref
  0.1 2.8 %cut_queries.1 = (bf16[64,2304]{1,0:T(8,128)(2,1)S(1)}, bf16[64,2048]{1,0:T(8,128)(2,1)S(1)}, bf16[256,3840]{1,0:T(8,128)(2,1)S(1)}) custom-call(s32[1]{0:T(128)} %bitcast.part_ref, bf16[1,64,8192]{2,1,0:T(8,128)(2,1)} %queries_ref.1, bf16[256,8192]{1,0:T(8,128)(2,1)} %codes_ref.3, s32[64,256]{1,0:T(8,128)} %bitcast.23), custom_call_target="tpu_custom_call" | custom-call | flops 2097152 | bytes 4194304 | tf_op jit(solution)/shard_map/cut_queries/pallas_call | solution.py:120
  2.9 3.0 %collective-permute-start.12 = (bf16[256,3840]{1,0:T(8,128)(2,1)S(1)}, bf16[256,3840]{1,0:T(8,128)(2,1)S(1)}, u32[]{:S(2)}, u32[]{:S(2)}) collective-permute-start(bf16[256,3840]{1,0:T(8,128)(2,1)S(1)} %get-tuple-element.75), channel_id=1, source_target_pairs={{0,16},{16,0},{1,17},{17,1},{2,18},{18,2},{3,19},{19,3},{4,20},{20... | collective-permute-start | bytes 5898248 | tf_op jit(solution)/shard_map/ppermute | solution.py:341
  6.0 1.6 %collective-permute-start = (bf16[64,2304]{1,0:T(8,128)(2,1)S(1)}, bf16[64,2304]{1,0:T(8,128)(2,1)S(1)}, u32[]{:S(2)}, u32[]{:S(2)}) collective-permute-start(bf16[64,2304]{1,0:T(8,128)(2,1)S(1)} %get-tuple-element.52.refs_0_), channel_id=1, source_target_pairs={{0,4},{2,6},{4,8},{6,10},{8,12},{10,14},{12,0},{14,2},{1,5},{3,7},... | collective-permute-start | bytes 884744 | tf_op jit(solution)/shard_map/ppermute | solution.py:330
  7.5 1.5 %collective-permute-start.1 = (bf16[64,2304]{1,0:T(8,128)(2,1)S(1)}, bf16[64,2304]{1,0:T(8,128)(2,1)S(1)}, u32[]{:S(2)}, u32[]{:S(2)}) collective-permute-start(bf16[64,2304]{1,0:T(8,128)(2,1)S(1)} %get-tuple-element.52.refs_0_), channel_id=1, source_target_pairs={{0,2},{2,0},{4,6},{6,4},{8,10},{10,8},{12,14},{14,12},{1,3},{3,1},... | collective-permute-start | bytes 884744 | tf_op jit(solution)/shard_map/ppermute | solution.py:330
  9.0 1.6 %collective-permute-start.6 = (bf16[64,2048]{1,0:T(8,128)(2,1)S(1)}, bf16[64,2048]{1,0:T(8,128)(2,1)S(1)}, u32[]{:S(2)}, u32[]{:S(2)}) collective-permute-start(bf16[64,2048]{1,0:T(8,128)(2,1)S(1)} %get-tuple-element.64.refs_0_), channel_id=1, source_target_pairs={{0,4},{2,6},{4,8},{6,10},{8,12},{10,14},{12,0},{14,2},{1,5},{3,7},... | collective-permute-start | bytes 786440 | tf_op jit(solution)/shard_map/ppermute | solution.py:330
  10.6 0.5 collective-permute-start.7
  11.1 2.6 %scale_codes.1.refs_4_.refs_2_ = bf16[256,4352]{1,0:T(8,128)(2,1)S(1)} custom-call(s32[1]{0:T(128)} %bitcast.part_ref, bf16[256,8192]{1,0:T(8,128)(2,1)} %codes_ref.3, s32[64,256]{1,0:T(8,128)} %bitcast.24), custom_call_target="tpu_custom_call" | custom-call | flops 2097152 | bytes 8388608 | tf_op jit(solution)/shard_map/scale_codes/pallas_call | solution.py:158
  13.7 4.0 %collective-permute-done.refs_1_ = bf16[64,2304]{1,0:T(8,128)(2,1)S(1)} collective-permute-done((bf16[64,2304]{1,0:T(8,128)(2,1)S(1)}, bf16[64,2304]{1,0:T(8,128)(2,1)S(1)}, u32[]{:S(2)}, u32[]{:S(2)}) %collective-permute-start) | collective-permute-done | bytes 294944 | tf_op jit(solution)/shard_map/ppermute | solution.py:330
  17.7 0.0 collective-permute-done.1.refs_1_
  17.7 1.4 %collective-permute-start.2 = (bf16[64,2304]{1,0:T(8,128)(2,1)S(1)}, bf16[64,2304]{1,0:T(8,128)(2,1)S(1)}, u32[]{:S(2)}, u32[]{:S(2)}) collective-permute-start(bf16[64,2304]{1,0:T(8,128)(2,1)S(1)} %collective-permute-done.refs_1_), channel_id=1, source_target_pairs={{0,4},{2,6},{4,8},{6,10},{8,12},{10,14},{12,0},{14,2},{1,5},{3,7},... | collective-permute-start | bytes 884744 | tf_op jit(solution)/shard_map/ppermute | solution.py:330
  19.1 1.5 %collective-permute-start.3 = (bf16[64,2304]{1,0:T(8,128)(2,1)S(1)}, bf16[64,2304]{1,0:T(8,128)(2,1)S(1)}, u32[]{:S(2)}, u32[]{:S(2)}) collective-permute-start(bf16[64,2304]{1,0:T(8,128)(2,1)S(1)} %collective-permute-done.refs_1_), channel_id=1, source_target_pairs={{0,2},{2,0},{4,6},{6,4},{8,10},{10,8},{12,14},{14,12},{1,3},{3,1},... | collective-permute-start | bytes 884744 | tf_op jit(solution)/shard_map/ppermute | solution.py:330
  20.5 2.7 %collective-permute-done.6.refs_1_ = bf16[64,2048]{1,0:T(8,128)(2,1)S(1)} collective-permute-done((bf16[64,2048]{1,0:T(8,128)(2,1)S(1)}, bf16[64,2048]{1,0:T(8,128)(2,1)S(1)}, u32[]{:S(2)}, u32[]{:S(2)}) %collective-permute-start.6) | collective-permute-done | bytes 262176 | tf_op jit(solution)/shard_map/ppermute | solution.py:330
  23.3 0.0 collective-permute-done.7.refs_1_
  23.3 1.4 %collective-permute-start.8 = (bf16[64,2048]{1,0:T(8,128)(2,1)S(1)}, bf16[64,2048]{1,0:T(8,128)(2,1)S(1)}, u32[]{:S(2)}, u32[]{:S(2)}) collective-permute-start(bf16[64,2048]{1,0:T(8,128)(2,1)S(1)} %collective-permute-done.6.refs_1_), channel_id=1, source_target_pairs={{0,4},{2,6},{4,8},{6,10},{8,12},{10,14},{12,0},{14,2},{1,5},{3,7},... | collective-permute-start | bytes 786440 | tf_op jit(solution)/shard_map/ppermute | solution.py:330
  24.7 1.5 %collective-permute-start.9 = (bf16[64,2048]{1,0:T(8,128)(2,1)S(1)}, bf16[64,2048]{1,0:T(8,128)(2,1)S(1)}, u32[]{:S(2)}, u32[]{:S(2)}) collective-permute-start(bf16[64,2048]{1,0:T(8,128)(2,1)S(1)} %collective-permute-done.6.refs_1_), channel_id=1, source_target_pairs={{0,2},{2,0},{4,6},{6,4},{8,10},{10,8},{12,14},{14,12},{1,3},{3,1},... | collective-permute-start | bytes 786440 | tf_op jit(solution)/shard_map/ppermute | solution.py:330
  26.2 3.4 %collective-permute-done.2.refs_1_ = bf16[64,2304]{1,0:T(8,128)(2,1)S(1)} collective-permute-done((bf16[64,2304]{1,0:T(8,128)(2,1)S(1)}, bf16[64,2304]{1,0:T(8,128)(2,1)S(1)}, u32[]{:S(2)}, u32[]{:S(2)}) %collective-permute-start.2) | collective-permute-done | bytes 294944 | tf_op jit(solution)/shard_map/ppermute | solution.py:330
  29.6 0.0 collective-permute-done.3.refs_2_
  29.6 1.4 %collective-permute-start.4 = (bf16[64,2304]{1,0:T(8,128)(2,1)S(1)}, bf16[64,2304]{1,0:T(8,128)(2,1)S(1)}, u32[]{:S(2)}, u32[]{:S(2)}) collective-permute-start(bf16[64,2304]{1,0:T(8,128)(2,1)S(1)} %collective-permute-done.2.refs_1_), channel_id=1, source_target_pairs={{0,4},{2,6},{4,8},{6,10},{8,12},{10,14},{12,0},{14,2},{1,5},{3,7},... | collective-permute-start | bytes 884744 | tf_op jit(solution)/shard_map/ppermute | solution.py:330
  31.0 1.5 %collective-permute-start.5 = (bf16[64,2304]{1,0:T(8,128)(2,1)S(1)}, bf16[64,2304]{1,0:T(8,128)(2,1)S(1)}, u32[]{:S(2)}, u32[]{:S(2)}) collective-permute-start(bf16[64,2304]{1,0:T(8,128)(2,1)S(1)} %collective-permute-done.2.refs_1_), channel_id=1, source_target_pairs={{0,2},{2,0},{4,6},{6,4},{8,10},{10,8},{12,14},{14,12},{1,3},{3,1},... | collective-permute-start | bytes 884744 | tf_op jit(solution)/shard_map/ppermute | solution.py:330
  32.5 2.7 %collective-permute-done.8.refs_5_.refs_1_ = bf16[64,2048]{1,0:T(8,128)(2,1)S(1)} collective-permute-done((bf16[64,2048]{1,0:T(8,128)(2,1)S(1)}, bf16[64,2048]{1,0:T(8,128)(2,1)S(1)}, u32[]{:S(2)}, u32[]{:S(2)}) %collective-permute-start.8) | collective-permute-done | bytes 262176 | tf_op jit(solution)/shard_map/ppermute | solution.py:330
  35.2 0.0 collective-permute-done.9.refs_2_
  35.2 1.4 %collective-permute-start.10 = (bf16[64,2048]{1,0:T(8,128)(2,1)S(1)}, bf16[64,2048]{1,0:T(8,128)(2,1)S(1)}, u32[]{:S(2)}, u32[]{:S(2)}) collective-permute-start(bf16[64,2048]{1,0:T(8,128)(2,1)S(1)} %collective-permute-done.8.refs_5_.refs_1_), channel_id=1, source_target_pairs={{0,4},{2,6},{4,8},{6,10},{8,12},{10,14},{12,0},{14,2},{1,5},{3,7},... | collective-permute-start | bytes 786440 | tf_op jit(solution)/shard_map/ppermute | solution.py:330
  36.6 1.5 %collective-permute-start.11 = (bf16[64,2048]{1,0:T(8,128)(2,1)S(1)}, bf16[64,2048]{1,0:T(8,128)(2,1)S(1)}, u32[]{:S(2)}, u32[]{:S(2)}) collective-permute-start(bf16[64,2048]{1,0:T(8,128)(2,1)S(1)} %collective-permute-done.8.refs_5_.refs_1_), channel_id=1, source_target_pairs={{0,2},{2,0},{4,6},{6,4},{8,10},{10,8},{12,14},{14,12},{1,3},{3,1},... | collective-permute-start | bytes 786440 | tf_op jit(solution)/shard_map/ppermute | solution.py:330
  38.2 3.4 %collective-permute-done.4.refs_3_ = bf16[64,2304]{1,0:T(8,128)(2,1)S(1)} collective-permute-done((bf16[64,2304]{1,0:T(8,128)(2,1)S(1)}, bf16[64,2304]{1,0:T(8,128)(2,1)S(1)}, u32[]{:S(2)}, u32[]{:S(2)}) %collective-permute-start.4) | collective-permute-done | bytes 294944 | tf_op jit(solution)/shard_map/ppermute | solution.py:330
  41.6 0.0 collective-permute-done.5.refs_2_
  41.6 1.5 %collective-permute-start.17 = (bf16[64,2304]{1,0:T(8,128)(2,1)S(1)}, bf16[64,2304]{1,0:T(8,128)(2,1)S(1)}, u32[]{:S(2)}, u32[]{:S(2)}) collective-permute-start(bf16[64,2304]{1,0:T(8,128)(2,1)S(1)} %collective-permute-done.4.refs_3_), channel_id=1, source_target_pairs={{0,2},{2,0},{4,6},{6,4},{8,10},{10,8},{12,14},{14,12},{1,3},{3,1},... | collective-permute-start | bytes 884744 | tf_op jit(solution)/shard_map/ppermute | solution.py:330
  43.0 0.7 %score.5.refs_5_ = f32[448,256]{1,0:T(8,128)S(1)} custom-call(s32[1]{0:T(128)} %bitcast.1.half_ref, bf16[256,2304]{1,0:T(8,128)(2,1)S(1)} %stash.5.refs_0_, bf16[64,2304]{1,0:T(8,128)(2,1)S(1)} %collective-permute-done.2.refs_1_, bf16[64,2304]{1,0:T(8,128)(2,1)S(1)} %collective-permute-done.5.refs_2_, bf16[64,2304]{1,0:T(8,128)(2,1)S(1)} %collective-permute-done.4.refs_3_, ...), custom_call_target="tpu_custom_call" | custom-call | flops 998244352 | bytes 2228224 | tf_op jit(solution)/shard_map/score/pallas_call | solution.py:249
  43.8 2.0 %collective-permute-done.10.refs_7_.refs_3_ = bf16[64,2048]{1,0:T(8,128)(2,1)S(1)} collective-permute-done((bf16[64,2048]{1,0:T(8,128)(2,1)S(1)}, bf16[64,2048]{1,0:T(8,128)(2,1)S(1)}, u32[]{:S(2)}, u32[]{:S(2)}) %collective-permute-start.10) | collective-permute-done | bytes 262176 | tf_op jit(solution)/shard_map/ppermute | solution.py:330
  45.8 1.2 %collective-permute-done.11.refs_6_.refs_2_ = bf16[64,2048]{1,0:T(8,128)(2,1)S(1)} collective-permute-done((bf16[64,2048]{1,0:T(8,128)(2,1)S(1)}, bf16[64,2048]{1,0:T(8,128)(2,1)S(1)}, u32[]{:S(2)}, u32[]{:S(2)}) %collective-permute-start.11) | collective-permute-done | bytes 262176 | tf_op jit(solution)/shard_map/ppermute | solution.py:330
  47.0 1.6 %collective-permute-start.16 = (bf16[64,2048]{1,0:T(8,128)(2,1)S(1)}, bf16[64,2048]{1,0:T(8,128)(2,1)S(1)}, u32[]{:S(2)}, u32[]{:S(2)}) collective-permute-start(bf16[64,2048]{1,0:T(8,128)(2,1)S(1)} %collective-permute-done.11.refs_6_.refs_2_), channel_id=1, source_target_pairs={{0,4},{2,6},{4,8},{6,10},{8,12},{10,14},{12,0},{14,2},{1,5},{3,7},... | collective-permute-start | bytes 786440 | tf_op jit(solution)/shard_map/ppermute | solution.py:330
  48.5 0.2 collective-permute-done.12.refs_8_.refs_1_
  48.8 1.1 %score.6 = (f32[7,32,256]{2,1,0:T(8,128)S(1)}, f32[7,32,256]{2,1,0:T(8,128)S(1)}) custom-call(s32[1]{0:T(128)} %bitcast.1.half_ref, bf16[256,2304]{1,0:T(8,128)(2,1)S(1)} %stash.5.refs_0_, bf16[64,2304]{1,0:T(8,128)(2,1)S(1)} %collective-permute-done.2.refs_1_, bf16[64,2304]{1,0:T(8,128)(2,1)S(1)} %collective-permute-done.5.refs_2_, ...), custom_call_target="tpu_custom_call" | custom-call | flops 880803840 | bytes 1966080 | tf_op jit(solution)/shard_map/score/pallas_call | solution.py:249
  49.9 0.1 collective-permute-start.13
  49.9 0.7 %score.7 = (f32[7,32,256]{2,1,0:T(8,128)S(1)}, f32[7,32,256]{2,1,0:T(8,128)S(1)}) custom-call(s32[1]{0:T(128)} %bitcast.1.half_ref, bf16[256,2048]{1,0:T(8,128)(2,1)S(1)} %stash.7.refs_4_.refs_0_, bf16[64,2048]{1,0:T(8,128)(2,1)S(1)} %collective-permute-done.8.refs_5_.refs_1_, bf16[64,2048]{1,0:T(8,128)(2,1)S(1)} %collective-permute-done.11.refs_6_.refs_2_, ...), custom_call_target="tpu_custom_call" | custom-call | flops 998244352 | bytes 2228224 | tf_op jit(solution)/shard_map/score/pallas_call | solution.py:249
  50.6 0.6 collective-permute-start.15
  51.2 0.2 collective-permute-done.13.b_ref
  51.5 1.8 %collective-permute-start.14 = (f32[7,32,256]{2,1,0:T(8,128)S(1)}, f32[7,32,256]{2,1,0:T(8,128)S(1)}, u32[]{:S(2)}, u32[]{:S(2)}) collective-permute-start(f32[7,32,256]{2,1,0:T(8,128)S(1)} %add.81), channel_id=1, source_target_pairs={{0,16},{16,0},{1,17},{17,1},{2,18},{18,2},{3,19},{19,3},{4,20},{20... | collective-permute-start | bytes 688136 | tf_op jit(solution)/shard_map/ppermute | solution.py:375
  53.3 0.0 collective-permute-done.17.refs_0_
  53.3 0.8 %score.8 = (f32[64,256]{1,0:T(8,128)S(1)}, f32[64,256]{1,0:T(8,128)S(1)}) custom-call(s32[1]{0:T(128)} %bitcast.1.half_ref, bf16[64,2304]{1,0:T(8,128)(2,1)S(1)} %collective-permute-done.17.refs_0_, bf16[256,3840]{1,0:T(8,128)(2,1)S(1)} %collective-permute-done.12.refs_8_.refs_1_, bf16[256,4352]{1,0:T(8,128)(2,1)S(1)} %scale_codes.1.refs_4_.refs_2_), custom_call_target="tpu_custom_call" | custom-call | flops 268435456 | bytes 1966080 | tf_op jit(solution)/shard_map/score/pallas_call | solution.py:249
  54.1 1.1 %collective-permute-done.16.refs_0_ = bf16[64,2048]{1,0:T(8,128)(2,1)S(1)} collective-permute-done((bf16[64,2048]{1,0:T(8,128)(2,1)S(1)}, bf16[64,2048]{1,0:T(8,128)(2,1)S(1)}, u32[]{:S(2)}, u32[]{:S(2)}) %collective-permute-start.16) | collective-permute-done | bytes 262176 | tf_op jit(solution)/shard_map/ppermute | solution.py:330
  55.1 0.0 copy-start
  55.1 0.7 %score.9 = (f32[1,32,256]{2,1,0:T(8,128)S(1)}, f32[1,32,256]{2,1,0:T(8,128)S(1)}, f32[1,32,256]{2,1,0:T(8,128)S(1)}, f32[1,32,256]{2,1,0:T(8,128)S(1)}) custom-call(s32[1]{0:T(128)} %bitcast.1.half_ref, bf16[64,2048]{1,0:T(8,128)(2,1)S(1)} %collective-permute-done.16.refs_0_, bf16[256,3840]{1,0:T(8,128)(2,1)S(1)} %collective-permute-done.12.refs_8_.refs_1_, ...), custom_call_target="tpu_custom_call" | custom-call | flops 8053063680 | bytes 1966080 | tf_op jit(solution)/shard_map/score/pallas_call | solution.py:249
  55.8 0.1 collective-permute-start.18
  55.9 0.5 collective-permute-start.20
  56.4 0.7 %collective-permute-done.18.b_ref = f32[1,32,256]{2,1,0:T(8,128)S(1)} collective-permute-done((f32[1,32,256]{2,1,0:T(8,128)S(1)}, f32[1,32,256]{2,1,0:T(8,128)S(1)}, u32[]{:S(2)}, u32[]{:S(2)}) %collective-permute-start.18) | collective-permute-done | bytes 32800 | tf_op jit(solution)/shard_map/ppermute | solution.py:370
  57.1 0.5 collective-permute-start.19
  57.6 0.0 collective-permute-done.15
  57.6 0.0 collective-permute-done.20
  57.6 3.4 %collective-permute-done.19 = f32[1,32,256]{2,1,0:T(8,128)S(1)} collective-permute-done((f32[1,32,256]{2,1,0:T(8,128)S(1)}, f32[1,32,256]{2,1,0:T(8,128)S(1)}, u32[]{:S(2)}, u32[]{:S(2)}) %collective-permute-start.19) | collective-permute-done | bytes 32800 | tf_op jit(solution)/shard_map/ppermute | solution.py:383
  61.0 0.0 collective-permute-done.14
  61.0 0.0 copy-done
  61.0 1.6 %place_scores.1 = f32[8,32,256]{2,1,0:T(8,128)} custom-call(s32[8]{0:T(128)S(1)} %stack.35.order_ref, s32[1,256]{1,0:T(1,128)S(1)} %copy-done, f32[224,256]{1,0:T(8,128)S(1)} %bitcast.19, f32[224,256]{1,0:T(8,128)S(1)} %bitcast.17, f32[224,256]{1,0:T(8,128)S(1)} %bitcast.18, f32[32,256]{1,0:T(8,128)S(1)} %bitcast.22, f32[32,256]{1,0:T(8,128)S(1)} %bitcast.20, ...), custom_call_target="tpu_custom_call" | custom-call | tf_op jit(solution)/shard_map/place_scores/pallas_call | solution.py:297
  (6 shorter events, 0.2 us)
Async XLA Ops:
  2.9 45.9 %collective-permute-start.12 = (bf16[256,3840]{1,0:T(8,128)(2,1)S(1)}, bf16[256,3840]{1,0:T(8,128)(2,1)S(1)}, u32[]{:S(2)}, u32[]{:S(2)}) collective-permute-start(bf16[256,3840]{1,0:T(8,128)(2,1)S(1)} %get-tuple-element.75), channel_id=1, source_target_pairs={{0,16},{16,0},{1,17},{17,1},{2,18},{18,2},{3,19},{19,3},{4,20},{20... | collective-permute-start | bytes 5898248 | tf_op jit(solution)/shard_map/ppermute | solution.py:341
  6.0 11.7 %collective-permute-start = (bf16[64,2304]{1,0:T(8,128)(2,1)S(1)}, bf16[64,2304]{1,0:T(8,128)(2,1)S(1)}, u32[]{:S(2)}, u32[]{:S(2)}) collective-permute-start(bf16[64,2304]{1,0:T(8,128)(2,1)S(1)} %get-tuple-element.52.refs_0_), channel_id=1, source_target_pairs={{0,4},{2,6},{4,8},{6,10},{8,12},{10,14},{12,0},{14,2},{1,5},{3,7},... | collective-permute-start | bytes 884744 | tf_op jit(solution)/shard_map/ppermute | solution.py:330
  7.5 10.2 %collective-permute-start.1 = (bf16[64,2304]{1,0:T(8,128)(2,1)S(1)}, bf16[64,2304]{1,0:T(8,128)(2,1)S(1)}, u32[]{:S(2)}, u32[]{:S(2)}) collective-permute-start(bf16[64,2304]{1,0:T(8,128)(2,1)S(1)} %get-tuple-element.52.refs_0_), channel_id=1, source_target_pairs={{0,2},{2,0},{4,6},{6,4},{8,10},{10,8},{12,14},{14,12},{1,3},{3,1},... | collective-permute-start | bytes 884744 | tf_op jit(solution)/shard_map/ppermute | solution.py:330
  9.0 14.3 %collective-permute-start.6 = (bf16[64,2048]{1,0:T(8,128)(2,1)S(1)}, bf16[64,2048]{1,0:T(8,128)(2,1)S(1)}, u32[]{:S(2)}, u32[]{:S(2)}) collective-permute-start(bf16[64,2048]{1,0:T(8,128)(2,1)S(1)} %get-tuple-element.64.refs_0_), channel_id=1, source_target_pairs={{0,4},{2,6},{4,8},{6,10},{8,12},{10,14},{12,0},{14,2},{1,5},{3,7},... | collective-permute-start | bytes 786440 | tf_op jit(solution)/shard_map/ppermute | solution.py:330
  10.6 12.7 %collective-permute-start.7 = (bf16[64,2048]{1,0:T(8,128)(2,1)S(1)}, bf16[64,2048]{1,0:T(8,128)(2,1)S(1)}, u32[]{:S(2)}, u32[]{:S(2)}) collective-permute-start(bf16[64,2048]{1,0:T(8,128)(2,1)S(1)} %get-tuple-element.64.refs_0_), channel_id=1, source_target_pairs={{0,2},{2,0},{4,6},{6,4},{8,10},{10,8},{12,14},{14,12},{1,3},{3,1},... | collective-permute-start | bytes 786440 | tf_op jit(solution)/shard_map/ppermute | solution.py:330
  17.7 11.9 %collective-permute-start.2 = (bf16[64,2304]{1,0:T(8,128)(2,1)S(1)}, bf16[64,2304]{1,0:T(8,128)(2,1)S(1)}, u32[]{:S(2)}, u32[]{:S(2)}) collective-permute-start(bf16[64,2304]{1,0:T(8,128)(2,1)S(1)} %collective-permute-done.refs_1_), channel_id=1, source_target_pairs={{0,4},{2,6},{4,8},{6,10},{8,12},{10,14},{12,0},{14,2},{1,5},{3,7},... | collective-permute-start | bytes 884744 | tf_op jit(solution)/shard_map/ppermute | solution.py:330
  19.1 10.6 %collective-permute-start.3 = (bf16[64,2304]{1,0:T(8,128)(2,1)S(1)}, bf16[64,2304]{1,0:T(8,128)(2,1)S(1)}, u32[]{:S(2)}, u32[]{:S(2)}) collective-permute-start(bf16[64,2304]{1,0:T(8,128)(2,1)S(1)} %collective-permute-done.refs_1_), channel_id=1, source_target_pairs={{0,2},{2,0},{4,6},{6,4},{8,10},{10,8},{12,14},{14,12},{1,3},{3,1},... | collective-permute-start | bytes 884744 | tf_op jit(solution)/shard_map/ppermute | solution.py:330
  23.3 11.9 %collective-permute-start.8 = (bf16[64,2048]{1,0:T(8,128)(2,1)S(1)}, bf16[64,2048]{1,0:T(8,128)(2,1)S(1)}, u32[]{:S(2)}, u32[]{:S(2)}) collective-permute-start(bf16[64,2048]{1,0:T(8,128)(2,1)S(1)} %collective-permute-done.6.refs_1_), channel_id=1, source_target_pairs={{0,4},{2,6},{4,8},{6,10},{8,12},{10,14},{12,0},{14,2},{1,5},{3,7},... | collective-permute-start | bytes 786440 | tf_op jit(solution)/shard_map/ppermute | solution.py:330
  24.7 10.6 %collective-permute-start.9 = (bf16[64,2048]{1,0:T(8,128)(2,1)S(1)}, bf16[64,2048]{1,0:T(8,128)(2,1)S(1)}, u32[]{:S(2)}, u32[]{:S(2)}) collective-permute-start(bf16[64,2048]{1,0:T(8,128)(2,1)S(1)} %collective-permute-done.6.refs_1_), channel_id=1, source_target_pairs={{0,2},{2,0},{4,6},{6,4},{8,10},{10,8},{12,14},{14,12},{1,3},{3,1},... | collective-permute-start | bytes 786440 | tf_op jit(solution)/shard_map/ppermute | solution.py:330
  29.6 11.9 %collective-permute-start.4 = (bf16[64,2304]{1,0:T(8,128)(2,1)S(1)}, bf16[64,2304]{1,0:T(8,128)(2,1)S(1)}, u32[]{:S(2)}, u32[]{:S(2)}) collective-permute-start(bf16[64,2304]{1,0:T(8,128)(2,1)S(1)} %collective-permute-done.2.refs_1_), channel_id=1, source_target_pairs={{0,4},{2,6},{4,8},{6,10},{8,12},{10,14},{12,0},{14,2},{1,5},{3,7},... | collective-permute-start | bytes 884744 | tf_op jit(solution)/shard_map/ppermute | solution.py:330
  31.0 10.6 %collective-permute-start.5 = (bf16[64,2304]{1,0:T(8,128)(2,1)S(1)}, bf16[64,2304]{1,0:T(8,128)(2,1)S(1)}, u32[]{:S(2)}, u32[]{:S(2)}) collective-permute-start(bf16[64,2304]{1,0:T(8,128)(2,1)S(1)} %collective-permute-done.2.refs_1_), channel_id=1, source_target_pairs={{0,2},{2,0},{4,6},{6,4},{8,10},{10,8},{12,14},{14,12},{1,3},{3,1},... | collective-permute-start | bytes 884744 | tf_op jit(solution)/shard_map/ppermute | solution.py:330
  35.2 10.5 %collective-permute-start.10 = (bf16[64,2048]{1,0:T(8,128)(2,1)S(1)}, bf16[64,2048]{1,0:T(8,128)(2,1)S(1)}, u32[]{:S(2)}, u32[]{:S(2)}) collective-permute-start(bf16[64,2048]{1,0:T(8,128)(2,1)S(1)} %collective-permute-done.8.refs_5_.refs_1_), channel_id=1, source_target_pairs={{0,4},{2,6},{4,8},{6,10},{8,12},{10,14},{12,0},{14,2},{1,5},{3,7},... | collective-permute-start | bytes 786440 | tf_op jit(solution)/shard_map/ppermute | solution.py:330
  36.6 10.4 %collective-permute-start.11 = (bf16[64,2048]{1,0:T(8,128)(2,1)S(1)}, bf16[64,2048]{1,0:T(8,128)(2,1)S(1)}, u32[]{:S(2)}, u32[]{:S(2)}) collective-permute-start(bf16[64,2048]{1,0:T(8,128)(2,1)S(1)} %collective-permute-done.8.refs_5_.refs_1_), channel_id=1, source_target_pairs={{0,2},{2,0},{4,6},{6,4},{8,10},{10,8},{12,14},{14,12},{1,3},{3,1},... | collective-permute-start | bytes 786440 | tf_op jit(solution)/shard_map/ppermute | solution.py:330
  41.6 11.7 %collective-permute-start.17 = (bf16[64,2304]{1,0:T(8,128)(2,1)S(1)}, bf16[64,2304]{1,0:T(8,128)(2,1)S(1)}, u32[]{:S(2)}, u32[]{:S(2)}) collective-permute-start(bf16[64,2304]{1,0:T(8,128)(2,1)S(1)} %collective-permute-done.4.refs_3_), channel_id=1, source_target_pairs={{0,2},{2,0},{4,6},{6,4},{8,10},{10,8},{12,14},{14,12},{1,3},{3,1},... | collective-permute-start | bytes 884744 | tf_op jit(solution)/shard_map/ppermute | solution.py:330
  47.0 8.2 %collective-permute-start.16 = (bf16[64,2048]{1,0:T(8,128)(2,1)S(1)}, bf16[64,2048]{1,0:T(8,128)(2,1)S(1)}, u32[]{:S(2)}, u32[]{:S(2)}) collective-permute-start(bf16[64,2048]{1,0:T(8,128)(2,1)S(1)} %collective-permute-done.11.refs_6_.refs_2_), channel_id=1, source_target_pairs={{0,4},{2,6},{4,8},{6,10},{8,12},{10,14},{12,0},{14,2},{1,5},{3,7},... | collective-permute-start | bytes 786440 | tf_op jit(solution)/shard_map/ppermute | solution.py:330
  49.9 1.6 %collective-permute-start.13 = (f32[7,32,256]{2,1,0:T(8,128)S(1)}, f32[7,32,256]{2,1,0:T(8,128)S(1)}, u32[]{:S(2)}, u32[]{:S(2)}) collective-permute-start(f32[7,32,256]{2,1,0:T(8,128)S(1)} %get-tuple-element.77), channel_id=1, source_target_pairs={{0,1},{1,0},{2,3},{3,2},{4,5},{5,4},{6,7},{7,6},{8,9},{9,8},{10,11... | collective-permute-start | bytes 688136 | tf_op jit(solution)/shard_map/ppermute | solution.py:370
  50.6 7.0 %collective-permute-start.15 = (f32[7,32,256]{2,1,0:T(8,128)S(1)}, f32[7,32,256]{2,1,0:T(8,128)S(1)}, u32[]{:S(2)}, u32[]{:S(2)}) collective-permute-start(f32[7,32,256]{2,1,0:T(8,128)S(1)} %get-tuple-element.81), channel_id=1, source_target_pairs={{0,1},{1,0},{2,3},{3,2},{4,5},{5,4},{6,7},{7,6},{8,9},{9,8},{10,11... | collective-permute-start | bytes 688136 | tf_op jit(solution)/shard_map/ppermute | solution.py:370
  51.5 9.6 %collective-permute-start.14 = (f32[7,32,256]{2,1,0:T(8,128)S(1)}, f32[7,32,256]{2,1,0:T(8,128)S(1)}, u32[]{:S(2)}, u32[]{:S(2)}) collective-permute-start(f32[7,32,256]{2,1,0:T(8,128)S(1)} %add.81), channel_id=1, source_target_pairs={{0,16},{16,0},{1,17},{17,1},{2,18},{18,2},{3,19},{19,3},{4,20},{20... | collective-permute-start | bytes 688136 | tf_op jit(solution)/shard_map/ppermute | solution.py:375
  55.1 5.9 %copy-start = (s32[1,256]{1,0:T(1,128)S(1)}, s32[1,256]{1,0:T(1,128)}, u32[]{:S(2)}) copy-start(s32[1,256]{1,0:T(1,128)} %ids_ref.1) | copy-start | bytes 3076
  55.8 1.3 %collective-permute-start.18 = (f32[1,32,256]{2,1,0:T(8,128)S(1)}, f32[1,32,256]{2,1,0:T(8,128)S(1)}, u32[]{:S(2)}, u32[]{:S(2)}) collective-permute-start(f32[1,32,256]{2,1,0:T(8,128)S(1)} %get-tuple-element.86), channel_id=1, source_target_pairs={{0,1},{1,0},{2,3},{3,2},{4,5},{5,4},{6,7},{7,6},{8,9},{9,8},{10,11... | collective-permute-start | bytes 98312 | tf_op jit(solution)/shard_map/ppermute | solution.py:370
  55.9 1.7 %collective-permute-start.20 = (f32[1,32,256]{2,1,0:T(8,128)S(1)}, f32[1,32,256]{2,1,0:T(8,128)S(1)}, u32[]{:S(2)}, u32[]{:S(2)}) collective-permute-start(f32[1,32,256]{2,1,0:T(8,128)S(1)} %get-tuple-element.88), channel_id=1, source_target_pairs={{0,1},{1,0},{2,3},{3,2},{4,5},{5,4},{6,7},{7,6},{8,9},{9,8},{10,11... | collective-permute-start | bytes 98312 | tf_op jit(solution)/shard_map/ppermute | solution.py:370
  57.1 3.9 %collective-permute-start.19 = (f32[1,32,256]{2,1,0:T(8,128)S(1)}, f32[1,32,256]{2,1,0:T(8,128)S(1)}, u32[]{:S(2)}, u32[]{:S(2)}) collective-permute-start(f32[1,32,256]{2,1,0:T(8,128)S(1)} %add.82), channel_id=1, source_target_pairs={{0,16},{16,0},{1,17},{17,1},{2,18},{18,2},{3,19},{19,3},{4,20},{20... | collective-permute-start | bytes 98312 | tf_op jit(solution)/shard_map/ppermute | solution.py:383
